TPU v7x, 128 devices: a whole 4x4x4 slice. The times are simulated.
128 devices in a mesh: dp: 4 (over z), vocab: 32 (over x, y, core).
Axes of the slice: x: 4, y: 4, z: 4, core: 2. Of those that a mesh axis runs over, the one named last changes fastest.
Arguments:
- input_grad: bfloat16 [65536, 4608], P(('dp', 'vocab')), may hold values from -6 to 6
- token_slab: int32 [65536, 1], P('dp'), may hold values from 0 to 31; in each aligned block of 512 rows (0 to 511, 512 to 1023, ...) at most 32 rows name the same one
- token_offset: int32 [65536, 1], P('dp'), may hold values from 0 to 383
- head_grad: bfloat16 [4, 12288, 4608], P('dp', 'vocab'), may hold values from -6 to 6
- master: float32 [12288, 4608], P(('vocab', 'dp')), may hold values from -0.15625 to 0.15625
- moment_one: float32 [12288, 4608], P(('vocab', 'dp')), may hold values from -4 to 4
- moment_two: float32 [12288, 4608], P(('vocab', 'dp')), may hold values from 0.01 to 1
Outputs:
- master_out: float32 [12288, 4608], P(('vocab', 'dp'))
- moment_one_out: float32 [12288, 4608], P(('vocab', 'dp'))
- moment_two_out: float32 [12288, 4608], P(('vocab', 'dp'))
- table_out: bfloat16 [12288, 4608], P('vocab')
Inputs may be any that keep to these rules, and one draw needn't show every extreme that they name: `token_slab`: in each aligned block of 512 rows (one sequence owner's tokens), no slab is named by more than 32 rows.
All inputs are finite; a program needn't handle non-finite values.
Results may differ from a plain program's by a relative error of at most 0.011.
Values may be sent and summed in bfloat16 or wider, within the bound.
No kernel may reach another device: no remote copies, remote signals or barrier semaphores. Data moves between devices by JAX's collectives and lax.ppermute only.
A program may use at most 128 MiB of HBM per device.

v0:
```python
import jax
import jax.numpy as jnp
from jax import lax
from jax.sharding import PartitionSpec as P

beta_first = 0.9
beta_second = 0.95
learn_rate = 0.01
weight_decay = 0.1
epsilon = 1e-08
correct_first = 1.0 - 0.9**10
correct_second = 1.0 - 0.95**10


def local(input_grad, token_slab, token_offset, head_grad, master, moment_one, moment_two):
    peers = lax.axis_size("vocab")
    myself = lax.axis_index("vocab")
    tok_rows = input_grad.shape[0]
    slab_rows = head_grad.shape[1]
    capacity = 2 * tok_rows // peers
    owners = token_slab[:, 0].reshape(peers, tok_rows)
    offsets = token_offset[:, 0].reshape(peers, tok_rows)
    owner_hits = owners[:, :, None] == jnp.arange(peers, dtype=jnp.int32)[None, None, :]
    running = jnp.cumsum(owner_hits.astype(jnp.int32), axis=1) - 1
    rank_of = jnp.sum(jnp.where(owner_hits, running, 0), axis=2)
    own_owner = lax.dynamic_index_in_dim(owners, myself, 0, keepdims=False)
    own_rank = lax.dynamic_index_in_dim(rank_of, myself, 0, keepdims=False)
    slot_of = own_owner * capacity + own_rank
    slot_ids = jnp.arange(peers * capacity, dtype=jnp.int32)
    picked = slot_ids[:, None] == slot_of[None, :]
    source = jnp.sum(jnp.where(picked, jnp.arange(tok_rows, dtype=jnp.int32)[None, :], 0), axis=1)
    filled = jnp.any(picked, axis=1)
    outgoing = jnp.where(
        filled[:, None], jnp.take(input_grad, source, axis=0), jnp.zeros((), jnp.bfloat16)
    )
    arrived = lax.all_to_all(outgoing, "vocab", split_axis=0, concat_axis=0, tiled=True)
    mine = owners == myself
    slot_hit = mine[:, :, None] & (
        rank_of[:, :, None] == jnp.arange(capacity, dtype=jnp.int32)[None, None, :]
    )
    target = jnp.sum(jnp.where(slot_hit, offsets[:, :, None], 0), axis=1)
    present = jnp.any(slot_hit, axis=1)
    target = jnp.where(present, target, -1).reshape(-1)
    scatter_table = (jnp.arange(slab_rows, dtype=jnp.int32)[:, None] == target[None, :]).astype(
        jnp.bfloat16
    )
    head_local = head_grad[0]
    head_sum = lax.psum_scatter(
        head_local.astype(jnp.float32).astype(jnp.bfloat16), "dp", scatter_dimension=0, tiled=True
    ).astype(jnp.float32)
    embed_sum = lax.psum_scatter(
        jnp.dot(scatter_table, arrived, preferred_element_type=jnp.float32),
        "dp",
        scatter_dimension=0,
        tiled=True,
    )
    grad = head_sum + embed_sum
    first = beta_first * moment_one + (1.0 - beta_first) * grad
    second = beta_second * moment_two + (1.0 - beta_second) * grad * grad
    step_dir = (
        first / correct_first / (jnp.sqrt(second / correct_second) + epsilon)
        + weight_decay * master
    )
    updated = master - learn_rate * step_dir
    table_out = lax.all_gather(updated.astype(jnp.bfloat16), "dp", axis=0, tiled=True)
    return (updated, first, second, table_out)


def solution(mesh):
    placed = (
        P(("dp", "vocab"), None),
        P("dp", None),
        P("dp", None),
        P("dp", "vocab", None),
        P(("vocab", "dp"), None),
        P(("vocab", "dp"), None),
        P(("vocab", "dp"), None),
    )
    return jax.shard_map(
        local,
        mesh=mesh,
        in_specs=placed,
        out_specs=(
            P(("vocab", "dp"), None),
            P(("vocab", "dp"), None),
            P(("vocab", "dp"), None),
            P("vocab", None),
        ),
        check_vma=False,
    )
```

profile of v0, /device:TPU:0, one launch (start us, length us, event | category | flops | bytes accessed | tf_op | source)
XLA Modules:
  0.0 403.9 jit_solution(3413353211278589550)
XLA Ops:
  7.2 0.5 broadcast.83
  7.7 1.6 reduce.6
  9.3 2.5 fusion.3
  11.8 64.4 %reduce-window.6 = s32[32,32,4,128]{3,1,2,0:T(8,128)S(1)} reduce-window(s32[32,32,4,128]{3,1,2,0:T(8,128)} %fusion.3, s32[]{:T(128)} %constant.19.clone.1), window={size=1x1x1x128 pad=0_0x0_0x0_0x127_0}, to_apply=%region_1.2 | reduce-window | flops 66584576 | bytes 4194308 | tf_op jit(solution)/shard_map/reduce-window
  76.2 1.9 slice.10
  78.1 2.4 copy.14
  80.5 0.1 fusion.9
  80.7 0.7 fusion.1
  81.5 0.3 select_reduce_fusion
  81.8 0.3 fusion.2
  82.1 0.1 reduce_sum.34
  82.2 0.1 broadcast_in_dim.69
  82.3 20.0 %gather_fusion = bf16[1024,4608]{1,0:T(8,128)(2,1)} fusion(bf16[512,4608]{1,0:T(8,128)(2,1)} %param.7, s32[1024]{0:T(1024)S(1)} %broadcast_clamp_fusion), kind=kCustom, calls=%fused_computation | custom fusion | bytes 18878464 | tf_op jit(solution)/shard_map/jit(_take)/gather | solution.py:34
  102.3 8.5 %select_select_fusion = bf16[32,32,4608]{2,1,0:T(8,128)(2,1)} fusion(bf16[32,32,4608]{2,1,0:T(8,128)(2,1)} %bitcast.28, pred[32,32]{1,0:T(8,128)(4,1)S(1)} %compare_and_fusion, pred[32,32]{1,0:T(8,128)(4,1)S(1)} %broadcast_in_dim.69), kind=kLoop, calls=%fused_computation.1 | loop fusion | flops 9437184 | bytes 18876416 | tf_op jit(solution)/shard_map/jit(_where)/select_n | solution.py:33
  110.8 7.5 %all-to-all-start = ((bf16[32,32,4608]{2,1,0:T(8,128)(2,1)}), bf16[32,32,4608]{2,1,0:T(8,128)(2,1)}, u32[]{:S(2)}, u32[]{:S(2)}) async-start(bf16[32,32,4608]{2,1,0:T(8,128)(2,1)} %select_select_fusion), calls=%async_computation.1 | async-start | bytes 18874368 | tf_op jit(solution)/shard_map/all_to_all | solution.py:36
  118.3 0.0 copy-start.2
  118.3 0.0 reduce-scatter.3.cloned.1.call-start
  118.4 0.7 reduce-scatter.3.cloned.1.call-update
  119.1 0.0 reduce-scatter.5.cloned.1.call-start
  119.1 0.0 copy-done.2
  119.1 0.8 reduce.7
  120.0 0.6 fusion.5
  120.6 0.6 select_reduce_fusion.1
  121.3 0.1 select_n.58
  121.4 125.6 %all-to-all-done = bf16[32,32,4608]{2,1,0:T(8,128)(2,1)} async-done(((bf16[32,32,4608]{2,1,0:T(8,128)(2,1)}), bf16[32,32,4608]{2,1,0:T(8,128)(2,1)}, u32[]{:S(2)}, u32[]{:S(2)}) %all-to-all-start) | async-done | bytes 9437216 | tf_op jit(solution)/shard_map/all_to_all | solution.py:36
  247.0 9.4 %fusion.7 = f32[384,4608]{1,0:T(8,128)} fusion(bf16[1024,4608]{1,0:T(8,128)(2,1)} %bitcast.8, s32[1024]{0:T(1024)S(1)} %select_n.58), kind=kOutput, calls=%fused_computation.22 | convolution fusion | flops 3624271872 | bytes 16519168 | tf_op jit(solution)/shard_map/dot_general | solution.py:52
  256.4 0.0 copy-start
  256.4 0.0 copy-start.1
  256.4 0.0 reduce-scatter.5.cloned.1.call-update
  256.4 0.0 all-gather.2.cloned.1.call-start
  256.5 0.0 reduce-scatter.3.cloned.1.call-done
  256.5 88.1 %reduce-scatter.5.cloned.1.call-done = f32[96,4608]{1,0:T(8,128)} async-done(((f32[384,4608]{1,0:T(8,128)}), f32[96,4608]{1,0:T(8,128)}) %reduce-scatter.5.cloned.1.call-update) | async-done | bytes 1769488 | tf_op jit(solution)/shard_map/reduce_scatter | solution.py:51
  344.6 0.0 copy-done
  344.6 0.0 copy-done.1
  344.6 5.9 %fusion.11 = (bf16[96,4608]{1,0:T(8,128)(2,1)}, f32[96,4608]{1,0:T(8,128)}, f32[96,4608]{1,0:T(8,128)}, f32[96,4608]{1,0:T(8,128)}) fusion(f32[96,4608]{1,0:T(8,128)S(1)} %copy-done, f32[96,4608]{1,0:T(8,128)} %reduce-scatter.5.cloned.1.call-done, bf16[96,4608]{1,0:T(8,128)(2,1)} %reduce-scatter.3.cloned.1.call-done, f32[96,4608]{1,0:T(8,128)S(1)} %copy-done.1, ...), kind=kLoop, calls=%fused_computation.33 | loop fusion | flops 7962624 | bytes 14155776 | tf_op jit(solution)/shard_map/convert_element_type | solution.py:65
  350.5 0.0 all-gather.2.cloned.1.call-update
  350.5 42.8 %all-gather.2.cloned.1.call-done = bf16[384,4608]{1,0:T(8,128)(2,1)} async-done(((bf16[96,4608]{1,0:T(8,128)(2,1)}), bf16[384,4608]{1,0:T(8,128)(2,1)}) %all-gather.2.cloned.1.call-update) | async-done | bytes 3538960 | tf_op jit(solution)/shard_map/all_gather | solution.py:65
  393.3 4.0 copy.20
  (10 shorter events, 0.1 us)
Async XLA Ops:
  110.8 136.2 %all-to-all-start = ((bf16[32,32,4608]{2,1,0:T(8,128)(2,1)}), bf16[32,32,4608]{2,1,0:T(8,128)(2,1)}, u32[]{:S(2)}, u32[]{:S(2)}) async-start(bf16[32,32,4608]{2,1,0:T(8,128)(2,1)} %select_select_fusion), calls=%async_computation.1 | async-start | bytes 18874368 | tf_op jit(solution)/shard_map/all_to_all | solution.py:36
  118.3 0.8 copy-start.2
  118.3 138.2 %reduce-scatter.3.cloned.1.call-start = ((), (), s32[]{:S(2)}) async-start(), calls=%async_computation.3 | async-start | bytes 4423680 | tf_op jit(solution)/shard_map/reduce_scatter | solution.py:48
  119.1 225.6 %reduce-scatter.5.cloned.1.call-start = ((), (), s32[]{:S(2)}) async-start(), calls=%async_computation.4 | async-start | bytes 8847360 | tf_op jit(solution)/shard_map/reduce_scatter | solution.py:51
  256.4 88.2 %copy-start = (f32[96,4608]{1,0:T(8,128)S(1)}, f32[96,4608]{1,0:T(8,128)}, u32[]{:S(2)}) copy-start(f32[96,4608]{1,0:T(8,128)} %param.11) | copy-start | bytes 5308420
  256.4 88.2 %copy-start.1 = (f32[96,4608]{1,0:T(8,128)S(1)}, f32[96,4608]{1,0:T(8,128)}, u32[]{:S(2)}) copy-start(f32[96,4608]{1,0:T(8,128)} %param.12) | copy-start | bytes 5308420
  256.4 136.9 %all-gather.2.cloned.1.call-start = ((), (), s32[]{:S(2)}) async-start(), calls=%async_computation.5 | async-start | bytes 4423680 | tf_op jit(solution)/shard_map/all_gather | solution.py:65
Sparse Core Ops, SparseCore 0:
  121.6 44.0 reduce-scatter.2
  256.6 88.0 reduce-scatter.4
  350.7 42.6 all-gather.1
where the time goes:
time: 410 us; the launch traced here: 404 us
  waiting for transfers between devices  257 us (63%)
  other arithmetic  86.5 us (21%)
  local copies, waits for them, and re-layouts  29.2 us (7%)
  between operations  13.9 us (3%)
  matrix products  9.43 us (2%)
  starting transfers between devices  7.64 us (2%)
    all_to_all x1, waiting for transfers between devices, local(): lax.all_to_all(outgoing, 'vocab', split_axis=0, concat_axis=0, tiled=True)  126 us
    reduce_scatter x1, waiting for transfers between devices, local(): lax.psum_scatter(jnp.dot(scatter_table, arrived, preferred_element_type=j...  88.1 us
    another operation x2, other arithmetic  64.5 us
    all_gather x1, waiting for transfers between devices, local(): lax.all_gather(updated.astype(jnp.bfloat16), 'dp', axis=0, tiled=True)  42.8 us
    gather x1, local copies, waits for them, and re-layouts, local(): jnp.take(input_grad, source, axis=0)  20 us
    dot_general x1, matrix products, local(): jnp.dot(scatter_table, arrived, preferred_element_type=jnp.float32)  9.43 us
    select_n x1, other arithmetic, local(): jnp.where(filled[:, None], jnp.take(input_grad, source, axis=0), jnp.zero...  8.53 us
  transfers between devices with their start and end apart: 4, of which 3 were waited for; matrix products, arithmetic and copies ran while one was open for 3% of the time, Pallas kernels for 0%

commit v1 on v0

v1 whole, which is shorter than its diff:
```python
import jax
import jax.numpy as jnp
from jax import lax
from jax.sharding import PartitionSpec as P

beta_first = 0.9
beta_second = 0.95
learn_rate = 0.01
weight_decay = 0.1
epsilon = 1e-08
correct_first = 1.0 - 0.9**10
correct_second = 1.0 - 0.95**10

CHUNKS = 4


def update(grad, master, moment_one, moment_two):
    first = beta_first * moment_one + (1.0 - beta_first) * grad
    second = beta_second * moment_two + (1.0 - beta_second) * grad * grad
    step_dir = (
        first / correct_first / (jnp.sqrt(second / correct_second) + epsilon)
        + weight_decay * master
    )
    return master - learn_rate * step_dir, first, second


def local(input_grad, token_slab, token_offset, head_grad, master, moment_one, moment_two):
    peers = lax.axis_size("vocab")
    groups = lax.axis_size("dp")
    myself = lax.axis_index("vocab")
    tok_rows, width = input_grad.shape
    slab_rows = head_grad.shape[1]
    capacity = 2 * tok_rows // peers
    slots = peers * capacity
    owners = token_slab[:, 0].reshape(peers, tok_rows)
    offsets = token_offset[:, 0].reshape(peers, tok_rows)

    place = jnp.arange(tok_rows, dtype=jnp.int32)
    earlier = (place[:, None] < place[None, :]).astype(jnp.bfloat16)

    own = lax.dynamic_index_in_dim(owners, myself, 0, keepdims=False)
    named = own[None, :] == jnp.arange(peers, dtype=jnp.int32)[:, None]
    before = jnp.dot(named.astype(jnp.bfloat16), earlier, preferred_element_type=jnp.float32)
    own_rank = jnp.sum(jnp.where(named, before, 0.0), axis=0).astype(jnp.int32)
    slot_of = own * capacity + own_rank
    dispatch = (jnp.arange(slots, dtype=jnp.int32)[:, None] == slot_of[None, :]).astype(jnp.bfloat16)

    mine = owners == myself
    rank = jnp.dot(
        mine.astype(jnp.bfloat16), earlier, preferred_element_type=jnp.float32
    ).astype(jnp.int32)
    held = mine[:, None, :] & (
        rank[:, None, :] == jnp.arange(capacity, dtype=jnp.int32)[None, :, None]
    )
    target = jnp.sum(jnp.where(held, offsets[:, None, :] + 1, 0), axis=2).reshape(-1) - 1
    combine = (jnp.arange(slab_rows, dtype=jnp.int32)[:, None] == target[None, :]).astype(
        jnp.bfloat16
    )

    step = width // CHUNKS
    share = slab_rows // groups
    here = lax.axis_index("dp")
    around = [[(z, (z + hop) % groups) for z in range(groups)] for hop in range(groups)]
    spans = [slice(i * step, (i + 1) * step) for i in range(CHUNKS)]
    table = jnp.zeros((slab_rows, width), jnp.bfloat16)
    results = []
    sent, gathered = [], []
    for i, span in enumerate(spans):
        outgoing = jnp.dot(
            dispatch, input_grad[:, span], preferred_element_type=jnp.float32
        ).astype(jnp.bfloat16)
        if i >= 2:
            outgoing, sent[i - 2] = lax.optimization_barrier((outgoing, sent[i - 2]))
        arrived = lax.all_to_all(outgoing, "vocab", split_axis=0, concat_axis=0, tiled=True)
        partial = jnp.dot(combine, arrived, preferred_element_type=jnp.float32)
        partial = (partial + head_grad[0, :, span].astype(jnp.float32)).astype(jnp.bfloat16)
        pieces = [
            lax.dynamic_slice_in_dim(partial, lax.bitwise_and(here + hop, groups - 1) * share, share, 0)
            for hop in range(groups)
        ]
        sent.append(pieces)
    for i, span in enumerate(spans):
        pieces = sent[i]
        grad = pieces[0].astype(jnp.float32)
        for hop in range(1, groups):
            grad = grad + lax.ppermute(pieces[hop], "dp", around[hop]).astype(jnp.float32)
        updated, first, second = update(
            grad, master[:, span], moment_one[:, span], moment_two[:, span]
        )
        rows = updated.astype(jnp.bfloat16)
        results.append((updated, first, second))
        for hop in range(groups):
            block = rows if hop == 0 else lax.ppermute(rows, "dp", around[hop])
            table = lax.dynamic_update_slice(
                table, block, (lax.bitwise_and(here - hop, groups - 1) * share, i * step)
            )
    return tuple(jnp.concatenate(parts, axis=1) for parts in zip(*results)) + (table,)


def solution(mesh):
    placed = (
        P(("dp", "vocab"), None),
        P("dp", None),
        P("dp", None),
        P("dp", "vocab", None),
        P(("vocab", "dp"), None),
        P(("vocab", "dp"), None),
        P(("vocab", "dp"), None),
    )
    return jax.shard_map(
        local,
        mesh=mesh,
        in_specs=placed,
        out_specs=(
            P(("vocab", "dp"), None),
            P(("vocab", "dp"), None),
            P(("vocab", "dp"), None),
            P("vocab", None),
        ),
        check_vma=False,
    )
```

time: 410 us -> 219 us (0.53); the launches traced: 404 us -> 218 us
  waiting for transfers between devices: 257 us -> 106 us
  other arithmetic: 86.5 us -> 14.1 us
  starting transfers between devices: 7.64 us -> 60 us
  local copies, waits for them, and re-layouts: 29.2 us -> 8.88 us
  matrix products: 9.43 us -> 28.6 us
  between operations: 13.9 us -> 1.02 us
    reduce_scatter x2 -> x0, waiting for transfers between devices: 88.1 us -> none  [the longest x1 88.1 us: local(): lax.psum_scatter(jnp.dot(scatter_table, arrived, preferred_element_type=j...]
    all_to_all x1 -> x4, waiting for transfers between devices: 126 us -> 55.4 us  [local(): lax.all_to_all(outgoing, 'vocab', split_axis=0, concat_axis=0, tiled=True)]
    another operation x2 -> x0, other arithmetic: 64.5 us -> none
    ppermute x0 -> x24, waiting for transfers between devices: none -> 50.3 us  [the longest x12 41.3 us: local(): block = rows if hop == 0 else lax.ppermute(rows, 'dp', around[hop])]
    all_gather x1 -> x0, waiting for transfers between devices: 42.8 us -> none  [local(): lax.all_gather(updated.astype(jnp.bfloat16), 'dp', axis=0, tiled=True)]
    ppermute x0 -> x24, starting transfers between devices: none -> 36.2 us  [the longest x12 19.6 us: local(): lax.ppermute(pieces[hop], 'dp', around[hop]).astype(jnp.float32)]
    gather x1 -> x0, local copies, waits for them, and re-layouts: 20 us -> none  [local(): jnp.take(input_grad, source, axis=0)]
    dot_general x1 -> x10, matrix products: 9.43 us -> 28.6 us  [the longest x4 17.2 us: local(): jnp.dot(dispatch, input_grad[:, span], preferred_element_type=jnp.float32)]
  transfers between devices with their start and end apart: 4 -> 28, of which waited for: 3 -> 16; matrix products, arithmetic and copies ran while one was open for 3% -> 18% of each run, Pallas kernels for 0% -> 0%
where the time goes in v1:
time: 219 us; the launch traced here: 218 us
  waiting for transfers between devices  106 us (48%)
  starting transfers between devices  60 us (27%)
  matrix products  28.6 us (13%)
  other arithmetic  14.1 us (6%)
  local copies, waits for them, and re-layouts  8.88 us (4%)
    all_to_all x4, waiting for transfers between devices, local(): lax.all_to_all(outgoing, 'vocab', split_axis=0, concat_axis=0, tiled=True)  55.4 us
    ppermute x12, waiting for transfers between devices, local(): block = rows if hop == 0 else lax.ppermute(rows, 'dp', around[hop])  41.3 us
    all_to_all x4, starting transfers between devices, local(): lax.all_to_all(outgoing, 'vocab', split_axis=0, concat_axis=0, tiled=True)  23.8 us
    ppermute x12, starting transfers between devices, local(): lax.ppermute(pieces[hop], 'dp', around[hop]).astype(jnp.float32)  19.6 us
    dot_general x4, matrix products, local(): jnp.dot(dispatch, input_grad[:, span], preferred_element_type=jnp.float32)  17.2 us
    ppermute x12, starting transfers between devices, local(): block = rows if hop == 0 else lax.ppermute(rows, 'dp', around[hop])  16.6 us
    dot_general x4, matrix products, local(): partial = jnp.dot(combine, arrived, preferred_element_type=jnp.float32)  11 us
    ppermute x12, waiting for transfers between devices, local(): lax.ppermute(pieces[hop], 'dp', around[hop]).astype(jnp.float32)  8.99 us
  transfers between devices with their start and end apart: 28, of which 16 were waited for; matrix products, arithmetic and copies ran while one was open for 18% of the time, Pallas kernels for 0%

profile of v1, /device:TPU:0, one launch (start us, length us, event | category | flops | bytes accessed | tf_op | source)
XLA Modules:
  0.0 218.3 jit_solution(6380382179799484971)
XLA Ops:
  0.6 0.5 broadcast.106
  1.1 1.6 reduce.7
  3.1 4.2 %convolution_convert_fusion.2 = bf16[1024,1152]{1,0:T(8,128)(2,1)} fusion(bf16[512,4608]{1,0:T(8,128)(2,1)} %param.7, s32[512]{0:T(512)S(1)} %bitcast.36), kind=kOutput, calls=%fused_computation.2 | convolution fusion | flops 1209663488 | bytes 3540992 | tf_op jit(solution)/shard_map/dot_general | solution.py:69
  7.3 7.4 %all-to-all-start = ((bf16[32,32,1152]{2,1,0:T(8,128)(2,1)}), bf16[32,32,1152]{2,1,0:T(8,128)(2,1)S(1)}, u32[]{:S(2)}, u32[]{:S(2)}) async-start(bf16[32,32,1152]{2,1,0:T(8,128)(2,1)} %bitcast.34), calls=%async_computation | async-start | bytes 4718592 | tf_op jit(solution)/shard_map/all_to_all | solution.py:74
  14.7 4.3 %convolution_convert_fusion = bf16[1024,1152]{1,0:T(8,128)(2,1)} fusion(bf16[512,4608]{1,0:T(8,128)(2,1)} %param.7, s32[512]{0:T(512)S(1)} %bitcast.37), kind=kOutput, calls=%fused_computation | convolution fusion | flops 1209663488 | bytes 3540992 | tf_op jit(solution)/shard_map/dot_general | solution.py:69
  19.0 27.5 %all-to-all-done = bf16[32,32,1152]{2,1,0:T(8,128)(2,1)S(1)} async-done(((bf16[32,32,1152]{2,1,0:T(8,128)(2,1)}), bf16[32,32,1152]{2,1,0:T(8,128)(2,1)S(1)}, u32[]{:S(2)}, u32[]{:S(2)}) %all-to-all-start) | async-done | bytes 2359328 | tf_op jit(solution)/shard_map/all_to_all | solution.py:74
  46.5 1.4 copy-done.1
  47.9 4.1 %all-to-all-start.1 = ((bf16[32,32,1152]{2,1,0:T(8,128)(2,1)}), bf16[32,32,1152]{2,1,0:T(8,128)(2,1)S(1)}, u32[]{:S(2)}, u32[]{:S(2)}) async-start(bf16[32,32,1152]{2,1,0:T(8,128)(2,1)} %bitcast.32), calls=%async_computation.1 | async-start | bytes 4718592 | tf_op jit(solution)/shard_map/all_to_all | solution.py:74
  52.5 0.6 select_reduce_fusion
  53.2 4.4 %convolution_convert_fusion.3 = bf16[1024,1152]{1,0:T(8,128)(2,1)} fusion(bf16[512,4608]{1,0:T(8,128)(2,1)} %param.7, s32[512]{0:T(512)S(1)} %bitcast.38), kind=kOutput, calls=%fused_computation.3 | convolution fusion | flops 1209663488 | bytes 3540992 | tf_op jit(solution)/shard_map/dot_general | solution.py:69
  57.6 2.4 %fusion = bf16[384,1152]{1,0:T(8,128)(2,1)S(1)} fusion(bf16[1024,1152]{1,0:T(8,128)(2,1)S(1)} %bitcast.33, bf16[1,384,4608]{2,1,0:T(8,128)(2,1)} %param.10, s32[1024]{0:T(1024)S(1)} %sub.37), kind=kOutput, calls=%fused_computation.8 | convolution fusion | flops 907689984 | bytes 4132864 | tf_op jit(solution)/shard_map/dot_general | solution.py:75
  60.0 0.8 constant_dynamic-slice_fusion.10
  60.8 23.0 %all-to-all-done.1 = bf16[32,32,1152]{2,1,0:T(8,128)(2,1)S(1)} async-done(((bf16[32,32,1152]{2,1,0:T(8,128)(2,1)}), bf16[32,32,1152]{2,1,0:T(8,128)(2,1)S(1)}, u32[]{:S(2)}, u32[]{:S(2)}) %all-to-all-start.1) | async-done | bytes 2359328 | tf_op jit(solution)/shard_map/all_to_all | solution.py:74
  83.8 4.8 %all-to-all-start.2 = ((bf16[32,32,1152]{2,1,0:T(8,128)(2,1)}), bf16[32,32,1152]{2,1,0:T(8,128)(2,1)}, u32[]{:S(2)}, u32[]{:S(2)}) async-start(bf16[32,32,1152]{2,1,0:T(8,128)(2,1)} %bitcast.31), calls=%async_computation.2 | async-start | bytes 4718592 | tf_op jit(solution)/shard_map/all_to_all | solution.py:74
  88.6 4.2 %convolution_convert_fusion.1 = bf16[1024,1152]{1,0:T(8,128)(2,1)} fusion(bf16[512,4608]{1,0:T(8,128)(2,1)} %param.7, s32[512]{0:T(512)S(1)} %bitcast.39), kind=kOutput, calls=%fused_computation.1 | convolution fusion | flops 1209663488 | bytes 3540992 | tf_op jit(solution)/shard_map/dot_general | solution.py:69
  92.8 1.9 collective-permute-start
  94.8 3.6 %collective-permute-start.1 = (bf16[96,1152]{1,0:T(8,128)(2,1)S(1)}, bf16[96,1152]{1,0:T(8,128)(2,1)S(1)}, u32[]{:S(2)}, u32[]{:S(2)}) collective-permute-start(bf16[96,1152]{1,0:T(8,128)(2,1)S(1)} %get-tuple-element.16), channel_id=1, source_target_pairs={{0,64},{32,96},{64,0},{96,32},{1,65},{33,97},{65,1},{97,33},{2,66}... | collective-permute-start | bytes 663560 | tf_op jit(solution)/shard_map/ppermute | solution.py:86
  98.3 1.0 collective-permute-start.2
  99.4 2.3 %fusion.1 = bf16[384,1152]{1,0:T(8,128)(2,1)S(1)} fusion(bf16[1024,1152]{1,0:T(8,128)(2,1)S(1)} %bitcast.30, bf16[1,384,4608]{2,1,0:T(8,128)(2,1)} %param.10, s32[1024]{0:T(1024)S(1)} %sub.37), kind=kOutput, calls=%fused_computation.9 | convolution fusion | flops 907689984 | bytes 4132864 | tf_op jit(solution)/shard_map/dot_general | solution.py:75
  101.7 0.8 collective-permute-done
  102.6 5.9 %collective-permute-done.1 = bf16[96,1152]{1,0:T(8,128)(2,1)S(1)} collective-permute-done((bf16[96,1152]{1,0:T(8,128)(2,1)S(1)}, bf16[96,1152]{1,0:T(8,128)(2,1)S(1)}, u32[]{:S(2)}, u32[]{:S(2)}) %collective-permute-start.1) | collective-permute-done | bytes 221216 | tf_op jit(solution)/shard_map/ppermute | solution.py:86
  108.7 2.8 %constant_dynamic-update-slice_fusion.3 = (bf16[384,4608]{1,0:T(8,128)(2,1)S(1)}, bf16[96,1152]{1,0:T(8,128)(2,1)}, f32[96,1152]{1,0:T(8,128)}, f32[96,1152]{1,0:T(8,128)}, f32[96,1152]{1,0:T(8,128)}) fusion(bf16[384,4608]{1,0:T(8,128)(2,1)S(1)} %broadcast_in_dim.21, s32[]{:T(128)S(6)} %select_n.29, f32[96,4608]{1,0:T(8,128)} %param.11, ...), kind=kLoop, calls=%fused_computation.64 | loop fusion | flops 2543616 | bytes 3981316 | tf_op jit(solution)/shard_map/dynamic_update_slice | solution.py:94
  111.5 1.1 collective-permute-start.12
  112.6 0.9 constant_dynamic-slice_fusion.6
  113.6 1.1 collective-permute-start.3
  114.6 2.5 %collective-permute-start.4 = (bf16[96,1152]{1,0:T(8,128)(2,1)}, bf16[96,1152]{1,0:T(8,128)(2,1)}, u32[]{:S(2)}, u32[]{:S(2)}) collective-permute-start(bf16[96,1152]{1,0:T(8,128)(2,1)} %get-tuple-element.20), channel_id=1, source_target_pairs={{0,64},{32,96},{64,0},{96,32},{1,65},{33,97},{65,1},{97,33},{2,66}... | collective-permute-start | bytes 663560 | tf_op jit(solution)/shard_map/ppermute | solution.py:86
  117.2 1.5 collective-permute-start.5
  118.6 1.1 collective-permute-start.13
  119.8 1.5 collective-permute-done.12
  121.3 0.8 collective-permute-start.14
  122.1 12.8 %collective-permute-done.13 = bf16[96,1152]{1,0:T(8,128)(2,1)S(1)} collective-permute-done((bf16[96,1152]{1,0:T(8,128)(2,1)}, bf16[96,1152]{1,0:T(8,128)(2,1)S(1)}, u32[]{:S(2)}, u32[]{:S(2)}) %collective-permute-start.13) | collective-permute-done | bytes 221216 | tf_op jit(solution)/shard_map/ppermute | solution.py:93
  134.9 7.5 %all-to-all-start.3 = ((bf16[32,32,1152]{2,1,0:T(8,128)(2,1)}), bf16[32,32,1152]{2,1,0:T(8,128)(2,1)}, u32[]{:S(2)}, u32[]{:S(2)}) async-start(bf16[32,32,1152]{2,1,0:T(8,128)(2,1)} %bitcast.29), calls=%async_computation.3 | async-start | bytes 4718592 | tf_op jit(solution)/shard_map/all_to_all | solution.py:74
  142.4 1.0 constant_dynamic-update-slice_fusion
  143.4 3.1 %constant_dynamic-update-slice_fusion.15 = (bf16[384,4608]{1,0:T(8,128)(2,1)S(1)}, bf16[96,1152]{1,0:T(8,128)(2,1)S(1)}, f32[96,1152]{1,0:T(8,128)}, f32[96,1152]{1,0:T(8,128)}, f32[96,1152]{1,0:T(8,128)}) fusion(bf16[384,4608]{1,0:T(8,128)(2,1)S(1)} %constant_dynamic-update-slice_fusion, s32[]{:T(128)S(6)} %select_n.29, f32[96,4608]{1,0:T(8,128)} %param.11, ...), kind=kLoop, calls=%fused_computation.92 | loop fusion | flops 2543616 | bytes 3981316 | tf_op jit(solution)/shard_map/dynamic_update_slice | solution.py:94
  146.5 0.6 collective-permute-start.15
  147.1 2.3 %collective-permute-start.16 = (bf16[96,1152]{1,0:T(8,128)(2,1)S(1)}, bf16[96,1152]{1,0:T(8,128)(2,1)S(1)}, u32[]{:S(2)}, u32[]{:S(2)}) collective-permute-start(bf16[96,1152]{1,0:T(8,128)(2,1)S(1)} %get-tuple-element.35), channel_id=1, source_target_pairs={{0,64},{32,96},{64,0},{96,32},{1,65},{33,97},{65,1},{97,33},{2,66}... | collective-permute-start | bytes 663560 | tf_op jit(solution)/shard_map/ppermute | solution.py:93
  149.5 0.4 collective-permute-start.17
  149.8 10.2 %collective-permute-done.15 = bf16[96,1152]{1,0:T(8,128)(2,1)S(1)} collective-permute-done((bf16[96,1152]{1,0:T(8,128)(2,1)S(1)}, bf16[96,1152]{1,0:T(8,128)(2,1)S(1)}, u32[]{:S(2)}, u32[]{:S(2)}) %collective-permute-start.15) | collective-permute-done | bytes 221216 | tf_op jit(solution)/shard_map/ppermute | solution.py:93
  160.1 0.6 collective-permute-done.17
  160.6 3.1 %fusion.2 = bf16[384,1152]{1,0:T(8,128)(2,1)S(1)} fusion(bf16[1024,1152]{1,0:T(8,128)(2,1)} %bitcast.10, bf16[1,384,4608]{2,1,0:T(8,128)(2,1)} %param.10, s32[1024]{0:T(1024)S(1)} %sub.37), kind=kOutput, calls=%fused_computation.10 | convolution fusion | flops 907689984 | bytes 4132864 | tf_op jit(solution)/shard_map/dot_general | solution.py:75
  163.7 0.9 copy-done.12
  164.6 0.9 constant_dynamic-slice_fusion.5
  165.8 2.9 %collective-permute-start.8 = (bf16[96,1152]{1,0:T(8,128)(2,1)}, bf16[96,1152]{1,0:T(8,128)(2,1)}, u32[]{:S(2)}, u32[]{:S(2)}) collective-permute-start(bf16[96,1152]{1,0:T(8,128)(2,1)} %get-tuple-element.48), channel_id=1, source_target_pairs={{0,96},{32,0},{64,32},{96,64},{1,97},{33,1},{65,33},{97,65},{2,98}... | collective-permute-start | bytes 663560 | tf_op jit(solution)/shard_map/ppermute | solution.py:86
  168.7 0.6 collective-permute-start.7
  169.4 4.9 %all-to-all-done.3 = bf16[32,32,1152]{2,1,0:T(8,128)(2,1)} async-done(((bf16[32,32,1152]{2,1,0:T(8,128)(2,1)}), bf16[32,32,1152]{2,1,0:T(8,128)(2,1)}, u32[]{:S(2)}, u32[]{:S(2)}) %all-to-all-start.3) | async-done | bytes 2359328 | tf_op jit(solution)/shard_map/all_to_all | solution.py:74
  174.2 3.2 %fusion.3 = bf16[384,1152]{1,0:T(8,128)(2,1)S(1)} fusion(bf16[1024,1152]{1,0:T(8,128)(2,1)} %bitcast.13, bf16[1,384,4608]{2,1,0:T(8,128)(2,1)} %param.10, s32[1024]{0:T(1024)S(1)} %sub.37), kind=kOutput, calls=%fused_computation.11 | convolution fusion | flops 907689984 | bytes 4132864 | tf_op jit(solution)/shard_map/dot_general | solution.py:75
  177.8 1.9 collective-permute-done.7
  179.6 1.8 constant_dynamic-update-slice_fusion.11
  181.4 1.2 collective-permute-start.18
  182.8 3.2 %collective-permute-start.11 = (bf16[96,1152]{1,0:T(8,128)(2,1)S(1)}, bf16[96,1152]{1,0:T(8,128)(2,1)S(1)}, u32[]{:S(2)}, u32[]{:S(2)}) collective-permute-start(bf16[96,1152]{1,0:T(8,128)(2,1)S(1)} %get-tuple-element.45), channel_id=1, source_target_pairs={{0,96},{32,0},{64,32},{96,64},{1,97},{33,1},{65,33},{97,65},{2,98}... | collective-permute-start | bytes 663560 | tf_op jit(solution)/shard_map/ppermute | solution.py:86
  186.0 0.9 collective-permute-start.10
  186.9 2.6 %collective-permute-start.19 = (bf16[96,1152]{1,0:T(8,128)(2,1)S(1)}, bf16[96,1152]{1,0:T(8,128)(2,1)S(1)}, u32[]{:S(2)}, u32[]{:S(2)}) collective-permute-start(bf16[96,1152]{1,0:T(8,128)(2,1)S(1)} %get-tuple-element.30), channel_id=1, source_target_pairs={{0,64},{32,96},{64,0},{96,32},{1,65},{33,97},{65,1},{97,33},{2,66}... | collective-permute-start | bytes 663560 | tf_op jit(solution)/shard_map/ppermute | solution.py:93
  189.5 2.3 %collective-permute-done.18 = bf16[96,1152]{1,0:T(8,128)(2,1)S(1)} collective-permute-done((bf16[96,1152]{1,0:T(8,128)(2,1)S(1)}, bf16[96,1152]{1,0:T(8,128)(2,1)S(1)}, u32[]{:S(2)}, u32[]{:S(2)}) %collective-permute-start.18) | collective-permute-done | bytes 221216 | tf_op jit(solution)/shard_map/ppermute | solution.py:93
  191.8 10.8 %collective-permute-done.19 = bf16[96,1152]{1,0:T(8,128)(2,1)S(1)} collective-permute-done((bf16[96,1152]{1,0:T(8,128)(2,1)S(1)}, bf16[96,1152]{1,0:T(8,128)(2,1)S(1)}, u32[]{:S(2)}, u32[]{:S(2)}) %collective-permute-start.19) | collective-permute-done | bytes 221216 | tf_op jit(solution)/shard_map/ppermute | solution.py:93
  202.7 0.5 collective-permute-done.20
  203.3 0.5 constant_dynamic-update-slice_fusion.7
  203.8 3.2 %collective-permute-start.22 = (bf16[96,1152]{1,0:T(8,128)(2,1)S(1)}, bf16[96,1152]{1,0:T(8,128)(2,1)S(1)}, u32[]{:S(2)}, u32[]{:S(2)}) collective-permute-start(bf16[96,1152]{1,0:T(8,128)(2,1)S(1)} %get-tuple-element.25), channel_id=1, source_target_pairs={{0,64},{32,96},{64,0},{96,32},{1,65},{33,97},{65,1},{97,33},{2,66}... | collective-permute-start | bytes 663560 | tf_op jit(solution)/shard_map/ppermute | solution.py:93
  207.0 1.4 collective-permute-start.21
  208.4 1.8 collective-permute-start.23
  210.2 2.2 %pad_maximum_fusion = (f32[96,4608]{1,0:T(8,128)}, f32[96,4608]{1,0:T(8,128)}) fusion(f32[96,1152]{1,0:T(8,128)S(1)} %get-tuple-element.26, f32[96,1152]{1,0:T(8,128)S(1)} %get-tuple-element.31, f32[96,1152]{1,0:T(8,128)S(1)} %copy-done.8, f32[96,1152]{1,0:T(8,128)S(1)} %copy-done.6, f32[96,1152]{1,0:T(8,128)S(1)} %get-tuple-element.27, ...), kind=kLoop, calls=%fused_computation.16 | loop fusion | flops 2654208 | bytes 7077888 | tf_op jit(solution)/shard_map/concatenate | solution.py:97
  212.4 1.4 pad_maximum_fusion.2
  213.8 1.7 collective-permute-done.21
  215.5 0.9 collective-permute-done.23
  216.5 1.8 copy-done
  (67 shorter events, 2.1 us)
Async XLA Ops:
  7.3 39.2 %all-to-all-start = ((bf16[32,32,1152]{2,1,0:T(8,128)(2,1)}), bf16[32,32,1152]{2,1,0:T(8,128)(2,1)S(1)}, u32[]{:S(2)}, u32[]{:S(2)}) async-start(bf16[32,32,1152]{2,1,0:T(8,128)(2,1)} %bitcast.34), calls=%async_computation | async-start | bytes 4718592 | tf_op jit(solution)/shard_map/all_to_all | solution.py:74
  46.5 1.4 copy-start.1
  46.5 5.5 %copy-start.14 = (s32[16384,1]{0,1:T(1,128)S(1)}, s32[16384,1]{0,1:T(1,128)}, u32[]{:S(2)}) copy-start(s32[16384,1]{0,1:T(1,128)} %param.9) | copy-start | bytes 196612
  47.9 35.8 %all-to-all-start.1 = ((bf16[32,32,1152]{2,1,0:T(8,128)(2,1)}), bf16[32,32,1152]{2,1,0:T(8,128)(2,1)S(1)}, u32[]{:S(2)}, u32[]{:S(2)}) async-start(bf16[32,32,1152]{2,1,0:T(8,128)(2,1)} %bitcast.32), calls=%async_computation.1 | async-start | bytes 4718592 | tf_op jit(solution)/shard_map/all_to_all | solution.py:74
  53.2 4.4 %copy-start.2 = (bf16[32,32,1152]{2,1,0:T(8,128)(2,1)S(1)}, bf16[32,32,1152]{2,1,0:T(8,128)(2,1)}, u32[]{:S(2)}) copy-start(bf16[32,32,1152]{2,1,0:T(8,128)(2,1)} %copy-done.1) | copy-start | bytes 7077892
  83.8 51.1 %all-to-all-start.2 = ((bf16[32,32,1152]{2,1,0:T(8,128)(2,1)}), bf16[32,32,1152]{2,1,0:T(8,128)(2,1)}, u32[]{:S(2)}, u32[]{:S(2)}) async-start(bf16[32,32,1152]{2,1,0:T(8,128)(2,1)} %bitcast.31), calls=%async_computation.2 | async-start | bytes 4718592 | tf_op jit(solution)/shard_map/all_to_all | solution.py:74
  92.8 9.7 %collective-permute-start = (bf16[96,1152]{1,0:T(8,128)(2,1)S(1)}, bf16[96,1152]{1,0:T(8,128)(2,1)S(1)}, u32[]{:S(2)}, u32[]{:S(2)}) collective-permute-start(bf16[96,1152]{1,0:T(8,128)(2,1)S(1)} %get-tuple-element.15), channel_id=1, source_target_pairs={{0,32},{32,64},{64,96},{96,0},{1,33},{33,65},{65,97},{97,1},{2,34}... | collective-permute-start | bytes 663560 | tf_op jit(solution)/shard_map/ppermute | solution.py:86
  94.8 13.7 %collective-permute-start.1 = (bf16[96,1152]{1,0:T(8,128)(2,1)S(1)}, bf16[96,1152]{1,0:T(8,128)(2,1)S(1)}, u32[]{:S(2)}, u32[]{:S(2)}) collective-permute-start(bf16[96,1152]{1,0:T(8,128)(2,1)S(1)} %get-tuple-element.16), channel_id=1, source_target_pairs={{0,64},{32,96},{64,0},{96,32},{1,65},{33,97},{65,1},{97,33},{2,66}... | collective-permute-start | bytes 663560 | tf_op jit(solution)/shard_map/ppermute | solution.py:86
  98.3 10.1 %collective-permute-start.2 = (bf16[96,1152]{1,0:T(8,128)(2,1)S(1)}, bf16[96,1152]{1,0:T(8,128)(2,1)S(1)}, u32[]{:S(2)}, u32[]{:S(2)}) collective-permute-start(bf16[96,1152]{1,0:T(8,128)(2,1)S(1)} %get-tuple-element.17), channel_id=1, source_target_pairs={{0,96},{32,0},{64,32},{96,64},{1,97},{33,1},{65,33},{97,65},{2,98}... | collective-permute-start | bytes 663560 | tf_op jit(solution)/shard_map/ppermute | solution.py:86
  101.7 7.0 %copy-start.13 = (bf16[96,1152]{1,0:T(8,128)(2,1)S(1)}, bf16[96,1152]{1,0:T(8,128)(2,1)}, u32[]{:S(2)}) copy-start(bf16[96,1152]{1,0:T(8,128)(2,1)} %get-tuple-element.14) | copy-start | bytes 663556
  111.5 9.8 %collective-permute-start.12 = (bf16[96,1152]{1,0:T(8,128)(2,1)}, bf16[96,1152]{1,0:T(8,128)(2,1)S(1)}, u32[]{:S(2)}, u32[]{:S(2)}) collective-permute-start(bf16[96,1152]{1,0:T(8,128)(2,1)} %get-tuple-element.40), channel_id=1, source_target_pairs={{0,32},{32,64},{64,96},{96,0},{1,33},{33,65},{65,97},{97,1},{2,34}... | collective-permute-start | bytes 663560 | tf_op jit(solution)/shard_map/ppermute | solution.py:93
  113.6 29.8 %collective-permute-start.3 = (bf16[96,1152]{1,0:T(8,128)(2,1)}, bf16[96,1152]{1,0:T(8,128)(2,1)}, u32[]{:S(2)}, u32[]{:S(2)}) collective-permute-start(bf16[96,1152]{1,0:T(8,128)(2,1)} %get-tuple-element.19), channel_id=1, source_target_pairs={{0,32},{32,64},{64,96},{96,0},{1,33},{33,65},{65,97},{97,1},{2,34}... | collective-permute-start | bytes 663560 | tf_op jit(solution)/shard_map/ppermute | solution.py:86
  114.6 28.8 %collective-permute-start.4 = (bf16[96,1152]{1,0:T(8,128)(2,1)}, bf16[96,1152]{1,0:T(8,128)(2,1)}, u32[]{:S(2)}, u32[]{:S(2)}) collective-permute-start(bf16[96,1152]{1,0:T(8,128)(2,1)} %get-tuple-element.20), channel_id=1, source_target_pairs={{0,64},{32,96},{64,0},{96,32},{1,65},{33,97},{65,1},{97,33},{2,66}... | collective-permute-start | bytes 663560 | tf_op jit(solution)/shard_map/ppermute | solution.py:86
  117.2 26.3 %collective-permute-start.5 = (bf16[96,1152]{1,0:T(8,128)(2,1)}, bf16[96,1152]{1,0:T(8,128)(2,1)}, u32[]{:S(2)}, u32[]{:S(2)}) collective-permute-start(bf16[96,1152]{1,0:T(8,128)(2,1)} %get-tuple-element.21), channel_id=1, source_target_pairs={{0,96},{32,0},{64,32},{96,64},{1,97},{33,1},{65,33},{97,65},{2,98}... | collective-permute-start | bytes 663560 | tf_op jit(solution)/shard_map/ppermute | solution.py:86
  118.6 16.3 %collective-permute-start.13 = (bf16[96,1152]{1,0:T(8,128)(2,1)}, bf16[96,1152]{1,0:T(8,128)(2,1)S(1)}, u32[]{:S(2)}, u32[]{:S(2)}) collective-permute-start(bf16[96,1152]{1,0:T(8,128)(2,1)} %get-tuple-element.40), channel_id=1, source_target_pairs={{0,64},{32,96},{64,0},{96,32},{1,65},{33,97},{65,1},{97,33},{2,66}... | collective-permute-start | bytes 663560 | tf_op jit(solution)/shard_map/ppermute | solution.py:93
  121.3 21.1 %collective-permute-start.14 = (bf16[96,1152]{1,0:T(8,128)(2,1)}, bf16[96,1152]{1,0:T(8,128)(2,1)}, u32[]{:S(2)}, u32[]{:S(2)}) collective-permute-start(bf16[96,1152]{1,0:T(8,128)(2,1)} %get-tuple-element.40), channel_id=1, source_target_pairs={{0,96},{32,0},{64,32},{96,64},{1,97},{33,1},{65,33},{97,65},{2,98}... | collective-permute-start | bytes 663560 | tf_op jit(solution)/shard_map/ppermute | solution.py:93
  134.9 39.3 %all-to-all-start.3 = ((bf16[32,32,1152]{2,1,0:T(8,128)(2,1)}), bf16[32,32,1152]{2,1,0:T(8,128)(2,1)}, u32[]{:S(2)}, u32[]{:S(2)}) async-start(bf16[32,32,1152]{2,1,0:T(8,128)(2,1)} %bitcast.29), calls=%async_computation.3 | async-start | bytes 4718592 | tf_op jit(solution)/shard_map/all_to_all | solution.py:74
  146.5 13.5 %collective-permute-start.15 = (bf16[96,1152]{1,0:T(8,128)(2,1)S(1)}, bf16[96,1152]{1,0:T(8,128)(2,1)S(1)}, u32[]{:S(2)}, u32[]{:S(2)}) collective-permute-start(bf16[96,1152]{1,0:T(8,128)(2,1)S(1)} %get-tuple-element.35), channel_id=1, source_target_pairs={{0,32},{32,64},{64,96},{96,0},{1,33},{33,65},{65,97},{97,1},{2,34}... | collective-permute-start | bytes 663560 | tf_op jit(solution)/shard_map/ppermute | solution.py:93
  147.1 12.9 %collective-permute-start.16 = (bf16[96,1152]{1,0:T(8,128)(2,1)S(1)}, bf16[96,1152]{1,0:T(8,128)(2,1)S(1)}, u32[]{:S(2)}, u32[]{:S(2)}) collective-permute-start(bf16[96,1152]{1,0:T(8,128)(2,1)S(1)} %get-tuple-element.35), channel_id=1, source_target_pairs={{0,64},{32,96},{64,0},{96,32},{1,65},{33,97},{65,1},{97,33},{2,66}... | collective-permute-start | bytes 663560 | tf_op jit(solution)/shard_map/ppermute | solution.py:93
  149.5 11.2 %collective-permute-start.17 = (bf16[96,1152]{1,0:T(8,128)(2,1)S(1)}, bf16[96,1152]{1,0:T(8,128)(2,1)S(1)}, u32[]{:S(2)}, u32[]{:S(2)}) collective-permute-start(bf16[96,1152]{1,0:T(8,128)(2,1)S(1)} %get-tuple-element.35), channel_id=1, source_target_pairs={{0,96},{32,0},{64,32},{96,64},{1,97},{33,1},{65,33},{97,65},{2,98}... | collective-permute-start | bytes 663560 | tf_op jit(solution)/shard_map/ppermute | solution.py:93
  163.7 0.9 copy-start.12
  165.5 12.0 %collective-permute-start.6 = (bf16[96,1152]{1,0:T(8,128)(2,1)}, bf16[96,1152]{1,0:T(8,128)(2,1)}, u32[]{:S(2)}, u32[]{:S(2)}) collective-permute-start(bf16[96,1152]{1,0:T(8,128)(2,1)} %get-tuple-element.47), channel_id=1, source_target_pairs={{0,32},{32,64},{64,96},{96,0},{1,33},{33,65},{65,97},{97,1},{2,34}... | collective-permute-start | bytes 663560 | tf_op jit(solution)/shard_map/ppermute | solution.py:86
  165.8 12.0 %collective-permute-start.8 = (bf16[96,1152]{1,0:T(8,128)(2,1)}, bf16[96,1152]{1,0:T(8,128)(2,1)}, u32[]{:S(2)}, u32[]{:S(2)}) collective-permute-start(bf16[96,1152]{1,0:T(8,128)(2,1)} %get-tuple-element.48), channel_id=1, source_target_pairs={{0,96},{32,0},{64,32},{96,64},{1,97},{33,1},{65,33},{97,65},{2,98}... | collective-permute-start | bytes 663560 | tf_op jit(solution)/shard_map/ppermute | solution.py:86
  168.7 10.9 %collective-permute-start.7 = (bf16[96,1152]{1,0:T(8,128)(2,1)}, bf16[96,1152]{1,0:T(8,128)(2,1)}, u32[]{:S(2)}, u32[]{:S(2)}) collective-permute-start(bf16[96,1152]{1,0:T(8,128)(2,1)} %get-tuple-element.49), channel_id=1, source_target_pairs={{0,64},{32,96},{64,0},{96,32},{1,65},{33,97},{65,1},{97,33},{2,66}... | collective-permute-start | bytes 663560 | tf_op jit(solution)/shard_map/ppermute | solution.py:86
  174.2 5.4 %copy-start.3 = (f32[96,4608]{1,0:T(8,128)S(1)}, f32[96,4608]{1,0:T(8,128)}, u32[]{:S(2)}) copy-start(f32[96,4608]{1,0:T(8,128)} %param.11) | copy-start | bytes 5308420
  174.2 5.4 %copy-start.4 = (f32[96,4608]{1,0:T(8,128)S(1)}, f32[96,4608]{1,0:T(8,128)}, u32[]{:S(2)}) copy-start(f32[96,4608]{1,0:T(8,128)} %param.12) | copy-start | bytes 5308420
  174.2 5.4 %copy-start.5 = (f32[96,4608]{1,0:T(8,128)S(1)}, f32[96,4608]{1,0:T(8,128)}, u32[]{:S(2)}) copy-start(f32[96,4608]{1,0:T(8,128)} %param.13) | copy-start | bytes 5308420
  181.4 10.4 %collective-permute-start.18 = (bf16[96,1152]{1,0:T(8,128)(2,1)S(1)}, bf16[96,1152]{1,0:T(8,128)(2,1)S(1)}, u32[]{:S(2)}, u32[]{:S(2)}) collective-permute-start(bf16[96,1152]{1,0:T(8,128)(2,1)S(1)} %get-tuple-element.30), channel_id=1, source_target_pairs={{0,32},{32,64},{64,96},{96,0},{1,33},{33,65},{65,97},{97,1},{2,34}... | collective-permute-start | bytes 663560 | tf_op jit(solution)/shard_map/ppermute | solution.py:93
  182.7 20.6 %collective-permute-start.9 = (bf16[96,1152]{1,0:T(8,128)(2,1)S(1)}, bf16[96,1152]{1,0:T(8,128)(2,1)S(1)}, u32[]{:S(2)}, u32[]{:S(2)}) collective-permute-start(bf16[96,1152]{1,0:T(8,128)(2,1)S(1)} %get-tuple-element.44), channel_id=1, source_target_pairs={{0,32},{32,64},{64,96},{96,0},{1,33},{33,65},{65,97},{97,1},{2,34}... | collective-permute-start | bytes 663560 | tf_op jit(solution)/shard_map/ppermute | solution.py:86
  182.8 20.5 %collective-permute-start.11 = (bf16[96,1152]{1,0:T(8,128)(2,1)S(1)}, bf16[96,1152]{1,0:T(8,128)(2,1)S(1)}, u32[]{:S(2)}, u32[]{:S(2)}) collective-permute-start(bf16[96,1152]{1,0:T(8,128)(2,1)S(1)} %get-tuple-element.45), channel_id=1, source_target_pairs={{0,96},{32,0},{64,32},{96,64},{1,97},{33,1},{65,33},{97,65},{2,98}... | collective-permute-start | bytes 663560 | tf_op jit(solution)/shard_map/ppermute | solution.py:86
  186.0 17.3 %collective-permute-start.10 = (bf16[96,1152]{1,0:T(8,128)(2,1)S(1)}, bf16[96,1152]{1,0:T(8,128)(2,1)S(1)}, u32[]{:S(2)}, u32[]{:S(2)}) collective-permute-start(bf16[96,1152]{1,0:T(8,128)(2,1)S(1)} %get-tuple-element.46), channel_id=1, source_target_pairs={{0,64},{32,96},{64,0},{96,32},{1,65},{33,97},{65,1},{97,33},{2,66}... | collective-permute-start | bytes 663560 | tf_op jit(solution)/shard_map/ppermute | solution.py:86
  186.9 15.8 %collective-permute-start.19 = (bf16[96,1152]{1,0:T(8,128)(2,1)S(1)}, bf16[96,1152]{1,0:T(8,128)(2,1)S(1)}, u32[]{:S(2)}, u32[]{:S(2)}) collective-permute-start(bf16[96,1152]{1,0:T(8,128)(2,1)S(1)} %get-tuple-element.30), channel_id=1, source_target_pairs={{0,64},{32,96},{64,0},{96,32},{1,65},{33,97},{65,1},{97,33},{2,66}... | collective-permute-start | bytes 663560 | tf_op jit(solution)/shard_map/ppermute | solution.py:93
  191.8 11.4 %collective-permute-start.20 = (bf16[96,1152]{1,0:T(8,128)(2,1)S(1)}, bf16[96,1152]{1,0:T(8,128)(2,1)S(1)}, u32[]{:S(2)}, u32[]{:S(2)}) collective-permute-start(bf16[96,1152]{1,0:T(8,128)(2,1)S(1)} %get-tuple-element.30), channel_id=1, source_target_pairs={{0,96},{32,0},{64,32},{96,64},{1,97},{33,1},{65,33},{97,65},{2,98}... | collective-permute-start | bytes 663560 | tf_op jit(solution)/shard_map/ppermute | solution.py:93
  191.8 18.4 %copy-start.6 = (f32[96,1152]{1,0:T(8,128)S(1)}, f32[96,1152]{1,0:T(8,128)}, u32[]{:S(2)}) copy-start(f32[96,1152]{1,0:T(8,128)} %get-tuple-element.41) | copy-start | bytes 1327108
  191.8 18.4 %copy-start.7 = (f32[96,1152]{1,0:T(8,128)S(1)}, f32[96,1152]{1,0:T(8,128)}, u32[]{:S(2)}) copy-start(f32[96,1152]{1,0:T(8,128)} %get-tuple-element.42) | copy-start | bytes 1327108
  191.8 18.4 %copy-start.8 = (f32[96,1152]{1,0:T(8,128)S(1)}, f32[96,1152]{1,0:T(8,128)}, u32[]{:S(2)}) copy-start(f32[96,1152]{1,0:T(8,128)} %get-tuple-element.36) | copy-start | bytes 1327108
  191.8 18.4 %copy-start.9 = (f32[96,1152]{1,0:T(8,128)S(1)}, f32[96,1152]{1,0:T(8,128)}, u32[]{:S(2)}) copy-start(f32[96,1152]{1,0:T(8,128)} %get-tuple-element.37) | copy-start | bytes 1327108
  203.8 11.7 %collective-permute-start.22 = (bf16[96,1152]{1,0:T(8,128)(2,1)S(1)}, bf16[96,1152]{1,0:T(8,128)(2,1)S(1)}, u32[]{:S(2)}, u32[]{:S(2)}) collective-permute-start(bf16[96,1152]{1,0:T(8,128)(2,1)S(1)} %get-tuple-element.25), channel_id=1, source_target_pairs={{0,64},{32,96},{64,0},{96,32},{1,65},{33,97},{65,1},{97,33},{2,66}... | collective-permute-start | bytes 663560 | tf_op jit(solution)/shard_map/ppermute | solution.py:93
  207.0 8.5 %collective-permute-start.21 = (bf16[96,1152]{1,0:T(8,128)(2,1)S(1)}, bf16[96,1152]{1,0:T(8,128)(2,1)S(1)}, u32[]{:S(2)}, u32[]{:S(2)}) collective-permute-start(bf16[96,1152]{1,0:T(8,128)(2,1)S(1)} %get-tuple-element.25), channel_id=1, source_target_pairs={{0,32},{32,64},{64,96},{96,0},{1,33},{33,65},{65,97},{97,1},{2,34}... | collective-permute-start | bytes 663560 | tf_op jit(solution)/shard_map/ppermute | solution.py:93
  208.4 8.1 %collective-permute-start.23 = (bf16[96,1152]{1,0:T(8,128)(2,1)S(1)}, bf16[96,1152]{1,0:T(8,128)(2,1)S(1)}, u32[]{:S(2)}, u32[]{:S(2)}) collective-permute-start(bf16[96,1152]{1,0:T(8,128)(2,1)S(1)} %get-tuple-element.25), channel_id=1, source_target_pairs={{0,96},{32,0},{64,32},{96,64},{1,97},{33,1},{65,33},{97,65},{2,98}... | collective-permute-start | bytes 663560 | tf_op jit(solution)/shard_map/ppermute | solution.py:93
  210.2 2.2 %copy-start.10 = (f32[96,1152]{1,0:T(8,128)S(1)}, f32[96,1152]{1,0:T(8,128)}, u32[]{:S(2)}) copy-start(f32[96,1152]{1,0:T(8,128)} %get-tuple-element.43) | copy-start | bytes 1327108
  210.2 2.2 %copy-start.11 = (f32[96,1152]{1,0:T(8,128)S(1)}, f32[96,1152]{1,0:T(8,128)}, u32[]{:S(2)}) copy-start(f32[96,1152]{1,0:T(8,128)} %get-tuple-element.38) | copy-start | bytes 1327108
  216.5 1.8 copy-start

commit v2 on v1

--- a/solution.py
+++ b/solution.py
@@ -1,6 +1,10 @@
+import functools
+
 import jax
 import jax.numpy as jnp
 from jax import lax
+from jax.experimental import pallas as pl
+from jax.experimental.pallas import tpu as pltpu
 from jax.sharding import PartitionSpec as P
 
 beta_first = 0.9
@@ -11,7 +15,46 @@
 correct_first = 1.0 - 0.9**10
 correct_second = 1.0 - 0.95**10
 
-CHUNKS = 4
+UNITS = (11, 10, 8, 7)
+
+
+def place_body(start, share, width, here_ref, *refs):
+    blocks, table_ref, sems = refs[-6:-2], refs[-2], refs[-1]
+    copies = []
+    for hop, block_ref in enumerate(blocks):
+        row = lax.bitwise_and(here_ref[0] - hop, len(blocks) - 1) * share
+        copies.append(
+            pltpu.make_async_copy(
+                block_ref,
+                table_ref.at[pl.ds(pl.multiple_of(row, share), share), pl.ds(start, width)],
+                sems.at[hop],
+            )
+        )
+    for copy in copies:
+        copy.start()
+    for copy in copies:
+        copy.wait()
+
+
+def place(table, here, blocks, start, shape):
+    share, width = blocks[0].shape
+    anywhere = pl.BlockSpec(memory_space=pl.ANY)
+    vmem = pl.BlockSpec(memory_space=pltpu.VMEM)
+    before = [] if table is None else [table]
+    operands = [here.reshape(1)] + before + blocks
+    return pl.pallas_call(
+        functools.partial(place_body, start, share, width),
+        out_shape=jax.ShapeDtypeStruct(shape, jnp.bfloat16),
+        in_specs=[pl.BlockSpec(memory_space=pltpu.SMEM)]
+        + [anywhere] * len(before)
+        + [vmem] * len(blocks),
+        out_specs=anywhere,
+        scratch_shapes=[pltpu.SemaphoreType.DMA((len(blocks),))],
+        input_output_aliases={} if table is None else {1: 0},
+        cost_estimate=pl.CostEstimate(
+            flops=0, bytes_accessed=4 * len(blocks) * share * width, transcendentals=0
+        ),
+    )(*operands)
 
 
 def update(grad, master, moment_one, moment_two):
@@ -35,8 +78,8 @@
     owners = token_slab[:, 0].reshape(peers, tok_rows)
     offsets = token_offset[:, 0].reshape(peers, tok_rows)
 
-    place = jnp.arange(tok_rows, dtype=jnp.int32)
-    earlier = (place[:, None] < place[None, :]).astype(jnp.bfloat16)
+    order = jnp.arange(tok_rows, dtype=jnp.int32)
+    earlier = (order[:, None] < order[None, :]).astype(jnp.bfloat16)
 
     own = lax.dynamic_index_in_dim(owners, myself, 0, keepdims=False)
     named = own[None, :] == jnp.arange(peers, dtype=jnp.int32)[:, None]
@@ -57,44 +100,55 @@
         jnp.bfloat16
     )
 
-    step = width // CHUNKS
     share = slab_rows // groups
     here = lax.axis_index("dp")
     around = [[(z, (z + hop) % groups) for z in range(groups)] for hop in range(groups)]
-    spans = [slice(i * step, (i + 1) * step) for i in range(CHUNKS)]
-    table = jnp.zeros((slab_rows, width), jnp.bfloat16)
-    results = []
-    sent, gathered = [], []
-    for i, span in enumerate(spans):
-        outgoing = jnp.dot(
+    unit = width // sum(UNITS)
+    edges = [unit * sum(UNITS[:i]) for i in range(len(UNITS) + 1)]
+    spans = [slice(low, high) for low, high in zip(edges, edges[1:])]
+
+    def send(span):
+        return jnp.dot(
             dispatch, input_grad[:, span], preferred_element_type=jnp.float32
         ).astype(jnp.bfloat16)
-        if i >= 2:
-            outgoing, sent[i - 2] = lax.optimization_barrier((outgoing, sent[i - 2]))
-        arrived = lax.all_to_all(outgoing, "vocab", split_axis=0, concat_axis=0, tiled=True)
+
+    def pieces_of(arrived, span):
         partial = jnp.dot(combine, arrived, preferred_element_type=jnp.float32)
         partial = (partial + head_grad[0, :, span].astype(jnp.float32)).astype(jnp.bfloat16)
-        pieces = [
+        return [
             lax.dynamic_slice_in_dim(partial, lax.bitwise_and(here + hop, groups - 1) * share, share, 0)
             for hop in range(groups)
         ]
-        sent.append(pieces)
+
+    def gather(block):
+        return [block] + [lax.ppermute(block, "dp", around[hop]) for hop in range(1, groups)]
+
+    last = len(spans) - 1
+    states, rows, gathered = [], [], []
     for i, span in enumerate(spans):
-        pieces = sent[i]
+        outgoing = send(span)
+        if i >= 2:
+            outgoing, rows[i - 2] = lax.optimization_barrier((outgoing, rows[i - 2]))
+        arrived = lax.all_to_all(outgoing, "vocab", split_axis=0, concat_axis=0, tiled=True)
+        if i >= 1:
+            arrived, rows[i - 1] = lax.optimization_barrier((arrived, rows[i - 1]))
+        pieces = pieces_of(arrived, span)
+        if i == last:
+            pieces, rows[i - 1] = lax.optimization_barrier((pieces, rows[i - 1]))
+        if i >= 1:
+            gathered.append(gather(rows[i - 1]))
         grad = pieces[0].astype(jnp.float32)
         for hop in range(1, groups):
             grad = grad + lax.ppermute(pieces[hop], "dp", around[hop]).astype(jnp.float32)
-        updated, first, second = update(
-            grad, master[:, span], moment_one[:, span], moment_two[:, span]
-        )
-        rows = updated.astype(jnp.bfloat16)
-        results.append((updated, first, second))
-        for hop in range(groups):
-            block = rows if hop == 0 else lax.ppermute(rows, "dp", around[hop])
-            table = lax.dynamic_update_slice(
-                table, block, (lax.bitwise_and(here - hop, groups - 1) * share, i * step)
-            )
-    return tuple(jnp.concatenate(parts, axis=1) for parts in zip(*results)) + (table,)
+        if 1 <= i < last:
+            grad, gathered[i - 1] = lax.optimization_barrier((grad, gathered[i - 1]))
+        states.append(update(grad, master[:, span], moment_one[:, span], moment_two[:, span]))
+        rows.append(states[-1][0].astype(jnp.bfloat16))
+    gathered.append(gather(rows[last]))
+    table = None
+    for blocks, span in zip(gathered, spans):
+        table = place(table, here, blocks, span.start, (slab_rows, width))
+    return tuple(jnp.concatenate(parts, axis=1) for parts in zip(*states)) + (table,)
 
 
 def solution(mesh):

time: 219 us -> 205 us (0.936)
  waiting for transfers between devices: 106 us -> 80.9 us
  Pallas kernels: 0 us -> 8.65 us
  starting transfers between devices: 60 us -> 63.9 us
  local copies, waits for them, and re-layouts: 8.88 us -> 5.9 us
    ppermute x12, waiting for transfers between devices: 41.3 us -> 22.5 us  [gather(): lax.ppermute(block, 'dp', around[hop])]
    all_to_all x4, waiting for transfers between devices: 55.4 us -> 44 us  [local(): lax.all_to_all(outgoing, 'vocab', split_axis=0, concat_axis=0, tiled=True)]
    pallas_call x0 -> x4, Pallas kernels: none -> 8.65 us  [place(): pl.pallas_call(functools.partial(place_body, start, share, width), out_sh...]
    convert_element_type x0 -> x4, other arithmetic: none -> 8.61 us  [local(): rows.append(states[-1][0].astype(jnp.bfloat16))]
    dynamic_update_slice x4 -> x0, other arithmetic: 8.07 us -> none  [local(): lax.dynamic_update_slice(table, block, (lax.bitwise_and(here - hop, group...]
    ppermute x12, waiting for transfers between devices: 8.99 us -> 14.4 us  [local(): lax.ppermute(pieces[hop], 'dp', around[hop]).astype(jnp.float32)]
    unnamed x31 -> x29, local copies, waits for them, and re-layouts: 4.66 us -> 4.73 us
  transfers between devices with their start and end apart: 28 -> 28, of which waited for: 16 -> 15; matrix products, arithmetic and copies ran while one was open for 18% -> 17% of each run, Pallas kernels for 0% -> 3%
where the time goes in v2:
time: 205 us; the launch traced here: 204 us
  waiting for transfers between devices  80.9 us (39%)
  starting transfers between devices  63.9 us (31%)
  matrix products  28.2 us (14%)
  other arithmetic  14.9 us (7%)
  Pallas kernels  8.65 us (4%)
  local copies, waits for them, and re-layouts  5.9 us (3%)
    all_to_all x4, waiting for transfers between devices, local(): lax.all_to_all(outgoing, 'vocab', split_axis=0, concat_axis=0, tiled=True)  44 us
    all_to_all x4, starting transfers between devices, local(): lax.all_to_all(outgoing, 'vocab', split_axis=0, concat_axis=0, tiled=True)  24.6 us
    ppermute x12, waiting for transfers between devices, gather(): lax.ppermute(block, 'dp', around[hop])  22.5 us
    ppermute x12, starting transfers between devices, local(): lax.ppermute(pieces[hop], 'dp', around[hop]).astype(jnp.float32)  21 us
    ppermute x12, starting transfers between devices, gather(): lax.ppermute(block, 'dp', around[hop])  18.3 us
    dot_general x4, matrix products, send(): jnp.dot(dispatch, input_grad[:, span], preferred_element_type=jnp.float32)  16.6 us
    ppermute x12, waiting for transfers between devices, local(): lax.ppermute(pieces[hop], 'dp', around[hop]).astype(jnp.float32)  14.4 us
    dot_general x4, matrix products, pieces_of(): partial = jnp.dot(combine, arrived, preferred_element_type=jnp.float32)  11.2 us
  transfers between devices with their start and end apart: 28, of which 15 were waited for; matrix products, arithmetic and copies ran while one was open for 17% of the time, Pallas kernels for 3%

profile of v2, /device:TPU:0, one launch (start us, length us, event | category | flops | bytes accessed | tf_op | source)
XLA Modules:
  0.0 203.5 jit_solution(14351000308444526648)
XLA Ops:
  0.6 0.5 broadcast.62
  1.1 1.6 reduce.7
  3.1 4.7 %convolution_convert_fusion.1 = bf16[1024,1408]{1,0:T(8,128)(2,1)} fusion(bf16[512,4608]{1,0:T(8,128)(2,1)} %param.7, s32[512]{0:T(512)S(1)} %bitcast.36), kind=kOutput, calls=%fused_computation.1 | convolution fusion | flops 1478361088 | bytes 4327424 | tf_op jit(solution)/shard_map/dot_general | solution.py:111
  7.8 7.4 %all-to-all-start = ((bf16[32,32,1408]{2,1,0:T(8,128)(2,1)}), bf16[32,32,1408]{2,1,0:T(8,128)(2,1)S(1)}, u32[]{:S(2)}, u32[]{:S(2)}) async-start(bf16[32,32,1408]{2,1,0:T(8,128)(2,1)} %bitcast.31), calls=%async_computation | async-start | bytes 5767168 | tf_op jit(solution)/shard_map/all_to_all | solution.py:132
  15.2 4.4 %convolution_convert_fusion = bf16[1024,1280]{1,0:T(8,128)(2,1)} fusion(bf16[512,4608]{1,0:T(8,128)(2,1)} %param.7, s32[512]{0:T(512)S(1)} %bitcast.37), kind=kOutput, calls=%fused_computation | convolution fusion | flops 1344012288 | bytes 3934208 | tf_op jit(solution)/shard_map/dot_general | solution.py:111
  19.6 33.0 %all-to-all-done = bf16[32,32,1408]{2,1,0:T(8,128)(2,1)S(1)} async-done(((bf16[32,32,1408]{2,1,0:T(8,128)(2,1)}), bf16[32,32,1408]{2,1,0:T(8,128)(2,1)S(1)}, u32[]{:S(2)}, u32[]{:S(2)}) %all-to-all-start) | async-done | bytes 2883616 | tf_op jit(solution)/shard_map/all_to_all | solution.py:132
  52.7 4.9 %all-to-all-start.1 = ((bf16[32,32,1280]{2,1,0:T(8,128)(2,1)}), bf16[32,32,1280]{2,1,0:T(8,128)(2,1)}, u32[]{:S(2)}, u32[]{:S(2)}) async-start(bf16[32,32,1280]{2,1,0:T(8,128)(2,1)} %bitcast.32), calls=%async_computation.1 | async-start | bytes 5242880 | tf_op jit(solution)/shard_map/all_to_all | solution.py:132
  58.0 0.6 select_reduce_fusion
  58.8 2.6 %fusion = bf16[384,1408]{1,0:T(8,128)(2,1)S(1)} fusion(bf16[1024,1408]{1,0:T(8,128)(2,1)S(1)} %bitcast.30, bf16[1,384,4608]{2,1,0:T(8,128)(2,1)} %param.10, s32[1024]{0:T(1024)S(1)} %sub.19), kind=kOutput, calls=%fused_computation.4 | convolution fusion | flops 1109311488 | bytes 5050368 | tf_op jit(solution)/shard_map/dot_general | solution.py:116
  61.5 2.0 collective-permute-start
  63.5 3.6 %collective-permute-start.1 = (bf16[96,1408]{1,0:T(8,128)(2,1)S(1)}, bf16[96,1408]{1,0:T(8,128)(2,1)S(1)}, u32[]{:S(2)}, u32[]{:S(2)}) collective-permute-start(bf16[96,1408]{1,0:T(8,128)(2,1)S(1)} %get-tuple-element.68), channel_id=1, source_target_pairs={{0,64},{32,96},{64,0},{96,32},{1,65},{33,97},{65,1},{97,33},{2,66}... | collective-permute-start | bytes 811016 | tf_op jit(solution)/shard_map/ppermute | solution.py:142
  67.0 1.0 collective-permute-start.2
  68.1 3.8 %fusion.5 = bf16[1024,1024]{1,0:T(8,128)(2,1)} fusion(bf16[512,4608]{1,0:T(8,128)(2,1)} %param.7, s32[512]{0:T(512)S(1)} %bitcast.38), kind=kOutput, calls=%fused_computation.12 | convolution fusion | flops 1075314688 | bytes 3147776 | tf_op jit(solution)/shard_map/dot_general | solution.py:111
  71.9 0.5 collective-permute-done
  72.3 7.0 %collective-permute-done.1 = bf16[96,1408]{1,0:T(8,128)(2,1)S(1)} collective-permute-done((bf16[96,1408]{1,0:T(8,128)(2,1)S(1)}, bf16[96,1408]{1,0:T(8,128)(2,1)S(1)}, u32[]{:S(2)}, u32[]{:S(2)}) %collective-permute-start.1) | collective-permute-done | bytes 270368 | tf_op jit(solution)/shard_map/ppermute | solution.py:142
  79.3 1.9 fusion.36
  81.2 11.0 %all-to-all-done.1 = bf16[32,32,1280]{2,1,0:T(8,128)(2,1)} async-done(((bf16[32,32,1280]{2,1,0:T(8,128)(2,1)}), bf16[32,32,1280]{2,1,0:T(8,128)(2,1)}, u32[]{:S(2)}, u32[]{:S(2)}) %all-to-all-start.1) | async-done | bytes 2621472 | tf_op jit(solution)/shard_map/all_to_all | solution.py:132
  92.2 4.8 %all-to-all-start.2 = ((bf16[32,32,1024]{2,1,0:T(8,128)(2,1)}), bf16[32,32,1024]{2,1,0:T(8,128)(2,1)}, u32[]{:S(2)}, u32[]{:S(2)}) async-start(bf16[32,32,1024]{2,1,0:T(8,128)(2,1)} %bitcast.33), calls=%async_computation.2 | async-start | bytes 4194304 | tf_op jit(solution)/shard_map/all_to_all | solution.py:132
  97.0 3.2 %fusion.1 = bf16[384,1280]{1,0:T(8,128)(2,1)S(1)} fusion(bf16[1024,1280]{1,0:T(8,128)(2,1)} %bitcast.7, bf16[1,384,4608]{2,1,0:T(8,128)(2,1)} %param.10, s32[1024]{0:T(1024)S(1)} %sub.19), kind=kOutput, calls=%fused_computation.5 | convolution fusion | flops 1008500736 | bytes 4591616 | tf_op jit(solution)/shard_map/dot_general | solution.py:116
  100.3 2.0 collective-permute-start.3
  102.3 3.6 %collective-permute-start.4 = (bf16[96,1280]{1,0:T(8,128)(2,1)S(1)}, bf16[96,1280]{1,0:T(8,128)(2,1)S(1)}, u32[]{:S(2)}, u32[]{:S(2)}) collective-permute-start(bf16[96,1280]{1,0:T(8,128)(2,1)S(1)} %get-tuple-element.71), channel_id=1, source_target_pairs={{0,64},{32,96},{64,0},{96,32},{1,65},{33,97},{65,1},{97,33},{2,66}... | collective-permute-start | bytes 737288 | tf_op jit(solution)/shard_map/ppermute | solution.py:142
  105.9 1.0 collective-permute-start.5
  106.9 3.7 %fusion.6 = bf16[1024,896]{1,0:T(8,128)(2,1)} fusion(s32[512]{0:T(512)S(1)} %bitcast.39, bf16[512,4608]{1,0:T(8,128)(2,1)} %param.7), kind=kOutput, calls=%fused_computation.13 | convolution fusion | flops 940965888 | bytes 2754560 | tf_op jit(solution)/shard_map/dot_general | solution.py:111
  110.5 1.0 collective-permute-start.6
  112.0 2.2 %collective-permute-start.8 = (bf16[96,1408]{1,0:T(8,128)(2,1)S(1)}, bf16[96,1408]{1,0:T(8,128)(2,1)S(1)}, u32[]{:S(2)}, u32[]{:S(2)}) collective-permute-start(bf16[96,1408]{1,0:T(8,128)(2,1)S(1)} %get-tuple-element.41.refs_0_), channel_id=1, source_target_pairs={{0,96},{32,0},{64,32},{96,64},{1,97},{33,1},{65,33},{97,65},{2,98}... | collective-permute-start | bytes 811016 | tf_op jit(solution)/shard_map/ppermute | solution.py:124
  114.2 3.7 %collective-permute-done.4 = bf16[96,1280]{1,0:T(8,128)(2,1)S(1)} collective-permute-done((bf16[96,1280]{1,0:T(8,128)(2,1)S(1)}, bf16[96,1280]{1,0:T(8,128)(2,1)S(1)}, u32[]{:S(2)}, u32[]{:S(2)}) %collective-permute-start.4) | collective-permute-done | bytes 245792 | tf_op jit(solution)/shard_map/ppermute | solution.py:142
  118.1 5.6 %collective-permute-done.6.refs_1_ = bf16[96,1408]{1,0:T(8,128)(2,1)S(1)} collective-permute-done((bf16[96,1408]{1,0:T(8,128)(2,1)S(1)}, bf16[96,1408]{1,0:T(8,128)(2,1)S(1)}, u32[]{:S(2)}, u32[]{:S(2)}) %collective-permute-start.6) | collective-permute-done | bytes 270368 | tf_op jit(solution)/shard_map/ppermute | solution.py:124
  123.7 5.0 %collective-permute-done.7.refs_2_ = bf16[96,1408]{1,0:T(8,128)(2,1)S(1)} collective-permute-done((bf16[96,1408]{1,0:T(8,128)(2,1)S(1)}, bf16[96,1408]{1,0:T(8,128)(2,1)S(1)}, u32[]{:S(2)}, u32[]{:S(2)}) %collective-permute-start.7) | collective-permute-done | bytes 270368 | tf_op jit(solution)/shard_map/ppermute | solution.py:124
  128.7 0.7 copy-done.5
  129.4 0.7 copy-done.6
  130.1 1.7 fusion.34
  131.8 7.5 %all-to-all-start.3 = ((bf16[32,32,896]{2,1,0:T(8,128)(2,1)}), bf16[32,32,896]{2,1,0:T(8,128)(2,1)}, u32[]{:S(2)}, u32[]{:S(2)}) async-start(bf16[32,32,896]{2,1,0:T(8,128)(2,1)} %bitcast.34), calls=%async_computation.3 | async-start | bytes 3670016 | tf_op jit(solution)/shard_map/all_to_all | solution.py:132
  139.3 2.7 %fusion.7 = bf16[384,1024]{1,0:T(8,128)(2,1)S(1)} fusion(bf16[1024,1024]{1,0:T(8,128)(2,1)} %bitcast.10, bf16[1,384,4608]{2,1,0:T(8,128)(2,1)} %param.10, s32[1024]{0:T(1024)S(1)} %sub.19), kind=kOutput, calls=%fused_computation.18 | convolution fusion | flops 806879232 | bytes 3674112 | tf_op jit(solution)/shard_map/dot_general | solution.py:116
  142.2 1.6 collective-permute-start.10
  143.8 1.8 collective-permute-start.11
  145.8 0.9 collective-permute-start.12
  146.7 3.6 %collective-permute-start.13 = (bf16[96,1280]{1,0:T(8,128)(2,1)S(1)}, bf16[96,1280]{1,0:T(8,128)(2,1)S(1)}, u32[]{:S(2)}, u32[]{:S(2)}) collective-permute-start(bf16[96,1280]{1,0:T(8,128)(2,1)S(1)} %get-tuple-element.45.refs_1_), channel_id=1, source_target_pairs={{0,64},{32,96},{64,0},{96,32},{1,65},{33,97},{65,1},{97,33},{2,66}... | collective-permute-start | bytes 737288 | tf_op jit(solution)/shard_map/ppermute | solution.py:124
  150.3 1.2 collective-permute-done.10
  151.5 1.6 collective-permute-start.14
  153.1 1.5 collective-permute-done.11
  154.7 0.5 collective-permute-done.9
  155.2 5.7 %collective-permute-done.12.refs_2_ = bf16[96,1280]{1,0:T(8,128)(2,1)S(1)} collective-permute-done((bf16[96,1280]{1,0:T(8,128)(2,1)S(1)}, bf16[96,1280]{1,0:T(8,128)(2,1)S(1)}, u32[]{:S(2)}, u32[]{:S(2)}) %collective-permute-start.12) | collective-permute-done | bytes 245792 | tf_op jit(solution)/shard_map/ppermute | solution.py:124
  161.0 4.5 %collective-permute-done.13.refs_3_ = bf16[96,1280]{1,0:T(8,128)(2,1)S(1)} collective-permute-done((bf16[96,1280]{1,0:T(8,128)(2,1)S(1)}, bf16[96,1280]{1,0:T(8,128)(2,1)S(1)}, u32[]{:S(2)}, u32[]{:S(2)}) %collective-permute-start.13) | collective-permute-done | bytes 245792 | tf_op jit(solution)/shard_map/ppermute | solution.py:124
  165.5 0.7 copy-done.8
  166.2 0.7 copy-done.9
  166.9 2.5 %fusion.32 = (bf16[96,1024]{1,0:T(8,128)(2,1)}, f32[96,1024]{1,0:T(8,128)}, f32[96,1024]{1,0:T(8,128)}, f32[96,1024]{1,0:T(8,128)S(1)}) fusion(f32[96,4608]{1,0:T(8,128)} %param.11, f32[96,1024]{1,0:T(8,128)S(1)} %convert_add_fusion.3, f32[96,4608]{1,0:T(8,128)} %param.12, f32[96,4608]{1,0:T(8,128)} %param.13), kind=kLoop, calls=%fused_computation.81 | loop fusion | flops 1572864 | bytes 2949120 | tf_op jit(solution)/shard_map/convert_element_type | solution.py:146
  169.4 2.6 %fusion.12 = bf16[384,896]{1,0:T(8,128)(2,1)S(1)} fusion(bf16[1024,896]{1,0:T(8,128)(2,1)} %bitcast.13, s32[1024]{0:T(1024)S(1)} %sub.19, bf16[1,384,4608]{2,1,0:T(8,128)(2,1)} %param.10), kind=kOutput, calls=%fused_computation.24 | convolution fusion | flops 706068480 | bytes 3215360 | tf_op jit(solution)/shard_map/dot_general | solution.py:116
  172.0 0.9 constant_dynamic-slice_fusion
  172.9 2.3 %collective-permute-start.16 = (bf16[96,896]{1,0:T(8,128)(2,1)}, bf16[96,896]{1,0:T(8,128)(2,1)}, u32[]{:S(2)}, u32[]{:S(2)}) collective-permute-start(bf16[96,896]{1,0:T(8,128)(2,1)} %get-tuple-element.39), channel_id=1, source_target_pairs={{0,64},{32,96},{64,0},{96,32},{1,65},{33,97},{65,1},{97,33},{2,66}... | collective-permute-start | bytes 516104 | tf_op jit(solution)/shard_map/ppermute | solution.py:142
  175.2 1.9 collective-permute-start.17
  177.1 2.2 %shard_map.102.refs_0_ = bf16[384,4608]{1,0:T(8,128)(2,1)} custom-call(s32[1]{0:T(128)} %bitcast.15.here_ref, bf16[96,1408]{1,0:T(8,128)(2,1)} %copy-done.2, bf16[96,1408]{1,0:T(8,128)(2,1)} %copy-done.4, bf16[96,1408]{1,0:T(8,128)(2,1)} %copy-done.5, bf16[96,1408]{1,0:T(8,128)(2,1)} %copy-done.6), custom_call_target="tpu_custom_call" | custom-call | bytes 2162688 | tf_op jit(solution)/shard_map/pallas_call | solution.py:45
  179.3 2.3 %shard_map.103.refs_0_ = bf16[384,4608]{1,0:T(8,128)(2,1)} custom-call(s32[1]{0:T(128)} %bitcast.15.here_ref, bf16[384,4608]{1,0:T(8,128)(2,1)} %shard_map.102.refs_0_, bf16[96,1280]{1,0:T(8,128)(2,1)} %copy-done.3, bf16[96,1280]{1,0:T(8,128)(2,1)} %copy-done.7, bf16[96,1280]{1,0:T(8,128)(2,1)} %copy-done.8, ...), custom_call_target="tpu_custom_call", output_to_operand_aliasing={{}: (1, {})} | custom-call | bytes 1966080 | tf_op jit(solution)/shard_map/pallas_call | solution.py:45
  181.9 1.9 collective-permute-start.19
  183.8 2.5 %collective-permute-start.20 = (bf16[96,1024]{1,0:T(8,128)(2,1)}, bf16[96,1024]{1,0:T(8,128)(2,1)}, u32[]{:S(2)}, u32[]{:S(2)}) collective-permute-start(bf16[96,1024]{1,0:T(8,128)(2,1)} %get-tuple-element.49.refs_1_), channel_id=1, source_target_pairs={{0,96},{32,0},{64,32},{96,64},{1,97},{33,1},{65,33},{97,65},{2,98}... | collective-permute-start | bytes 589832 | tf_op jit(solution)/shard_map/ppermute | solution.py:124
  186.3 2.5 %fusion.30 = (bf16[96,896]{1,0:T(8,128)(2,1)}, f32[96,896]{1,0:T(8,128)S(1)}, f32[96,896]{1,0:T(8,128)S(1)}, f32[96,896]{1,0:T(8,128)S(1)}) fusion(f32[96,4608]{1,0:T(8,128)} %param.11, bf16[96,896]{1,0:T(8,128)(2,1)} %collective-permute-done.17, bf16[96,896]{1,0:T(8,128)(2,1)} %collective-permute-done.16, bf16[96,896]{1,0:T(8,128)(2,1)} %collective-permute-done.15, ...), kind=kLoop, calls=%fused_computation.80 | loop fusion | flops 1978368 | bytes 2924544 | tf_op jit(solution)/shard_map/convert_element_type | solution.py:146
  188.8 2.2 %collective-permute-start.22 = (bf16[96,896]{1,0:T(8,128)(2,1)}, bf16[96,896]{1,0:T(8,128)(2,1)}, u32[]{:S(2)}, u32[]{:S(2)}) collective-permute-start(bf16[96,896]{1,0:T(8,128)(2,1)} %get-tuple-element.50.refs_1_), channel_id=1, source_target_pairs={{0,64},{32,96},{64,0},{96,32},{1,65},{33,97},{65,1},{97,33},{2,66}... | collective-permute-start | bytes 516104 | tf_op jit(solution)/shard_map/ppermute | solution.py:124
  191.0 2.2 %pad_maximum_fusion = (f32[96,4608]{1,0:T(8,128)}, f32[96,4608]{1,0:T(8,128)}) fusion(f32[96,896]{1,0:T(8,128)S(1)} %get-tuple-element.51, f32[96,1024]{1,0:T(8,128)S(1)} %copy-done, f32[96,1280]{1,0:T(8,128)S(1)} %get-tuple-element.59, f32[96,1408]{1,0:T(8,128)S(1)} %get-tuple-element.63, f32[96,896]{1,0:T(8,128)S(1)} %get-tuple-element.52, ...), kind=kLoop, calls=%fused_computation.14 | loop fusion | flops 2654208 | bytes 7077888 | tf_op jit(solution)/shard_map/concatenate | solution.py:151
  193.5 1.7 collective-permute-start.23
  195.2 1.4 pad_maximum_fusion.2
  196.5 0.7 copy-done.11
  197.2 2.1 %shard_map.104.refs_0_ = bf16[384,4608]{1,0:T(8,128)(2,1)} custom-call(s32[1]{0:T(128)} %bitcast.15.here_ref, bf16[384,4608]{1,0:T(8,128)(2,1)} %shard_map.103.refs_0_, bf16[96,1024]{1,0:T(8,128)(2,1)} %get-tuple-element.49.refs_1_, bf16[96,1024]{1,0:T(8,128)(2,1)} %copy-done.10, bf16[96,1024]{1,0:T(8,128)(2,1)} %copy-done.11, ...), custom_call_target="tpu_custom_call", output_to_operand_aliasing={{}: (1, {})} | custom-call | bytes 1572864 | tf_op jit(solution)/shard_map/pallas_call | solution.py:45
  199.4 0.8 collective-permute-done.21.refs_2_
  200.6 0.7 copy-done.12
  201.3 2.0 %shard_map.105 = bf16[384,4608]{1,0:T(8,128)(2,1)} custom-call(s32[1]{0:T(128)} %bitcast.15.here_ref, bf16[384,4608]{1,0:T(8,128)(2,1)} %shard_map.104.refs_0_, bf16[96,896]{1,0:T(8,128)(2,1)} %get-tuple-element.50.refs_1_, bf16[96,896]{1,0:T(8,128)(2,1)} %collective-permute-done.21.refs_2_, ...), custom_call_target="tpu_custom_call", output_to_operand_aliasing={{}: (1, {})} | custom-call | bytes 1376256 | tf_op jit(solution)/shard_map/pallas_call | solution.py:45
  (58 shorter events, 2.9 us)
Async XLA Ops:
  7.8 44.9 %all-to-all-start = ((bf16[32,32,1408]{2,1,0:T(8,128)(2,1)}), bf16[32,32,1408]{2,1,0:T(8,128)(2,1)S(1)}, u32[]{:S(2)}, u32[]{:S(2)}) async-start(bf16[32,32,1408]{2,1,0:T(8,128)(2,1)} %bitcast.31), calls=%async_computation | async-start | bytes 5767168 | tf_op jit(solution)/shard_map/all_to_all | solution.py:132
  52.7 4.9 %copy-start.13 = (s32[16384,1]{0,1:T(1,128)S(1)}, s32[16384,1]{0,1:T(1,128)}, u32[]{:S(2)}) copy-start(s32[16384,1]{0,1:T(1,128)} %param.9) | copy-start | bytes 196612
  52.7 39.6 %all-to-all-start.1 = ((bf16[32,32,1280]{2,1,0:T(8,128)(2,1)}), bf16[32,32,1280]{2,1,0:T(8,128)(2,1)}, u32[]{:S(2)}, u32[]{:S(2)}) async-start(bf16[32,32,1280]{2,1,0:T(8,128)(2,1)} %bitcast.32), calls=%async_computation.1 | async-start | bytes 5242880 | tf_op jit(solution)/shard_map/all_to_all | solution.py:132
  61.5 10.8 %collective-permute-start = (bf16[96,1408]{1,0:T(8,128)(2,1)S(1)}, bf16[96,1408]{1,0:T(8,128)(2,1)S(1)}, u32[]{:S(2)}, u32[]{:S(2)}) collective-permute-start(bf16[96,1408]{1,0:T(8,128)(2,1)S(1)} %get-tuple-element.66), channel_id=1, source_target_pairs={{0,32},{32,64},{64,96},{96,0},{1,33},{33,65},{65,97},{97,1},{2,34}... | collective-permute-start | bytes 811016 | tf_op jit(solution)/shard_map/ppermute | solution.py:142
  63.5 15.8 %collective-permute-start.1 = (bf16[96,1408]{1,0:T(8,128)(2,1)S(1)}, bf16[96,1408]{1,0:T(8,128)(2,1)S(1)}, u32[]{:S(2)}, u32[]{:S(2)}) collective-permute-start(bf16[96,1408]{1,0:T(8,128)(2,1)S(1)} %get-tuple-element.68), channel_id=1, source_target_pairs={{0,64},{32,96},{64,0},{96,32},{1,65},{33,97},{65,1},{97,33},{2,66}... | collective-permute-start | bytes 811016 | tf_op jit(solution)/shard_map/ppermute | solution.py:142
  67.0 12.3 %collective-permute-start.2 = (bf16[96,1408]{1,0:T(8,128)(2,1)S(1)}, bf16[96,1408]{1,0:T(8,128)(2,1)S(1)}, u32[]{:S(2)}, u32[]{:S(2)}) collective-permute-start(bf16[96,1408]{1,0:T(8,128)(2,1)S(1)} %get-tuple-element.67), channel_id=1, source_target_pairs={{0,96},{32,0},{64,32},{96,64},{1,97},{33,1},{65,33},{97,65},{2,98}... | collective-permute-start | bytes 811016 | tf_op jit(solution)/shard_map/ppermute | solution.py:142
  81.2 30.8 %copy-start.2 = (bf16[96,1408]{1,0:T(8,128)(2,1)}, bf16[96,1408]{1,0:T(8,128)(2,1)S(1)}, u32[]{:S(2)}) copy-start(bf16[96,1408]{1,0:T(8,128)(2,1)S(1)} %get-tuple-element.41.refs_0_) | copy-start | bytes 811012
  92.2 39.6 %all-to-all-start.2 = ((bf16[32,32,1024]{2,1,0:T(8,128)(2,1)}), bf16[32,32,1024]{2,1,0:T(8,128)(2,1)}, u32[]{:S(2)}, u32[]{:S(2)}) async-start(bf16[32,32,1024]{2,1,0:T(8,128)(2,1)} %bitcast.33), calls=%async_computation.2 | async-start | bytes 4194304 | tf_op jit(solution)/shard_map/all_to_all | solution.py:132
  100.3 11.7 %collective-permute-start.3 = (bf16[96,1280]{1,0:T(8,128)(2,1)S(1)}, bf16[96,1280]{1,0:T(8,128)(2,1)S(1)}, u32[]{:S(2)}, u32[]{:S(2)}) collective-permute-start(bf16[96,1280]{1,0:T(8,128)(2,1)S(1)} %get-tuple-element.69), channel_id=1, source_target_pairs={{0,32},{32,64},{64,96},{96,0},{1,33},{33,65},{65,97},{97,1},{2,34}... | collective-permute-start | bytes 737288 | tf_op jit(solution)/shard_map/ppermute | solution.py:142
  102.3 15.7 %collective-permute-start.4 = (bf16[96,1280]{1,0:T(8,128)(2,1)S(1)}, bf16[96,1280]{1,0:T(8,128)(2,1)S(1)}, u32[]{:S(2)}, u32[]{:S(2)}) collective-permute-start(bf16[96,1280]{1,0:T(8,128)(2,1)S(1)} %get-tuple-element.71), channel_id=1, source_target_pairs={{0,64},{32,96},{64,0},{96,32},{1,65},{33,97},{65,1},{97,33},{2,66}... | collective-permute-start | bytes 737288 | tf_op jit(solution)/shard_map/ppermute | solution.py:142
  105.9 12.1 %collective-permute-start.5 = (bf16[96,1280]{1,0:T(8,128)(2,1)S(1)}, bf16[96,1280]{1,0:T(8,128)(2,1)S(1)}, u32[]{:S(2)}, u32[]{:S(2)}) collective-permute-start(bf16[96,1280]{1,0:T(8,128)(2,1)S(1)} %get-tuple-element.70), channel_id=1, source_target_pairs={{0,96},{32,0},{64,32},{96,64},{1,97},{33,1},{65,33},{97,65},{2,98}... | collective-permute-start | bytes 737288 | tf_op jit(solution)/shard_map/ppermute | solution.py:142
  110.5 13.1 %collective-permute-start.6 = (bf16[96,1408]{1,0:T(8,128)(2,1)S(1)}, bf16[96,1408]{1,0:T(8,128)(2,1)S(1)}, u32[]{:S(2)}, u32[]{:S(2)}) collective-permute-start(bf16[96,1408]{1,0:T(8,128)(2,1)S(1)} %get-tuple-element.41.refs_0_), channel_id=1, source_target_pairs={{0,32},{32,64},{64,96},{96,0},{1,33},{33,65},{65,97},{97,1},{2,34}... | collective-permute-start | bytes 811016 | tf_op jit(solution)/shard_map/ppermute | solution.py:124
  111.6 17.1 %collective-permute-start.7 = (bf16[96,1408]{1,0:T(8,128)(2,1)S(1)}, bf16[96,1408]{1,0:T(8,128)(2,1)S(1)}, u32[]{:S(2)}, u32[]{:S(2)}) collective-permute-start(bf16[96,1408]{1,0:T(8,128)(2,1)S(1)} %get-tuple-element.41.refs_0_), channel_id=1, source_target_pairs={{0,64},{32,96},{64,0},{96,32},{1,65},{33,97},{65,1},{97,33},{2,66}... | collective-permute-start | bytes 811016 | tf_op jit(solution)/shard_map/ppermute | solution.py:124
  112.0 16.7 %collective-permute-start.8 = (bf16[96,1408]{1,0:T(8,128)(2,1)S(1)}, bf16[96,1408]{1,0:T(8,128)(2,1)S(1)}, u32[]{:S(2)}, u32[]{:S(2)}) collective-permute-start(bf16[96,1408]{1,0:T(8,128)(2,1)S(1)} %get-tuple-element.41.refs_0_), channel_id=1, source_target_pairs={{0,96},{32,0},{64,32},{96,64},{1,97},{33,1},{65,33},{97,65},{2,98}... | collective-permute-start | bytes 811016 | tf_op jit(solution)/shard_map/ppermute | solution.py:124
  123.6 5.0 %copy-start.4 = (bf16[96,1408]{1,0:T(8,128)(2,1)}, bf16[96,1408]{1,0:T(8,128)(2,1)S(1)}, u32[]{:S(2)}) copy-start(bf16[96,1408]{1,0:T(8,128)(2,1)S(1)} %collective-permute-done.6.refs_1_) | copy-start | bytes 811012
  128.7 0.7 copy-start.5
  129.4 0.7 copy-start.6
  131.8 19.7 %copy-start.3 = (bf16[96,1280]{1,0:T(8,128)(2,1)}, bf16[96,1280]{1,0:T(8,128)(2,1)S(1)}, u32[]{:S(2)}) copy-start(bf16[96,1280]{1,0:T(8,128)(2,1)S(1)} %get-tuple-element.45.refs_1_) | copy-start | bytes 737284
  131.8 37.5 %all-to-all-start.3 = ((bf16[32,32,896]{2,1,0:T(8,128)(2,1)}), bf16[32,32,896]{2,1,0:T(8,128)(2,1)}, u32[]{:S(2)}, u32[]{:S(2)}) async-start(bf16[32,32,896]{2,1,0:T(8,128)(2,1)} %bitcast.34), calls=%async_computation.3 | async-start | bytes 3670016 | tf_op jit(solution)/shard_map/all_to_all | solution.py:132
  142.2 9.3 %collective-permute-start.10 = (bf16[96,1024]{1,0:T(8,128)(2,1)S(1)}, bf16[96,1024]{1,0:T(8,128)(2,1)S(1)}, u32[]{:S(2)}, u32[]{:S(2)}) collective-permute-start(bf16[96,1024]{1,0:T(8,128)(2,1)S(1)} %get-tuple-element.74), channel_id=1, source_target_pairs={{0,64},{32,96},{64,0},{96,32},{1,65},{33,97},{65,1},{97,33},{2,66}... | collective-permute-start | bytes 589832 | tf_op jit(solution)/shard_map/ppermute | solution.py:142
  143.8 10.9 %collective-permute-start.11 = (bf16[96,1024]{1,0:T(8,128)(2,1)S(1)}, bf16[96,1024]{1,0:T(8,128)(2,1)S(1)}, u32[]{:S(2)}, u32[]{:S(2)}) collective-permute-start(bf16[96,1024]{1,0:T(8,128)(2,1)S(1)} %get-tuple-element.73), channel_id=1, source_target_pairs={{0,96},{32,0},{64,32},{96,64},{1,97},{33,1},{65,33},{97,65},{2,98}... | collective-permute-start | bytes 589832 | tf_op jit(solution)/shard_map/ppermute | solution.py:142
  145.6 9.6 %collective-permute-start.9 = (bf16[96,1024]{1,0:T(8,128)(2,1)S(1)}, bf16[96,1024]{1,0:T(8,128)(2,1)S(1)}, u32[]{:S(2)}, u32[]{:S(2)}) collective-permute-start(bf16[96,1024]{1,0:T(8,128)(2,1)S(1)} %get-tuple-element.72), channel_id=1, source_target_pairs={{0,32},{32,64},{64,96},{96,0},{1,33},{33,65},{65,97},{97,1},{2,34}... | collective-permute-start | bytes 589832 | tf_op jit(solution)/shard_map/ppermute | solution.py:142
  145.8 15.2 %collective-permute-start.12 = (bf16[96,1280]{1,0:T(8,128)(2,1)S(1)}, bf16[96,1280]{1,0:T(8,128)(2,1)S(1)}, u32[]{:S(2)}, u32[]{:S(2)}) collective-permute-start(bf16[96,1280]{1,0:T(8,128)(2,1)S(1)} %get-tuple-element.45.refs_1_), channel_id=1, source_target_pairs={{0,32},{32,64},{64,96},{96,0},{1,33},{33,65},{65,97},{97,1},{2,34}... | collective-permute-start | bytes 737288 | tf_op jit(solution)/shard_map/ppermute | solution.py:124
  146.7 18.8 %collective-permute-start.13 = (bf16[96,1280]{1,0:T(8,128)(2,1)S(1)}, bf16[96,1280]{1,0:T(8,128)(2,1)S(1)}, u32[]{:S(2)}, u32[]{:S(2)}) collective-permute-start(bf16[96,1280]{1,0:T(8,128)(2,1)S(1)} %get-tuple-element.45.refs_1_), channel_id=1, source_target_pairs={{0,64},{32,96},{64,0},{96,32},{1,65},{33,97},{65,1},{97,33},{2,66}... | collective-permute-start | bytes 737288 | tf_op jit(solution)/shard_map/ppermute | solution.py:124
  151.5 14.0 %collective-permute-start.14 = (bf16[96,1280]{1,0:T(8,128)(2,1)S(1)}, bf16[96,1280]{1,0:T(8,128)(2,1)S(1)}, u32[]{:S(2)}, u32[]{:S(2)}) collective-permute-start(bf16[96,1280]{1,0:T(8,128)(2,1)S(1)} %get-tuple-element.45.refs_1_), channel_id=1, source_target_pairs={{0,96},{32,0},{64,32},{96,64},{1,97},{33,1},{65,33},{97,65},{2,98}... | collective-permute-start | bytes 737288 | tf_op jit(solution)/shard_map/ppermute | solution.py:124
  161.0 4.5 %copy-start.7 = (bf16[96,1280]{1,0:T(8,128)(2,1)}, bf16[96,1280]{1,0:T(8,128)(2,1)S(1)}, u32[]{:S(2)}) copy-start(bf16[96,1280]{1,0:T(8,128)(2,1)S(1)} %collective-permute-done.12.refs_2_) | copy-start | bytes 737284
  165.5 0.7 copy-start.8
  166.2 0.7 copy-start.9
  172.9 10.9 %collective-permute-start.15 = (bf16[96,896]{1,0:T(8,128)(2,1)}, bf16[96,896]{1,0:T(8,128)(2,1)}, u32[]{:S(2)}, u32[]{:S(2)}) collective-permute-start(bf16[96,896]{1,0:T(8,128)(2,1)} %get-tuple-element.38), channel_id=1, source_target_pairs={{0,32},{32,64},{64,96},{96,0},{1,33},{33,65},{65,97},{97,1},{2,34}... | collective-permute-start | bytes 516104 | tf_op jit(solution)/shard_map/ppermute | solution.py:142
  172.9 13.4 %collective-permute-start.16 = (bf16[96,896]{1,0:T(8,128)(2,1)}, bf16[96,896]{1,0:T(8,128)(2,1)}, u32[]{:S(2)}, u32[]{:S(2)}) collective-permute-start(bf16[96,896]{1,0:T(8,128)(2,1)} %get-tuple-element.39), channel_id=1, source_target_pairs={{0,64},{32,96},{64,0},{96,32},{1,65},{33,97},{65,1},{97,33},{2,66}... | collective-permute-start | bytes 516104 | tf_op jit(solution)/shard_map/ppermute | solution.py:142
  175.2 11.1 %collective-permute-start.17 = (bf16[96,896]{1,0:T(8,128)(2,1)}, bf16[96,896]{1,0:T(8,128)(2,1)}, u32[]{:S(2)}, u32[]{:S(2)}) collective-permute-start(bf16[96,896]{1,0:T(8,128)(2,1)} %get-tuple-element.40), channel_id=1, source_target_pairs={{0,96},{32,0},{64,32},{96,64},{1,97},{33,1},{65,33},{97,65},{2,98}... | collective-permute-start | bytes 516104 | tf_op jit(solution)/shard_map/ppermute | solution.py:142
  181.6 9.4 %copy-start = (f32[96,1024]{1,0:T(8,128)S(1)}, f32[96,1024]{1,0:T(8,128)}, u32[]{:S(2)}) copy-start(f32[96,1024]{1,0:T(8,128)} %get-tuple-element.55) | copy-start | bytes 1179652
  181.6 9.4 %copy-start.1 = (f32[96,1024]{1,0:T(8,128)S(1)}, f32[96,1024]{1,0:T(8,128)}, u32[]{:S(2)}) copy-start(f32[96,1024]{1,0:T(8,128)} %get-tuple-element.56) | copy-start | bytes 1179652
  181.6 11.9 %collective-permute-start.18 = (bf16[96,1024]{1,0:T(8,128)(2,1)}, bf16[96,1024]{1,0:T(8,128)(2,1)S(1)}, u32[]{:S(2)}, u32[]{:S(2)}) collective-permute-start(bf16[96,1024]{1,0:T(8,128)(2,1)} %get-tuple-element.49.refs_1_), channel_id=1, source_target_pairs={{0,32},{32,64},{64,96},{96,0},{1,33},{33,65},{65,97},{97,1},{2,34}... | collective-permute-start | bytes 589832 | tf_op jit(solution)/shard_map/ppermute | solution.py:124
  181.9 14.7 %collective-permute-start.19 = (bf16[96,1024]{1,0:T(8,128)(2,1)}, bf16[96,1024]{1,0:T(8,128)(2,1)S(1)}, u32[]{:S(2)}, u32[]{:S(2)}) collective-permute-start(bf16[96,1024]{1,0:T(8,128)(2,1)} %get-tuple-element.49.refs_1_), channel_id=1, source_target_pairs={{0,64},{32,96},{64,0},{96,32},{1,65},{33,97},{65,1},{97,33},{2,66}... | collective-permute-start | bytes 589832 | tf_op jit(solution)/shard_map/ppermute | solution.py:124
  183.8 13.4 %collective-permute-start.20 = (bf16[96,1024]{1,0:T(8,128)(2,1)}, bf16[96,1024]{1,0:T(8,128)(2,1)}, u32[]{:S(2)}, u32[]{:S(2)}) collective-permute-start(bf16[96,1024]{1,0:T(8,128)(2,1)} %get-tuple-element.49.refs_1_), channel_id=1, source_target_pairs={{0,96},{32,0},{64,32},{96,64},{1,97},{33,1},{65,33},{97,65},{2,98}... | collective-permute-start | bytes 589832 | tf_op jit(solution)/shard_map/ppermute | solution.py:124
  188.8 11.4 %collective-permute-start.21 = (bf16[96,896]{1,0:T(8,128)(2,1)}, bf16[96,896]{1,0:T(8,128)(2,1)}, u32[]{:S(2)}, u32[]{:S(2)}) collective-permute-start(bf16[96,896]{1,0:T(8,128)(2,1)} %get-tuple-element.50.refs_1_), channel_id=1, source_target_pairs={{0,32},{32,64},{64,96},{96,0},{1,33},{33,65},{65,97},{97,1},{2,34}... | collective-permute-start | bytes 516104 | tf_op jit(solution)/shard_map/ppermute | solution.py:124
  188.8 11.4 %collective-permute-start.22 = (bf16[96,896]{1,0:T(8,128)(2,1)}, bf16[96,896]{1,0:T(8,128)(2,1)}, u32[]{:S(2)}, u32[]{:S(2)}) collective-permute-start(bf16[96,896]{1,0:T(8,128)(2,1)} %get-tuple-element.50.refs_1_), channel_id=1, source_target_pairs={{0,64},{32,96},{64,0},{96,32},{1,65},{33,97},{65,1},{97,33},{2,66}... | collective-permute-start | bytes 516104 | tf_op jit(solution)/shard_map/ppermute | solution.py:124
  193.5 3.0 %copy-start.10 = (bf16[96,1024]{1,0:T(8,128)(2,1)}, bf16[96,1024]{1,0:T(8,128)(2,1)S(1)}, u32[]{:S(2)}) copy-start(bf16[96,1024]{1,0:T(8,128)(2,1)S(1)} %collective-permute-done.18.refs_2_) | copy-start | bytes 589828
  193.5 7.2 %collective-permute-start.23 = (bf16[96,896]{1,0:T(8,128)(2,1)}, bf16[96,896]{1,0:T(8,128)(2,1)S(1)}, u32[]{:S(2)}, u32[]{:S(2)}) collective-permute-start(bf16[96,896]{1,0:T(8,128)(2,1)} %get-tuple-element.50.refs_1_), channel_id=1, source_target_pairs={{0,96},{32,0},{64,32},{96,64},{1,97},{33,1},{65,33},{97,65},{2,98}... | collective-permute-start | bytes 516104 | tf_op jit(solution)/shard_map/ppermute | solution.py:124
  196.5 0.7 copy-start.11
  200.6 0.7 copy-start.12

commit v3 on v1

v3 whole, which is shorter than its diff:
```python
import functools

import jax
import jax.numpy as jnp
from jax import lax
from jax.experimental import pallas as pl
from jax.experimental.pallas import tpu as pltpu
from jax.sharding import PartitionSpec as P

beta_first = 0.9
beta_second = 0.95
learn_rate = 0.01
weight_decay = 0.1
epsilon = 1e-08
correct_first = 1.0 - 0.9**10
correct_second = 1.0 - 0.95**10

GROUPS = 4
OWNERS = 32
CAPACITY = 32
UNITS = (12, 10, 8, 6)
TILE = 2
MIB = 1024 * 1024


def after(value, *others):
    return lax.optimization_barrier((value, others))[0]


def swap_z(block, flip):
    return lax.ppermute(block, "dp", [(i, i ^ flip) for i in range(GROUPS)])


def whole(memory_space):
    return pl.BlockSpec(memory_space=memory_space)


def cost(flops, moved):
    return pl.CostEstimate(flops=flops, bytes_accessed=moved, transcendentals=0)


def combine_body(here_ref, target_ref, head_ref, part_ref, own_ref, *refs):
    out_refs, table_ref = (own_ref,) + refs[:-1], refs[-1]
    share = own_ref.shape[0]
    slots = target_ref.shape[1]
    starts = [lax.bitwise_xor(here_ref[0], flip) * share for flip in range(GROUPS)]

    @pl.when(pl.program_id(0) == 0)
    def _():
        for flip, start in enumerate(starts):
            row = lax.broadcasted_iota(jnp.int32, (share, slots), 0) + start
            hit = row == target_ref[...]
            table_ref[pl.ds(flip * share, share), :] = jnp.where(hit, 1.0, 0.0).astype(jnp.bfloat16)

    total = jnp.dot(table_ref[...], part_ref[...], preferred_element_type=jnp.float32)
    for flip, (start, out_ref) in enumerate(zip(starts, out_refs)):
        head = head_ref[0, pl.ds(pl.multiple_of(start, share), share), :].astype(jnp.float32)
        block = total[flip * share : (flip + 1) * share, :] + head
        out_ref[...] = block.astype(out_ref.dtype)


def combine(here, target, head_grad, part, start, tile):
    slots = target.shape[1]
    width = part.shape[1]
    slab_rows = head_grad.shape[1]
    share = slab_rows // GROUPS
    return pl.pallas_call(
        combine_body,
        grid=(width // tile,),
        out_shape=[jax.ShapeDtypeStruct((share, width), jnp.float32)]
        + [jax.ShapeDtypeStruct((share, width), jnp.bfloat16)] * (GROUPS - 1),
        in_specs=[
            whole(pltpu.SMEM),
            pl.BlockSpec((1, slots), lambda i: (0, 0)),
            pl.BlockSpec((1, slab_rows, tile), lambda i: (0, 0, start // tile + i)),
            pl.BlockSpec((slots, tile), lambda i: (0, i)),
        ],
        out_specs=[pl.BlockSpec((share, tile), lambda i: (0, i))] * GROUPS,
        scratch_shapes=[pltpu.VMEM((slab_rows, slots), jnp.bfloat16)],
        compiler_params=pltpu.CompilerParams(vmem_limit_bytes=16 * MIB),
        cost_estimate=cost(2 * slab_rows * slots * width, (2 * slots + 5 * slab_rows) * width),
    )(here.reshape(1), target, head_grad, part)


def place_body(first, spots, share, here_ref, *refs):
    blocks, table_ref, sems = refs[first:-2], refs[-2], refs[-1]
    copies = []
    for at, (block, offset, flip, start) in enumerate(spots):
        row = pl.multiple_of(lax.bitwise_xor(here_ref[0], flip) * share, share)
        source = blocks[block]
        copies.append(
            pltpu.make_async_copy(
                source.at[pl.ds(offset, share), :],
                table_ref.at[pl.ds(row, share), pl.ds(start, source.shape[1])],
                sems.at[at],
            )
        )
    for copy in copies:
        copy.start()
    for copy in copies:
        copy.wait()


def place(table, here, blocks, spots, share, shape):
    before = [] if table is None else [table]
    return pl.pallas_call(
        functools.partial(place_body, len(before), spots, share),
        out_shape=jax.ShapeDtypeStruct(shape, jnp.bfloat16),
        in_specs=[whole(pltpu.SMEM)]
        + [whole(pl.ANY)] * len(before)
        + [whole(pltpu.VMEM)] * len(blocks),
        out_specs=whole(pl.ANY),
        scratch_shapes=[pltpu.SemaphoreType.DMA((len(spots),))],
        input_output_aliases={1: 0} if before else {},
        compiler_params=pltpu.CompilerParams(vmem_limit_bytes=8 * MIB),
        cost_estimate=cost(0, 4 * sum(block.size for block in blocks)),
    )(here.reshape(1), *before, *blocks)


def update(grad, master, moment_one, moment_two):
    first = beta_first * moment_one + (1.0 - beta_first) * grad
    second = beta_second * moment_two + (1.0 - beta_second) * grad * grad
    step_dir = (
        first / correct_first / (jnp.sqrt(second / correct_second) + epsilon)
        + weight_decay * master
    )
    return master - learn_rate * step_dir, first, second


def local(input_grad, token_slab, token_offset, head_grad, master, moment_one, moment_two):
    here, myself = lax.axis_index("dp"), lax.axis_index("vocab")
    tok_rows, width = input_grad.shape
    slab_rows = head_grad.shape[1]
    share = slab_rows // GROUPS
    slots = OWNERS * CAPACITY
    owners = token_slab[:, 0].reshape(OWNERS, tok_rows)
    offsets = token_offset[:, 0].reshape(OWNERS, tok_rows)

    order = jnp.arange(tok_rows, dtype=jnp.int32)
    earlier = (order[:, None] < order[None, :]).astype(jnp.bfloat16)

    own = lax.dynamic_index_in_dim(owners, myself, 0, keepdims=False)
    named = own[None, :] == jnp.arange(OWNERS, dtype=jnp.int32)[:, None]
    before = jnp.dot(named.astype(jnp.bfloat16), earlier, preferred_element_type=jnp.float32)
    own_rank = jnp.sum(jnp.where(named, before, 0.0), axis=0).astype(jnp.int32)
    slot_of = own * CAPACITY + own_rank
    slot_ids = jnp.arange(slots, dtype=jnp.int32)[:, None]

    dispatch = (slot_ids == slot_of[None, :]).astype(jnp.bfloat16)

    mine = owners == myself
    rank = jnp.dot(
        mine.astype(jnp.bfloat16), earlier, preferred_element_type=jnp.float32
    ).astype(jnp.int32)
    held = mine[:, None, :] & (
        rank[:, None, :] == jnp.arange(CAPACITY, dtype=jnp.int32)[None, :, None]
    )
    target = jnp.sum(jnp.where(held, offsets[:, None, :] + 1, 0), axis=2) - 1
    target = target.reshape(1, slots)

    unit = width // sum(UNITS)
    edges = [unit * sum(UNITS[:i]) for i in range(len(UNITS) + 1)]
    spans = [slice(low, high) for low, high in zip(edges, edges[1:])]
    states, rows, joined, fars, blocks, spots = [], [], [], [], [], []
    arrived, last = (), len(spans) - 1
    for number, span in enumerate(spans):
        outgoing = jnp.dot(
            dispatch, input_grad[:, span], preferred_element_type=jnp.float32
        ).astype(jnp.bfloat16)
        earlier_work = target if number == 1 else rows[: max(0, number - 1)]
        outgoing = after(outgoing, arrived, earlier_work)
        arrived = lax.all_to_all(outgoing, "vocab", split_axis=0, concat_axis=0, tiled=True)
        ready = after(arrived, rows)
        grad, *pieces = combine(here, target, head_grad, ready, span.start, TILE * unit)
        if number == last:
            pieces = after(pieces, fars[: number - 1])
        for flip, piece in enumerate(pieces, 1):
            grad = grad + swap_z(piece, flip).astype(jnp.float32)
        if 1 <= number < last:
            grad = after(grad, joined, fars[: number - 1])
        states.append(update(grad, master[:, span], moment_one[:, span], moment_two[:, span]))
        block = states[-1][0].astype(jnp.bfloat16)
        rows.append(block)
        if number < last:
            both = jnp.concatenate([block, swap_z(block, 3)], axis=0)
            joined.append(both)
            spots += [
                (len(blocks), 0, 0, span.start),
                (len(blocks), share, 3, span.start),
                (len(blocks) + 1, 0, 1, span.start),
                (len(blocks) + 1, share, 2, span.start),
            ]
            fars.append(swap_z(both, 1))
            blocks += [both, fars[-1]]
    shape = (slab_rows, width)
    blocks = after(blocks, rows)
    table = place(None, here, blocks, tuple(spots), share, shape)
    blocks = [block] + [swap_z(block, flip) for flip in range(1, GROUPS)]
    spots = [(flip, 0, flip, span.start) for flip in range(GROUPS)]
    table = place(table, here, blocks, tuple(spots), share, shape)
    return tuple(jnp.concatenate(parts, axis=1) for parts in zip(*states)) + (table,)


def solution(mesh):
    placed = (
        P(("dp", "vocab"), None),
        P("dp", None),
        P("dp", None),
        P("dp", "vocab", None),
        P(("vocab", "dp"), None),
        P(("vocab", "dp"), None),
        P(("vocab", "dp"), None),
    )
    return jax.shard_map(
        local,
        mesh=mesh,
        in_specs=placed,
        out_specs=(
            P(("vocab", "dp"), None),
            P(("vocab", "dp"), None),
            P(("vocab", "dp"), None),
            P("vocab", None),
        ),
        check_vma=False,
    )
```

time: 219 us -> 199 us (0.909)
  waiting for transfers between devices: 106 us -> 79 us
  Pallas kernels: 0 us -> 17.7 us
  matrix products: 28.6 us -> 16.7 us
  other arithmetic: 14.1 us -> 18.8 us
  local copies, waits for them, and re-layouts: 8.88 us -> 5.37 us
    pallas_call x0 -> x6, Pallas kernels: none -> 17.7 us  [the longest x4 14 us: combine(): pl.pallas_call(combine_body, grid=(width // tile,), out_shape=[jax.ShapeD...]
    all_to_all x4, waiting for transfers between devices: 55.4 us -> 41.3 us  [local(): lax.all_to_all(outgoing, 'vocab', split_axis=0, concat_axis=0, tiled=True)]
    ppermute x24 -> x21, waiting for transfers between devices: 50.3 us -> 37.7 us  [swap_z(): return lax.ppermute(block, 'dp', [(i, i ^ flip) for i in range(GROUPS)])]
    dot_general x4 -> x0, matrix products: 11 us -> none  [local(): partial = jnp.dot(combine, arrived, preferred_element_type=jnp.float32)]
    convert_element_type x0 -> x4, other arithmetic: none -> 9.92 us  [local(): block = states[-1][0].astype(jnp.bfloat16)]
    dynamic_update_slice x4 -> x0, other arithmetic: 8.07 us -> none  [local(): lax.dynamic_update_slice(table, block, (lax.bitwise_and(here - hop, group...]
    concatenate x0 -> x3, other arithmetic: none -> 2.76 us  [local(): both = jnp.concatenate([block, swap_z(block, 3)], axis=0)]
    dynamic_slice x4 -> x0, local copies, waits for them, and re-layouts: 2.63 us -> none  [local(): lax.dynamic_slice_in_dim(partial, lax.bitwise_and(here + hop, groups - 1)...]
  transfers between devices with their start and end apart: 28 -> 25, of which waited for: 16 -> 14; matrix products, arithmetic and copies ran while one was open for 18% -> 15% of each run, Pallas kernels for 0% -> 9%
where the time goes in v3:
time: 199 us; the launch traced here: 197 us
  waiting for transfers between devices  79 us (40%)
  starting transfers between devices  58.5 us (29%)
  other arithmetic  18.8 us (9%)
  Pallas kernels  17.7 us (9%)
  matrix products  16.7 us (8%)
  local copies, waits for them, and re-layouts  5.37 us (3%)
    all_to_all x4, waiting for transfers between devices, local(): lax.all_to_all(outgoing, 'vocab', split_axis=0, concat_axis=0, tiled=True)  41.3 us
    ppermute x21, waiting for transfers between devices, swap_z(): return lax.ppermute(block, 'dp', [(i, i ^ flip) for i in range(GROUPS)])  37.7 us
    ppermute x21, starting transfers between devices, swap_z(): return lax.ppermute(block, 'dp', [(i, i ^ flip) for i in range(GROUPS)])  35.5 us
    all_to_all x4, starting transfers between devices, local(): lax.all_to_all(outgoing, 'vocab', split_axis=0, concat_axis=0, tiled=True)  23.1 us
    dot_general x4, matrix products, local(): jnp.dot(dispatch, input_grad[:, span], preferred_element_type=jnp.float32)  16.3 us
    pallas_call x4, Pallas kernels, combine(): pl.pallas_call(combine_body, grid=(width // tile,), out_shape=[jax.ShapeD...  14 us
    convert_element_type x4, other arithmetic, local(): block = states[-1][0].astype(jnp.bfloat16)  9.92 us
    unnamed x37, local copies, waits for them, and re-layouts  5.26 us
  transfers between devices with their start and end apart: 25, of which 14 were waited for; matrix products, arithmetic and copies ran while one was open for 15% of the time, Pallas kernels for 9%

profile of v3, /device:TPU:0, one launch (start us, length us, event | category | flops | bytes accessed | tf_op | source)
XLA Modules:
  0.0 197.3 jit_solution(10961311551481490464)
XLA Ops:
  0.6 0.5 broadcast.65
  1.1 1.6 reduce.7
  2.8 0.2 fusion.7
  3.1 4.9 %convolution_convert_fusion.1 = bf16[1024,1536]{1,0:T(8,128)(2,1)} fusion(bf16[512,4608]{1,0:T(8,128)(2,1)} %param.7, s32[512]{0:T(512)S(1)} %bitcast.20), kind=kOutput, calls=%fused_computation.1 | convolution fusion | flops 1612709888 | bytes 4720640 | tf_op jit(solution)/shard_map/dot_general | solution.py:167
  7.9 7.5 %all-to-all-start = ((bf16[32,32,1536]{2,1,0:T(8,128)(2,1)}), bf16[32,32,1536]{2,1,0:T(8,128)(2,1)S(1)}, u32[]{:S(2)}, u32[]{:S(2)}) async-start(bf16[32,32,1536]{2,1,0:T(8,128)(2,1)} %bitcast.15), calls=%async_computation | async-start | bytes 6291456 | tf_op jit(solution)/shard_map/all_to_all | solution.py:172
  15.5 0.2 add_reduce_fusion
  15.7 0.2 convolution_convert_fusion.2
  15.9 0.6 select_reduce_fusion
  16.7 4.4 %convolution_convert_fusion = bf16[1024,1280]{1,0:T(8,128)(2,1)} fusion(bf16[512,4608]{1,0:T(8,128)(2,1)} %param.7, s32[512]{0:T(512)S(1)} %bitcast.21), kind=kOutput, calls=%fused_computation | convolution fusion | flops 1344012288 | bytes 3934208 | tf_op jit(solution)/shard_map/dot_general | solution.py:167
  21.1 34.4 %all-to-all-done = bf16[32,32,1536]{2,1,0:T(8,128)(2,1)S(1)} async-done(((bf16[32,32,1536]{2,1,0:T(8,128)(2,1)}), bf16[32,32,1536]{2,1,0:T(8,128)(2,1)S(1)}, u32[]{:S(2)}, u32[]{:S(2)}) %all-to-all-start) | async-done | bytes 3145760 | tf_op jit(solution)/shard_map/all_to_all | solution.py:172
  55.4 1.7 copy-done.1
  57.1 5.2 %all-to-all-start.1 = ((bf16[32,32,1280]{2,1,0:T(8,128)(2,1)}), bf16[32,32,1280]{2,1,0:T(8,128)(2,1)}, u32[]{:S(2)}, u32[]{:S(2)}) async-start(bf16[32,32,1280]{2,1,0:T(8,128)(2,1)} %bitcast.16), calls=%async_computation.1 | async-start | bytes 5242880 | tf_op jit(solution)/shard_map/all_to_all | solution.py:172
  62.3 1.9 copy-done.2
  64.2 2.9 %shard_map.102 = (f32[96,1536]{1,0:T(8,128)S(1)}, bf16[96,1536]{1,0:T(8,128)(2,1)S(1)}, bf16[96,1536]{1,0:T(8,128)(2,1)S(1)}, bf16[96,1536]{1,0:T(8,128)(2,1)S(1)}) custom-call(s32[1]{0:T(128)} %bitcast.here_ref, s32[1,1024]{1,0:T(1,128)S(1)} %sub.19.target_ref, bf16[1,384,4608]{2,1,0:T(8,128)(2,1)S(1)} %copy-done, bf16[1024,1536]{1,0:T(8,128)(2,1)S(1)} %bitcast.14), custom_call_target="tpu_custom_call" | custom-call | flops 1207959552 | bytes 6094848 | tf_op jit(solution)/shard_map/pallas_call | solution.py:67
  67.1 2.0 %collective-permute-start = (bf16[96,1536]{1,0:T(8,128)(2,1)S(1)}, bf16[96,1536]{1,0:T(8,128)(2,1)S(1)}, u32[]{:S(2)}, u32[]{:S(2)}) collective-permute-start(bf16[96,1536]{1,0:T(8,128)(2,1)S(1)} %get-tuple-element.38), channel_id=1, source_target_pairs={{0,32},{32,0},{64,96},{96,64},{1,33},{33,1},{65,97},{97,65},{2,34}... | collective-permute-start | bytes 884744 | tf_op jit(solution)/shard_map/ppermute | solution.py:31
  69.1 3.6 %collective-permute-start.1 = (bf16[96,1536]{1,0:T(8,128)(2,1)S(1)}, bf16[96,1536]{1,0:T(8,128)(2,1)S(1)}, u32[]{:S(2)}, u32[]{:S(2)}) collective-permute-start(bf16[96,1536]{1,0:T(8,128)(2,1)S(1)} %get-tuple-element.39), channel_id=1, source_target_pairs={{0,64},{32,96},{64,0},{96,32},{1,65},{33,97},{65,1},{97,33},{2,66}... | collective-permute-start | bytes 884744 | tf_op jit(solution)/shard_map/ppermute | solution.py:31
  72.7 3.8 %fusion.3 = bf16[1024,1024]{1,0:T(8,128)(2,1)} fusion(bf16[512,4608]{1,0:T(8,128)(2,1)} %param.7, s32[512]{0:T(512)S(1)} %bitcast.22), kind=kOutput, calls=%fused_computation.8 | convolution fusion | flops 1075314688 | bytes 3147776 | tf_op jit(solution)/shard_map/dot_general | solution.py:167
  76.5 0.5 collective-permute-done
  77.0 9.2 %collective-permute-done.1 = bf16[96,1536]{1,0:T(8,128)(2,1)S(1)} collective-permute-done((bf16[96,1536]{1,0:T(8,128)(2,1)S(1)}, bf16[96,1536]{1,0:T(8,128)(2,1)S(1)}, u32[]{:S(2)}, u32[]{:S(2)}) %collective-permute-start.1) | collective-permute-done | bytes 294944 | tf_op jit(solution)/shard_map/ppermute | solution.py:31
  86.2 2.6 %collective-permute-done.2 = bf16[96,1536]{1,0:T(8,128)(2,1)S(1)} collective-permute-done((bf16[96,1536]{1,0:T(8,128)(2,1)S(1)}, bf16[96,1536]{1,0:T(8,128)(2,1)S(1)}, u32[]{:S(2)}, u32[]{:S(2)}) %collective-permute-start.2) | collective-permute-done | bytes 294944 | tf_op jit(solution)/shard_map/ppermute | solution.py:31
  88.8 3.1 %fusion.25 = (bf16[96,1536]{1,0:T(8,128)(2,1)}, f32[96,1536]{1,0:T(8,128)}, f32[96,1536]{1,0:T(8,128)}, f32[96,1536]{1,0:T(8,128)}) fusion(f32[96,4608]{1,0:T(8,128)} %param.11, bf16[96,1536]{1,0:T(8,128)(2,1)S(1)} %collective-permute-done.2, bf16[96,1536]{1,0:T(8,128)(2,1)S(1)} %collective-permute-done.1, f32[96,1536]{1,0:T(8,128)S(1)} %get-tuple-element.37, ...), kind=kLoop, calls=%fused_computation.58 | loop fusion | flops 3244032 | bytes 5308416 | tf_op jit(solution)/shard_map/convert_element_type | solution.py:182
  91.9 5.0 %all-to-all-done.1 = bf16[32,32,1280]{2,1,0:T(8,128)(2,1)} async-done(((bf16[32,32,1280]{2,1,0:T(8,128)(2,1)}), bf16[32,32,1280]{2,1,0:T(8,128)(2,1)}, u32[]{:S(2)}, u32[]{:S(2)}) %all-to-all-start.1) | async-done | bytes 2621472 | tf_op jit(solution)/shard_map/all_to_all | solution.py:172
  96.9 4.8 %all-to-all-start.2 = ((bf16[32,32,1024]{2,1,0:T(8,128)(2,1)}), bf16[32,32,1024]{2,1,0:T(8,128)(2,1)}, u32[]{:S(2)}, u32[]{:S(2)}) async-start(bf16[32,32,1024]{2,1,0:T(8,128)(2,1)} %bitcast.17), calls=%async_computation.2 | async-start | bytes 4194304 | tf_op jit(solution)/shard_map/all_to_all | solution.py:172
  101.7 4.1 %collective-permute-start.6 = (bf16[96,1536]{1,0:T(8,128)(2,1)}, bf16[96,1536]{1,0:T(8,128)(2,1)S(1)}, u32[]{:S(2)}, u32[]{:S(2)}) collective-permute-start(bf16[96,1536]{1,0:T(8,128)(2,1)} %get-tuple-element.82), channel_id=1, source_target_pairs={{0,96},{32,64},{64,32},{96,0},{1,97},{33,65},{65,33},{97,1},{2,98}... | collective-permute-start | bytes 884744 | tf_op jit(solution)/shard_map/ppermute | solution.py:31
  105.8 4.5 %shard_map.103 = (f32[96,1280]{1,0:T(8,128)S(1)}, bf16[96,1280]{1,0:T(8,128)(2,1)S(1)}, bf16[96,1280]{1,0:T(8,128)(2,1)S(1)}, bf16[96,1280]{1,0:T(8,128)(2,1)S(1)}) custom-call(s32[1]{0:T(128)} %bitcast.here_ref, s32[1,1024]{1,0:T(1,128)S(1)} %sub.19.target_ref, bf16[1,384,4608]{2,1,0:T(8,128)(2,1)S(1)} %copy-done, bf16[1024,1280]{1,0:T(8,128)(2,1)} %bitcast.7.part_ref), custom_call_target="tpu_custom_call" | custom-call | flops 1006632960 | bytes 5079040 | tf_op jit(solution)/shard_map/pallas_call | solution.py:67
  110.4 1.5 collective-permute-start.4
  111.9 3.2 %collective-permute-start.5 = (bf16[96,1280]{1,0:T(8,128)(2,1)S(1)}, bf16[96,1280]{1,0:T(8,128)(2,1)S(1)}, u32[]{:S(2)}, u32[]{:S(2)}) collective-permute-start(bf16[96,1280]{1,0:T(8,128)(2,1)S(1)} %get-tuple-element.46), channel_id=1, source_target_pairs={{0,96},{32,64},{64,32},{96,0},{1,97},{33,65},{65,33},{97,1},{2,98}... | collective-permute-start | bytes 737288 | tf_op jit(solution)/shard_map/ppermute | solution.py:31
  115.1 3.3 %fusion.4 = bf16[1024,768]{1,0:T(8,128)(2,1)} fusion(s32[512]{0:T(512)S(1)} %bitcast.23, bf16[512,4608]{1,0:T(8,128)(2,1)} %param.7), kind=kOutput, calls=%fused_computation.12 | convolution fusion | flops 806617088 | bytes 2361344 | tf_op jit(solution)/shard_map/dot_general | solution.py:167
  118.4 0.9 pad_maximum_fusion.3.refs_0_
  119.3 3.9 %collective-permute-done.4 = bf16[96,1280]{1,0:T(8,128)(2,1)S(1)} collective-permute-done((bf16[96,1280]{1,0:T(8,128)(2,1)S(1)}, bf16[96,1280]{1,0:T(8,128)(2,1)S(1)}, u32[]{:S(2)}, u32[]{:S(2)}) %collective-permute-start.4) | collective-permute-done | bytes 245792 | tf_op jit(solution)/shard_map/ppermute | solution.py:31
  123.2 2.6 %collective-permute-done.5 = bf16[96,1280]{1,0:T(8,128)(2,1)S(1)} collective-permute-done((bf16[96,1280]{1,0:T(8,128)(2,1)S(1)}, bf16[96,1280]{1,0:T(8,128)(2,1)S(1)}, u32[]{:S(2)}, u32[]{:S(2)}) %collective-permute-start.5) | collective-permute-done | bytes 245792 | tf_op jit(solution)/shard_map/ppermute | solution.py:31
  125.8 0.1 convert_add_fusion.1
  125.9 2.8 %fusion.23 = (bf16[96,1280]{1,0:T(8,128)(2,1)}, f32[96,1280]{1,0:T(8,128)}, f32[96,1280]{1,0:T(8,128)}, f32[96,1280]{1,0:T(8,128)}) fusion(f32[96,4608]{1,0:T(8,128)} %param.11, f32[96,1280]{1,0:T(8,128)S(1)} %convert_add_fusion.1, f32[96,4608]{1,0:T(8,128)} %param.12, f32[96,4608]{1,0:T(8,128)} %param.13), kind=kLoop, calls=%fused_computation.57 | loop fusion | flops 1966080 | bytes 3686400 | tf_op jit(solution)/shard_map/convert_element_type | solution.py:182
  128.7 1.9 all-to-all-done.2
  130.6 5.6 %all-to-all-start.3 = ((bf16[32,32,768]{2,1,0:T(8,128)(2,1)}), bf16[32,32,768]{2,1,0:T(8,128)(2,1)}, u32[]{:S(2)}, u32[]{:S(2)}) async-start(bf16[32,32,768]{2,1,0:T(8,128)(2,1)} %bitcast.18), calls=%async_computation.3 | async-start | bytes 3145728 | tf_op jit(solution)/shard_map/all_to_all | solution.py:172
  136.2 3.2 %collective-permute-start.10 = (bf16[96,1280]{1,0:T(8,128)(2,1)}, bf16[96,1280]{1,0:T(8,128)(2,1)S(1)}, u32[]{:S(2)}, u32[]{:S(2)}) collective-permute-start(bf16[96,1280]{1,0:T(8,128)(2,1)} %get-tuple-element.78), channel_id=1, source_target_pairs={{0,96},{32,64},{64,32},{96,0},{1,97},{33,65},{65,33},{97,1},{2,98}... | collective-permute-start | bytes 737288 | tf_op jit(solution)/shard_map/ppermute | solution.py:31
  139.4 3.5 %shard_map.104 = (f32[96,1024]{1,0:T(8,128)S(1)}, bf16[96,1024]{1,0:T(8,128)(2,1)S(1)}, bf16[96,1024]{1,0:T(8,128)(2,1)S(1)}, bf16[96,1024]{1,0:T(8,128)(2,1)S(1)}) custom-call(s32[1]{0:T(128)} %bitcast.here_ref, s32[1,1024]{1,0:T(1,128)S(1)} %sub.19.target_ref, bf16[1,384,4608]{2,1,0:T(8,128)(2,1)S(1)} %copy-done, bf16[1024,1024]{1,0:T(8,128)(2,1)} %bitcast.9.part_ref), custom_call_target="tpu_custom_call" | custom-call | flops 805306368 | bytes 4063232 | tf_op jit(solution)/shard_map/pallas_call | solution.py:67
  142.9 2.1 %collective-permute-start.7 = (bf16[96,1024]{1,0:T(8,128)(2,1)S(1)}, bf16[96,1024]{1,0:T(8,128)(2,1)S(1)}, u32[]{:S(2)}, u32[]{:S(2)}) collective-permute-start(bf16[96,1024]{1,0:T(8,128)(2,1)S(1)} %get-tuple-element.51), channel_id=1, source_target_pairs={{0,32},{32,0},{64,96},{96,64},{1,33},{33,1},{65,97},{97,65},{2,34}... | collective-permute-start | bytes 589832 | tf_op jit(solution)/shard_map/ppermute | solution.py:31
  145.1 2.8 %collective-permute-start.9 = (bf16[96,1024]{1,0:T(8,128)(2,1)S(1)}, bf16[96,1024]{1,0:T(8,128)(2,1)S(1)}, u32[]{:S(2)}, u32[]{:S(2)}) collective-permute-start(bf16[96,1024]{1,0:T(8,128)(2,1)S(1)} %get-tuple-element.53), channel_id=1, source_target_pairs={{0,96},{32,64},{64,32},{96,0},{1,97},{33,65},{65,33},{97,1},{2,98}... | collective-permute-start | bytes 589832 | tf_op jit(solution)/shard_map/ppermute | solution.py:31
  147.8 0.8 pad_maximum_fusion.4.refs_2_
  148.6 0.7 collective-permute-start.12
  149.4 10.7 %collective-permute-done.7 = bf16[96,1024]{1,0:T(8,128)(2,1)S(1)} collective-permute-done((bf16[96,1024]{1,0:T(8,128)(2,1)S(1)}, bf16[96,1024]{1,0:T(8,128)(2,1)S(1)}, u32[]{:S(2)}, u32[]{:S(2)}) %collective-permute-start.7) | collective-permute-done | bytes 196640 | tf_op jit(solution)/shard_map/ppermute | solution.py:31
  160.0 3.7 %collective-permute-done.8 = bf16[96,1024]{1,0:T(8,128)(2,1)S(1)} collective-permute-done((bf16[96,1024]{1,0:T(8,128)(2,1)S(1)}, bf16[96,1024]{1,0:T(8,128)(2,1)S(1)}, u32[]{:S(2)}, u32[]{:S(2)}) %collective-permute-start.8) | collective-permute-done | bytes 196640 | tf_op jit(solution)/shard_map/ppermute | solution.py:31
  163.8 0.1 convert_add_fusion.2
  163.9 0.8 copy-done.4
  164.7 2.6 %fusion.21 = (bf16[96,1024]{1,0:T(8,128)(2,1)}, f32[96,1024]{1,0:T(8,128)}, f32[96,1024]{1,0:T(8,128)}, f32[96,1024]{1,0:T(8,128)}) fusion(f32[96,4608]{1,0:T(8,128)} %param.11, f32[96,1024]{1,0:T(8,128)S(1)} %convert_add_fusion.2, f32[96,4608]{1,0:T(8,128)} %param.12, f32[96,4608]{1,0:T(8,128)} %param.13), kind=kLoop, calls=%fused_computation.56 | loop fusion | flops 1572864 | bytes 2949120 | tf_op jit(solution)/shard_map/convert_element_type | solution.py:182
  167.2 3.2 %collective-permute-start.16 = (bf16[96,1024]{1,0:T(8,128)(2,1)}, bf16[96,1024]{1,0:T(8,128)(2,1)}, u32[]{:S(2)}, u32[]{:S(2)}) collective-permute-start(bf16[96,1024]{1,0:T(8,128)(2,1)} %get-tuple-element.74), channel_id=1, source_target_pairs={{0,96},{32,64},{64,32},{96,0},{1,97},{33,65},{65,33},{97,1},{2,98}... | collective-permute-start | bytes 589832 | tf_op jit(solution)/shard_map/ppermute | solution.py:31
  170.4 3.1 %shard_map.105 = (f32[96,768]{1,0:T(8,128)S(1)}, bf16[96,768]{1,0:T(8,128)(2,1)S(1)}, bf16[96,768]{1,0:T(8,128)(2,1)S(1)}, bf16[96,768]{1,0:T(8,128)(2,1)S(1)}) custom-call(s32[1]{0:T(128)} %bitcast.here_ref, s32[1,1024]{1,0:T(1,128)S(1)} %sub.19.target_ref, bf16[1,384,4608]{2,1,0:T(8,128)(2,1)S(1)} %copy-done, bf16[1024,768]{1,0:T(8,128)(2,1)} %bitcast.11.part_ref), custom_call_target="tpu_custom_call" | custom-call | flops 603979776 | bytes 3047424 | tf_op jit(solution)/shard_map/pallas_call | solution.py:67
  173.6 0.2 collective-permute-done.12.refs_3_
  173.7 0.3 collective-permute-start.13
  174.0 1.6 collective-permute-start.14
  175.6 2.9 %collective-permute-start.15 = (bf16[96,768]{1,0:T(8,128)(2,1)S(1)}, bf16[96,768]{1,0:T(8,128)(2,1)S(1)}, u32[]{:S(2)}, u32[]{:S(2)}) collective-permute-start(bf16[96,768]{1,0:T(8,128)(2,1)S(1)} %get-tuple-element.63), channel_id=1, source_target_pairs={{0,96},{32,64},{64,32},{96,0},{1,97},{33,65},{65,33},{97,1},{2,98}... | collective-permute-start | bytes 442376 | tf_op jit(solution)/shard_map/ppermute | solution.py:31
  178.4 1.0 pad_maximum_fusion.5.refs_4_
  179.6 0.4 collective-permute-done.13
  180.0 3.2 %collective-permute-done.14 = bf16[96,768]{1,0:T(8,128)(2,1)S(1)} collective-permute-done((bf16[96,768]{1,0:T(8,128)(2,1)S(1)}, bf16[96,768]{1,0:T(8,128)(2,1)S(1)}, u32[]{:S(2)}, u32[]{:S(2)}) %collective-permute-start.14) | collective-permute-done | bytes 147488 | tf_op jit(solution)/shard_map/ppermute | solution.py:31
  183.2 0.7 collective-permute-done.15
  183.9 1.5 fusion.19
  185.3 2.3 %collective-permute-start.20 = (bf16[96,768]{1,0:T(8,128)(2,1)S(1)}, bf16[96,768]{1,0:T(8,128)(2,1)S(1)}, u32[]{:S(2)}, u32[]{:S(2)}) collective-permute-start(bf16[96,768]{1,0:T(8,128)(2,1)S(1)} %get-tuple-element.70.refs_1_), channel_id=1, source_target_pairs={{0,96},{32,64},{64,32},{96,0},{1,97},{33,65},{65,33},{97,1},{2,98}... | collective-permute-start | bytes 442376 | tf_op jit(solution)/shard_map/ppermute | solution.py:31
  187.7 1.9 collective-permute-start.18
  189.6 2.1 %pad_maximum_fusion = (f32[96,4608]{1,0:T(8,128)}, f32[96,4608]{1,0:T(8,128)}) fusion(f32[96,768]{1,0:T(8,128)S(1)} %get-tuple-element.71, f32[96,1024]{1,0:T(8,128)S(1)} %copy-done.13, f32[96,1280]{1,0:T(8,128)S(1)} %copy-done.10, f32[96,1536]{1,0:T(8,128)S(1)} %copy-done.6, f32[96,768]{1,0:T(8,128)S(1)} %get-tuple-element.72, f32[96,1024]{1,0:T(8,128)S(1)} %copy-done.14, ...), kind=kLoop, calls=%fused_computation.9 | loop fusion | flops 2654208 | bytes 7077888 | tf_op jit(solution)/shard_map/concatenate | solution.py:201
  191.7 1.3 pad_maximum_fusion.2
  193.1 0.3 copy-done.5
  193.4 2.9 %shard_map.106.refs_0_ = bf16[384,4608]{1,0:T(8,128)(2,1)} custom-call(s32[1]{0:T(128)} %bitcast.here_ref, bf16[192,1536]{1,0:T(8,128)(2,1)S(1)} %copy-done.3, bf16[192,1536]{1,0:T(8,128)(2,1)S(1)} %copy-done.5, bf16[192,1280]{1,0:T(8,128)(2,1)} %pad_maximum_fusion.4.refs_2_, bf16[192,1280]{1,0:T(8,128)(2,1)} %collective-permute-done.12.refs_3_, ...), custom_call_target="tpu_custom_call" | custom-call | bytes 5898240 | tf_op jit(solution)/shard_map/pallas_call | solution.py:106
  196.3 0.8 shard_map.107
  (57 shorter events, 0.5 us)
Async XLA Ops:
  7.9 7.5 %copy-start.17 = (s32[16384,1]{0,1:T(1,128)S(1)}, s32[16384,1]{0,1:T(1,128)}, u32[]{:S(2)}) copy-start(s32[16384,1]{0,1:T(1,128)} %param.9) | copy-start | bytes 196612
  7.9 47.5 %all-to-all-start = ((bf16[32,32,1536]{2,1,0:T(8,128)(2,1)}), bf16[32,32,1536]{2,1,0:T(8,128)(2,1)S(1)}, u32[]{:S(2)}, u32[]{:S(2)}) async-start(bf16[32,32,1536]{2,1,0:T(8,128)(2,1)} %bitcast.15), calls=%async_computation | async-start | bytes 6291456 | tf_op jit(solution)/shard_map/all_to_all | solution.py:172
  55.4 1.7 copy-start.1
  57.1 5.2 %copy-start = (bf16[1,384,4608]{2,1,0:T(8,128)(2,1)S(1)}, bf16[1,384,4608]{2,1,0:T(8,128)(2,1)}, u32[]{:S(2)}) copy-start(bf16[1,384,4608]{2,1,0:T(8,128)(2,1)} %head_ref.7) | copy-start | bytes 10616836
  57.1 39.8 %all-to-all-start.1 = ((bf16[32,32,1280]{2,1,0:T(8,128)(2,1)}), bf16[32,32,1280]{2,1,0:T(8,128)(2,1)}, u32[]{:S(2)}, u32[]{:S(2)}) async-start(bf16[32,32,1280]{2,1,0:T(8,128)(2,1)} %bitcast.16), calls=%async_computation.1 | async-start | bytes 5242880 | tf_op jit(solution)/shard_map/all_to_all | solution.py:172
  62.3 1.9 copy-start.2
  67.1 9.9 %collective-permute-start = (bf16[96,1536]{1,0:T(8,128)(2,1)S(1)}, bf16[96,1536]{1,0:T(8,128)(2,1)S(1)}, u32[]{:S(2)}, u32[]{:S(2)}) collective-permute-start(bf16[96,1536]{1,0:T(8,128)(2,1)S(1)} %get-tuple-element.38), channel_id=1, source_target_pairs={{0,32},{32,0},{64,96},{96,64},{1,33},{33,1},{65,97},{97,65},{2,34}... | collective-permute-start | bytes 884744 | tf_op jit(solution)/shard_map/ppermute | solution.py:31
  69.1 17.1 %collective-permute-start.1 = (bf16[96,1536]{1,0:T(8,128)(2,1)S(1)}, bf16[96,1536]{1,0:T(8,128)(2,1)S(1)}, u32[]{:S(2)}, u32[]{:S(2)}) collective-permute-start(bf16[96,1536]{1,0:T(8,128)(2,1)S(1)} %get-tuple-element.39), channel_id=1, source_target_pairs={{0,64},{32,96},{64,0},{96,32},{1,65},{33,97},{65,1},{97,33},{2,66}... | collective-permute-start | bytes 884744 | tf_op jit(solution)/shard_map/ppermute | solution.py:31
  72.7 16.1 %collective-permute-start.2 = (bf16[96,1536]{1,0:T(8,128)(2,1)S(1)}, bf16[96,1536]{1,0:T(8,128)(2,1)S(1)}, u32[]{:S(2)}, u32[]{:S(2)}) collective-permute-start(bf16[96,1536]{1,0:T(8,128)(2,1)S(1)} %get-tuple-element.40), channel_id=1, source_target_pairs={{0,96},{32,64},{64,32},{96,0},{1,97},{33,65},{65,33},{97,1},{2,98}... | collective-permute-start | bytes 884744 | tf_op jit(solution)/shard_map/ppermute | solution.py:31
  96.9 33.7 %all-to-all-start.2 = ((bf16[32,32,1024]{2,1,0:T(8,128)(2,1)}), bf16[32,32,1024]{2,1,0:T(8,128)(2,1)}, u32[]{:S(2)}, u32[]{:S(2)}) async-start(bf16[32,32,1024]{2,1,0:T(8,128)(2,1)} %bitcast.17), calls=%async_computation.2 | async-start | bytes 4194304 | tf_op jit(solution)/shard_map/all_to_all | solution.py:172
  101.7 16.7 %collective-permute-start.6 = (bf16[96,1536]{1,0:T(8,128)(2,1)}, bf16[96,1536]{1,0:T(8,128)(2,1)S(1)}, u32[]{:S(2)}, u32[]{:S(2)}) collective-permute-start(bf16[96,1536]{1,0:T(8,128)(2,1)} %get-tuple-element.82), channel_id=1, source_target_pairs={{0,96},{32,64},{64,32},{96,0},{1,97},{33,65},{65,33},{97,1},{2,98}... | collective-permute-start | bytes 884744 | tf_op jit(solution)/shard_map/ppermute | solution.py:31
  110.3 9.0 %collective-permute-start.3 = (bf16[96,1280]{1,0:T(8,128)(2,1)S(1)}, bf16[96,1280]{1,0:T(8,128)(2,1)S(1)}, u32[]{:S(2)}, u32[]{:S(2)}) collective-permute-start(bf16[96,1280]{1,0:T(8,128)(2,1)S(1)} %get-tuple-element.44), channel_id=1, source_target_pairs={{0,32},{32,0},{64,96},{96,64},{1,33},{33,1},{65,97},{97,65},{2,34}... | collective-permute-start | bytes 737288 | tf_op jit(solution)/shard_map/ppermute | solution.py:31
  110.4 12.8 %collective-permute-start.4 = (bf16[96,1280]{1,0:T(8,128)(2,1)S(1)}, bf16[96,1280]{1,0:T(8,128)(2,1)S(1)}, u32[]{:S(2)}, u32[]{:S(2)}) collective-permute-start(bf16[96,1280]{1,0:T(8,128)(2,1)S(1)} %get-tuple-element.45), channel_id=1, source_target_pairs={{0,64},{32,96},{64,0},{96,32},{1,65},{33,97},{65,1},{97,33},{2,66}... | collective-permute-start | bytes 737288 | tf_op jit(solution)/shard_map/ppermute | solution.py:31
  111.9 6.5 %copy-start.15 = (bf16[96,1536]{1,0:T(8,128)(2,1)S(1)}, bf16[96,1536]{1,0:T(8,128)(2,1)}, u32[]{:S(2)}) copy-start(bf16[96,1536]{1,0:T(8,128)(2,1)} %get-tuple-element.82) | copy-start | bytes 884740
  111.9 13.9 %collective-permute-start.5 = (bf16[96,1280]{1,0:T(8,128)(2,1)S(1)}, bf16[96,1280]{1,0:T(8,128)(2,1)S(1)}, u32[]{:S(2)}, u32[]{:S(2)}) collective-permute-start(bf16[96,1280]{1,0:T(8,128)(2,1)S(1)} %get-tuple-element.46), channel_id=1, source_target_pairs={{0,96},{32,64},{64,32},{96,0},{1,97},{33,65},{65,33},{97,1},{2,98}... | collective-permute-start | bytes 737288 | tf_op jit(solution)/shard_map/ppermute | solution.py:31
  130.6 39.9 %all-to-all-start.3 = ((bf16[32,32,768]{2,1,0:T(8,128)(2,1)}), bf16[32,32,768]{2,1,0:T(8,128)(2,1)}, u32[]{:S(2)}, u32[]{:S(2)}) async-start(bf16[32,32,768]{2,1,0:T(8,128)(2,1)} %bitcast.18), calls=%async_computation.3 | async-start | bytes 3145728 | tf_op jit(solution)/shard_map/all_to_all | solution.py:172
  136.1 11.7 %copy-start.16 = (bf16[96,1280]{1,0:T(8,128)(2,1)S(1)}, bf16[96,1280]{1,0:T(8,128)(2,1)}, u32[]{:S(2)}) copy-start(bf16[96,1280]{1,0:T(8,128)(2,1)} %get-tuple-element.78) | copy-start | bytes 737284
  136.2 11.7 %collective-permute-start.10 = (bf16[96,1280]{1,0:T(8,128)(2,1)}, bf16[96,1280]{1,0:T(8,128)(2,1)S(1)}, u32[]{:S(2)}, u32[]{:S(2)}) collective-permute-start(bf16[96,1280]{1,0:T(8,128)(2,1)} %get-tuple-element.78), channel_id=1, source_target_pairs={{0,96},{32,64},{64,32},{96,0},{1,97},{33,65},{65,33},{97,1},{2,98}... | collective-permute-start | bytes 737288 | tf_op jit(solution)/shard_map/ppermute | solution.py:31
  139.4 24.4 %collective-permute-start.11 = (bf16[192,1536]{1,0:T(8,128)(2,1)}, bf16[192,1536]{1,0:T(8,128)(2,1)S(1)}, u32[]{:S(2)}, u32[]{:S(2)}) collective-permute-start(bf16[192,1536]{1,0:T(8,128)(2,1)} %pad_maximum_fusion.3.refs_0_), channel_id=1, source_target_pairs={{0,32},{32,0},{64,96},{96,64},{1,33},{33,1},{65,97},{97,65},{2,34}... | collective-permute-start | bytes 1769480 | tf_op jit(solution)/shard_map/ppermute | solution.py:31
  142.9 17.1 %collective-permute-start.7 = (bf16[96,1024]{1,0:T(8,128)(2,1)S(1)}, bf16[96,1024]{1,0:T(8,128)(2,1)S(1)}, u32[]{:S(2)}, u32[]{:S(2)}) collective-permute-start(bf16[96,1024]{1,0:T(8,128)(2,1)S(1)} %get-tuple-element.51), channel_id=1, source_target_pairs={{0,32},{32,0},{64,96},{96,64},{1,33},{33,1},{65,97},{97,65},{2,34}... | collective-permute-start | bytes 589832 | tf_op jit(solution)/shard_map/ppermute | solution.py:31
  145.0 18.7 %collective-permute-start.8 = (bf16[96,1024]{1,0:T(8,128)(2,1)S(1)}, bf16[96,1024]{1,0:T(8,128)(2,1)S(1)}, u32[]{:S(2)}, u32[]{:S(2)}) collective-permute-start(bf16[96,1024]{1,0:T(8,128)(2,1)S(1)} %get-tuple-element.52), channel_id=1, source_target_pairs={{0,64},{32,96},{64,0},{96,32},{1,65},{33,97},{65,1},{97,33},{2,66}... | collective-permute-start | bytes 589832 | tf_op jit(solution)/shard_map/ppermute | solution.py:31
  145.1 18.7 %collective-permute-start.9 = (bf16[96,1024]{1,0:T(8,128)(2,1)S(1)}, bf16[96,1024]{1,0:T(8,128)(2,1)S(1)}, u32[]{:S(2)}, u32[]{:S(2)}) collective-permute-start(bf16[96,1024]{1,0:T(8,128)(2,1)S(1)} %get-tuple-element.53), channel_id=1, source_target_pairs={{0,96},{32,64},{64,32},{96,0},{1,97},{33,65},{65,33},{97,1},{2,98}... | collective-permute-start | bytes 589832 | tf_op jit(solution)/shard_map/ppermute | solution.py:31
  148.6 25.1 %collective-permute-start.12 = (bf16[192,1280]{1,0:T(8,128)(2,1)}, bf16[192,1280]{1,0:T(8,128)(2,1)}, u32[]{:S(2)}, u32[]{:S(2)}) collective-permute-start(bf16[192,1280]{1,0:T(8,128)(2,1)} %pad_maximum_fusion.4.refs_2_), channel_id=1, source_target_pairs={{0,32},{32,0},{64,96},{96,64},{1,33},{33,1},{65,97},{97,65},{2,34}... | collective-permute-start | bytes 1474568 | tf_op jit(solution)/shard_map/ppermute | solution.py:31
  163.9 0.8 copy-start.4
  167.2 11.2 %collective-permute-start.16 = (bf16[96,1024]{1,0:T(8,128)(2,1)}, bf16[96,1024]{1,0:T(8,128)(2,1)}, u32[]{:S(2)}, u32[]{:S(2)}) collective-permute-start(bf16[96,1024]{1,0:T(8,128)(2,1)} %get-tuple-element.74), channel_id=1, source_target_pairs={{0,96},{32,64},{64,32},{96,0},{1,97},{33,65},{65,33},{97,1},{2,98}... | collective-permute-start | bytes 589832 | tf_op jit(solution)/shard_map/ppermute | solution.py:31
  173.5 16.0 %copy-start.6 = (f32[96,1536]{1,0:T(8,128)S(1)}, f32[96,1536]{1,0:T(8,128)}, u32[]{:S(2)}) copy-start(f32[96,1536]{1,0:T(8,128)} %get-tuple-element.83) | copy-start | bytes 1769476
  173.5 16.0 %copy-start.7 = (f32[96,1536]{1,0:T(8,128)S(1)}, f32[96,1536]{1,0:T(8,128)}, u32[]{:S(2)}) copy-start(f32[96,1536]{1,0:T(8,128)} %get-tuple-element.84) | copy-start | bytes 1769476
  173.5 16.0 %copy-start.10 = (f32[96,1280]{1,0:T(8,128)S(1)}, f32[96,1280]{1,0:T(8,128)}, u32[]{:S(2)}) copy-start(f32[96,1280]{1,0:T(8,128)} %get-tuple-element.79) | copy-start | bytes 1474564
  173.5 16.0 %copy-start.11 = (f32[96,1280]{1,0:T(8,128)S(1)}, f32[96,1280]{1,0:T(8,128)}, u32[]{:S(2)}) copy-start(f32[96,1280]{1,0:T(8,128)} %get-tuple-element.80) | copy-start | bytes 1474564
  173.5 16.0 %copy-start.13 = (f32[96,1024]{1,0:T(8,128)S(1)}, f32[96,1024]{1,0:T(8,128)}, u32[]{:S(2)}) copy-start(f32[96,1024]{1,0:T(8,128)} %get-tuple-element.75) | copy-start | bytes 1179652
  173.6 16.0 %copy-start.14 = (f32[96,1024]{1,0:T(8,128)S(1)}, f32[96,1024]{1,0:T(8,128)}, u32[]{:S(2)}) copy-start(f32[96,1024]{1,0:T(8,128)} %get-tuple-element.76) | copy-start | bytes 1179652
  173.7 6.3 %collective-permute-start.13 = (bf16[96,768]{1,0:T(8,128)(2,1)S(1)}, bf16[96,768]{1,0:T(8,128)(2,1)S(1)}, u32[]{:S(2)}, u32[]{:S(2)}) collective-permute-start(bf16[96,768]{1,0:T(8,128)(2,1)S(1)} %get-tuple-element.61), channel_id=1, source_target_pairs={{0,32},{32,0},{64,96},{96,64},{1,33},{33,1},{65,97},{97,65},{2,34}... | collective-permute-start | bytes 442376 | tf_op jit(solution)/shard_map/ppermute | solution.py:31
  174.0 9.2 %collective-permute-start.14 = (bf16[96,768]{1,0:T(8,128)(2,1)S(1)}, bf16[96,768]{1,0:T(8,128)(2,1)S(1)}, u32[]{:S(2)}, u32[]{:S(2)}) collective-permute-start(bf16[96,768]{1,0:T(8,128)(2,1)S(1)} %get-tuple-element.62), channel_id=1, source_target_pairs={{0,64},{32,96},{64,0},{96,32},{1,65},{33,97},{65,1},{97,33},{2,66}... | collective-permute-start | bytes 442376 | tf_op jit(solution)/shard_map/ppermute | solution.py:31
  175.6 8.3 %collective-permute-start.15 = (bf16[96,768]{1,0:T(8,128)(2,1)S(1)}, bf16[96,768]{1,0:T(8,128)(2,1)S(1)}, u32[]{:S(2)}, u32[]{:S(2)}) collective-permute-start(bf16[96,768]{1,0:T(8,128)(2,1)S(1)} %get-tuple-element.63), channel_id=1, source_target_pairs={{0,96},{32,64},{64,32},{96,0},{1,97},{33,65},{65,33},{97,1},{2,98}... | collective-permute-start | bytes 442376 | tf_op jit(solution)/shard_map/ppermute | solution.py:31
  179.5 13.6 %collective-permute-start.17 = (bf16[192,1024]{1,0:T(8,128)(2,1)S(1)}, bf16[192,1024]{1,0:T(8,128)(2,1)S(1)}, u32[]{:S(2)}, u32[]{:S(2)}) collective-permute-start(bf16[192,1024]{1,0:T(8,128)(2,1)S(1)} %pad_maximum_fusion.5.refs_4_), channel_id=1, source_target_pairs={{0,32},{32,0},{64,96},{96,64},{1,33},{33,1},{65,97},{97,65},{2,34}... | collective-permute-start | bytes 1179656 | tf_op jit(solution)/shard_map/ppermute | solution.py:31
  185.3 10.9 %collective-permute-start.20 = (bf16[96,768]{1,0:T(8,128)(2,1)S(1)}, bf16[96,768]{1,0:T(8,128)(2,1)S(1)}, u32[]{:S(2)}, u32[]{:S(2)}) collective-permute-start(bf16[96,768]{1,0:T(8,128)(2,1)S(1)} %get-tuple-element.70.refs_1_), channel_id=1, source_target_pairs={{0,96},{32,64},{64,32},{96,0},{1,97},{33,65},{65,33},{97,1},{2,98}... | collective-permute-start | bytes 442376 | tf_op jit(solution)/shard_map/ppermute | solution.py:31
  187.7 8.6 %collective-permute-start.19 = (bf16[96,768]{1,0:T(8,128)(2,1)S(1)}, bf16[96,768]{1,0:T(8,128)(2,1)S(1)}, u32[]{:S(2)}, u32[]{:S(2)}) collective-permute-start(bf16[96,768]{1,0:T(8,128)(2,1)S(1)} %get-tuple-element.70.refs_1_), channel_id=1, source_target_pairs={{0,64},{32,96},{64,0},{96,32},{1,65},{33,97},{65,1},{97,33},{2,66}... | collective-permute-start | bytes 442376 | tf_op jit(solution)/shard_map/ppermute | solution.py:31
  187.7 8.7 %collective-permute-start.18 = (bf16[96,768]{1,0:T(8,128)(2,1)S(1)}, bf16[96,768]{1,0:T(8,128)(2,1)S(1)}, u32[]{:S(2)}, u32[]{:S(2)}) collective-permute-start(bf16[96,768]{1,0:T(8,128)(2,1)S(1)} %get-tuple-element.70.refs_1_), channel_id=1, source_target_pairs={{0,32},{32,0},{64,96},{96,64},{1,33},{33,1},{65,97},{97,65},{2,34}... | collective-permute-start | bytes 442376 | tf_op jit(solution)/shard_map/ppermute | solution.py:31
  189.6 2.1 %copy-start.8 = (f32[96,1536]{1,0:T(8,128)S(1)}, f32[96,1536]{1,0:T(8,128)}, u32[]{:S(2)}) copy-start(f32[96,1536]{1,0:T(8,128)} %get-tuple-element.85) | copy-start | bytes 1769476
  189.6 2.1 %copy-start.9 = (f32[96,1280]{1,0:T(8,128)S(1)}, f32[96,1280]{1,0:T(8,128)}, u32[]{:S(2)}) copy-start(f32[96,1280]{1,0:T(8,128)} %get-tuple-element.81) | copy-start | bytes 1474564
  189.6 2.1 %copy-start.12 = (f32[96,1024]{1,0:T(8,128)S(1)}, f32[96,1024]{1,0:T(8,128)}, u32[]{:S(2)}) copy-start(f32[96,1024]{1,0:T(8,128)} %get-tuple-element.77) | copy-start | bytes 1179652
  191.7 1.4 copy-start.3
  191.7 1.7 copy-start.5

commit v4 on v3

--- a/solution.py
+++ b/solution.py
@@ -18,7 +18,7 @@
 GROUPS = 4
 OWNERS = 32
 CAPACITY = 32
-UNITS = (12, 10, 8, 6)
+UNITS = (10, 10, 8, 8)
 TILE = 2
 MIB = 1024 * 1024
 
@@ -168,16 +168,14 @@
             dispatch, input_grad[:, span], preferred_element_type=jnp.float32
         ).astype(jnp.bfloat16)
         earlier_work = target if number == 1 else rows[: max(0, number - 1)]
-        outgoing = after(outgoing, arrived, earlier_work)
+        outgoing = after(outgoing, arrived, earlier_work, joined[: max(0, number - 1)])
         arrived = lax.all_to_all(outgoing, "vocab", split_axis=0, concat_axis=0, tiled=True)
         ready = after(arrived, rows)
         grad, *pieces = combine(here, target, head_grad, ready, span.start, TILE * unit)
-        if number == last:
-            pieces = after(pieces, fars[: number - 1])
         for flip, piece in enumerate(pieces, 1):
             grad = grad + swap_z(piece, flip).astype(jnp.float32)
         if 1 <= number < last:
-            grad = after(grad, joined, fars[: number - 1])
+            grad = after(grad, fars)
         states.append(update(grad, master[:, span], moment_one[:, span], moment_two[:, span]))
         block = states[-1][0].astype(jnp.bfloat16)
         rows.append(block)

time: 199 us -> 210 us (1.055)
  waiting for transfers between devices: 79 us -> 94 us
  starting transfers between devices: 58.5 us -> 55.2 us
    ppermute x21, waiting for transfers between devices: 37.7 us -> 64.2 us  [swap_z(): return lax.ppermute(block, 'dp', [(i, i ^ flip) for i in range(GROUPS)])]
    all_to_all x4, waiting for transfers between devices: 41.3 us -> 29.8 us  [local(): lax.all_to_all(outgoing, 'vocab', split_axis=0, concat_axis=0, tiled=True)]
    ppermute x21, starting transfers between devices: 35.5 us -> 27.7 us  [swap_z(): return lax.ppermute(block, 'dp', [(i, i ^ flip) for i in range(GROUPS)])]
    all_to_all x4, starting transfers between devices: 23.1 us -> 27.5 us  [local(): lax.all_to_all(outgoing, 'vocab', split_axis=0, concat_axis=0, tiled=True)]
    unnamed x37 -> x41, local copies, waits for them, and re-layouts: 5.26 us -> 6.14 us
  transfers between devices with their start and end apart: 25 -> 25, of which waited for: 14 -> 19; matrix products, arithmetic and copies ran while one was open for 15% -> 14% of each run, Pallas kernels for 9% -> 8%
where the time goes in v4:
time: 210 us; the launch traced here: 209 us
  waiting for transfers between devices  94 us (45%)
  starting transfers between devices  55.2 us (26%)
  other arithmetic  18.8 us (9%)
  matrix products  16.8 us (8%)
  Pallas kernels  16.6 us (8%)
  local copies, waits for them, and re-layouts  6.26 us (3%)
    ppermute x21, waiting for transfers between devices, swap_z(): return lax.ppermute(block, 'dp', [(i, i ^ flip) for i in range(GROUPS)])  64.2 us
    all_to_all x4, waiting for transfers between devices, local(): lax.all_to_all(outgoing, 'vocab', split_axis=0, concat_axis=0, tiled=True)  29.8 us
    ppermute x21, starting transfers between devices, swap_z(): return lax.ppermute(block, 'dp', [(i, i ^ flip) for i in range(GROUPS)])  27.7 us
    all_to_all x4, starting transfers between devices, local(): lax.all_to_all(outgoing, 'vocab', split_axis=0, concat_axis=0, tiled=True)  27.5 us
    dot_general x4, matrix products, local(): jnp.dot(dispatch, input_grad[:, span], preferred_element_type=jnp.float32)  16.4 us
    pallas_call x4, Pallas kernels, combine(): pl.pallas_call(combine_body, grid=(width // tile,), out_shape=[jax.ShapeD...  14.1 us
    convert_element_type x4, other arithmetic, local(): block = states[-1][0].astype(jnp.bfloat16)  9.81 us
    unnamed x41, local copies, waits for them, and re-layouts  6.14 us
  transfers between devices with their start and end apart: 25, of which 19 were waited for; matrix products, arithmetic and copies ran while one was open for 14% of the time, Pallas kernels for 8%

profile of v4, /device:TPU:0, one launch (start us, length us, event | category | flops | bytes accessed | tf_op | source)
XLA Modules:
  0.0 208.8 jit_solution(3110283266541849540)
XLA Ops:
  0.6 0.5 broadcast.141
  1.1 1.6 reduce.7
  3.1 4.4 %convolution_convert_fusion.1 = bf16[1024,1280]{1,0:T(8,128)(2,1)} fusion(bf16[512,4608]{1,0:T(8,128)(2,1)} %param.7, s32[512]{0:T(512)S(1)} %bitcast.20), kind=kOutput, calls=%fused_computation.1 | convolution fusion | flops 1344012288 | bytes 3934208 | tf_op jit(solution)/shard_map/dot_general | solution.py:167
  7.4 7.5 %all-to-all-start = ((bf16[32,32,1280]{2,1,0:T(8,128)(2,1)}), bf16[32,32,1280]{2,1,0:T(8,128)(2,1)S(1)}, u32[]{:S(2)}, u32[]{:S(2)}) async-start(bf16[32,32,1280]{2,1,0:T(8,128)(2,1)} %bitcast.16), calls=%async_computation | async-start | bytes 5242880 | tf_op jit(solution)/shard_map/all_to_all | solution.py:172
  15.4 0.6 select_reduce_fusion
  16.2 4.4 %convolution_convert_fusion = bf16[1024,1280]{1,0:T(8,128)(2,1)} fusion(bf16[512,4608]{1,0:T(8,128)(2,1)} %param.7, s32[512]{0:T(512)S(1)} %bitcast.21), kind=kOutput, calls=%fused_computation | convolution fusion | flops 1344012288 | bytes 3934208 | tf_op jit(solution)/shard_map/dot_general | solution.py:167
  20.5 29.1 %all-to-all-done = bf16[32,32,1280]{2,1,0:T(8,128)(2,1)S(1)} async-done(((bf16[32,32,1280]{2,1,0:T(8,128)(2,1)}), bf16[32,32,1280]{2,1,0:T(8,128)(2,1)S(1)}, u32[]{:S(2)}, u32[]{:S(2)}) %all-to-all-start) | async-done | bytes 2621472 | tf_op jit(solution)/shard_map/all_to_all | solution.py:172
  49.6 1.5 copy-done.1
  51.1 5.1 %all-to-all-start.1 = ((bf16[32,32,1280]{2,1,0:T(8,128)(2,1)}), bf16[32,32,1280]{2,1,0:T(8,128)(2,1)}, u32[]{:S(2)}, u32[]{:S(2)}) async-start(bf16[32,32,1280]{2,1,0:T(8,128)(2,1)} %bitcast.15), calls=%async_computation.1 | async-start | bytes 5242880 | tf_op jit(solution)/shard_map/all_to_all | solution.py:172
  56.2 1.7 copy-done.2
  58.0 2.4 %shard_map.102 = (f32[96,1280]{1,0:T(8,128)S(1)}, bf16[96,1280]{1,0:T(8,128)(2,1)S(1)}, bf16[96,1280]{1,0:T(8,128)(2,1)S(1)}, bf16[96,1280]{1,0:T(8,128)(2,1)S(1)}) custom-call(s32[1]{0:T(128)} %bitcast.here_ref, s32[1,1024]{1,0:T(1,128)S(1)} %sub.19.target_ref, bf16[1,384,4608]{2,1,0:T(8,128)(2,1)S(1)} %copy-done, bf16[1024,1280]{1,0:T(8,128)(2,1)S(1)} %bitcast.14), custom_call_target="tpu_custom_call" | custom-call | flops 1006632960 | bytes 5079040 | tf_op jit(solution)/shard_map/pallas_call | solution.py:67
  60.4 2.0 collective-permute-start
  62.4 3.6 %collective-permute-start.1 = (bf16[96,1280]{1,0:T(8,128)(2,1)S(1)}, bf16[96,1280]{1,0:T(8,128)(2,1)S(1)}, u32[]{:S(2)}, u32[]{:S(2)}) collective-permute-start(bf16[96,1280]{1,0:T(8,128)(2,1)S(1)} %get-tuple-element.36), channel_id=1, source_target_pairs={{0,64},{32,96},{64,0},{96,32},{1,65},{33,97},{65,1},{97,33},{2,66}... | collective-permute-start | bytes 737288 | tf_op jit(solution)/shard_map/ppermute | solution.py:31
  66.0 3.3 %collective-permute-done = bf16[96,1280]{1,0:T(8,128)(2,1)S(1)} collective-permute-done((bf16[96,1280]{1,0:T(8,128)(2,1)S(1)}, bf16[96,1280]{1,0:T(8,128)(2,1)S(1)}, u32[]{:S(2)}, u32[]{:S(2)}) %collective-permute-start) | collective-permute-done | bytes 245792 | tf_op jit(solution)/shard_map/ppermute | solution.py:31
  69.3 8.0 %collective-permute-done.1 = bf16[96,1280]{1,0:T(8,128)(2,1)S(1)} collective-permute-done((bf16[96,1280]{1,0:T(8,128)(2,1)S(1)}, bf16[96,1280]{1,0:T(8,128)(2,1)S(1)}, u32[]{:S(2)}, u32[]{:S(2)}) %collective-permute-start.1) | collective-permute-done | bytes 245792 | tf_op jit(solution)/shard_map/ppermute | solution.py:31
  77.3 2.6 %collective-permute-done.2 = bf16[96,1280]{1,0:T(8,128)(2,1)S(1)} collective-permute-done((bf16[96,1280]{1,0:T(8,128)(2,1)S(1)}, bf16[96,1280]{1,0:T(8,128)(2,1)S(1)}, u32[]{:S(2)}, u32[]{:S(2)}) %collective-permute-start.2) | collective-permute-done | bytes 245792 | tf_op jit(solution)/shard_map/ppermute | solution.py:31
  79.9 2.8 %fusion.25 = (bf16[96,1280]{1,0:T(8,128)(2,1)S(1)}, f32[96,1280]{1,0:T(8,128)}, f32[96,1280]{1,0:T(8,128)}, f32[96,1280]{1,0:T(8,128)}) fusion(f32[96,4608]{1,0:T(8,128)} %param.11, bf16[96,1280]{1,0:T(8,128)(2,1)S(1)} %collective-permute-done.2, bf16[96,1280]{1,0:T(8,128)(2,1)S(1)} %collective-permute-done.1, f32[96,1280]{1,0:T(8,128)S(1)} %get-tuple-element.34, ...), kind=kLoop, calls=%fused_computation.58 | loop fusion | flops 2703360 | bytes 4423680 | tf_op jit(solution)/shard_map/convert_element_type | solution.py:180
  82.6 0.3 collective-permute-start.6
  82.9 3.8 %fusion.3 = bf16[1024,1024]{1,0:T(8,128)(2,1)} fusion(bf16[512,4608]{1,0:T(8,128)(2,1)} %param.7, s32[512]{0:T(512)S(1)} %bitcast.22), kind=kOutput, calls=%fused_computation.8 | convolution fusion | flops 1075314688 | bytes 3147776 | tf_op jit(solution)/shard_map/dot_general | solution.py:167
  86.8 3.7 %collective-permute-done.6 = bf16[96,1280]{1,0:T(8,128)(2,1)S(1)} collective-permute-done((bf16[96,1280]{1,0:T(8,128)(2,1)S(1)}, bf16[96,1280]{1,0:T(8,128)(2,1)S(1)}, u32[]{:S(2)}, u32[]{:S(2)}) %collective-permute-start.6) | collective-permute-done | bytes 245792 | tf_op jit(solution)/shard_map/ppermute | solution.py:31
  90.4 0.9 pad_maximum_fusion.3.refs_0_
  91.3 7.6 %all-to-all-start.2 = ((bf16[32,32,1024]{2,1,0:T(8,128)(2,1)}), bf16[32,32,1024]{2,1,0:T(8,128)(2,1)}, u32[]{:S(2)}, u32[]{:S(2)}) async-start(bf16[32,32,1024]{2,1,0:T(8,128)(2,1)} %bitcast.17), calls=%async_computation.2 | async-start | bytes 4194304 | tf_op jit(solution)/shard_map/all_to_all | solution.py:172
  98.9 4.6 %shard_map.103 = (f32[96,1280]{1,0:T(8,128)S(1)}, bf16[96,1280]{1,0:T(8,128)(2,1)S(1)}, bf16[96,1280]{1,0:T(8,128)(2,1)S(1)}, bf16[96,1280]{1,0:T(8,128)(2,1)S(1)}) custom-call(s32[1]{0:T(128)} %bitcast.here_ref, s32[1,1024]{1,0:T(1,128)S(1)} %sub.19.target_ref, bf16[1,384,4608]{2,1,0:T(8,128)(2,1)S(1)} %copy-done, bf16[1024,1280]{1,0:T(8,128)(2,1)} %bitcast.7.part_ref), custom_call_target="tpu_custom_call" | custom-call | flops 1006632960 | bytes 5079040 | tf_op jit(solution)/shard_map/pallas_call | solution.py:67
  103.6 2.2 %collective-permute-start.4 = (bf16[96,1280]{1,0:T(8,128)(2,1)S(1)}, bf16[96,1280]{1,0:T(8,128)(2,1)S(1)}, u32[]{:S(2)}, u32[]{:S(2)}) collective-permute-start(bf16[96,1280]{1,0:T(8,128)(2,1)S(1)} %get-tuple-element.42), channel_id=1, source_target_pairs={{0,64},{32,96},{64,0},{96,32},{1,65},{33,97},{65,1},{97,33},{2,66}... | collective-permute-start | bytes 737288 | tf_op jit(solution)/shard_map/ppermute | solution.py:31
  105.8 2.5 %collective-permute-start.5 = (bf16[96,1280]{1,0:T(8,128)(2,1)S(1)}, bf16[96,1280]{1,0:T(8,128)(2,1)S(1)}, u32[]{:S(2)}, u32[]{:S(2)}) collective-permute-start(bf16[96,1280]{1,0:T(8,128)(2,1)S(1)} %get-tuple-element.43), channel_id=1, source_target_pairs={{0,96},{32,64},{64,32},{96,0},{1,97},{33,65},{65,33},{97,1},{2,98}... | collective-permute-start | bytes 737288 | tf_op jit(solution)/shard_map/ppermute | solution.py:31
  108.3 4.1 %collective-permute-done.3 = bf16[96,1280]{1,0:T(8,128)(2,1)S(1)} collective-permute-done((bf16[96,1280]{1,0:T(8,128)(2,1)S(1)}, bf16[96,1280]{1,0:T(8,128)(2,1)S(1)}, u32[]{:S(2)}, u32[]{:S(2)}) %collective-permute-start.3) | collective-permute-done | bytes 245792 | tf_op jit(solution)/shard_map/ppermute | solution.py:31
  112.4 5.5 %collective-permute-done.4 = bf16[96,1280]{1,0:T(8,128)(2,1)S(1)} collective-permute-done((bf16[96,1280]{1,0:T(8,128)(2,1)S(1)}, bf16[96,1280]{1,0:T(8,128)(2,1)S(1)}, u32[]{:S(2)}, u32[]{:S(2)}) %collective-permute-start.4) | collective-permute-done | bytes 245792 | tf_op jit(solution)/shard_map/ppermute | solution.py:31
  117.9 1.8 collective-permute-done.5
  119.8 7.7 %collective-permute-done.7.refs_1_ = bf16[192,1280]{1,0:T(8,128)(2,1)S(1)} collective-permute-done((bf16[192,1280]{1,0:T(8,128)(2,1)S(1)}, bf16[192,1280]{1,0:T(8,128)(2,1)S(1)}, u32[]{:S(2)}, u32[]{:S(2)}) %collective-permute-start.7) | collective-permute-done | bytes 491552 | tf_op jit(solution)/shard_map/ppermute | solution.py:31
  127.5 0.8 copy-done.6
  128.3 2.7 %fusion.23 = (bf16[96,1280]{1,0:T(8,128)(2,1)S(1)}, f32[96,1280]{1,0:T(8,128)}, f32[96,1280]{1,0:T(8,128)}, f32[96,1280]{1,0:T(8,128)}) fusion(f32[96,4608]{1,0:T(8,128)} %param.11, f32[96,1280]{1,0:T(8,128)S(1)} %convert_add_fusion, f32[96,4608]{1,0:T(8,128)} %param.12, f32[96,4608]{1,0:T(8,128)} %param.13), kind=kLoop, calls=%fused_computation.57 | loop fusion | flops 1966080 | bytes 3686400 | tf_op jit(solution)/shard_map/convert_element_type | solution.py:180
  131.0 0.7 collective-permute-start.11
  131.6 3.8 %fusion.4 = bf16[1024,1024]{1,0:T(8,128)(2,1)} fusion(bf16[512,4608]{1,0:T(8,128)(2,1)} %param.7, s32[512]{0:T(512)S(1)} %bitcast.23), kind=kOutput, calls=%fused_computation.9 | convolution fusion | flops 1075314688 | bytes 3147776 | tf_op jit(solution)/shard_map/dot_general | solution.py:167
  135.4 4.0 %collective-permute-done.11 = bf16[96,1280]{1,0:T(8,128)(2,1)S(1)} collective-permute-done((bf16[96,1280]{1,0:T(8,128)(2,1)S(1)}, bf16[96,1280]{1,0:T(8,128)(2,1)S(1)}, u32[]{:S(2)}, u32[]{:S(2)}) %collective-permute-start.11) | collective-permute-done | bytes 245792 | tf_op jit(solution)/shard_map/ppermute | solution.py:31
  139.4 0.9 pad_maximum_fusion.4.refs_2_
  140.3 7.3 %all-to-all-start.3 = ((bf16[32,32,1024]{2,1,0:T(8,128)(2,1)}), bf16[32,32,1024]{2,1,0:T(8,128)(2,1)}, u32[]{:S(2)}, u32[]{:S(2)}) async-start(bf16[32,32,1024]{2,1,0:T(8,128)(2,1)} %bitcast.18), calls=%async_computation.3 | async-start | bytes 4194304 | tf_op jit(solution)/shard_map/all_to_all | solution.py:172
  147.7 3.6 %shard_map.104 = (f32[96,1024]{1,0:T(8,128)S(1)}, bf16[96,1024]{1,0:T(8,128)(2,1)S(1)}, bf16[96,1024]{1,0:T(8,128)(2,1)S(1)}, bf16[96,1024]{1,0:T(8,128)(2,1)S(1)}) custom-call(s32[1]{0:T(128)} %bitcast.here_ref, s32[1,1024]{1,0:T(1,128)S(1)} %sub.19.target_ref, bf16[1,384,4608]{2,1,0:T(8,128)(2,1)S(1)} %copy-done, bf16[1024,1024]{1,0:T(8,128)(2,1)} %bitcast.9.part_ref), custom_call_target="tpu_custom_call" | custom-call | flops 805306368 | bytes 4063232 | tf_op jit(solution)/shard_map/pallas_call | solution.py:67
  151.3 2.1 collective-permute-start.8
  153.3 0.3 collective-permute-start.9
  153.6 2.5 %collective-permute-start.10 = (bf16[96,1024]{1,0:T(8,128)(2,1)S(1)}, bf16[96,1024]{1,0:T(8,128)(2,1)S(1)}, u32[]{:S(2)}, u32[]{:S(2)}) collective-permute-start(bf16[96,1024]{1,0:T(8,128)(2,1)S(1)} %get-tuple-element.50), channel_id=1, source_target_pairs={{0,96},{32,64},{64,32},{96,0},{1,97},{33,65},{65,33},{97,1},{2,98}... | collective-permute-start | bytes 589832 | tf_op jit(solution)/shard_map/ppermute | solution.py:31
  156.1 10.1 %collective-permute-done.8 = bf16[96,1024]{1,0:T(8,128)(2,1)S(1)} collective-permute-done((bf16[96,1024]{1,0:T(8,128)(2,1)S(1)}, bf16[96,1024]{1,0:T(8,128)(2,1)S(1)}, u32[]{:S(2)}, u32[]{:S(2)}) %collective-permute-start.8) | collective-permute-done | bytes 196640 | tf_op jit(solution)/shard_map/ppermute | solution.py:31
  166.2 3.7 %collective-permute-done.9 = bf16[96,1024]{1,0:T(8,128)(2,1)S(1)} collective-permute-done((bf16[96,1024]{1,0:T(8,128)(2,1)S(1)}, bf16[96,1024]{1,0:T(8,128)(2,1)S(1)}, u32[]{:S(2)}, u32[]{:S(2)}) %collective-permute-start.9) | collective-permute-done | bytes 196640 | tf_op jit(solution)/shard_map/ppermute | solution.py:31
  170.0 0.8 copy-done.8
  170.8 2.6 %fusion.21 = (bf16[96,1024]{1,0:T(8,128)(2,1)}, f32[96,1024]{1,0:T(8,128)}, f32[96,1024]{1,0:T(8,128)}, f32[96,1024]{1,0:T(8,128)}) fusion(f32[96,4608]{1,0:T(8,128)} %param.11, f32[96,1024]{1,0:T(8,128)S(1)} %convert_add_fusion.3, f32[96,4608]{1,0:T(8,128)} %param.12, f32[96,4608]{1,0:T(8,128)} %param.13), kind=kLoop, calls=%fused_computation.56 | loop fusion | flops 1572864 | bytes 2949120 | tf_op jit(solution)/shard_map/convert_element_type | solution.py:180
  173.3 2.5 %collective-permute-start.16 = (bf16[96,1024]{1,0:T(8,128)(2,1)}, bf16[96,1024]{1,0:T(8,128)(2,1)}, u32[]{:S(2)}, u32[]{:S(2)}) collective-permute-start(bf16[96,1024]{1,0:T(8,128)(2,1)} %get-tuple-element.68), channel_id=1, source_target_pairs={{0,96},{32,64},{64,32},{96,0},{1,97},{33,65},{65,33},{97,1},{2,98}... | collective-permute-start | bytes 589832 | tf_op jit(solution)/shard_map/ppermute | solution.py:31
  175.8 0.7 all-to-all-done.3
  176.5 3.5 %shard_map.105 = (f32[96,1024]{1,0:T(8,128)S(1)}, bf16[96,1024]{1,0:T(8,128)(2,1)S(1)}, bf16[96,1024]{1,0:T(8,128)(2,1)S(1)}, bf16[96,1024]{1,0:T(8,128)(2,1)S(1)}) custom-call(s32[1]{0:T(128)} %bitcast.here_ref, s32[1,1024]{1,0:T(1,128)S(1)} %sub.19.target_ref, bf16[1,384,4608]{2,1,0:T(8,128)(2,1)S(1)} %copy-done, bf16[1024,1024]{1,0:T(8,128)(2,1)} %bitcast.11.part_ref), custom_call_target="tpu_custom_call" | custom-call | flops 805306368 | bytes 4063232 | tf_op jit(solution)/shard_map/pallas_call | solution.py:67
  180.1 2.2 %collective-permute-start.14 = (bf16[96,1024]{1,0:T(8,128)(2,1)S(1)}, bf16[96,1024]{1,0:T(8,128)(2,1)S(1)}, u32[]{:S(2)}, u32[]{:S(2)}) collective-permute-start(bf16[96,1024]{1,0:T(8,128)(2,1)S(1)} %get-tuple-element.56), channel_id=1, source_target_pairs={{0,64},{32,96},{64,0},{96,32},{1,65},{33,97},{65,1},{97,33},{2,66}... | collective-permute-start | bytes 589832 | tf_op jit(solution)/shard_map/ppermute | solution.py:31
  182.4 2.5 %collective-permute-start.15 = (bf16[96,1024]{1,0:T(8,128)(2,1)S(1)}, bf16[96,1024]{1,0:T(8,128)(2,1)S(1)}, u32[]{:S(2)}, u32[]{:S(2)}) collective-permute-start(bf16[96,1024]{1,0:T(8,128)(2,1)S(1)} %get-tuple-element.57), channel_id=1, source_target_pairs={{0,96},{32,64},{64,32},{96,0},{1,97},{33,65},{65,33},{97,1},{2,98}... | collective-permute-start | bytes 589832 | tf_op jit(solution)/shard_map/ppermute | solution.py:31
  184.8 1.0 pad_maximum_fusion.5.refs_4_
  186.0 2.0 collective-permute-done.13
  188.0 4.5 %collective-permute-done.14 = bf16[96,1024]{1,0:T(8,128)(2,1)S(1)} collective-permute-done((bf16[96,1024]{1,0:T(8,128)(2,1)S(1)}, bf16[96,1024]{1,0:T(8,128)(2,1)S(1)}, u32[]{:S(2)}, u32[]{:S(2)}) %collective-permute-start.14) | collective-permute-done | bytes 196640 | tf_op jit(solution)/shard_map/ppermute | solution.py:31
  192.4 1.3 collective-permute-done.15
  193.7 1.8 fusion.19
  195.5 2.6 %collective-permute-start.20 = (bf16[96,1024]{1,0:T(8,128)(2,1)S(1)}, bf16[96,1024]{1,0:T(8,128)(2,1)S(1)}, u32[]{:S(2)}, u32[]{:S(2)}) collective-permute-start(bf16[96,1024]{1,0:T(8,128)(2,1)S(1)} %get-tuple-element.64.refs_1_), channel_id=1, source_target_pairs={{0,96},{32,64},{64,32},{96,0},{1,97},{33,65},{65,33},{97,1},{2,98}... | collective-permute-start | bytes 589832 | tf_op jit(solution)/shard_map/ppermute | solution.py:31
  198.1 1.6 collective-permute-start.18
  199.7 2.1 %pad_maximum_fusion = (f32[96,4608]{1,0:T(8,128)}, f32[96,4608]{1,0:T(8,128)}) fusion(f32[96,1024]{1,0:T(8,128)S(1)} %get-tuple-element.65, f32[96,1024]{1,0:T(8,128)S(1)} %copy-done.17, f32[96,1280]{1,0:T(8,128)S(1)} %copy-done.12, f32[96,1280]{1,0:T(8,128)S(1)} %copy-done.14, f32[96,1024]{1,0:T(8,128)S(1)} %get-tuple-element.66, ...), kind=kLoop, calls=%fused_computation.10 | loop fusion | flops 2654208 | bytes 7077888 | tf_op jit(solution)/shard_map/concatenate | solution.py:199
  201.9 1.3 pad_maximum_fusion.2
  203.3 0.5 copy-done.7
  204.0 1.6 shard_map.106.refs_0_
  205.6 0.6 collective-permute-done.20.refs_4_
  206.3 1.0 collective-permute-done.19.refs_3_
  207.3 0.5 collective-permute-done.18.refs_2_
  207.7 0.9 shard_map.107
  (61 shorter events, 1.6 us)
Async XLA Ops:
  7.4 7.5 %copy-start.19 = (s32[16384,1]{0,1:T(1,128)S(1)}, s32[16384,1]{0,1:T(1,128)}, u32[]{:S(2)}) copy-start(s32[16384,1]{0,1:T(1,128)} %param.9) | copy-start | bytes 196612
  7.4 42.2 %all-to-all-start = ((bf16[32,32,1280]{2,1,0:T(8,128)(2,1)}), bf16[32,32,1280]{2,1,0:T(8,128)(2,1)S(1)}, u32[]{:S(2)}, u32[]{:S(2)}) async-start(bf16[32,32,1280]{2,1,0:T(8,128)(2,1)} %bitcast.16), calls=%async_computation | async-start | bytes 5242880 | tf_op jit(solution)/shard_map/all_to_all | solution.py:172
  49.6 1.5 copy-start.1
  51.1 5.1 %copy-start = (bf16[1,384,4608]{2,1,0:T(8,128)(2,1)S(1)}, bf16[1,384,4608]{2,1,0:T(8,128)(2,1)}, u32[]{:S(2)}) copy-start(bf16[1,384,4608]{2,1,0:T(8,128)(2,1)} %head_ref.7) | copy-start | bytes 10616836
  51.1 40.2 %all-to-all-start.1 = ((bf16[32,32,1280]{2,1,0:T(8,128)(2,1)}), bf16[32,32,1280]{2,1,0:T(8,128)(2,1)}, u32[]{:S(2)}, u32[]{:S(2)}) async-start(bf16[32,32,1280]{2,1,0:T(8,128)(2,1)} %bitcast.15), calls=%async_computation.1 | async-start | bytes 5242880 | tf_op jit(solution)/shard_map/all_to_all | solution.py:172
  56.2 1.7 copy-start.2
  60.4 8.9 %collective-permute-start = (bf16[96,1280]{1,0:T(8,128)(2,1)S(1)}, bf16[96,1280]{1,0:T(8,128)(2,1)S(1)}, u32[]{:S(2)}, u32[]{:S(2)}) collective-permute-start(bf16[96,1280]{1,0:T(8,128)(2,1)S(1)} %get-tuple-element.35), channel_id=1, source_target_pairs={{0,32},{32,0},{64,96},{96,64},{1,33},{33,1},{65,97},{97,65},{2,34}... | collective-permute-start | bytes 737288 | tf_op jit(solution)/shard_map/ppermute | solution.py:31
  62.4 14.9 %collective-permute-start.1 = (bf16[96,1280]{1,0:T(8,128)(2,1)S(1)}, bf16[96,1280]{1,0:T(8,128)(2,1)S(1)}, u32[]{:S(2)}, u32[]{:S(2)}) collective-permute-start(bf16[96,1280]{1,0:T(8,128)(2,1)S(1)} %get-tuple-element.36), channel_id=1, source_target_pairs={{0,64},{32,96},{64,0},{96,32},{1,65},{33,97},{65,1},{97,33},{2,66}... | collective-permute-start | bytes 737288 | tf_op jit(solution)/shard_map/ppermute | solution.py:31
  66.0 13.9 %collective-permute-start.2 = (bf16[96,1280]{1,0:T(8,128)(2,1)S(1)}, bf16[96,1280]{1,0:T(8,128)(2,1)S(1)}, u32[]{:S(2)}, u32[]{:S(2)}) collective-permute-start(bf16[96,1280]{1,0:T(8,128)(2,1)S(1)} %get-tuple-element.37), channel_id=1, source_target_pairs={{0,96},{32,64},{64,32},{96,0},{1,97},{33,65},{65,33},{97,1},{2,98}... | collective-permute-start | bytes 737288 | tf_op jit(solution)/shard_map/ppermute | solution.py:31
  82.6 7.8 %collective-permute-start.6 = (bf16[96,1280]{1,0:T(8,128)(2,1)S(1)}, bf16[96,1280]{1,0:T(8,128)(2,1)S(1)}, u32[]{:S(2)}, u32[]{:S(2)}) collective-permute-start(bf16[96,1280]{1,0:T(8,128)(2,1)S(1)} %get-tuple-element.76), channel_id=1, source_target_pairs={{0,96},{32,64},{64,32},{96,0},{1,97},{33,65},{65,33},{97,1},{2,98}... | collective-permute-start | bytes 737288 | tf_op jit(solution)/shard_map/ppermute | solution.py:31
  91.3 49.0 %all-to-all-start.2 = ((bf16[32,32,1024]{2,1,0:T(8,128)(2,1)}), bf16[32,32,1024]{2,1,0:T(8,128)(2,1)}, u32[]{:S(2)}, u32[]{:S(2)}) async-start(bf16[32,32,1024]{2,1,0:T(8,128)(2,1)} %bitcast.17), calls=%async_computation.2 | async-start | bytes 4194304 | tf_op jit(solution)/shard_map/all_to_all | solution.py:172
  98.9 9.4 %copy-start.3 = (bf16[192,1280]{1,0:T(8,128)(2,1)S(1)}, bf16[192,1280]{1,0:T(8,128)(2,1)}, u32[]{:S(2)}) copy-start(bf16[192,1280]{1,0:T(8,128)(2,1)} %pad_maximum_fusion.3.refs_0_) | copy-start | bytes 1474564
  103.5 8.9 %collective-permute-start.3 = (bf16[96,1280]{1,0:T(8,128)(2,1)S(1)}, bf16[96,1280]{1,0:T(8,128)(2,1)S(1)}, u32[]{:S(2)}, u32[]{:S(2)}) collective-permute-start(bf16[96,1280]{1,0:T(8,128)(2,1)S(1)} %get-tuple-element.41), channel_id=1, source_target_pairs={{0,32},{32,0},{64,96},{96,64},{1,33},{33,1},{65,97},{97,65},{2,34}... | collective-permute-start | bytes 737288 | tf_op jit(solution)/shard_map/ppermute | solution.py:31
  103.6 14.3 %collective-permute-start.4 = (bf16[96,1280]{1,0:T(8,128)(2,1)S(1)}, bf16[96,1280]{1,0:T(8,128)(2,1)S(1)}, u32[]{:S(2)}, u32[]{:S(2)}) collective-permute-start(bf16[96,1280]{1,0:T(8,128)(2,1)S(1)} %get-tuple-element.42), channel_id=1, source_target_pairs={{0,64},{32,96},{64,0},{96,32},{1,65},{33,97},{65,1},{97,33},{2,66}... | collective-permute-start | bytes 737288 | tf_op jit(solution)/shard_map/ppermute | solution.py:31
  105.8 13.9 %collective-permute-start.5 = (bf16[96,1280]{1,0:T(8,128)(2,1)S(1)}, bf16[96,1280]{1,0:T(8,128)(2,1)S(1)}, u32[]{:S(2)}, u32[]{:S(2)}) collective-permute-start(bf16[96,1280]{1,0:T(8,128)(2,1)S(1)} %get-tuple-element.43), channel_id=1, source_target_pairs={{0,96},{32,64},{64,32},{96,0},{1,97},{33,65},{65,33},{97,1},{2,98}... | collective-permute-start | bytes 737288 | tf_op jit(solution)/shard_map/ppermute | solution.py:31
  108.3 19.2 %collective-permute-start.7 = (bf16[192,1280]{1,0:T(8,128)(2,1)S(1)}, bf16[192,1280]{1,0:T(8,128)(2,1)S(1)}, u32[]{:S(2)}, u32[]{:S(2)}) collective-permute-start(bf16[192,1280]{1,0:T(8,128)(2,1)S(1)} %copy-done.3), channel_id=1, source_target_pairs={{0,32},{32,0},{64,96},{96,64},{1,33},{33,1},{65,97},{97,65},{2,34}... | collective-permute-start | bytes 1474568 | tf_op jit(solution)/shard_map/ppermute | solution.py:31
  127.5 0.8 copy-start.6
  131.0 8.4 %collective-permute-start.11 = (bf16[96,1280]{1,0:T(8,128)(2,1)S(1)}, bf16[96,1280]{1,0:T(8,128)(2,1)S(1)}, u32[]{:S(2)}, u32[]{:S(2)}) collective-permute-start(bf16[96,1280]{1,0:T(8,128)(2,1)S(1)} %get-tuple-element.72), channel_id=1, source_target_pairs={{0,96},{32,64},{64,32},{96,0},{1,97},{33,65},{65,33},{97,1},{2,98}... | collective-permute-start | bytes 737288 | tf_op jit(solution)/shard_map/ppermute | solution.py:31
  140.3 36.2 %all-to-all-start.3 = ((bf16[32,32,1024]{2,1,0:T(8,128)(2,1)}), bf16[32,32,1024]{2,1,0:T(8,128)(2,1)}, u32[]{:S(2)}, u32[]{:S(2)}) async-start(bf16[32,32,1024]{2,1,0:T(8,128)(2,1)} %bitcast.18), calls=%async_computation.3 | async-start | bytes 4194304 | tf_op jit(solution)/shard_map/all_to_all | solution.py:172
  147.6 22.3 %collective-permute-start.12 = (bf16[192,1280]{1,0:T(8,128)(2,1)}, bf16[192,1280]{1,0:T(8,128)(2,1)S(1)}, u32[]{:S(2)}, u32[]{:S(2)}) collective-permute-start(bf16[192,1280]{1,0:T(8,128)(2,1)} %pad_maximum_fusion.4.refs_2_), channel_id=1, source_target_pairs={{0,32},{32,0},{64,96},{96,64},{1,33},{33,1},{65,97},{97,65},{2,34}... | collective-permute-start | bytes 1474568 | tf_op jit(solution)/shard_map/ppermute | solution.py:31
  151.3 14.9 %collective-permute-start.8 = (bf16[96,1024]{1,0:T(8,128)(2,1)S(1)}, bf16[96,1024]{1,0:T(8,128)(2,1)S(1)}, u32[]{:S(2)}, u32[]{:S(2)}) collective-permute-start(bf16[96,1024]{1,0:T(8,128)(2,1)S(1)} %get-tuple-element.48), channel_id=1, source_target_pairs={{0,32},{32,0},{64,96},{96,64},{1,33},{33,1},{65,97},{97,65},{2,34}... | collective-permute-start | bytes 589832 | tf_op jit(solution)/shard_map/ppermute | solution.py:31
  153.3 16.5 %collective-permute-start.9 = (bf16[96,1024]{1,0:T(8,128)(2,1)S(1)}, bf16[96,1024]{1,0:T(8,128)(2,1)S(1)}, u32[]{:S(2)}, u32[]{:S(2)}) collective-permute-start(bf16[96,1024]{1,0:T(8,128)(2,1)S(1)} %get-tuple-element.49), channel_id=1, source_target_pairs={{0,64},{32,96},{64,0},{96,32},{1,65},{33,97},{65,1},{97,33},{2,66}... | collective-permute-start | bytes 589832 | tf_op jit(solution)/shard_map/ppermute | solution.py:31
  153.6 16.2 %collective-permute-start.10 = (bf16[96,1024]{1,0:T(8,128)(2,1)S(1)}, bf16[96,1024]{1,0:T(8,128)(2,1)S(1)}, u32[]{:S(2)}, u32[]{:S(2)}) collective-permute-start(bf16[96,1024]{1,0:T(8,128)(2,1)S(1)} %get-tuple-element.50), channel_id=1, source_target_pairs={{0,96},{32,64},{64,32},{96,0},{1,97},{33,65},{65,33},{97,1},{2,98}... | collective-permute-start | bytes 589832 | tf_op jit(solution)/shard_map/ppermute | solution.py:31
  170.0 0.8 copy-start.8
  173.3 11.5 %collective-permute-start.16 = (bf16[96,1024]{1,0:T(8,128)(2,1)}, bf16[96,1024]{1,0:T(8,128)(2,1)}, u32[]{:S(2)}, u32[]{:S(2)}) collective-permute-start(bf16[96,1024]{1,0:T(8,128)(2,1)} %get-tuple-element.68), channel_id=1, source_target_pairs={{0,96},{32,64},{64,32},{96,0},{1,97},{33,65},{65,33},{97,1},{2,98}... | collective-permute-start | bytes 589832 | tf_op jit(solution)/shard_map/ppermute | solution.py:31
  180.1 7.9 %collective-permute-start.13 = (bf16[96,1024]{1,0:T(8,128)(2,1)S(1)}, bf16[96,1024]{1,0:T(8,128)(2,1)S(1)}, u32[]{:S(2)}, u32[]{:S(2)}) collective-permute-start(bf16[96,1024]{1,0:T(8,128)(2,1)S(1)} %get-tuple-element.55), channel_id=1, source_target_pairs={{0,32},{32,0},{64,96},{96,64},{1,33},{33,1},{65,97},{97,65},{2,34}... | collective-permute-start | bytes 589832 | tf_op jit(solution)/shard_map/ppermute | solution.py:31
  180.1 12.3 %collective-permute-start.14 = (bf16[96,1024]{1,0:T(8,128)(2,1)S(1)}, bf16[96,1024]{1,0:T(8,128)(2,1)S(1)}, u32[]{:S(2)}, u32[]{:S(2)}) collective-permute-start(bf16[96,1024]{1,0:T(8,128)(2,1)S(1)} %get-tuple-element.56), channel_id=1, source_target_pairs={{0,64},{32,96},{64,0},{96,32},{1,65},{33,97},{65,1},{97,33},{2,66}... | collective-permute-start | bytes 589832 | tf_op jit(solution)/shard_map/ppermute | solution.py:31
  182.4 11.3 %collective-permute-start.15 = (bf16[96,1024]{1,0:T(8,128)(2,1)S(1)}, bf16[96,1024]{1,0:T(8,128)(2,1)S(1)}, u32[]{:S(2)}, u32[]{:S(2)}) collective-permute-start(bf16[96,1024]{1,0:T(8,128)(2,1)S(1)} %get-tuple-element.57), channel_id=1, source_target_pairs={{0,96},{32,64},{64,32},{96,0},{1,97},{33,65},{65,33},{97,1},{2,98}... | collective-permute-start | bytes 589832 | tf_op jit(solution)/shard_map/ppermute | solution.py:31
  185.9 17.4 %collective-permute-start.17 = (bf16[192,1024]{1,0:T(8,128)(2,1)S(1)}, bf16[192,1024]{1,0:T(8,128)(2,1)S(1)}, u32[]{:S(2)}, u32[]{:S(2)}) collective-permute-start(bf16[192,1024]{1,0:T(8,128)(2,1)S(1)} %pad_maximum_fusion.5.refs_4_), channel_id=1, source_target_pairs={{0,32},{32,0},{64,96},{96,64},{1,33},{33,1},{65,97},{97,65},{2,34}... | collective-permute-start | bytes 1179656 | tf_op jit(solution)/shard_map/ppermute | solution.py:31
  193.7 6.0 %copy-start.12 = (f32[96,1280]{1,0:T(8,128)S(1)}, f32[96,1280]{1,0:T(8,128)}, u32[]{:S(2)}) copy-start(f32[96,1280]{1,0:T(8,128)} %get-tuple-element.73) | copy-start | bytes 1474564
  193.7 6.0 %copy-start.13 = (f32[96,1280]{1,0:T(8,128)S(1)}, f32[96,1280]{1,0:T(8,128)}, u32[]{:S(2)}) copy-start(f32[96,1280]{1,0:T(8,128)} %get-tuple-element.74) | copy-start | bytes 1474564
  193.7 6.0 %copy-start.14 = (f32[96,1280]{1,0:T(8,128)S(1)}, f32[96,1280]{1,0:T(8,128)}, u32[]{:S(2)}) copy-start(f32[96,1280]{1,0:T(8,128)} %get-tuple-element.77) | copy-start | bytes 1474564
  193.7 6.0 %copy-start.15 = (f32[96,1280]{1,0:T(8,128)S(1)}, f32[96,1280]{1,0:T(8,128)}, u32[]{:S(2)}) copy-start(f32[96,1280]{1,0:T(8,128)} %get-tuple-element.78) | copy-start | bytes 1474564
  193.7 6.0 %copy-start.17 = (f32[96,1024]{1,0:T(8,128)S(1)}, f32[96,1024]{1,0:T(8,128)}, u32[]{:S(2)}) copy-start(f32[96,1024]{1,0:T(8,128)} %get-tuple-element.69) | copy-start | bytes 1179652
  193.7 6.0 %copy-start.18 = (f32[96,1024]{1,0:T(8,128)S(1)}, f32[96,1024]{1,0:T(8,128)}, u32[]{:S(2)}) copy-start(f32[96,1024]{1,0:T(8,128)} %get-tuple-element.70) | copy-start | bytes 1179652
  195.5 10.8 %collective-permute-start.20 = (bf16[96,1024]{1,0:T(8,128)(2,1)S(1)}, bf16[96,1024]{1,0:T(8,128)(2,1)S(1)}, u32[]{:S(2)}, u32[]{:S(2)}) collective-permute-start(bf16[96,1024]{1,0:T(8,128)(2,1)S(1)} %get-tuple-element.64.refs_1_), channel_id=1, source_target_pairs={{0,96},{32,64},{64,32},{96,0},{1,97},{33,65},{65,33},{97,1},{2,98}... | collective-permute-start | bytes 589832 | tf_op jit(solution)/shard_map/ppermute | solution.py:31
  198.1 9.2 %collective-permute-start.19 = (bf16[96,1024]{1,0:T(8,128)(2,1)S(1)}, bf16[96,1024]{1,0:T(8,128)(2,1)S(1)}, u32[]{:S(2)}, u32[]{:S(2)}) collective-permute-start(bf16[96,1024]{1,0:T(8,128)(2,1)S(1)} %get-tuple-element.64.refs_1_), channel_id=1, source_target_pairs={{0,64},{32,96},{64,0},{96,32},{1,65},{33,97},{65,1},{97,33},{2,66}... | collective-permute-start | bytes 589832 | tf_op jit(solution)/shard_map/ppermute | solution.py:31
  198.1 9.7 %collective-permute-start.18 = (bf16[96,1024]{1,0:T(8,128)(2,1)S(1)}, bf16[96,1024]{1,0:T(8,128)(2,1)S(1)}, u32[]{:S(2)}, u32[]{:S(2)}) collective-permute-start(bf16[96,1024]{1,0:T(8,128)(2,1)S(1)} %get-tuple-element.64.refs_1_), channel_id=1, source_target_pairs={{0,32},{32,0},{64,96},{96,64},{1,33},{33,1},{65,97},{97,65},{2,34}... | collective-permute-start | bytes 589832 | tf_op jit(solution)/shard_map/ppermute | solution.py:31
  199.7 2.2 %copy-start.10 = (f32[96,1280]{1,0:T(8,128)S(1)}, f32[96,1280]{1,0:T(8,128)}, u32[]{:S(2)}) copy-start(f32[96,1280]{1,0:T(8,128)} %get-tuple-element.75) | copy-start | bytes 1474564
  199.7 2.2 %copy-start.11 = (f32[96,1280]{1,0:T(8,128)S(1)}, f32[96,1280]{1,0:T(8,128)}, u32[]{:S(2)}) copy-start(f32[96,1280]{1,0:T(8,128)} %get-tuple-element.79) | copy-start | bytes 1474564
  199.7 2.1 %copy-start.16 = (f32[96,1024]{1,0:T(8,128)S(1)}, f32[96,1024]{1,0:T(8,128)}, u32[]{:S(2)}) copy-start(f32[96,1024]{1,0:T(8,128)} %get-tuple-element.71) | copy-start | bytes 1179652
  201.9 1.4 copy-start.4
  201.9 1.4 copy-start.5
  201.9 1.9 copy-start.7
  201.9 2.1 %copy-start.9 = (bf16[192,1280]{1,0:T(8,128)(2,1)S(1)}, bf16[192,1280]{1,0:T(8,128)(2,1)}, u32[]{:S(2)}) copy-start(bf16[192,1280]{1,0:T(8,128)(2,1)} %copy-done.8) | copy-start | bytes 1474564

commit v5 on v4

--- a/solution.py
+++ b/solution.py
@@ -18,8 +18,8 @@
 GROUPS = 4
 OWNERS = 32
 CAPACITY = 32
-UNITS = (10, 10, 8, 8)
-TILE = 2
+UNITS = (12, 8, 8, 8)
+HALVES = ((1, 3), (3, 1))
 MIB = 1024 * 1024
 
 
@@ -39,9 +39,9 @@
     return pl.CostEstimate(flops=flops, bytes_accessed=moved, transcendentals=0)
 
 
-def combine_body(here_ref, target_ref, head_ref, part_ref, own_ref, *refs):
-    out_refs, table_ref = (own_ref,) + refs[:-1], refs[-1]
-    share = own_ref.shape[0]
+def combine_body(here_ref, target_ref, head_ref, part_ref, *refs):
+    table_ref = refs[-1]
+    share = head_ref.shape[1] // GROUPS
     slots = target_ref.shape[1]
     starts = [lax.bitwise_xor(here_ref[0], flip) * share for flip in range(GROUPS)]
 
@@ -53,31 +53,42 @@
             table_ref[pl.ds(flip * share, share), :] = jnp.where(hit, 1.0, 0.0).astype(jnp.bfloat16)
 
     total = jnp.dot(table_ref[...], part_ref[...], preferred_element_type=jnp.float32)
-    for flip, (start, out_ref) in enumerate(zip(starts, out_refs)):
+    blocks = []
+    for flip, start in enumerate(starts):
         head = head_ref[0, pl.ds(pl.multiple_of(start, share), share), :].astype(jnp.float32)
-        block = total[flip * share : (flip + 1) * share, :] + head
-        out_ref[...] = block.astype(out_ref.dtype)
-
-
-def combine(here, target, head_grad, part, start, tile):
+        blocks.append(total[flip * share : (flip + 1) * share, :] + head)
+
+    for side, (one, two) in enumerate(HALVES):
+
+        @pl.when(pl.program_id(0) == side)
+        def _(side=side, one=one, two=two):
+            keep_ref, send_ref = refs[2 * side], refs[2 * side + 1]
+            for at, flip in enumerate((0, two)):
+                keep_ref[pl.ds(at * share, share), :] = blocks[flip]
+            for at, flip in enumerate((one, one ^ two)):
+                send_ref[pl.ds(at * share, share), :] = blocks[flip].astype(jnp.bfloat16)
+
+
+def combine(here, target, head_grad, part, start):
     slots = target.shape[1]
     width = part.shape[1]
     slab_rows = head_grad.shape[1]
-    share = slab_rows // GROUPS
+    tile = width // 2
+    kept = jax.ShapeDtypeStruct((slab_rows // 2, tile), jnp.float32)
+    sent = jax.ShapeDtypeStruct((slab_rows // 2, tile), jnp.bfloat16)
     return pl.pallas_call(
         combine_body,
-        grid=(width // tile,),
-        out_shape=[jax.ShapeDtypeStruct((share, width), jnp.float32)]
-        + [jax.ShapeDtypeStruct((share, width), jnp.bfloat16)] * (GROUPS - 1),
+        grid=(2,),
+        out_shape=[kept, sent] * 2,
         in_specs=[
             whole(pltpu.SMEM),
             pl.BlockSpec((1, slots), lambda i: (0, 0)),
             pl.BlockSpec((1, slab_rows, tile), lambda i: (0, 0, start // tile + i)),
             pl.BlockSpec((slots, tile), lambda i: (0, i)),
         ],
-        out_specs=[pl.BlockSpec((share, tile), lambda i: (0, i))] * GROUPS,
+        out_specs=[pl.BlockSpec((slab_rows // 2, tile), lambda i: (0, 0))] * 4,
         scratch_shapes=[pltpu.VMEM((slab_rows, slots), jnp.bfloat16)],
-        compiler_params=pltpu.CompilerParams(vmem_limit_bytes=16 * MIB),
+        compiler_params=pltpu.CompilerParams(vmem_limit_bytes=24 * MIB),
         cost_estimate=cost(2 * slab_rows * slots * width, (2 * slots + 5 * slab_rows) * width),
     )(here.reshape(1), target, head_grad, part)
 
@@ -163,19 +174,28 @@
     spans = [slice(low, high) for low, high in zip(edges, edges[1:])]
     states, rows, joined, fars, blocks, spots = [], [], [], [], [], []
     arrived, last = (), len(spans) - 1
+    picked = [
+        jnp.dot(dispatch, input_grad[:, span], preferred_element_type=jnp.float32).astype(jnp.bfloat16)
+        for span in spans
+    ]
     for number, span in enumerate(spans):
-        outgoing = jnp.dot(
-            dispatch, input_grad[:, span], preferred_element_type=jnp.float32
-        ).astype(jnp.bfloat16)
+        outgoing = picked[number]
         earlier_work = target if number == 1 else rows[: max(0, number - 1)]
-        outgoing = after(outgoing, arrived, earlier_work, joined[: max(0, number - 1)])
+        outgoing = after(outgoing, arrived, earlier_work)
         arrived = lax.all_to_all(outgoing, "vocab", split_axis=0, concat_axis=0, tiled=True)
-        ready = after(arrived, rows)
-        grad, *pieces = combine(here, target, head_grad, ready, span.start, TILE * unit)
-        for flip, piece in enumerate(pieces, 1):
-            grad = grad + swap_z(piece, flip).astype(jnp.float32)
+        ready = after(arrived, rows, picked[: number + 2])
+        sums = combine(here, target, head_grad, ready, span.start)
+        grads = []
+        for side, (one, two) in enumerate(HALVES):
+            keep, sent = sums[2 * side : 2 * side + 2]
+            half = swap_z(sent, one).astype(jnp.float32)
+            onward = (keep[share:] + half[share:]).astype(jnp.bfloat16)
+            if number == last:
+                onward = after(onward, fars[: number - 1])
+            grads.append(keep[:share] + half[:share] + swap_z(onward, two).astype(jnp.float32))
+        grad = jnp.concatenate(grads, axis=1)
         if 1 <= number < last:
-            grad = after(grad, fars)
+            grad = after(grad, fars[: number - 1], joined)
         states.append(update(grad, master[:, span], moment_one[:, span], moment_two[:, span]))
         block = states[-1][0].astype(jnp.bfloat16)
         rows.append(block)

time: 210 us -> 205 us (0.976)
  waiting for transfers between devices: 94 us -> 89.5 us
  starting transfers between devices: 55.2 us -> 59.6 us
  Pallas kernels: 16.6 us -> 12.7 us
    ppermute x21 -> x25, waiting for transfers between devices: 64.2 us -> 50.1 us  [swap_z(): return lax.ppermute(block, 'dp', [(i, i ^ flip) for i in range(GROUPS)])]
    all_to_all x4, waiting for transfers between devices: 29.8 us -> 39.4 us  [local(): lax.all_to_all(outgoing, 'vocab', split_axis=0, concat_axis=0, tiled=True)]
    ppermute x21 -> x25, starting transfers between devices: 27.7 us -> 35.8 us  [swap_z(): return lax.ppermute(block, 'dp', [(i, i ^ flip) for i in range(GROUPS)])]
    pallas_call x4, Pallas kernels: 14.1 us -> 10.2 us  [combine(): pl.pallas_call(combine_body, grid=(2,), out_shape=[kept, sent] * 2, in_sp...]
    all_to_all x4, starting transfers between devices: 27.5 us -> 23.7 us  [local(): lax.all_to_all(outgoing, 'vocab', split_axis=0, concat_axis=0, tiled=True)]
  transfers between devices with their start and end apart: 25 -> 29, of which waited for: 19 -> 23; matrix products, arithmetic and copies ran while one was open for 14% -> 14% of each run, Pallas kernels for 8% -> 6%
where the time goes in v5:
time: 205 us; the launch traced here: 204 us
  waiting for transfers between devices  89.5 us (44%)
  starting transfers between devices  59.6 us (29%)
  other arithmetic  19.2 us (9%)
  matrix products  16.7 us (8%)
  Pallas kernels  12.7 us (6%)
  local copies, waits for them, and re-layouts  5.43 us (3%)
    ppermute x25, waiting for transfers between devices, swap_z(): return lax.ppermute(block, 'dp', [(i, i ^ flip) for i in range(GROUPS)])  50.1 us
    all_to_all x4, waiting for transfers between devices, local(): lax.all_to_all(outgoing, 'vocab', split_axis=0, concat_axis=0, tiled=True)  39.4 us
    ppermute x25, starting transfers between devices, swap_z(): return lax.ppermute(block, 'dp', [(i, i ^ flip) for i in range(GROUPS)])  35.8 us
    all_to_all x4, starting transfers between devices, local(): lax.all_to_all(outgoing, 'vocab', split_axis=0, concat_axis=0, tiled=True)  23.7 us
    dot_general x4, matrix products, local(): jnp.dot(dispatch, input_grad[:, span], preferred_element_type=jnp.float32)  16.3 us
    pallas_call x4, Pallas kernels, combine(): pl.pallas_call(combine_body, grid=(2,), out_shape=[kept, sent] * 2, in_sp...  10.2 us
    convert_element_type x4, other arithmetic, local(): block = states[-1][0].astype(jnp.bfloat16)  9.66 us
    unnamed x41, local copies, waits for them, and re-layouts  5.31 us
  transfers between devices with their start and end apart: 29, of which 23 were waited for; matrix products, arithmetic and copies ran while one was open for 14% of the time, Pallas kernels for 6%

profile of v5, /device:TPU:0, one launch (start us, length us, event | category | flops | bytes accessed | tf_op | source)
XLA Modules:
  0.0 204.5 jit_solution(15739265592192594656)
XLA Ops:
  0.6 0.5 broadcast.106
  1.1 1.6 reduce.7
  3.1 4.9 %convolution_convert_fusion = bf16[1024,1536]{1,0:T(8,128)(2,1)} fusion(bf16[512,4608]{1,0:T(8,128)(2,1)} %param.7, s32[512]{0:T(512)S(1)} %bitcast.20), kind=kOutput, calls=%fused_computation | convolution fusion | flops 1612709888 | bytes 4720640 | tf_op jit(solution)/shard_map/dot_general | solution.py:178
  7.9 7.5 %all-to-all-start = ((bf16[32,32,1536]{2,1,0:T(8,128)(2,1)}), bf16[32,32,1536]{2,1,0:T(8,128)(2,1)S(1)}, u32[]{:S(2)}, u32[]{:S(2)}) async-start(bf16[32,32,1536]{2,1,0:T(8,128)(2,1)} %bitcast.15), calls=%async_computation | async-start | bytes 6291456 | tf_op jit(solution)/shard_map/all_to_all | solution.py:185
  15.9 0.6 select_reduce_fusion
  16.7 3.8 %fusion.4 = bf16[1024,1024]{1,0:T(8,128)(2,1)} fusion(bf16[512,4608]{1,0:T(8,128)(2,1)} %param.7, s32[512]{0:T(512)S(1)} %bitcast.21), kind=kOutput, calls=%fused_computation.8 | convolution fusion | flops 1075314688 | bytes 3147776 | tf_op jit(solution)/shard_map/dot_general | solution.py:178
  20.5 35.0 %all-to-all-done = bf16[32,32,1536]{2,1,0:T(8,128)(2,1)S(1)} async-done(((bf16[32,32,1536]{2,1,0:T(8,128)(2,1)}), bf16[32,32,1536]{2,1,0:T(8,128)(2,1)S(1)}, u32[]{:S(2)}, u32[]{:S(2)}) %all-to-all-start) | async-done | bytes 3145760 | tf_op jit(solution)/shard_map/all_to_all | solution.py:185
  55.4 1.7 copy-done.1
  57.1 5.2 %all-to-all-start.1 = ((bf16[32,32,1024]{2,1,0:T(8,128)(2,1)}), bf16[32,32,1024]{2,1,0:T(8,128)(2,1)}, u32[]{:S(2)}, u32[]{:S(2)}) async-start(bf16[32,32,1024]{2,1,0:T(8,128)(2,1)} %bitcast.18), calls=%async_computation.1 | async-start | bytes 4194304 | tf_op jit(solution)/shard_map/all_to_all | solution.py:185
  62.3 1.9 copy-done.2
  64.2 2.2 %shard_map.102 = (f32[192,768]{1,0:T(8,128)S(1)}, bf16[192,768]{1,0:T(8,128)(2,1)S(1)}, f32[192,768]{1,0:T(8,128)S(1)}, bf16[192,768]{1,0:T(8,128)(2,1)S(1)}) custom-call(s32[1]{0:T(128)} %bitcast.here_ref, s32[1,1024]{1,0:T(1,128)S(1)} %sub.19.target_ref, bf16[1,384,4608]{2,1,0:T(8,128)(2,1)S(1)} %copy-done, bf16[1024,1536]{1,0:T(8,128)(2,1)S(1)} %bitcast.14), custom_call_target="tpu_custom_call" | custom-call | flops 1207959552 | bytes 6094848 | tf_op jit(solution)/shard_map/pallas_call | solution.py:79
  66.4 2.0 collective-permute-start
  68.4 2.5 %collective-permute-start.2 = (bf16[192,768]{1,0:T(8,128)(2,1)S(1)}, bf16[192,768]{1,0:T(8,128)(2,1)S(1)}, u32[]{:S(2)}, u32[]{:S(2)}) collective-permute-start(bf16[192,768]{1,0:T(8,128)(2,1)S(1)} %get-tuple-element.41), channel_id=1, source_target_pairs={{0,96},{32,64},{64,32},{96,0},{1,97},{33,65},{65,33},{97,1},{2,98}... | collective-permute-start | bytes 884744 | tf_op jit(solution)/shard_map/ppermute | solution.py:31
  70.9 3.8 %fusion.5 = bf16[1024,1024]{1,0:T(8,128)(2,1)} fusion(bf16[512,4608]{1,0:T(8,128)(2,1)} %param.7, s32[512]{0:T(512)S(1)} %bitcast.22), kind=kOutput, calls=%fused_computation.9 | convolution fusion | flops 1075314688 | bytes 3147776 | tf_op jit(solution)/shard_map/dot_general | solution.py:178
  74.7 1.0 collective-permute-done
  75.8 3.9 %collective-permute-start.1 = (bf16[96,768]{1,0:T(8,128)(2,1)S(1)}, bf16[96,768]{1,0:T(8,128)(2,1)S(1)}, u32[]{:S(2)}, u32[]{:S(2)}) collective-permute-start(bf16[96,768]{1,0:T(8,128)(2,1)S(1)} %fusion.22), channel_id=1, source_target_pairs={{0,96},{32,64},{64,32},{96,0},{1,97},{33,65},{65,33},{97,1},{2,98}... | collective-permute-start | bytes 442376 | tf_op jit(solution)/shard_map/ppermute | solution.py:31
  79.9 3.3 %collective-permute-done.1 = bf16[96,768]{1,0:T(8,128)(2,1)S(1)} collective-permute-done((bf16[96,768]{1,0:T(8,128)(2,1)S(1)}, bf16[96,768]{1,0:T(8,128)(2,1)S(1)}, u32[]{:S(2)}, u32[]{:S(2)}) %collective-permute-start.1) | collective-permute-done | bytes 147488 | tf_op jit(solution)/shard_map/ppermute | solution.py:31
  83.3 1.8 collective-permute-done.3
  85.1 3.0 %fusion.43 = (bf16[96,1536]{1,0:T(8,128)(2,1)}, f32[96,1536]{1,0:T(8,128)}, f32[96,1536]{1,0:T(8,128)}, f32[96,1536]{1,0:T(8,128)}) fusion(f32[96,4608]{1,0:T(8,128)} %param.11, f32[96,768]{1,0:T(8,128)S(1)} %fusion.21, f32[96,768]{1,0:T(8,128)S(1)} %fusion.23, f32[96,4608]{1,0:T(8,128)} %param.12, f32[96,4608]{1,0:T(8,128)} %param.13), kind=kLoop, calls=%fused_computation.91 | loop fusion | flops 2506752 | bytes 4423680 | tf_op jit(solution)/shard_map/convert_element_type | solution.py:200
  88.1 3.1 %all-to-all-done.1 = bf16[32,32,1024]{2,1,0:T(8,128)(2,1)} async-done(((bf16[32,32,1024]{2,1,0:T(8,128)(2,1)}), bf16[32,32,1024]{2,1,0:T(8,128)(2,1)}, u32[]{:S(2)}, u32[]{:S(2)}) %all-to-all-start.1) | async-done | bytes 2097184 | tf_op jit(solution)/shard_map/all_to_all | solution.py:185
  91.2 4.8 %all-to-all-start.2 = ((bf16[32,32,1024]{2,1,0:T(8,128)(2,1)}), bf16[32,32,1024]{2,1,0:T(8,128)(2,1)}, u32[]{:S(2)}, u32[]{:S(2)}) async-start(bf16[32,32,1024]{2,1,0:T(8,128)(2,1)} %bitcast.17), calls=%async_computation.2 | async-start | bytes 4194304 | tf_op jit(solution)/shard_map/all_to_all | solution.py:185
  96.0 4.1 %collective-permute-start.8 = (bf16[96,1536]{1,0:T(8,128)(2,1)}, bf16[96,1536]{1,0:T(8,128)(2,1)S(1)}, u32[]{:S(2)}, u32[]{:S(2)}) collective-permute-start(bf16[96,1536]{1,0:T(8,128)(2,1)} %get-tuple-element.82), channel_id=1, source_target_pairs={{0,96},{32,64},{64,32},{96,0},{1,97},{33,65},{65,33},{97,1},{2,98}... | collective-permute-start | bytes 884744 | tf_op jit(solution)/shard_map/ppermute | solution.py:31
  100.1 3.8 %fusion.6 = bf16[1024,1024]{1,0:T(8,128)(2,1)} fusion(bf16[512,4608]{1,0:T(8,128)(2,1)} %param.7, s32[512]{0:T(512)S(1)} %bitcast.23), kind=kOutput, calls=%fused_computation.10 | convolution fusion | flops 1075314688 | bytes 3147776 | tf_op jit(solution)/shard_map/dot_general | solution.py:178
  103.9 2.7 %shard_map.103 = (f32[192,512]{1,0:T(8,128)S(1)}, bf16[192,512]{1,0:T(8,128)(2,1)S(1)}, f32[192,512]{1,0:T(8,128)S(1)}, bf16[192,512]{1,0:T(8,128)(2,1)S(1)}) custom-call(s32[1]{0:T(128)} %bitcast.here_ref, s32[1,1024]{1,0:T(1,128)S(1)} %sub.19.target_ref, bf16[1,384,4608]{2,1,0:T(8,128)(2,1)S(1)} %copy-done, bf16[1024,1024]{1,0:T(8,128)(2,1)} %bitcast.7.part_ref), custom_call_target="tpu_custom_call" | custom-call | flops 805306368 | bytes 4063232 | tf_op jit(solution)/shard_map/pallas_call | solution.py:79
  106.9 0.7 collective-permute-done.8
  107.6 0.9 pad_maximum_fusion.4.refs_0_
  108.4 3.0 %collective-permute-start.6 = (bf16[192,512]{1,0:T(8,128)(2,1)S(1)}, bf16[192,512]{1,0:T(8,128)(2,1)S(1)}, u32[]{:S(2)}, u32[]{:S(2)}) collective-permute-start(bf16[192,512]{1,0:T(8,128)(2,1)S(1)} %get-tuple-element.47), channel_id=1, source_target_pairs={{0,96},{32,64},{64,32},{96,0},{1,97},{33,65},{65,33},{97,1},{2,98}... | collective-permute-start | bytes 589832 | tf_op jit(solution)/shard_map/ppermute | solution.py:31
  111.4 2.1 %collective-permute-done.4 = bf16[192,512]{1,0:T(8,128)(2,1)S(1)} collective-permute-done((bf16[192,512]{1,0:T(8,128)(2,1)S(1)}, bf16[192,512]{1,0:T(8,128)(2,1)S(1)}, u32[]{:S(2)}, u32[]{:S(2)}) %collective-permute-start.4) | collective-permute-done | bytes 196640 | tf_op jit(solution)/shard_map/ppermute | solution.py:31
  113.9 2.2 %collective-permute-done.6 = bf16[192,512]{1,0:T(8,128)(2,1)S(1)} collective-permute-done((bf16[192,512]{1,0:T(8,128)(2,1)S(1)}, bf16[192,512]{1,0:T(8,128)(2,1)S(1)}, u32[]{:S(2)}, u32[]{:S(2)}) %collective-permute-start.6) | collective-permute-done | bytes 196640 | tf_op jit(solution)/shard_map/ppermute | solution.py:31
  116.4 3.1 %collective-permute-done.5 = bf16[96,512]{1,0:T(8,128)(2,1)S(1)} collective-permute-done((bf16[96,512]{1,0:T(8,128)(2,1)S(1)}, bf16[96,512]{1,0:T(8,128)(2,1)S(1)}, u32[]{:S(2)}, u32[]{:S(2)}) %collective-permute-start.5) | collective-permute-done | bytes 98336 | tf_op jit(solution)/shard_map/ppermute | solution.py:31
  119.5 1.4 collective-permute-done.7
  121.0 2.6 %fusion.41 = (bf16[96,1024]{1,0:T(8,128)(2,1)}, f32[96,1024]{1,0:T(8,128)}, f32[96,1024]{1,0:T(8,128)}, f32[96,1024]{1,0:T(8,128)}) fusion(f32[96,4608]{1,0:T(8,128)} %param.11, f32[96,1024]{1,0:T(8,128)S(1)} %pad_maximum_fusion.5, f32[96,4608]{1,0:T(8,128)} %param.12, f32[96,4608]{1,0:T(8,128)} %param.13), kind=kLoop, calls=%fused_computation.90 | loop fusion | flops 1572864 | bytes 2949120 | tf_op jit(solution)/shard_map/convert_element_type | solution.py:200
  123.5 1.3 all-to-all-done.2
  124.8 6.2 %all-to-all-start.3 = ((bf16[32,32,1024]{2,1,0:T(8,128)(2,1)}), bf16[32,32,1024]{2,1,0:T(8,128)(2,1)}, u32[]{:S(2)}, u32[]{:S(2)}) async-start(bf16[32,32,1024]{2,1,0:T(8,128)(2,1)} %bitcast.16), calls=%async_computation.3 | async-start | bytes 4194304 | tf_op jit(solution)/shard_map/all_to_all | solution.py:185
  131.1 3.7 %collective-permute-start.14 = (bf16[96,1024]{1,0:T(8,128)(2,1)}, bf16[96,1024]{1,0:T(8,128)(2,1)S(1)}, u32[]{:S(2)}, u32[]{:S(2)}) collective-permute-start(bf16[96,1024]{1,0:T(8,128)(2,1)} %get-tuple-element.78), channel_id=1, source_target_pairs={{0,96},{32,64},{64,32},{96,0},{1,97},{33,65},{65,33},{97,1},{2,98}... | collective-permute-start | bytes 589832 | tf_op jit(solution)/shard_map/ppermute | solution.py:31
  134.8 2.7 %shard_map.104 = (f32[192,512]{1,0:T(8,128)S(1)}, bf16[192,512]{1,0:T(8,128)(2,1)S(1)}, f32[192,512]{1,0:T(8,128)S(1)}, bf16[192,512]{1,0:T(8,128)(2,1)S(1)}) custom-call(s32[1]{0:T(128)} %bitcast.here_ref, s32[1,1024]{1,0:T(1,128)S(1)} %sub.19.target_ref, bf16[1,384,4608]{2,1,0:T(8,128)(2,1)S(1)} %copy-done, bf16[1024,1024]{1,0:T(8,128)(2,1)} %bitcast.9.part_ref), custom_call_target="tpu_custom_call" | custom-call | flops 805306368 | bytes 4063232 | tf_op jit(solution)/shard_map/pallas_call | solution.py:79
  137.5 2.0 collective-permute-start.13
  139.6 0.7 collective-permute-done.14
  140.3 0.8 pad_maximum_fusion.7.refs_2_
  141.1 3.0 %collective-permute-start.11 = (bf16[192,512]{1,0:T(8,128)(2,1)S(1)}, bf16[192,512]{1,0:T(8,128)(2,1)S(1)}, u32[]{:S(2)}, u32[]{:S(2)}) collective-permute-start(bf16[192,512]{1,0:T(8,128)(2,1)S(1)} %get-tuple-element.54), channel_id=1, source_target_pairs={{0,96},{32,64},{64,32},{96,0},{1,97},{33,65},{65,33},{97,1},{2,98}... | collective-permute-start | bytes 589832 | tf_op jit(solution)/shard_map/ppermute | solution.py:31
  144.0 1.3 collective-permute-done.9
  145.5 4.4 %collective-permute-done.11 = bf16[192,512]{1,0:T(8,128)(2,1)S(1)} collective-permute-done((bf16[192,512]{1,0:T(8,128)(2,1)S(1)}, bf16[192,512]{1,0:T(8,128)(2,1)S(1)}, u32[]{:S(2)}, u32[]{:S(2)}) %collective-permute-start.11) | collective-permute-done | bytes 196640 | tf_op jit(solution)/shard_map/ppermute | solution.py:31
  150.1 1.2 collective-permute-done.10
  151.3 7.7 %collective-permute-done.12 = bf16[96,512]{1,0:T(8,128)(2,1)S(1)} collective-permute-done((bf16[96,512]{1,0:T(8,128)(2,1)S(1)}, bf16[96,512]{1,0:T(8,128)(2,1)S(1)}, u32[]{:S(2)}, u32[]{:S(2)}) %collective-permute-start.12) | collective-permute-done | bytes 98336 | tf_op jit(solution)/shard_map/ppermute | solution.py:31
  159.1 0.8 copy-done.6
  159.9 2.5 %fusion.39 = (bf16[96,1024]{1,0:T(8,128)(2,1)}, f32[96,1024]{1,0:T(8,128)}, f32[96,1024]{1,0:T(8,128)}, f32[96,1024]{1,0:T(8,128)}) fusion(f32[96,4608]{1,0:T(8,128)} %param.11, f32[96,1024]{1,0:T(8,128)S(1)} %pad_maximum_fusion.6, f32[96,4608]{1,0:T(8,128)} %param.12, f32[96,4608]{1,0:T(8,128)} %param.13), kind=kLoop, calls=%fused_computation.89 | loop fusion | flops 1572864 | bytes 2949120 | tf_op jit(solution)/shard_map/convert_element_type | solution.py:200
  162.8 2.7 %shard_map.105 = (f32[192,512]{1,0:T(8,128)S(1)}, bf16[192,512]{1,0:T(8,128)(2,1)S(1)}, f32[192,512]{1,0:T(8,128)S(1)}, bf16[192,512]{1,0:T(8,128)(2,1)S(1)}) custom-call(s32[1]{0:T(128)} %bitcast.here_ref, s32[1,1024]{1,0:T(1,128)S(1)} %sub.19.target_ref, bf16[1,384,4608]{2,1,0:T(8,128)(2,1)S(1)} %copy-done, bf16[1024,1024]{1,0:T(8,128)(2,1)} %bitcast.11.part_ref), custom_call_target="tpu_custom_call" | custom-call | flops 805306368 | bytes 4063232 | tf_op jit(solution)/shard_map/pallas_call | solution.py:79
  165.7 2.0 collective-permute-start.16
  167.7 2.3 %collective-permute-done.20 = bf16[96,1024]{1,0:T(8,128)(2,1)} collective-permute-done((bf16[96,1024]{1,0:T(8,128)(2,1)}, bf16[96,1024]{1,0:T(8,128)(2,1)}, u32[]{:S(2)}, u32[]{:S(2)}) %collective-permute-start.20) | collective-permute-done | bytes 196640 | tf_op jit(solution)/shard_map/ppermute | solution.py:31
  169.9 1.0 pad_maximum_fusion.9.refs_4_
  171.1 0.8 collective-permute-start.18
  171.9 1.6 collective-permute-done.15
  173.5 8.3 %collective-permute-done.16.refs_3_ = bf16[192,1024]{1,0:T(8,128)(2,1)S(1)} collective-permute-done((bf16[192,1024]{1,0:T(8,128)(2,1)S(1)}, bf16[192,1024]{1,0:T(8,128)(2,1)S(1)}, u32[]{:S(2)}, u32[]{:S(2)}) %collective-permute-start.16) | collective-permute-done | bytes 393248 | tf_op jit(solution)/shard_map/ppermute | solution.py:31
  181.9 2.8 %collective-permute-start.17 = (bf16[96,512]{1,0:T(8,128)(2,1)S(1)}, bf16[96,512]{1,0:T(8,128)(2,1)S(1)}, u32[]{:S(2)}, u32[]{:S(2)}) collective-permute-start(bf16[96,512]{1,0:T(8,128)(2,1)S(1)} %fusion.26), channel_id=1, source_target_pairs={{0,96},{32,64},{64,32},{96,0},{1,97},{33,65},{65,33},{97,1},{2,98}... | collective-permute-start | bytes 294920 | tf_op jit(solution)/shard_map/ppermute | solution.py:31
  184.9 2.8 %collective-permute-done.17 = bf16[96,512]{1,0:T(8,128)(2,1)S(1)} collective-permute-done((bf16[96,512]{1,0:T(8,128)(2,1)S(1)}, bf16[96,512]{1,0:T(8,128)(2,1)S(1)}, u32[]{:S(2)}, u32[]{:S(2)}) %collective-permute-start.17) | collective-permute-done | bytes 98336 | tf_op jit(solution)/shard_map/ppermute | solution.py:31
  187.8 2.8 %collective-permute-done.19 = bf16[96,512]{1,0:T(8,128)(2,1)S(1)} collective-permute-done((bf16[96,512]{1,0:T(8,128)(2,1)S(1)}, bf16[96,512]{1,0:T(8,128)(2,1)S(1)}, u32[]{:S(2)}, u32[]{:S(2)}) %collective-permute-start.19) | collective-permute-done | bytes 98336 | tf_op jit(solution)/shard_map/ppermute | solution.py:31
  190.6 1.6 fusion.37
  192.2 2.6 %collective-permute-start.24 = (bf16[96,1024]{1,0:T(8,128)(2,1)S(1)}, bf16[96,1024]{1,0:T(8,128)(2,1)S(1)}, u32[]{:S(2)}, u32[]{:S(2)}) collective-permute-start(bf16[96,1024]{1,0:T(8,128)(2,1)S(1)} %get-tuple-element.70.refs_1_), channel_id=1, source_target_pairs={{0,96},{32,64},{64,32},{96,0},{1,97},{33,65},{65,33},{97,1},{2,98}... | collective-permute-start | bytes 589832 | tf_op jit(solution)/shard_map/ppermute | solution.py:31
  194.8 1.6 collective-permute-start.22
  196.4 2.1 %pad_maximum_fusion = (f32[96,4608]{1,0:T(8,128)}, f32[96,4608]{1,0:T(8,128)}) fusion(f32[96,1024]{1,0:T(8,128)S(1)} %get-tuple-element.71, f32[96,1024]{1,0:T(8,128)S(1)} %copy-done.15, f32[96,1024]{1,0:T(8,128)S(1)} %copy-done.12, f32[96,1536]{1,0:T(8,128)S(1)} %copy-done.8, f32[96,1024]{1,0:T(8,128)S(1)} %get-tuple-element.72, ...), kind=kLoop, calls=%fused_computation.11 | loop fusion | flops 2654208 | bytes 7077888 | tf_op jit(solution)/shard_map/concatenate | solution.py:219
  198.5 1.3 pad_maximum_fusion.2
  200.2 1.6 shard_map.106.refs_0_
  201.9 1.1 collective-permute-done.23.refs_3_
  203.4 0.9 shard_map.107
  (93 shorter events, 4.5 us)
Async XLA Ops:
  7.9 7.5 %copy-start.19 = (s32[16384,1]{0,1:T(1,128)S(1)}, s32[16384,1]{0,1:T(1,128)}, u32[]{:S(2)}) copy-start(s32[16384,1]{0,1:T(1,128)} %param.9) | copy-start | bytes 196612
  7.9 47.5 %all-to-all-start = ((bf16[32,32,1536]{2,1,0:T(8,128)(2,1)}), bf16[32,32,1536]{2,1,0:T(8,128)(2,1)S(1)}, u32[]{:S(2)}, u32[]{:S(2)}) async-start(bf16[32,32,1536]{2,1,0:T(8,128)(2,1)} %bitcast.15), calls=%async_computation | async-start | bytes 6291456 | tf_op jit(solution)/shard_map/all_to_all | solution.py:185
  55.4 1.7 copy-start.1
  57.1 5.2 %copy-start = (bf16[1,384,4608]{2,1,0:T(8,128)(2,1)S(1)}, bf16[1,384,4608]{2,1,0:T(8,128)(2,1)}, u32[]{:S(2)}) copy-start(bf16[1,384,4608]{2,1,0:T(8,128)(2,1)} %head_ref.7) | copy-start | bytes 10616836
  57.1 34.1 %all-to-all-start.1 = ((bf16[32,32,1024]{2,1,0:T(8,128)(2,1)}), bf16[32,32,1024]{2,1,0:T(8,128)(2,1)}, u32[]{:S(2)}, u32[]{:S(2)}) async-start(bf16[32,32,1024]{2,1,0:T(8,128)(2,1)} %bitcast.18), calls=%async_computation.1 | async-start | bytes 4194304 | tf_op jit(solution)/shard_map/all_to_all | solution.py:185
  62.3 1.9 copy-start.2
  66.4 9.4 %collective-permute-start = (bf16[192,768]{1,0:T(8,128)(2,1)S(1)}, bf16[192,768]{1,0:T(8,128)(2,1)S(1)}, u32[]{:S(2)}, u32[]{:S(2)}) collective-permute-start(bf16[192,768]{1,0:T(8,128)(2,1)S(1)} %get-tuple-element.39), channel_id=1, source_target_pairs={{0,32},{32,0},{64,96},{96,64},{1,33},{33,1},{65,97},{97,65},{2,34}... | collective-permute-start | bytes 884744 | tf_op jit(solution)/shard_map/ppermute | solution.py:31
  68.4 11.4 %collective-permute-start.2 = (bf16[192,768]{1,0:T(8,128)(2,1)S(1)}, bf16[192,768]{1,0:T(8,128)(2,1)S(1)}, u32[]{:S(2)}, u32[]{:S(2)}) collective-permute-start(bf16[192,768]{1,0:T(8,128)(2,1)S(1)} %get-tuple-element.41), channel_id=1, source_target_pairs={{0,96},{32,64},{64,32},{96,0},{1,97},{33,65},{65,33},{97,1},{2,98}... | collective-permute-start | bytes 884744 | tf_op jit(solution)/shard_map/ppermute | solution.py:31
  75.8 7.4 %collective-permute-start.1 = (bf16[96,768]{1,0:T(8,128)(2,1)S(1)}, bf16[96,768]{1,0:T(8,128)(2,1)S(1)}, u32[]{:S(2)}, u32[]{:S(2)}) collective-permute-start(bf16[96,768]{1,0:T(8,128)(2,1)S(1)} %fusion.22), channel_id=1, source_target_pairs={{0,96},{32,64},{64,32},{96,0},{1,97},{33,65},{65,33},{97,1},{2,98}... | collective-permute-start | bytes 442376 | tf_op jit(solution)/shard_map/ppermute | solution.py:31
  79.9 5.2 %collective-permute-start.3 = (bf16[96,768]{1,0:T(8,128)(2,1)S(1)}, bf16[96,768]{1,0:T(8,128)(2,1)S(1)}, u32[]{:S(2)}, u32[]{:S(2)}) collective-permute-start(bf16[96,768]{1,0:T(8,128)(2,1)S(1)} %fusion.20), channel_id=1, source_target_pairs={{0,32},{32,0},{64,96},{96,64},{1,33},{33,1},{65,97},{97,65},{2,34}... | collective-permute-start | bytes 442376 | tf_op jit(solution)/shard_map/ppermute | solution.py:31
  91.2 33.6 %all-to-all-start.2 = ((bf16[32,32,1024]{2,1,0:T(8,128)(2,1)}), bf16[32,32,1024]{2,1,0:T(8,128)(2,1)}, u32[]{:S(2)}, u32[]{:S(2)}) async-start(bf16[32,32,1024]{2,1,0:T(8,128)(2,1)} %bitcast.17), calls=%async_computation.2 | async-start | bytes 4194304 | tf_op jit(solution)/shard_map/all_to_all | solution.py:185
  96.0 11.6 %collective-permute-start.8 = (bf16[96,1536]{1,0:T(8,128)(2,1)}, bf16[96,1536]{1,0:T(8,128)(2,1)S(1)}, u32[]{:S(2)}, u32[]{:S(2)}) collective-permute-start(bf16[96,1536]{1,0:T(8,128)(2,1)} %get-tuple-element.82), channel_id=1, source_target_pairs={{0,96},{32,64},{64,32},{96,0},{1,97},{33,65},{65,33},{97,1},{2,98}... | collective-permute-start | bytes 884744 | tf_op jit(solution)/shard_map/ppermute | solution.py:31
  103.9 3.7 %copy-start.17 = (bf16[96,1536]{1,0:T(8,128)(2,1)S(1)}, bf16[96,1536]{1,0:T(8,128)(2,1)}, u32[]{:S(2)}) copy-start(bf16[96,1536]{1,0:T(8,128)(2,1)} %get-tuple-element.82) | copy-start | bytes 884740
  106.6 6.9 %collective-permute-start.4 = (bf16[192,512]{1,0:T(8,128)(2,1)S(1)}, bf16[192,512]{1,0:T(8,128)(2,1)S(1)}, u32[]{:S(2)}, u32[]{:S(2)}) collective-permute-start(bf16[192,512]{1,0:T(8,128)(2,1)S(1)} %get-tuple-element.45), channel_id=1, source_target_pairs={{0,32},{32,0},{64,96},{96,64},{1,33},{33,1},{65,97},{97,65},{2,34}... | collective-permute-start | bytes 589832 | tf_op jit(solution)/shard_map/ppermute | solution.py:31
  108.4 7.7 %collective-permute-start.6 = (bf16[192,512]{1,0:T(8,128)(2,1)S(1)}, bf16[192,512]{1,0:T(8,128)(2,1)S(1)}, u32[]{:S(2)}, u32[]{:S(2)}) collective-permute-start(bf16[192,512]{1,0:T(8,128)(2,1)S(1)} %get-tuple-element.47), channel_id=1, source_target_pairs={{0,96},{32,64},{64,32},{96,0},{1,97},{33,65},{65,33},{97,1},{2,98}... | collective-permute-start | bytes 589832 | tf_op jit(solution)/shard_map/ppermute | solution.py:31
  113.5 5.9 %collective-permute-start.5 = (bf16[96,512]{1,0:T(8,128)(2,1)S(1)}, bf16[96,512]{1,0:T(8,128)(2,1)S(1)}, u32[]{:S(2)}, u32[]{:S(2)}) collective-permute-start(bf16[96,512]{1,0:T(8,128)(2,1)S(1)} %fusion.34), channel_id=1, source_target_pairs={{0,96},{32,64},{64,32},{96,0},{1,97},{33,65},{65,33},{97,1},{2,98}... | collective-permute-start | bytes 294920 | tf_op jit(solution)/shard_map/ppermute | solution.py:31
  116.2 4.7 %collective-permute-start.7 = (bf16[96,512]{1,0:T(8,128)(2,1)S(1)}, bf16[96,512]{1,0:T(8,128)(2,1)S(1)}, u32[]{:S(2)}, u32[]{:S(2)}) collective-permute-start(bf16[96,512]{1,0:T(8,128)(2,1)S(1)} %fusion.32), channel_id=1, source_target_pairs={{0,32},{32,0},{64,96},{96,64},{1,33},{33,1},{65,97},{97,65},{2,34}... | collective-permute-start | bytes 294920 | tf_op jit(solution)/shard_map/ppermute | solution.py:31
  124.8 38.0 %all-to-all-start.3 = ((bf16[32,32,1024]{2,1,0:T(8,128)(2,1)}), bf16[32,32,1024]{2,1,0:T(8,128)(2,1)}, u32[]{:S(2)}, u32[]{:S(2)}) async-start(bf16[32,32,1024]{2,1,0:T(8,128)(2,1)} %bitcast.16), calls=%async_computation.3 | async-start | bytes 4194304 | tf_op jit(solution)/shard_map/all_to_all | solution.py:185
  131.1 6.4 %copy-start.3 = (bf16[192,1536]{1,0:T(8,128)(2,1)S(1)}, bf16[192,1536]{1,0:T(8,128)(2,1)}, u32[]{:S(2)}) copy-start(bf16[192,1536]{1,0:T(8,128)(2,1)} %pad_maximum_fusion.4.refs_0_) | copy-start | bytes 1769476
  131.1 9.2 %copy-start.18 = (bf16[96,1024]{1,0:T(8,128)(2,1)S(1)}, bf16[96,1024]{1,0:T(8,128)(2,1)}, u32[]{:S(2)}) copy-start(bf16[96,1024]{1,0:T(8,128)(2,1)} %get-tuple-element.78) | copy-start | bytes 589828
  131.1 9.1 %collective-permute-start.14 = (bf16[96,1024]{1,0:T(8,128)(2,1)}, bf16[96,1024]{1,0:T(8,128)(2,1)S(1)}, u32[]{:S(2)}, u32[]{:S(2)}) collective-permute-start(bf16[96,1024]{1,0:T(8,128)(2,1)} %get-tuple-element.78), channel_id=1, source_target_pairs={{0,96},{32,64},{64,32},{96,0},{1,97},{33,65},{65,33},{97,1},{2,98}... | collective-permute-start | bytes 589832 | tf_op jit(solution)/shard_map/ppermute | solution.py:31
  137.4 7.9 %collective-permute-start.9 = (bf16[192,512]{1,0:T(8,128)(2,1)S(1)}, bf16[192,512]{1,0:T(8,128)(2,1)S(1)}, u32[]{:S(2)}, u32[]{:S(2)}) collective-permute-start(bf16[192,512]{1,0:T(8,128)(2,1)S(1)} %get-tuple-element.52), channel_id=1, source_target_pairs={{0,32},{32,0},{64,96},{96,64},{1,33},{33,1},{65,97},{97,65},{2,34}... | collective-permute-start | bytes 589832 | tf_op jit(solution)/shard_map/ppermute | solution.py:31
  137.5 21.5 %collective-permute-start.13 = (bf16[192,1536]{1,0:T(8,128)(2,1)S(1)}, bf16[192,1536]{1,0:T(8,128)(2,1)S(1)}, u32[]{:S(2)}, u32[]{:S(2)}) collective-permute-start(bf16[192,1536]{1,0:T(8,128)(2,1)S(1)} %copy-done.3), channel_id=1, source_target_pairs={{0,32},{32,0},{64,96},{96,64},{1,33},{33,1},{65,97},{97,65},{2,34}... | collective-permute-start | bytes 1769480 | tf_op jit(solution)/shard_map/ppermute | solution.py:31
  141.1 8.9 %collective-permute-start.11 = (bf16[192,512]{1,0:T(8,128)(2,1)S(1)}, bf16[192,512]{1,0:T(8,128)(2,1)S(1)}, u32[]{:S(2)}, u32[]{:S(2)}) collective-permute-start(bf16[192,512]{1,0:T(8,128)(2,1)S(1)} %get-tuple-element.54), channel_id=1, source_target_pairs={{0,96},{32,64},{64,32},{96,0},{1,97},{33,65},{65,33},{97,1},{2,98}... | collective-permute-start | bytes 589832 | tf_op jit(solution)/shard_map/ppermute | solution.py:31
  145.4 5.9 %collective-permute-start.10 = (bf16[96,512]{1,0:T(8,128)(2,1)S(1)}, bf16[96,512]{1,0:T(8,128)(2,1)S(1)}, u32[]{:S(2)}, u32[]{:S(2)}) collective-permute-start(bf16[96,512]{1,0:T(8,128)(2,1)S(1)} %fusion.30), channel_id=1, source_target_pairs={{0,96},{32,64},{64,32},{96,0},{1,97},{33,65},{65,33},{97,1},{2,98}... | collective-permute-start | bytes 294920 | tf_op jit(solution)/shard_map/ppermute | solution.py:31
  150.0 9.0 %collective-permute-start.12 = (bf16[96,512]{1,0:T(8,128)(2,1)S(1)}, bf16[96,512]{1,0:T(8,128)(2,1)S(1)}, u32[]{:S(2)}, u32[]{:S(2)}) collective-permute-start(bf16[96,512]{1,0:T(8,128)(2,1)S(1)} %fusion.28), channel_id=1, source_target_pairs={{0,32},{32,0},{64,96},{96,64},{1,33},{33,1},{65,97},{97,65},{2,34}... | collective-permute-start | bytes 294920 | tf_op jit(solution)/shard_map/ppermute | solution.py:31
  159.1 0.8 copy-start.6
  162.4 7.5 %collective-permute-start.20 = (bf16[96,1024]{1,0:T(8,128)(2,1)}, bf16[96,1024]{1,0:T(8,128)(2,1)}, u32[]{:S(2)}, u32[]{:S(2)}) collective-permute-start(bf16[96,1024]{1,0:T(8,128)(2,1)} %get-tuple-element.74), channel_id=1, source_target_pairs={{0,96},{32,64},{64,32},{96,0},{1,97},{33,65},{65,33},{97,1},{2,98}... | collective-permute-start | bytes 589832 | tf_op jit(solution)/shard_map/ppermute | solution.py:31
  162.8 2.8 %copy-start.5 = (bf16[192,1024]{1,0:T(8,128)(2,1)S(1)}, bf16[192,1024]{1,0:T(8,128)(2,1)}, u32[]{:S(2)}) copy-start(bf16[192,1024]{1,0:T(8,128)(2,1)} %pad_maximum_fusion.7.refs_2_) | copy-start | bytes 1179652
  165.6 7.9 %collective-permute-start.15 = (bf16[192,512]{1,0:T(8,128)(2,1)S(1)}, bf16[192,512]{1,0:T(8,128)(2,1)S(1)}, u32[]{:S(2)}, u32[]{:S(2)}) collective-permute-start(bf16[192,512]{1,0:T(8,128)(2,1)S(1)} %get-tuple-element.59), channel_id=1, source_target_pairs={{0,32},{32,0},{64,96},{96,64},{1,33},{33,1},{65,97},{97,65},{2,34}... | collective-permute-start | bytes 589832 | tf_op jit(solution)/shard_map/ppermute | solution.py:31
  165.7 16.2 %collective-permute-start.16 = (bf16[192,1024]{1,0:T(8,128)(2,1)S(1)}, bf16[192,1024]{1,0:T(8,128)(2,1)S(1)}, u32[]{:S(2)}, u32[]{:S(2)}) collective-permute-start(bf16[192,1024]{1,0:T(8,128)(2,1)S(1)} %copy-done.5), channel_id=1, source_target_pairs={{0,32},{32,0},{64,96},{96,64},{1,33},{33,1},{65,97},{97,65},{2,34}... | collective-permute-start | bytes 1179656 | tf_op jit(solution)/shard_map/ppermute | solution.py:31
  171.0 28.9 %collective-permute-start.21 = (bf16[192,1024]{1,0:T(8,128)(2,1)S(1)}, bf16[192,1024]{1,0:T(8,128)(2,1)S(1)}, u32[]{:S(2)}, u32[]{:S(2)}) collective-permute-start(bf16[192,1024]{1,0:T(8,128)(2,1)S(1)} %pad_maximum_fusion.9.refs_4_), channel_id=1, source_target_pairs={{0,32},{32,0},{64,96},{96,64},{1,33},{33,1},{65,97},{97,65},{2,34}... | collective-permute-start | bytes 1179656 | tf_op jit(solution)/shard_map/ppermute | solution.py:31
  171.1 13.7 %collective-permute-start.18 = (bf16[192,512]{1,0:T(8,128)(2,1)S(1)}, bf16[192,512]{1,0:T(8,128)(2,1)S(1)}, u32[]{:S(2)}, u32[]{:S(2)}) collective-permute-start(bf16[192,512]{1,0:T(8,128)(2,1)S(1)} %get-tuple-element.62), channel_id=1, source_target_pairs={{0,96},{32,64},{64,32},{96,0},{1,97},{33,65},{65,33},{97,1},{2,98}... | collective-permute-start | bytes 589832 | tf_op jit(solution)/shard_map/ppermute | solution.py:31
  181.9 5.8 %collective-permute-start.17 = (bf16[96,512]{1,0:T(8,128)(2,1)S(1)}, bf16[96,512]{1,0:T(8,128)(2,1)S(1)}, u32[]{:S(2)}, u32[]{:S(2)}) collective-permute-start(bf16[96,512]{1,0:T(8,128)(2,1)S(1)} %fusion.26), channel_id=1, source_target_pairs={{0,96},{32,64},{64,32},{96,0},{1,97},{33,65},{65,33},{97,1},{2,98}... | collective-permute-start | bytes 294920 | tf_op jit(solution)/shard_map/ppermute | solution.py:31
  184.8 5.8 %collective-permute-start.19 = (bf16[96,512]{1,0:T(8,128)(2,1)S(1)}, bf16[96,512]{1,0:T(8,128)(2,1)S(1)}, u32[]{:S(2)}, u32[]{:S(2)}) collective-permute-start(bf16[96,512]{1,0:T(8,128)(2,1)S(1)} %fusion.24), channel_id=1, source_target_pairs={{0,32},{32,0},{64,96},{96,64},{1,33},{33,1},{65,97},{97,65},{2,34}... | collective-permute-start | bytes 294920 | tf_op jit(solution)/shard_map/ppermute | solution.py:31
  187.8 8.6 %copy-start.8 = (f32[96,1536]{1,0:T(8,128)S(1)}, f32[96,1536]{1,0:T(8,128)}, u32[]{:S(2)}) copy-start(f32[96,1536]{1,0:T(8,128)} %get-tuple-element.83) | copy-start | bytes 1769476
  187.8 8.6 %copy-start.9 = (f32[96,1536]{1,0:T(8,128)S(1)}, f32[96,1536]{1,0:T(8,128)}, u32[]{:S(2)}) copy-start(f32[96,1536]{1,0:T(8,128)} %get-tuple-element.84) | copy-start | bytes 1769476
  187.8 8.6 %copy-start.12 = (f32[96,1024]{1,0:T(8,128)S(1)}, f32[96,1024]{1,0:T(8,128)}, u32[]{:S(2)}) copy-start(f32[96,1024]{1,0:T(8,128)} %get-tuple-element.79) | copy-start | bytes 1179652
  187.8 8.6 %copy-start.13 = (f32[96,1024]{1,0:T(8,128)S(1)}, f32[96,1024]{1,0:T(8,128)}, u32[]{:S(2)}) copy-start(f32[96,1024]{1,0:T(8,128)} %get-tuple-element.80) | copy-start | bytes 1179652
  187.8 8.6 %copy-start.15 = (f32[96,1024]{1,0:T(8,128)S(1)}, f32[96,1024]{1,0:T(8,128)}, u32[]{:S(2)}) copy-start(f32[96,1024]{1,0:T(8,128)} %get-tuple-element.75) | copy-start | bytes 1179652
  187.8 8.6 %copy-start.16 = (f32[96,1024]{1,0:T(8,128)S(1)}, f32[96,1024]{1,0:T(8,128)}, u32[]{:S(2)}) copy-start(f32[96,1024]{1,0:T(8,128)} %get-tuple-element.76) | copy-start | bytes 1179652
  192.2 9.7 %collective-permute-start.24 = (bf16[96,1024]{1,0:T(8,128)(2,1)S(1)}, bf16[96,1024]{1,0:T(8,128)(2,1)S(1)}, u32[]{:S(2)}, u32[]{:S(2)}) collective-permute-start(bf16[96,1024]{1,0:T(8,128)(2,1)S(1)} %get-tuple-element.70.refs_1_), channel_id=1, source_target_pairs={{0,96},{32,64},{64,32},{96,0},{1,97},{33,65},{65,33},{97,1},{2,98}... | collective-permute-start | bytes 589832 | tf_op jit(solution)/shard_map/ppermute | solution.py:31
  194.8 8.1 %collective-permute-start.23 = (bf16[96,1024]{1,0:T(8,128)(2,1)S(1)}, bf16[96,1024]{1,0:T(8,128)(2,1)S(1)}, u32[]{:S(2)}, u32[]{:S(2)}) collective-permute-start(bf16[96,1024]{1,0:T(8,128)(2,1)S(1)} %get-tuple-element.70.refs_1_), channel_id=1, source_target_pairs={{0,64},{32,96},{64,0},{96,32},{1,65},{33,97},{65,1},{97,33},{2,66}... | collective-permute-start | bytes 589832 | tf_op jit(solution)/shard_map/ppermute | solution.py:31
  194.8 8.6 %collective-permute-start.22 = (bf16[96,1024]{1,0:T(8,128)(2,1)S(1)}, bf16[96,1024]{1,0:T(8,128)(2,1)S(1)}, u32[]{:S(2)}, u32[]{:S(2)}) collective-permute-start(bf16[96,1024]{1,0:T(8,128)(2,1)S(1)} %get-tuple-element.70.refs_1_), channel_id=1, source_target_pairs={{0,32},{32,0},{64,96},{96,64},{1,33},{33,1},{65,97},{97,65},{2,34}... | collective-permute-start | bytes 589832 | tf_op jit(solution)/shard_map/ppermute | solution.py:31
  196.4 2.1 %copy-start.10 = (f32[96,1536]{1,0:T(8,128)S(1)}, f32[96,1536]{1,0:T(8,128)}, u32[]{:S(2)}) copy-start(f32[96,1536]{1,0:T(8,128)} %get-tuple-element.85) | copy-start | bytes 1769476
  196.4 2.1 %copy-start.11 = (f32[96,1024]{1,0:T(8,128)S(1)}, f32[96,1024]{1,0:T(8,128)}, u32[]{:S(2)}) copy-start(f32[96,1024]{1,0:T(8,128)} %get-tuple-element.81) | copy-start | bytes 1179652
  196.4 2.1 %copy-start.14 = (f32[96,1024]{1,0:T(8,128)S(1)}, f32[96,1024]{1,0:T(8,128)}, u32[]{:S(2)}) copy-start(f32[96,1024]{1,0:T(8,128)} %get-tuple-element.77) | copy-start | bytes 1179652
  198.5 1.4 copy-start.4
  198.5 1.7 copy-start.7

commit v6 on v5

--- a/solution.py
+++ b/solution.py
@@ -172,7 +172,7 @@
     unit = width // sum(UNITS)
     edges = [unit * sum(UNITS[:i]) for i in range(len(UNITS) + 1)]
     spans = [slice(low, high) for low, high in zip(edges, edges[1:])]
-    states, rows, joined, fars, blocks, spots = [], [], [], [], [], []
+    states, rows, blocks, spots = [], [], [], []
     arrived, last = (), len(spans) - 1
     picked = [
         jnp.dot(dispatch, input_grad[:, span], preferred_element_type=jnp.float32).astype(jnp.bfloat16)
@@ -180,40 +180,42 @@
     ]
     for number, span in enumerate(spans):
         outgoing = picked[number]
-        earlier_work = target if number == 1 else rows[: max(0, number - 1)]
+        earlier_work = (target, picked) if number == 1 else rows[: max(0, number - 1)]
         outgoing = after(outgoing, arrived, earlier_work)
         arrived = lax.all_to_all(outgoing, "vocab", split_axis=0, concat_axis=0, tiled=True)
-        ready = after(arrived, rows, picked[: number + 2])
+        ready = after(arrived, rows, blocks if number == last else ())
         sums = combine(here, target, head_grad, ready, span.start)
-        grads = []
+        grads, onwards = [], []
         for side, (one, two) in enumerate(HALVES):
             keep, sent = sums[2 * side : 2 * side + 2]
             half = swap_z(sent, one).astype(jnp.float32)
-            onward = (keep[share:] + half[share:]).astype(jnp.bfloat16)
-            if number == last:
-                onward = after(onward, fars[: number - 1])
-            grads.append(keep[:share] + half[:share] + swap_z(onward, two).astype(jnp.float32))
+            onwards.append((keep[share:] + half[share:]).astype(jnp.bfloat16))
+            came = swap_z(onwards[side], two).astype(jnp.float32)
+            grads.append(keep[:share] + half[:share] + came)
         grad = jnp.concatenate(grads, axis=1)
-        if 1 <= number < last:
-            grad = after(grad, fars[: number - 1], joined)
+        if number:
+            one, two = HALVES[number % 2]
+            near = swap_z(rows[-1], one)
+            if number > 1:
+                near = after(near, onwards)
+            both = jnp.concatenate([rows[-1], near], axis=0)
+            far = swap_z(both, two)
+            start = spans[number - 1].start
+            spots += [
+                (len(blocks), 0, 0, start),
+                (len(blocks), share, one, start),
+                (len(blocks) + 1, 0, two, start),
+                (len(blocks) + 1, share, one ^ two, start),
+            ]
+            blocks += [both, far]
+            if number < last:
+                grad = after(grad, far if number == 1 else both)
         states.append(update(grad, master[:, span], moment_one[:, span], moment_two[:, span]))
-        block = states[-1][0].astype(jnp.bfloat16)
-        rows.append(block)
-        if number < last:
-            both = jnp.concatenate([block, swap_z(block, 3)], axis=0)
-            joined.append(both)
-            spots += [
-                (len(blocks), 0, 0, span.start),
-                (len(blocks), share, 3, span.start),
-                (len(blocks) + 1, 0, 1, span.start),
-                (len(blocks) + 1, share, 2, span.start),
-            ]
-            fars.append(swap_z(both, 1))
-            blocks += [both, fars[-1]]
+        rows.append(states[-1][0].astype(jnp.bfloat16))
     shape = (slab_rows, width)
     blocks = after(blocks, rows)
     table = place(None, here, blocks, tuple(spots), share, shape)
-    blocks = [block] + [swap_z(block, flip) for flip in range(1, GROUPS)]
+    blocks = [rows[last]] + [swap_z(rows[last], flip) for flip in range(1, GROUPS)]
     spots = [(flip, 0, flip, span.start) for flip in range(GROUPS)]
     table = place(table, here, blocks, tuple(spots), share, shape)
     return tuple(jnp.concatenate(parts, axis=1) for parts in zip(*states)) + (table,)

time: 205 us -> 202 us (0.985)
  waiting for transfers between devices: 89.5 us -> 82 us
  starting transfers between devices: 59.6 us -> 64.8 us
  other arithmetic: 19.2 us -> 16.5 us
    all_to_all x4, waiting for transfers between devices: 39.4 us -> 32.6 us  [local(): lax.all_to_all(outgoing, 'vocab', split_axis=0, concat_axis=0, tiled=True)]
    ppermute x25, starting transfers between devices: 35.8 us -> 39.7 us  [swap_z(): return lax.ppermute(block, 'dp', [(i, i ^ flip) for i in range(GROUPS)])]
    concatenate x3, other arithmetic: 2.69 us -> 0.09 us  [local(): both = jnp.concatenate([rows[-1], near], axis=0)]
    unnamed x41 -> x49, local copies, waits for them, and re-layouts: 5.31 us -> 6.45 us
  transfers between devices with their start and end apart: 29 -> 29, of which waited for: 23 -> 19; matrix products, arithmetic and copies ran while one was open for 14% -> 13% of each run, Pallas kernels for 6% -> 5%
where the time goes in v6:
time: 202 us; the launch traced here: 201 us
  waiting for transfers between devices  82 us (41%)
  starting transfers between devices  64.8 us (32%)
  matrix products  16.8 us (8%)
  other arithmetic  16.5 us (8%)
  Pallas kernels  12.7 us (6%)
  local copies, waits for them, and re-layouts  6.57 us (3%)
    ppermute x25, waiting for transfers between devices, swap_z(): return lax.ppermute(block, 'dp', [(i, i ^ flip) for i in range(GROUPS)])  49.4 us
    ppermute x25, starting transfers between devices, swap_z(): return lax.ppermute(block, 'dp', [(i, i ^ flip) for i in range(GROUPS)])  39.7 us
    all_to_all x4, waiting for transfers between devices, local(): lax.all_to_all(outgoing, 'vocab', split_axis=0, concat_axis=0, tiled=True)  32.6 us
    all_to_all x4, starting transfers between devices, local(): lax.all_to_all(outgoing, 'vocab', split_axis=0, concat_axis=0, tiled=True)  25.1 us
    dot_general x4, matrix products, local(): jnp.dot(dispatch, input_grad[:, span], preferred_element_type=jnp.float32)  16.4 us
    pallas_call x4, Pallas kernels, combine(): pl.pallas_call(combine_body, grid=(2,), out_shape=[kept, sent] * 2, in_sp...  10.2 us
    convert_element_type x4, other arithmetic, local(): rows.append(states[-1][0].astype(jnp.bfloat16))  9.62 us
    unnamed x49, local copies, waits for them, and re-layouts  6.45 us
  transfers between devices with their start and end apart: 29, of which 19 were waited for; matrix products, arithmetic and copies ran while one was open for 13% of the time, Pallas kernels for 5%

profile of v6, /device:TPU:0, one launch (start us, length us, event | category | flops | bytes accessed | tf_op | source)
XLA Modules:
  0.0 200.7 jit_solution(13527423859412754543)
XLA Ops:
  0.6 0.5 broadcast.106
  1.1 1.6 reduce.7
  3.1 4.9 %convolution_convert_fusion = bf16[1024,1536]{1,0:T(8,128)(2,1)} fusion(bf16[512,4608]{1,0:T(8,128)(2,1)} %param.7, s32[512]{0:T(512)S(1)} %bitcast.20), kind=kOutput, calls=%fused_computation | convolution fusion | flops 1612709888 | bytes 4720640 | tf_op jit(solution)/shard_map/dot_general | solution.py:178
  7.9 7.5 %all-to-all-start = ((bf16[32,32,1536]{2,1,0:T(8,128)(2,1)}), bf16[32,32,1536]{2,1,0:T(8,128)(2,1)S(1)}, u32[]{:S(2)}, u32[]{:S(2)}) async-start(bf16[32,32,1536]{2,1,0:T(8,128)(2,1)} %bitcast.15), calls=%async_computation | async-start | bytes 6291456 | tf_op jit(solution)/shard_map/all_to_all | solution.py:185
  15.9 0.6 select_reduce_fusion
  16.7 3.8 %fusion.6 = bf16[1024,1024]{1,0:T(8,128)(2,1)} fusion(bf16[512,4608]{1,0:T(8,128)(2,1)} %param.7, s32[512]{0:T(512)S(1)} %bitcast.21), kind=kOutput, calls=%fused_computation.10 | convolution fusion | flops 1075314688 | bytes 3147776 | tf_op jit(solution)/shard_map/dot_general | solution.py:178
  20.5 3.8 %fusion.5 = bf16[1024,1024]{1,0:T(8,128)(2,1)} fusion(bf16[512,4608]{1,0:T(8,128)(2,1)} %param.7, s32[512]{0:T(512)S(1)} %bitcast.22), kind=kOutput, calls=%fused_computation.9 | convolution fusion | flops 1075314688 | bytes 3147776 | tf_op jit(solution)/shard_map/dot_general | solution.py:178
  24.3 3.8 %fusion.4 = bf16[1024,1024]{1,0:T(8,128)(2,1)} fusion(bf16[512,4608]{1,0:T(8,128)(2,1)} %param.7, s32[512]{0:T(512)S(1)} %bitcast.23), kind=kOutput, calls=%fused_computation.8 | convolution fusion | flops 1075314688 | bytes 3147776 | tf_op jit(solution)/shard_map/dot_general | solution.py:178
  28.2 27.3 %all-to-all-done = bf16[32,32,1536]{2,1,0:T(8,128)(2,1)S(1)} async-done(((bf16[32,32,1536]{2,1,0:T(8,128)(2,1)}), bf16[32,32,1536]{2,1,0:T(8,128)(2,1)S(1)}, u32[]{:S(2)}, u32[]{:S(2)}) %all-to-all-start) | async-done | bytes 3145760 | tf_op jit(solution)/shard_map/all_to_all | solution.py:185
  55.4 1.7 copy-done.1
  57.1 5.2 %all-to-all-start.1 = ((bf16[32,32,1024]{2,1,0:T(8,128)(2,1)}), bf16[32,32,1024]{2,1,0:T(8,128)(2,1)}, u32[]{:S(2)}, u32[]{:S(2)}) async-start(bf16[32,32,1024]{2,1,0:T(8,128)(2,1)} %bitcast.18), calls=%async_computation.1 | async-start | bytes 4194304 | tf_op jit(solution)/shard_map/all_to_all | solution.py:185
  62.3 1.9 copy-done.2
  64.2 2.1 %shard_map.102 = (f32[192,768]{1,0:T(8,128)S(1)}, bf16[192,768]{1,0:T(8,128)(2,1)S(1)}, f32[192,768]{1,0:T(8,128)S(1)}, bf16[192,768]{1,0:T(8,128)(2,1)S(1)}) custom-call(s32[1]{0:T(128)} %bitcast.here_ref, s32[1,1024]{1,0:T(1,128)S(1)} %sub.19.target_ref, bf16[1,384,4608]{2,1,0:T(8,128)(2,1)S(1)} %copy-done, bf16[1024,1536]{1,0:T(8,128)(2,1)S(1)} %bitcast.14), custom_call_target="tpu_custom_call" | custom-call | flops 1207959552 | bytes 6094848 | tf_op jit(solution)/shard_map/pallas_call | solution.py:79
  66.4 2.0 collective-permute-start
  68.4 2.5 %collective-permute-start.2 = (bf16[192,768]{1,0:T(8,128)(2,1)S(1)}, bf16[192,768]{1,0:T(8,128)(2,1)S(1)}, u32[]{:S(2)}, u32[]{:S(2)}) collective-permute-start(bf16[192,768]{1,0:T(8,128)(2,1)S(1)} %get-tuple-element.39), channel_id=1, source_target_pairs={{0,96},{32,64},{64,32},{96,0},{1,97},{33,65},{65,33},{97,1},{2,98}... | collective-permute-start | bytes 884744 | tf_op jit(solution)/shard_map/ppermute | solution.py:31
  70.9 4.8 %collective-permute-done = bf16[192,768]{1,0:T(8,128)(2,1)S(1)} collective-permute-done((bf16[192,768]{1,0:T(8,128)(2,1)S(1)}, bf16[192,768]{1,0:T(8,128)(2,1)S(1)}, u32[]{:S(2)}, u32[]{:S(2)}) %collective-permute-start) | collective-permute-done | bytes 294944 | tf_op jit(solution)/shard_map/ppermute | solution.py:31
  75.8 3.9 %collective-permute-start.1 = (bf16[96,768]{1,0:T(8,128)(2,1)S(1)}, bf16[96,768]{1,0:T(8,128)(2,1)S(1)}, u32[]{:S(2)}, u32[]{:S(2)}) collective-permute-start(bf16[96,768]{1,0:T(8,128)(2,1)S(1)} %fusion.22), channel_id=1, source_target_pairs={{0,96},{32,64},{64,32},{96,0},{1,97},{33,65},{65,33},{97,1},{2,98}... | collective-permute-start | bytes 442376 | tf_op jit(solution)/shard_map/ppermute | solution.py:31
  79.9 3.3 %collective-permute-done.1 = bf16[96,768]{1,0:T(8,128)(2,1)S(1)} collective-permute-done((bf16[96,768]{1,0:T(8,128)(2,1)S(1)}, bf16[96,768]{1,0:T(8,128)(2,1)S(1)}, u32[]{:S(2)}, u32[]{:S(2)}) %collective-permute-start.1) | collective-permute-done | bytes 147488 | tf_op jit(solution)/shard_map/ppermute | solution.py:31
  83.3 1.8 collective-permute-done.3
  85.1 3.0 %fusion.43 = (bf16[96,1536]{1,0:T(8,128)(2,1)}, f32[96,1536]{1,0:T(8,128)}, f32[96,1536]{1,0:T(8,128)}, f32[96,1536]{1,0:T(8,128)}) fusion(f32[96,4608]{1,0:T(8,128)} %param.11, f32[96,768]{1,0:T(8,128)S(1)} %fusion.21, f32[96,768]{1,0:T(8,128)S(1)} %fusion.23, f32[96,4608]{1,0:T(8,128)} %param.12, f32[96,4608]{1,0:T(8,128)} %param.13), kind=kLoop, calls=%fused_computation.91 | loop fusion | flops 2506752 | bytes 4423680 | tf_op jit(solution)/shard_map/convert_element_type | solution.py:214
  88.1 3.1 %all-to-all-done.1 = bf16[32,32,1024]{2,1,0:T(8,128)(2,1)} async-done(((bf16[32,32,1024]{2,1,0:T(8,128)(2,1)}), bf16[32,32,1024]{2,1,0:T(8,128)(2,1)}, u32[]{:S(2)}, u32[]{:S(2)}) %all-to-all-start.1) | async-done | bytes 2097184 | tf_op jit(solution)/shard_map/all_to_all | solution.py:185
  91.2 4.8 %all-to-all-start.2 = ((bf16[32,32,1024]{2,1,0:T(8,128)(2,1)}), bf16[32,32,1024]{2,1,0:T(8,128)(2,1)}, u32[]{:S(2)}, u32[]{:S(2)}) async-start(bf16[32,32,1024]{2,1,0:T(8,128)(2,1)} %bitcast.17), calls=%async_computation.2 | async-start | bytes 4194304 | tf_op jit(solution)/shard_map/all_to_all | solution.py:185
  96.0 4.1 %collective-permute-start.8 = (bf16[96,1536]{1,0:T(8,128)(2,1)}, bf16[96,1536]{1,0:T(8,128)(2,1)S(1)}, u32[]{:S(2)}, u32[]{:S(2)}) collective-permute-start(bf16[96,1536]{1,0:T(8,128)(2,1)} %get-tuple-element.80), channel_id=1, source_target_pairs={{0,96},{32,64},{64,32},{96,0},{1,97},{33,65},{65,33},{97,1},{2,98}... | collective-permute-start | bytes 884744 | tf_op jit(solution)/shard_map/ppermute | solution.py:31
  100.1 2.7 %shard_map.103 = (f32[192,512]{1,0:T(8,128)S(1)}, bf16[192,512]{1,0:T(8,128)(2,1)S(1)}, f32[192,512]{1,0:T(8,128)S(1)}, bf16[192,512]{1,0:T(8,128)(2,1)S(1)}) custom-call(s32[1]{0:T(128)} %bitcast.here_ref, s32[1,1024]{1,0:T(1,128)S(1)} %sub.19.target_ref, bf16[1,384,4608]{2,1,0:T(8,128)(2,1)S(1)} %copy-done, bf16[1024,1024]{1,0:T(8,128)(2,1)} %bitcast.7.part_ref), custom_call_target="tpu_custom_call" | custom-call | flops 805306368 | bytes 4063232 | tf_op jit(solution)/shard_map/pallas_call | solution.py:79
  103.0 4.5 %collective-permute-done.8 = bf16[96,1536]{1,0:T(8,128)(2,1)S(1)} collective-permute-done((bf16[96,1536]{1,0:T(8,128)(2,1)}, bf16[96,1536]{1,0:T(8,128)(2,1)S(1)}, u32[]{:S(2)}, u32[]{:S(2)}) %collective-permute-start.8) | collective-permute-done | bytes 294944 | tf_op jit(solution)/shard_map/ppermute | solution.py:31
  107.7 3.0 %collective-permute-start.6 = (bf16[192,512]{1,0:T(8,128)(2,1)S(1)}, bf16[192,512]{1,0:T(8,128)(2,1)S(1)}, u32[]{:S(2)}, u32[]{:S(2)}) collective-permute-start(bf16[192,512]{1,0:T(8,128)(2,1)S(1)} %get-tuple-element.45), channel_id=1, source_target_pairs={{0,96},{32,64},{64,32},{96,0},{1,97},{33,65},{65,33},{97,1},{2,98}... | collective-permute-start | bytes 589832 | tf_op jit(solution)/shard_map/ppermute | solution.py:31
  110.8 0.4 collective-permute-start.5
  111.2 5.3 %collective-permute-done.6 = bf16[192,512]{1,0:T(8,128)(2,1)S(1)} collective-permute-done((bf16[192,512]{1,0:T(8,128)(2,1)S(1)}, bf16[192,512]{1,0:T(8,128)(2,1)S(1)}, u32[]{:S(2)}, u32[]{:S(2)}) %collective-permute-start.6) | collective-permute-done | bytes 196640 | tf_op jit(solution)/shard_map/ppermute | solution.py:31
  116.6 0.8 collective-permute-start.7
  117.7 7.1 %collective-permute-done.7 = bf16[96,512]{1,0:T(8,128)(2,1)S(1)} collective-permute-done((bf16[96,512]{1,0:T(8,128)(2,1)S(1)}, bf16[96,512]{1,0:T(8,128)(2,1)S(1)}, u32[]{:S(2)}, u32[]{:S(2)}) %collective-permute-start.7) | collective-permute-done | bytes 98336 | tf_op jit(solution)/shard_map/ppermute | solution.py:31
  124.9 0.8 copy-done.7
  125.7 2.5 %fusion.41 = (bf16[96,1024]{1,0:T(8,128)(2,1)}, f32[96,1024]{1,0:T(8,128)}, f32[96,1024]{1,0:T(8,128)}, f32[96,1024]{1,0:T(8,128)}) fusion(f32[96,4608]{1,0:T(8,128)} %param.11, f32[96,1024]{1,0:T(8,128)S(1)} %pad_maximum_fusion.5, f32[96,4608]{1,0:T(8,128)} %param.12, f32[96,4608]{1,0:T(8,128)} %param.13), kind=kLoop, calls=%fused_computation.90 | loop fusion | flops 1572864 | bytes 2949120 | tf_op jit(solution)/shard_map/convert_element_type | solution.py:214
  128.2 7.6 %all-to-all-start.3 = ((bf16[32,32,1024]{2,1,0:T(8,128)(2,1)}), bf16[32,32,1024]{2,1,0:T(8,128)(2,1)}, u32[]{:S(2)}, u32[]{:S(2)}) async-start(bf16[32,32,1024]{2,1,0:T(8,128)(2,1)} %bitcast.16), calls=%async_computation.3 | async-start | bytes 4194304 | tf_op jit(solution)/shard_map/all_to_all | solution.py:185
  135.8 2.7 %shard_map.104 = (f32[192,512]{1,0:T(8,128)S(1)}, bf16[192,512]{1,0:T(8,128)(2,1)S(1)}, f32[192,512]{1,0:T(8,128)S(1)}, bf16[192,512]{1,0:T(8,128)(2,1)S(1)}) custom-call(s32[1]{0:T(128)} %bitcast.here_ref, s32[1,1024]{1,0:T(1,128)S(1)} %sub.19.target_ref, bf16[1,384,4608]{2,1,0:T(8,128)(2,1)S(1)} %copy-done, bf16[1024,1024]{1,0:T(8,128)(2,1)} %bitcast.9.part_ref), custom_call_target="tpu_custom_call" | custom-call | flops 805306368 | bytes 4063232 | tf_op jit(solution)/shard_map/pallas_call | solution.py:79
  138.5 0.4 collective-permute-start.10
  138.9 1.7 collective-permute-start.14
  140.6 2.5 %collective-permute-start.12 = (bf16[192,512]{1,0:T(8,128)(2,1)S(1)}, bf16[192,512]{1,0:T(8,128)(2,1)S(1)}, u32[]{:S(2)}, u32[]{:S(2)}) collective-permute-start(bf16[192,512]{1,0:T(8,128)(2,1)S(1)} %get-tuple-element.52), channel_id=1, source_target_pairs={{0,96},{32,64},{64,32},{96,0},{1,97},{33,65},{65,33},{97,1},{2,98}... | collective-permute-start | bytes 589832 | tf_op jit(solution)/shard_map/ppermute | solution.py:31
  143.1 3.2 %collective-permute-done.10 = bf16[192,512]{1,0:T(8,128)(2,1)S(1)} collective-permute-done((bf16[192,512]{1,0:T(8,128)(2,1)S(1)}, bf16[192,512]{1,0:T(8,128)(2,1)S(1)}, u32[]{:S(2)}, u32[]{:S(2)}) %collective-permute-start.10) | collective-permute-done | bytes 196640 | tf_op jit(solution)/shard_map/ppermute | solution.py:31
  146.4 2.6 %collective-permute-start.11 = (bf16[96,512]{1,0:T(8,128)(2,1)S(1)}, bf16[96,512]{1,0:T(8,128)(2,1)S(1)}, u32[]{:S(2)}, u32[]{:S(2)}) collective-permute-start(bf16[96,512]{1,0:T(8,128)(2,1)S(1)} %fusion.30), channel_id=1, source_target_pairs={{0,96},{32,64},{64,32},{96,0},{1,97},{33,65},{65,33},{97,1},{2,98}... | collective-permute-start | bytes 294920 | tf_op jit(solution)/shard_map/ppermute | solution.py:31
  149.2 0.6 collective-permute-done.14
  149.8 2.6 %collective-permute-start.15 = (bf16[192,1024]{1,0:T(8,128)(2,1)S(1)}, bf16[192,1024]{1,0:T(8,128)(2,1)S(1)}, u32[]{:S(2)}, u32[]{:S(2)}) collective-permute-start(bf16[192,1024]{1,0:T(8,128)(2,1)S(1)} %pad_maximum_fusion.7.refs_2_), channel_id=1, source_target_pairs={{0,96},{32,64},{64,32},{96,0},{1,97},{33,65},{65,33},{97,1},{2,98}... | collective-permute-start | bytes 1179656 | tf_op jit(solution)/shard_map/ppermute | solution.py:31
  152.5 1.3 collective-permute-done.13
  153.9 2.5 %fusion.39 = (bf16[96,1024]{1,0:T(8,128)(2,1)}, f32[96,1024]{1,0:T(8,128)}, f32[96,1024]{1,0:T(8,128)}, f32[96,1024]{1,0:T(8,128)}) fusion(f32[96,4608]{1,0:T(8,128)} %param.11, f32[96,1024]{1,0:T(8,128)S(1)} %pad_maximum_fusion.6, f32[96,4608]{1,0:T(8,128)} %param.12, f32[96,4608]{1,0:T(8,128)} %param.13), kind=kLoop, calls=%fused_computation.89 | loop fusion | flops 1572864 | bytes 2949120 | tf_op jit(solution)/shard_map/convert_element_type | solution.py:214
  156.4 5.2 %collective-permute-done.15.refs_3_ = bf16[192,1024]{1,0:T(8,128)(2,1)S(1)} collective-permute-done((bf16[192,1024]{1,0:T(8,128)(2,1)S(1)}, bf16[192,1024]{1,0:T(8,128)(2,1)S(1)}, u32[]{:S(2)}, u32[]{:S(2)}) %collective-permute-start.15) | collective-permute-done | bytes 393248 | tf_op jit(solution)/shard_map/ppermute | solution.py:31
  161.6 0.8 copy-done.9
  162.4 2.3 %all-to-all-done.3 = bf16[32,32,1024]{2,1,0:T(8,128)(2,1)} async-done(((bf16[32,32,1024]{2,1,0:T(8,128)(2,1)}), bf16[32,32,1024]{2,1,0:T(8,128)(2,1)}, u32[]{:S(2)}, u32[]{:S(2)}) %all-to-all-start.3) | async-done | bytes 2097184 | tf_op jit(solution)/shard_map/all_to_all | solution.py:185
  164.7 2.7 %shard_map.105 = (f32[192,512]{1,0:T(8,128)S(1)}, bf16[192,512]{1,0:T(8,128)(2,1)S(1)}, f32[192,512]{1,0:T(8,128)S(1)}, bf16[192,512]{1,0:T(8,128)(2,1)S(1)}) custom-call(s32[1]{0:T(128)} %bitcast.here_ref, s32[1,1024]{1,0:T(1,128)S(1)} %sub.19.target_ref, bf16[1,384,4608]{2,1,0:T(8,128)(2,1)S(1)} %copy-done, bf16[1024,1024]{1,0:T(8,128)(2,1)} %bitcast.11.part_ref), custom_call_target="tpu_custom_call" | custom-call | flops 805306368 | bytes 4063232 | tf_op jit(solution)/shard_map/pallas_call | solution.py:79
  167.7 2.5 %collective-permute-start.20 = (bf16[96,1024]{1,0:T(8,128)(2,1)S(1)}, bf16[96,1024]{1,0:T(8,128)(2,1)S(1)}, u32[]{:S(2)}, u32[]{:S(2)}) collective-permute-start(bf16[96,1024]{1,0:T(8,128)(2,1)S(1)} %copy-done.22), channel_id=1, source_target_pairs={{0,96},{32,64},{64,32},{96,0},{1,97},{33,65},{65,33},{97,1},{2,98}... | collective-permute-start | bytes 589832 | tf_op jit(solution)/shard_map/ppermute | solution.py:31
  170.3 0.7 collective-permute-start.18
  171.0 2.9 %collective-permute-done.16 = bf16[192,512]{1,0:T(8,128)(2,1)S(1)} collective-permute-done((bf16[192,512]{1,0:T(8,128)(2,1)S(1)}, bf16[192,512]{1,0:T(8,128)(2,1)S(1)}, u32[]{:S(2)}, u32[]{:S(2)}) %collective-permute-start.16) | collective-permute-done | bytes 196640 | tf_op jit(solution)/shard_map/ppermute | solution.py:31
  174.0 2.6 %collective-permute-start.17 = (bf16[96,512]{1,0:T(8,128)(2,1)S(1)}, bf16[96,512]{1,0:T(8,128)(2,1)S(1)}, u32[]{:S(2)}, u32[]{:S(2)}) collective-permute-start(bf16[96,512]{1,0:T(8,128)(2,1)S(1)} %fusion.26), channel_id=1, source_target_pairs={{0,96},{32,64},{64,32},{96,0},{1,97},{33,65},{65,33},{97,1},{2,98}... | collective-permute-start | bytes 294920 | tf_op jit(solution)/shard_map/ppermute | solution.py:31
  176.6 3.9 %collective-permute-done.18 = bf16[192,512]{1,0:T(8,128)(2,1)S(1)} collective-permute-done((bf16[192,512]{1,0:T(8,128)(2,1)S(1)}, bf16[192,512]{1,0:T(8,128)(2,1)S(1)}, u32[]{:S(2)}, u32[]{:S(2)}) %collective-permute-start.18) | collective-permute-done | bytes 196640 | tf_op jit(solution)/shard_map/ppermute | solution.py:31
  180.6 0.7 collective-permute-start.19
  181.3 1.5 collective-permute-start.21
  182.9 3.5 %collective-permute-done.19 = bf16[96,512]{1,0:T(8,128)(2,1)S(1)} collective-permute-done((bf16[96,512]{1,0:T(8,128)(2,1)S(1)}, bf16[96,512]{1,0:T(8,128)(2,1)S(1)}, u32[]{:S(2)}, u32[]{:S(2)}) %collective-permute-start.19) | collective-permute-done | bytes 98336 | tf_op jit(solution)/shard_map/ppermute | solution.py:31
  186.4 1.6 fusion.37
  188.0 2.6 %collective-permute-start.24 = (bf16[96,1024]{1,0:T(8,128)(2,1)S(1)}, bf16[96,1024]{1,0:T(8,128)(2,1)S(1)}, u32[]{:S(2)}, u32[]{:S(2)}) collective-permute-start(bf16[96,1024]{1,0:T(8,128)(2,1)S(1)} %get-tuple-element.68.refs_1_), channel_id=1, source_target_pairs={{0,96},{32,64},{64,32},{96,0},{1,97},{33,65},{65,33},{97,1},{2,98}... | collective-permute-start | bytes 589832 | tf_op jit(solution)/shard_map/ppermute | solution.py:31
  190.7 1.4 collective-permute-start.22
  192.2 2.1 %pad_maximum_fusion = (f32[96,4608]{1,0:T(8,128)}, f32[96,4608]{1,0:T(8,128)}) fusion(f32[96,1024]{1,0:T(8,128)S(1)} %get-tuple-element.69, f32[96,1024]{1,0:T(8,128)S(1)} %copy-done.18, f32[96,1024]{1,0:T(8,128)S(1)} %copy-done.15, f32[96,1536]{1,0:T(8,128)S(1)} %copy-done.11, f32[96,1024]{1,0:T(8,128)S(1)} %get-tuple-element.70, ...), kind=kLoop, calls=%fused_computation.11 | loop fusion | flops 2654208 | bytes 7077888 | tf_op jit(solution)/shard_map/concatenate | solution.py:221
  194.3 1.3 pad_maximum_fusion.2
  195.7 0.5 copy-done.8
  196.4 1.6 shard_map.106.refs_0_
  198.0 1.5 collective-permute-done.23.refs_3_
  199.7 0.9 shard_map.107
  (101 shorter events, 3.5 us)
Async XLA Ops:
  7.9 7.5 %copy-start.23 = (s32[16384,1]{0,1:T(1,128)S(1)}, s32[16384,1]{0,1:T(1,128)}, u32[]{:S(2)}) copy-start(s32[16384,1]{0,1:T(1,128)} %param.9) | copy-start | bytes 196612
  7.9 47.5 %all-to-all-start = ((bf16[32,32,1536]{2,1,0:T(8,128)(2,1)}), bf16[32,32,1536]{2,1,0:T(8,128)(2,1)S(1)}, u32[]{:S(2)}, u32[]{:S(2)}) async-start(bf16[32,32,1536]{2,1,0:T(8,128)(2,1)} %bitcast.15), calls=%async_computation | async-start | bytes 6291456 | tf_op jit(solution)/shard_map/all_to_all | solution.py:185
  55.4 1.7 copy-start.1
  57.1 5.2 %copy-start = (bf16[1,384,4608]{2,1,0:T(8,128)(2,1)S(1)}, bf16[1,384,4608]{2,1,0:T(8,128)(2,1)}, u32[]{:S(2)}) copy-start(bf16[1,384,4608]{2,1,0:T(8,128)(2,1)} %head_ref.7) | copy-start | bytes 10616836
  57.1 34.1 %all-to-all-start.1 = ((bf16[32,32,1024]{2,1,0:T(8,128)(2,1)}), bf16[32,32,1024]{2,1,0:T(8,128)(2,1)}, u32[]{:S(2)}, u32[]{:S(2)}) async-start(bf16[32,32,1024]{2,1,0:T(8,128)(2,1)} %bitcast.18), calls=%async_computation.1 | async-start | bytes 4194304 | tf_op jit(solution)/shard_map/all_to_all | solution.py:185
  62.3 1.9 copy-start.2
  66.4 9.4 %collective-permute-start = (bf16[192,768]{1,0:T(8,128)(2,1)S(1)}, bf16[192,768]{1,0:T(8,128)(2,1)S(1)}, u32[]{:S(2)}, u32[]{:S(2)}) collective-permute-start(bf16[192,768]{1,0:T(8,128)(2,1)S(1)} %get-tuple-element.37), channel_id=1, source_target_pairs={{0,32},{32,0},{64,96},{96,64},{1,33},{33,1},{65,97},{97,65},{2,34}... | collective-permute-start | bytes 884744 | tf_op jit(solution)/shard_map/ppermute | solution.py:31
  68.4 11.4 %collective-permute-start.2 = (bf16[192,768]{1,0:T(8,128)(2,1)S(1)}, bf16[192,768]{1,0:T(8,128)(2,1)S(1)}, u32[]{:S(2)}, u32[]{:S(2)}) collective-permute-start(bf16[192,768]{1,0:T(8,128)(2,1)S(1)} %get-tuple-element.39), channel_id=1, source_target_pairs={{0,96},{32,64},{64,32},{96,0},{1,97},{33,65},{65,33},{97,1},{2,98}... | collective-permute-start | bytes 884744 | tf_op jit(solution)/shard_map/ppermute | solution.py:31
  75.8 7.4 %collective-permute-start.1 = (bf16[96,768]{1,0:T(8,128)(2,1)S(1)}, bf16[96,768]{1,0:T(8,128)(2,1)S(1)}, u32[]{:S(2)}, u32[]{:S(2)}) collective-permute-start(bf16[96,768]{1,0:T(8,128)(2,1)S(1)} %fusion.22), channel_id=1, source_target_pairs={{0,96},{32,64},{64,32},{96,0},{1,97},{33,65},{65,33},{97,1},{2,98}... | collective-permute-start | bytes 442376 | tf_op jit(solution)/shard_map/ppermute | solution.py:31
  79.8 5.2 %collective-permute-start.3 = (bf16[96,768]{1,0:T(8,128)(2,1)S(1)}, bf16[96,768]{1,0:T(8,128)(2,1)S(1)}, u32[]{:S(2)}, u32[]{:S(2)}) collective-permute-start(bf16[96,768]{1,0:T(8,128)(2,1)S(1)} %fusion.20), channel_id=1, source_target_pairs={{0,32},{32,0},{64,96},{96,64},{1,33},{33,1},{65,97},{97,65},{2,34}... | collective-permute-start | bytes 442376 | tf_op jit(solution)/shard_map/ppermute | solution.py:31
  91.2 37.0 %all-to-all-start.2 = ((bf16[32,32,1024]{2,1,0:T(8,128)(2,1)}), bf16[32,32,1024]{2,1,0:T(8,128)(2,1)}, u32[]{:S(2)}, u32[]{:S(2)}) async-start(bf16[32,32,1024]{2,1,0:T(8,128)(2,1)} %bitcast.17), calls=%async_computation.2 | async-start | bytes 4194304 | tf_op jit(solution)/shard_map/all_to_all | solution.py:185
  96.0 11.6 %copy-start.20 = (bf16[96,1536]{1,0:T(8,128)(2,1)S(1)}, bf16[96,1536]{1,0:T(8,128)(2,1)}, u32[]{:S(2)}) copy-start(bf16[96,1536]{1,0:T(8,128)(2,1)} %get-tuple-element.80) | copy-start | bytes 884740
  96.0 11.6 %collective-permute-start.8 = (bf16[96,1536]{1,0:T(8,128)(2,1)}, bf16[96,1536]{1,0:T(8,128)(2,1)S(1)}, u32[]{:S(2)}, u32[]{:S(2)}) collective-permute-start(bf16[96,1536]{1,0:T(8,128)(2,1)} %get-tuple-element.80), channel_id=1, source_target_pairs={{0,96},{32,64},{64,32},{96,0},{1,97},{33,65},{65,33},{97,1},{2,98}... | collective-permute-start | bytes 884744 | tf_op jit(solution)/shard_map/ppermute | solution.py:31
  102.8 8.0 %collective-permute-start.4 = (bf16[192,512]{1,0:T(8,128)(2,1)S(1)}, bf16[192,512]{1,0:T(8,128)(2,1)S(1)}, u32[]{:S(2)}, u32[]{:S(2)}) collective-permute-start(bf16[192,512]{1,0:T(8,128)(2,1)S(1)} %get-tuple-element.43), channel_id=1, source_target_pairs={{0,32},{32,0},{64,96},{96,64},{1,33},{33,1},{65,97},{97,65},{2,34}... | collective-permute-start | bytes 589832 | tf_op jit(solution)/shard_map/ppermute | solution.py:31
  107.6 17.2 %copy-start.3 = (bf16[192,1536]{1,0:T(8,128)(2,1)}, bf16[192,1536]{1,0:T(8,128)(2,1)S(1)}, u32[]{:S(2)}) copy-start(bf16[192,1536]{1,0:T(8,128)(2,1)S(1)} %pad_maximum_fusion.4.refs_0_) | copy-start | bytes 1769476
  107.6 17.2 %collective-permute-start.9 = (bf16[192,1536]{1,0:T(8,128)(2,1)S(1)}, bf16[192,1536]{1,0:T(8,128)(2,1)S(1)}, u32[]{:S(2)}, u32[]{:S(2)}) collective-permute-start(bf16[192,1536]{1,0:T(8,128)(2,1)S(1)} %pad_maximum_fusion.4.refs_0_), channel_id=1, source_target_pairs={{0,32},{32,0},{64,96},{96,64},{1,33},{33,1},{65,97},{97,65},{2,34}... | collective-permute-start | bytes 1769480 | tf_op jit(solution)/shard_map/ppermute | solution.py:31
  107.7 8.8 %collective-permute-start.6 = (bf16[192,512]{1,0:T(8,128)(2,1)S(1)}, bf16[192,512]{1,0:T(8,128)(2,1)S(1)}, u32[]{:S(2)}, u32[]{:S(2)}) collective-permute-start(bf16[192,512]{1,0:T(8,128)(2,1)S(1)} %get-tuple-element.45), channel_id=1, source_target_pairs={{0,96},{32,64},{64,32},{96,0},{1,97},{33,65},{65,33},{97,1},{2,98}... | collective-permute-start | bytes 589832 | tf_op jit(solution)/shard_map/ppermute | solution.py:31
  110.8 6.8 %collective-permute-start.5 = (bf16[96,512]{1,0:T(8,128)(2,1)S(1)}, bf16[96,512]{1,0:T(8,128)(2,1)S(1)}, u32[]{:S(2)}, u32[]{:S(2)}) collective-permute-start(bf16[96,512]{1,0:T(8,128)(2,1)S(1)} %fusion.34), channel_id=1, source_target_pairs={{0,96},{32,64},{64,32},{96,0},{1,97},{33,65},{65,33},{97,1},{2,98}... | collective-permute-start | bytes 294920 | tf_op jit(solution)/shard_map/ppermute | solution.py:31
  116.6 8.1 %collective-permute-start.7 = (bf16[96,512]{1,0:T(8,128)(2,1)S(1)}, bf16[96,512]{1,0:T(8,128)(2,1)S(1)}, u32[]{:S(2)}, u32[]{:S(2)}) collective-permute-start(bf16[96,512]{1,0:T(8,128)(2,1)S(1)} %fusion.32), channel_id=1, source_target_pairs={{0,32},{32,0},{64,96},{96,64},{1,33},{33,1},{65,97},{97,65},{2,34}... | collective-permute-start | bytes 294920 | tf_op jit(solution)/shard_map/ppermute | solution.py:31
  124.8 0.8 copy-start.7
  128.2 36.5 %all-to-all-start.3 = ((bf16[32,32,1024]{2,1,0:T(8,128)(2,1)}), bf16[32,32,1024]{2,1,0:T(8,128)(2,1)}, u32[]{:S(2)}, u32[]{:S(2)}) async-start(bf16[32,32,1024]{2,1,0:T(8,128)(2,1)} %bitcast.16), calls=%async_computation.3 | async-start | bytes 4194304 | tf_op jit(solution)/shard_map/all_to_all | solution.py:185
  135.8 3.1 %copy-start.21 = (bf16[96,1024]{1,0:T(8,128)(2,1)S(1)}, bf16[96,1024]{1,0:T(8,128)(2,1)}, u32[]{:S(2)}) copy-start(bf16[96,1024]{1,0:T(8,128)(2,1)} %get-tuple-element.76) | copy-start | bytes 589828
  138.5 7.8 %collective-permute-start.10 = (bf16[192,512]{1,0:T(8,128)(2,1)S(1)}, bf16[192,512]{1,0:T(8,128)(2,1)S(1)}, u32[]{:S(2)}, u32[]{:S(2)}) collective-permute-start(bf16[192,512]{1,0:T(8,128)(2,1)S(1)} %get-tuple-element.50), channel_id=1, source_target_pairs={{0,32},{32,0},{64,96},{96,64},{1,33},{33,1},{65,97},{97,65},{2,34}... | collective-permute-start | bytes 589832 | tf_op jit(solution)/shard_map/ppermute | solution.py:31
  138.9 10.9 %collective-permute-start.14 = (bf16[96,1024]{1,0:T(8,128)(2,1)S(1)}, bf16[96,1024]{1,0:T(8,128)(2,1)S(1)}, u32[]{:S(2)}, u32[]{:S(2)}) collective-permute-start(bf16[96,1024]{1,0:T(8,128)(2,1)S(1)} %copy-done.21), channel_id=1, source_target_pairs={{0,32},{32,0},{64,96},{96,64},{1,33},{33,1},{65,97},{97,65},{2,34}... | collective-permute-start | bytes 589832 | tf_op jit(solution)/shard_map/ppermute | solution.py:31
  140.6 8.4 %collective-permute-start.12 = (bf16[192,512]{1,0:T(8,128)(2,1)S(1)}, bf16[192,512]{1,0:T(8,128)(2,1)S(1)}, u32[]{:S(2)}, u32[]{:S(2)}) collective-permute-start(bf16[192,512]{1,0:T(8,128)(2,1)S(1)} %get-tuple-element.52), channel_id=1, source_target_pairs={{0,96},{32,64},{64,32},{96,0},{1,97},{33,65},{65,33},{97,1},{2,98}... | collective-permute-start | bytes 589832 | tf_op jit(solution)/shard_map/ppermute | solution.py:31
  146.4 6.0 %collective-permute-start.11 = (bf16[96,512]{1,0:T(8,128)(2,1)S(1)}, bf16[96,512]{1,0:T(8,128)(2,1)S(1)}, u32[]{:S(2)}, u32[]{:S(2)}) collective-permute-start(bf16[96,512]{1,0:T(8,128)(2,1)S(1)} %fusion.30), channel_id=1, source_target_pairs={{0,96},{32,64},{64,32},{96,0},{1,97},{33,65},{65,33},{97,1},{2,98}... | collective-permute-start | bytes 294920 | tf_op jit(solution)/shard_map/ppermute | solution.py:31
  149.1 4.7 %collective-permute-start.13 = (bf16[96,512]{1,0:T(8,128)(2,1)S(1)}, bf16[96,512]{1,0:T(8,128)(2,1)S(1)}, u32[]{:S(2)}, u32[]{:S(2)}) collective-permute-start(bf16[96,512]{1,0:T(8,128)(2,1)S(1)} %fusion.28), channel_id=1, source_target_pairs={{0,32},{32,0},{64,96},{96,64},{1,33},{33,1},{65,97},{97,65},{2,34}... | collective-permute-start | bytes 294920 | tf_op jit(solution)/shard_map/ppermute | solution.py:31
  149.8 6.6 %copy-start.5 = (bf16[192,1024]{1,0:T(8,128)(2,1)}, bf16[192,1024]{1,0:T(8,128)(2,1)S(1)}, u32[]{:S(2)}) copy-start(bf16[192,1024]{1,0:T(8,128)(2,1)S(1)} %pad_maximum_fusion.7.refs_2_) | copy-start | bytes 1179652
  149.8 11.8 %collective-permute-start.15 = (bf16[192,1024]{1,0:T(8,128)(2,1)S(1)}, bf16[192,1024]{1,0:T(8,128)(2,1)S(1)}, u32[]{:S(2)}, u32[]{:S(2)}) collective-permute-start(bf16[192,1024]{1,0:T(8,128)(2,1)S(1)} %pad_maximum_fusion.7.refs_2_), channel_id=1, source_target_pairs={{0,96},{32,64},{64,32},{96,0},{1,97},{33,65},{65,33},{97,1},{2,98}... | collective-permute-start | bytes 1179656 | tf_op jit(solution)/shard_map/ppermute | solution.py:31
  161.6 0.8 copy-start.9
  164.7 3.1 %copy-start.22 = (bf16[96,1024]{1,0:T(8,128)(2,1)S(1)}, bf16[96,1024]{1,0:T(8,128)(2,1)}, u32[]{:S(2)}) copy-start(bf16[96,1024]{1,0:T(8,128)(2,1)} %get-tuple-element.72) | copy-start | bytes 589828
  167.4 6.5 %collective-permute-start.16 = (bf16[192,512]{1,0:T(8,128)(2,1)S(1)}, bf16[192,512]{1,0:T(8,128)(2,1)S(1)}, u32[]{:S(2)}, u32[]{:S(2)}) collective-permute-start(bf16[192,512]{1,0:T(8,128)(2,1)S(1)} %get-tuple-element.58), channel_id=1, source_target_pairs={{0,32},{32,0},{64,96},{96,64},{1,33},{33,1},{65,97},{97,65},{2,34}... | collective-permute-start | bytes 589832 | tf_op jit(solution)/shard_map/ppermute | solution.py:31
  167.7 13.5 %collective-permute-start.20 = (bf16[96,1024]{1,0:T(8,128)(2,1)S(1)}, bf16[96,1024]{1,0:T(8,128)(2,1)S(1)}, u32[]{:S(2)}, u32[]{:S(2)}) collective-permute-start(bf16[96,1024]{1,0:T(8,128)(2,1)S(1)} %copy-done.22), channel_id=1, source_target_pairs={{0,96},{32,64},{64,32},{96,0},{1,97},{33,65},{65,33},{97,1},{2,98}... | collective-permute-start | bytes 589832 | tf_op jit(solution)/shard_map/ppermute | solution.py:31
  170.3 10.2 %collective-permute-start.18 = (bf16[192,512]{1,0:T(8,128)(2,1)S(1)}, bf16[192,512]{1,0:T(8,128)(2,1)S(1)}, u32[]{:S(2)}, u32[]{:S(2)}) collective-permute-start(bf16[192,512]{1,0:T(8,128)(2,1)S(1)} %get-tuple-element.60), channel_id=1, source_target_pairs={{0,96},{32,64},{64,32},{96,0},{1,97},{33,65},{65,33},{97,1},{2,98}... | collective-permute-start | bytes 589832 | tf_op jit(solution)/shard_map/ppermute | solution.py:31
  174.0 8.8 %collective-permute-start.17 = (bf16[96,512]{1,0:T(8,128)(2,1)S(1)}, bf16[96,512]{1,0:T(8,128)(2,1)S(1)}, u32[]{:S(2)}, u32[]{:S(2)}) collective-permute-start(bf16[96,512]{1,0:T(8,128)(2,1)S(1)} %fusion.26), channel_id=1, source_target_pairs={{0,96},{32,64},{64,32},{96,0},{1,97},{33,65},{65,33},{97,1},{2,98}... | collective-permute-start | bytes 294920 | tf_op jit(solution)/shard_map/ppermute | solution.py:31
  180.6 5.8 %collective-permute-start.19 = (bf16[96,512]{1,0:T(8,128)(2,1)S(1)}, bf16[96,512]{1,0:T(8,128)(2,1)S(1)}, u32[]{:S(2)}, u32[]{:S(2)}) collective-permute-start(bf16[96,512]{1,0:T(8,128)(2,1)S(1)} %fusion.24), channel_id=1, source_target_pairs={{0,32},{32,0},{64,96},{96,64},{1,33},{33,1},{65,97},{97,65},{2,34}... | collective-permute-start | bytes 294920 | tf_op jit(solution)/shard_map/ppermute | solution.py:31
  181.3 14.4 %collective-permute-start.21 = (bf16[192,1024]{1,0:T(8,128)(2,1)S(1)}, bf16[192,1024]{1,0:T(8,128)(2,1)S(1)}, u32[]{:S(2)}, u32[]{:S(2)}) collective-permute-start(bf16[192,1024]{1,0:T(8,128)(2,1)S(1)} %pad_maximum_fusion.9.refs_4_), channel_id=1, source_target_pairs={{0,32},{32,0},{64,96},{96,64},{1,33},{33,1},{65,97},{97,65},{2,34}... | collective-permute-start | bytes 1179656 | tf_op jit(solution)/shard_map/ppermute | solution.py:31
  182.8 9.3 %copy-start.11 = (f32[96,1536]{1,0:T(8,128)S(1)}, f32[96,1536]{1,0:T(8,128)}, u32[]{:S(2)}) copy-start(f32[96,1536]{1,0:T(8,128)} %get-tuple-element.81) | copy-start | bytes 1769476
  182.8 9.3 %copy-start.12 = (f32[96,1536]{1,0:T(8,128)S(1)}, f32[96,1536]{1,0:T(8,128)}, u32[]{:S(2)}) copy-start(f32[96,1536]{1,0:T(8,128)} %get-tuple-element.82) | copy-start | bytes 1769476
  182.8 9.3 %copy-start.15 = (f32[96,1024]{1,0:T(8,128)S(1)}, f32[96,1024]{1,0:T(8,128)}, u32[]{:S(2)}) copy-start(f32[96,1024]{1,0:T(8,128)} %get-tuple-element.77) | copy-start | bytes 1179652
  182.9 9.3 %copy-start.16 = (f32[96,1024]{1,0:T(8,128)S(1)}, f32[96,1024]{1,0:T(8,128)}, u32[]{:S(2)}) copy-start(f32[96,1024]{1,0:T(8,128)} %get-tuple-element.78) | copy-start | bytes 1179652
  182.9 9.3 %copy-start.18 = (f32[96,1024]{1,0:T(8,128)S(1)}, f32[96,1024]{1,0:T(8,128)}, u32[]{:S(2)}) copy-start(f32[96,1024]{1,0:T(8,128)} %get-tuple-element.73) | copy-start | bytes 1179652
  182.9 9.3 %copy-start.19 = (f32[96,1024]{1,0:T(8,128)S(1)}, f32[96,1024]{1,0:T(8,128)}, u32[]{:S(2)}) copy-start(f32[96,1024]{1,0:T(8,128)} %get-tuple-element.74) | copy-start | bytes 1179652
  188.0 10.1 %collective-permute-start.24 = (bf16[96,1024]{1,0:T(8,128)(2,1)S(1)}, bf16[96,1024]{1,0:T(8,128)(2,1)S(1)}, u32[]{:S(2)}, u32[]{:S(2)}) collective-permute-start(bf16[96,1024]{1,0:T(8,128)(2,1)S(1)} %get-tuple-element.68.refs_1_), channel_id=1, source_target_pairs={{0,96},{32,64},{64,32},{96,0},{1,97},{33,65},{65,33},{97,1},{2,98}... | collective-permute-start | bytes 589832 | tf_op jit(solution)/shard_map/ppermute | solution.py:31
  190.6 8.9 %collective-permute-start.23 = (bf16[96,1024]{1,0:T(8,128)(2,1)S(1)}, bf16[96,1024]{1,0:T(8,128)(2,1)S(1)}, u32[]{:S(2)}, u32[]{:S(2)}) collective-permute-start(bf16[96,1024]{1,0:T(8,128)(2,1)S(1)} %get-tuple-element.68.refs_1_), channel_id=1, source_target_pairs={{0,64},{32,96},{64,0},{96,32},{1,65},{33,97},{65,1},{97,33},{2,66}... | collective-permute-start | bytes 589832 | tf_op jit(solution)/shard_map/ppermute | solution.py:31
  190.7 8.9 %collective-permute-start.22 = (bf16[96,1024]{1,0:T(8,128)(2,1)S(1)}, bf16[96,1024]{1,0:T(8,128)(2,1)S(1)}, u32[]{:S(2)}, u32[]{:S(2)}) collective-permute-start(bf16[96,1024]{1,0:T(8,128)(2,1)S(1)} %get-tuple-element.68.refs_1_), channel_id=1, source_target_pairs={{0,32},{32,0},{64,96},{96,64},{1,33},{33,1},{65,97},{97,65},{2,34}... | collective-permute-start | bytes 589832 | tf_op jit(solution)/shard_map/ppermute | solution.py:31
  192.2 2.1 %copy-start.13 = (f32[96,1536]{1,0:T(8,128)S(1)}, f32[96,1536]{1,0:T(8,128)}, u32[]{:S(2)}) copy-start(f32[96,1536]{1,0:T(8,128)} %get-tuple-element.83) | copy-start | bytes 1769476
  192.2 2.1 %copy-start.14 = (f32[96,1024]{1,0:T(8,128)S(1)}, f32[96,1024]{1,0:T(8,128)}, u32[]{:S(2)}) copy-start(f32[96,1024]{1,0:T(8,128)} %get-tuple-element.79) | copy-start | bytes 1179652
  192.2 2.1 %copy-start.17 = (f32[96,1024]{1,0:T(8,128)S(1)}, f32[96,1024]{1,0:T(8,128)}, u32[]{:S(2)}) copy-start(f32[96,1024]{1,0:T(8,128)} %get-tuple-element.75) | copy-start | bytes 1179652
  194.3 1.4 copy-start.4
  194.3 1.4 copy-start.6
  194.3 2.0 copy-start.8
  194.3 2.1 %copy-start.10 = (bf16[192,1024]{1,0:T(8,128)(2,1)S(1)}, bf16[192,1024]{1,0:T(8,128)(2,1)}, u32[]{:S(2)}) copy-start(bf16[192,1024]{1,0:T(8,128)(2,1)} %copy-done.9) | copy-start | bytes 1179652

commit v7 on v6

--- a/solution.py
+++ b/solution.py
@@ -18,7 +18,7 @@
 GROUPS = 4
 OWNERS = 32
 CAPACITY = 32
-UNITS = (12, 8, 8, 8)
+UNITS = (10, 10, 10, 6)
 HALVES = ((1, 3), (3, 1))
 MIB = 1024 * 1024
 
@@ -183,7 +183,7 @@
         earlier_work = (target, picked) if number == 1 else rows[: max(0, number - 1)]
         outgoing = after(outgoing, arrived, earlier_work)
         arrived = lax.all_to_all(outgoing, "vocab", split_axis=0, concat_axis=0, tiled=True)
-        ready = after(arrived, rows, blocks if number == last else ())
+        ready = after(arrived, (rows[:-1], onwards) if number == last else rows)
         sums = combine(here, target, head_grad, ready, span.start)
         grads, onwards = [], []
         for side, (one, two) in enumerate(HALVES):

time: 202 us -> 204 us (level)
  starting transfers between devices: 64.8 us -> 51.2 us
  waiting for transfers between devices: 82 us -> 92 us
  Pallas kernels: 12.7 us -> 15.7 us
  other arithmetic: 16.5 us -> 19.2 us
    ppermute x25, starting transfers between devices: 39.7 us -> 29.1 us  [swap_z(): return lax.ppermute(block, 'dp', [(i, i ^ flip) for i in range(GROUPS)])]
    all_to_all x4, waiting for transfers between devices: 32.6 us -> 39.5 us  [local(): lax.all_to_all(outgoing, 'vocab', split_axis=0, concat_axis=0, tiled=True)]
    ppermute x25, waiting for transfers between devices: 49.4 us -> 52.6 us  [swap_z(): return lax.ppermute(block, 'dp', [(i, i ^ flip) for i in range(GROUPS)])]
    all_to_all x4, starting transfers between devices: 25.1 us -> 22.1 us  [local(): lax.all_to_all(outgoing, 'vocab', split_axis=0, concat_axis=0, tiled=True)]
    unnamed x49 -> x45, local copies, waits for them, and re-layouts: 6.45 us -> 6.91 us
  transfers between devices with their start and end apart: 29 -> 29, of which waited for: 19 -> 20; matrix products, arithmetic and copies ran while one was open for 13% -> 15% of each run, Pallas kernels for 5% -> 5%
where the time goes in v7:
time: 204 us; the launch traced here: 203 us
  waiting for transfers between devices  92 us (45%)
  starting transfers between devices  51.2 us (25%)
  other arithmetic  19.2 us (9%)
  matrix products  16.9 us (8%)
  Pallas kernels  15.7 us (8%)
  local copies, waits for them, and re-layouts  7.02 us (3%)
    ppermute x25, waiting for transfers between devices, swap_z(): return lax.ppermute(block, 'dp', [(i, i ^ flip) for i in range(GROUPS)])  52.6 us
    all_to_all x4, waiting for transfers between devices, local(): lax.all_to_all(outgoing, 'vocab', split_axis=0, concat_axis=0, tiled=True)  39.5 us
    ppermute x25, starting transfers between devices, swap_z(): return lax.ppermute(block, 'dp', [(i, i ^ flip) for i in range(GROUPS)])  29.1 us
    all_to_all x4, starting transfers between devices, local(): lax.all_to_all(outgoing, 'vocab', split_axis=0, concat_axis=0, tiled=True)  22.1 us
    dot_general x4, matrix products, local(): jnp.dot(dispatch, input_grad[:, span], preferred_element_type=jnp.float32)  16.5 us
    pallas_call x4, Pallas kernels, combine(): pl.pallas_call(combine_body, grid=(2,), out_shape=[kept, sent] * 2, in_sp...  12 us
    convert_element_type x4, other arithmetic, local(): rows.append(states[-1][0].astype(jnp.bfloat16))  8.7 us
    unnamed x45, local copies, waits for them, and re-layouts  6.91 us
  transfers between devices with their start and end apart: 29, of which 20 were waited for; matrix products, arithmetic and copies ran while one was open for 15% of the time, Pallas kernels for 5%

profile of v7, /device:TPU:0, one launch (start us, length us, event | category | flops | bytes accessed | tf_op | source)
XLA Modules:
  0.0 203.3 jit_solution(3024266665694825878)
XLA Ops:
  0.6 0.5 broadcast.106
  1.1 1.6 reduce.7
  3.1 4.4 %convolution_convert_fusion.2 = bf16[1024,1280]{1,0:T(8,128)(2,1)} fusion(bf16[512,4608]{1,0:T(8,128)(2,1)} %param.7, s32[512]{0:T(512)S(1)} %bitcast.20), kind=kOutput, calls=%fused_computation.2 | convolution fusion | flops 1344012288 | bytes 3934208 | tf_op jit(solution)/shard_map/dot_general | solution.py:178
  7.5 7.5 %all-to-all-start = ((bf16[32,32,1280]{2,1,0:T(8,128)(2,1)}), bf16[32,32,1280]{2,1,0:T(8,128)(2,1)S(1)}, u32[]{:S(2)}, u32[]{:S(2)}) async-start(bf16[32,32,1280]{2,1,0:T(8,128)(2,1)} %bitcast.17), calls=%async_computation | async-start | bytes 5242880 | tf_op jit(solution)/shard_map/all_to_all | solution.py:185
  15.5 0.6 select_reduce_fusion
  16.2 3.3 %fusion.2 = bf16[1024,768]{1,0:T(8,128)(2,1)} fusion(s32[512]{0:T(512)S(1)} %bitcast.21, bf16[512,4608]{1,0:T(8,128)(2,1)} %param.7), kind=kOutput, calls=%fused_computation.11 | convolution fusion | flops 806617088 | bytes 2361344 | tf_op jit(solution)/shard_map/dot_general | solution.py:178
  19.5 4.4 %convolution_convert_fusion = bf16[1024,1280]{1,0:T(8,128)(2,1)} fusion(bf16[512,4608]{1,0:T(8,128)(2,1)} %param.7, s32[512]{0:T(512)S(1)} %bitcast.22), kind=kOutput, calls=%fused_computation | convolution fusion | flops 1344012288 | bytes 3934208 | tf_op jit(solution)/shard_map/dot_general | solution.py:178
  23.9 4.4 %convolution_convert_fusion.1 = bf16[1024,1280]{1,0:T(8,128)(2,1)} fusion(bf16[512,4608]{1,0:T(8,128)(2,1)} %param.7, s32[512]{0:T(512)S(1)} %bitcast.23), kind=kOutput, calls=%fused_computation.1 | convolution fusion | flops 1344012288 | bytes 3934208 | tf_op jit(solution)/shard_map/dot_general | solution.py:178
  28.3 21.4 %all-to-all-done = bf16[32,32,1280]{2,1,0:T(8,128)(2,1)S(1)} async-done(((bf16[32,32,1280]{2,1,0:T(8,128)(2,1)}), bf16[32,32,1280]{2,1,0:T(8,128)(2,1)S(1)}, u32[]{:S(2)}, u32[]{:S(2)}) %all-to-all-start) | async-done | bytes 2621472 | tf_op jit(solution)/shard_map/all_to_all | solution.py:185
  49.7 1.5 copy-done.1
  51.2 5.1 %all-to-all-start.1 = ((bf16[32,32,1280]{2,1,0:T(8,128)(2,1)}), bf16[32,32,1280]{2,1,0:T(8,128)(2,1)}, u32[]{:S(2)}, u32[]{:S(2)}) async-start(bf16[32,32,1280]{2,1,0:T(8,128)(2,1)} %bitcast.16), calls=%async_computation.1 | async-start | bytes 5242880 | tf_op jit(solution)/shard_map/all_to_all | solution.py:185
  56.3 1.7 copy-done.2
  58.0 2.2 %shard_map.102 = (f32[192,640]{1,0:T(8,128)S(1)}, bf16[192,640]{1,0:T(8,128)(2,1)S(1)}, f32[192,640]{1,0:T(8,128)S(1)}, bf16[192,640]{1,0:T(8,128)(2,1)S(1)}) custom-call(s32[1]{0:T(128)} %bitcast.here_ref, s32[1,1024]{1,0:T(1,128)S(1)} %sub.19.target_ref, bf16[1,384,4608]{2,1,0:T(8,128)(2,1)S(1)} %copy-done, bf16[1024,1280]{1,0:T(8,128)(2,1)S(1)} %bitcast.14), custom_call_target="tpu_custom_call" | custom-call | flops 1006632960 | bytes 5079040 | tf_op jit(solution)/shard_map/pallas_call | solution.py:79
  60.2 4.1 %collective-permute-start.2 = (bf16[192,640]{1,0:T(8,128)(2,1)S(1)}, bf16[192,640]{1,0:T(8,128)(2,1)S(1)}, u32[]{:S(2)}, u32[]{:S(2)}) collective-permute-start(bf16[192,640]{1,0:T(8,128)(2,1)S(1)} %get-tuple-element.39), channel_id=1, source_target_pairs={{0,96},{32,64},{64,32},{96,0},{1,97},{33,65},{65,33},{97,1},{2,98}... | collective-permute-start | bytes 737288 | tf_op jit(solution)/shard_map/ppermute | solution.py:31
  64.4 6.2 %collective-permute-done.2 = bf16[192,640]{1,0:T(8,128)(2,1)S(1)} collective-permute-done((bf16[192,640]{1,0:T(8,128)(2,1)S(1)}, bf16[192,640]{1,0:T(8,128)(2,1)S(1)}, u32[]{:S(2)}, u32[]{:S(2)}) %collective-permute-start.2) | collective-permute-done | bytes 245792 | tf_op jit(solution)/shard_map/ppermute | solution.py:31
  70.7 1.3 collective-permute-done
  72.1 1.8 collective-permute-start.1
  73.9 1.8 collective-permute-done.3
  75.7 2.6 %collective-permute-done.1 = bf16[96,640]{1,0:T(8,128)(2,1)S(1)} collective-permute-done((bf16[96,640]{1,0:T(8,128)(2,1)S(1)}, bf16[96,640]{1,0:T(8,128)(2,1)S(1)}, u32[]{:S(2)}, u32[]{:S(2)}) %collective-permute-start.1) | collective-permute-done | bytes 122912 | tf_op jit(solution)/shard_map/ppermute | solution.py:31
  78.3 2.8 %fusion.39 = (bf16[96,1280]{1,0:T(8,128)(2,1)}, f32[96,1280]{1,0:T(8,128)}, f32[96,1280]{1,0:T(8,128)}, f32[96,1280]{1,0:T(8,128)}) fusion(f32[96,4608]{1,0:T(8,128)} %param.11, f32[96,640]{1,0:T(8,128)S(1)} %fusion.25, f32[96,640]{1,0:T(8,128)S(1)} %fusion.27, f32[96,4608]{1,0:T(8,128)} %param.12, f32[96,4608]{1,0:T(8,128)} %param.13), kind=kLoop, calls=%fused_computation.89 | loop fusion | flops 2088960 | bytes 3686400 | tf_op jit(solution)/shard_map/convert_element_type | solution.py:214
  81.1 9.8 %all-to-all-done.1 = bf16[32,32,1280]{2,1,0:T(8,128)(2,1)} async-done(((bf16[32,32,1280]{2,1,0:T(8,128)(2,1)}), bf16[32,32,1280]{2,1,0:T(8,128)(2,1)}, u32[]{:S(2)}, u32[]{:S(2)}) %all-to-all-start.1) | async-done | bytes 2621472 | tf_op jit(solution)/shard_map/all_to_all | solution.py:185
  90.9 4.8 %all-to-all-start.2 = ((bf16[32,32,1280]{2,1,0:T(8,128)(2,1)}), bf16[32,32,1280]{2,1,0:T(8,128)(2,1)}, u32[]{:S(2)}, u32[]{:S(2)}) async-start(bf16[32,32,1280]{2,1,0:T(8,128)(2,1)} %bitcast.15), calls=%async_computation.2 | async-start | bytes 5242880 | tf_op jit(solution)/shard_map/all_to_all | solution.py:185
  95.7 4.3 %collective-permute-start.8 = (bf16[96,1280]{1,0:T(8,128)(2,1)}, bf16[96,1280]{1,0:T(8,128)(2,1)S(1)}, u32[]{:S(2)}, u32[]{:S(2)}) collective-permute-start(bf16[96,1280]{1,0:T(8,128)(2,1)} %get-tuple-element.80), channel_id=1, source_target_pairs={{0,96},{32,64},{64,32},{96,0},{1,97},{33,65},{65,33},{97,1},{2,98}... | collective-permute-start | bytes 737288 | tf_op jit(solution)/shard_map/ppermute | solution.py:31
  100.0 3.2 %shard_map.103 = (f32[192,640]{1,0:T(8,128)S(1)}, bf16[192,640]{1,0:T(8,128)(2,1)S(1)}, f32[192,640]{1,0:T(8,128)S(1)}, bf16[192,640]{1,0:T(8,128)(2,1)S(1)}) custom-call(s32[1]{0:T(128)} %bitcast.here_ref, s32[1,1024]{1,0:T(1,128)S(1)} %sub.19.target_ref, bf16[1,384,4608]{2,1,0:T(8,128)(2,1)S(1)} %copy-done, bf16[1024,1280]{1,0:T(8,128)(2,1)} %bitcast.7.part_ref), custom_call_target="tpu_custom_call" | custom-call | flops 1006632960 | bytes 5079040 | tf_op jit(solution)/shard_map/pallas_call | solution.py:79
  103.4 3.2 %collective-permute-done.8 = bf16[96,1280]{1,0:T(8,128)(2,1)S(1)} collective-permute-done((bf16[96,1280]{1,0:T(8,128)(2,1)}, bf16[96,1280]{1,0:T(8,128)(2,1)S(1)}, u32[]{:S(2)}, u32[]{:S(2)}) %collective-permute-start.8) | collective-permute-done | bytes 245792 | tf_op jit(solution)/shard_map/ppermute | solution.py:31
  106.7 0.3 collective-permute-start.9
  107.0 5.2 %collective-permute-done.6 = bf16[192,640]{1,0:T(8,128)(2,1)S(1)} collective-permute-done((bf16[192,640]{1,0:T(8,128)(2,1)S(1)}, bf16[192,640]{1,0:T(8,128)(2,1)S(1)}, u32[]{:S(2)}, u32[]{:S(2)}) %collective-permute-start.6) | collective-permute-done | bytes 245792 | tf_op jit(solution)/shard_map/ppermute | solution.py:31
  112.5 3.1 %collective-permute-start.5 = (bf16[96,640]{1,0:T(8,128)(2,1)S(1)}, bf16[96,640]{1,0:T(8,128)(2,1)S(1)}, u32[]{:S(2)}, u32[]{:S(2)}) collective-permute-start(bf16[96,640]{1,0:T(8,128)(2,1)S(1)} %fusion.22), channel_id=1, source_target_pairs={{0,96},{32,64},{64,32},{96,0},{1,97},{33,65},{65,33},{97,1},{2,98}... | collective-permute-start | bytes 368648 | tf_op jit(solution)/shard_map/ppermute | solution.py:31
  115.6 8.7 %collective-permute-done.7 = bf16[96,640]{1,0:T(8,128)(2,1)S(1)} collective-permute-done((bf16[96,640]{1,0:T(8,128)(2,1)S(1)}, bf16[96,640]{1,0:T(8,128)(2,1)S(1)}, u32[]{:S(2)}, u32[]{:S(2)}) %collective-permute-start.7) | collective-permute-done | bytes 122912 | tf_op jit(solution)/shard_map/ppermute | solution.py:31
  124.4 0.8 copy-done.5
  125.2 2.8 %fusion.37 = (bf16[96,1280]{1,0:T(8,128)(2,1)}, f32[96,1280]{1,0:T(8,128)}, f32[96,1280]{1,0:T(8,128)}, f32[96,1280]{1,0:T(8,128)}) fusion(f32[96,4608]{1,0:T(8,128)} %param.11, f32[96,1280]{1,0:T(8,128)S(1)} %pad_maximum_fusion.4, f32[96,4608]{1,0:T(8,128)} %param.12, f32[96,4608]{1,0:T(8,128)} %param.13), kind=kLoop, calls=%fused_computation.88 | loop fusion | flops 1966080 | bytes 3686400 | tf_op jit(solution)/shard_map/convert_element_type | solution.py:214
  128.0 2.3 %all-to-all-done.2 = bf16[32,32,1280]{2,1,0:T(8,128)(2,1)} async-done(((bf16[32,32,1280]{2,1,0:T(8,128)(2,1)}), bf16[32,32,1280]{2,1,0:T(8,128)(2,1)}, u32[]{:S(2)}, u32[]{:S(2)}) %all-to-all-start.2) | async-done | bytes 2621472 | tf_op jit(solution)/shard_map/all_to_all | solution.py:185
  130.3 3.9 %shard_map.104 = (f32[192,640]{1,0:T(8,128)S(1)}, bf16[192,640]{1,0:T(8,128)(2,1)S(1)}, f32[192,640]{1,0:T(8,128)S(1)}, bf16[192,640]{1,0:T(8,128)(2,1)}) custom-call(s32[1]{0:T(128)} %bitcast.here_ref, s32[1,1024]{1,0:T(1,128)S(1)} %sub.19.target_ref, bf16[1,384,4608]{2,1,0:T(8,128)(2,1)S(1)} %copy-done, bf16[1024,1280]{1,0:T(8,128)(2,1)} %bitcast.9.part_ref), custom_call_target="tpu_custom_call" | custom-call | flops 1006632960 | bytes 5079040 | tf_op jit(solution)/shard_map/pallas_call | solution.py:79
  134.2 0.8 copy-done.7
  135.0 0.8 copy-done.9
  135.8 0.7 copy-done.11
  136.5 4.0 %collective-permute-start.12 = (bf16[192,640]{1,0:T(8,128)(2,1)}, bf16[192,640]{1,0:T(8,128)(2,1)}, u32[]{:S(2)}, u32[]{:S(2)}) collective-permute-start(bf16[192,640]{1,0:T(8,128)(2,1)} %get-tuple-element.52), channel_id=1, source_target_pairs={{0,96},{32,64},{64,32},{96,0},{1,97},{33,65},{65,33},{97,1},{2,98}... | collective-permute-start | bytes 737288 | tf_op jit(solution)/shard_map/ppermute | solution.py:31
  140.5 4.7 %all-to-all-start.3 = ((bf16[32,32,768]{2,1,0:T(8,128)(2,1)}), bf16[32,32,768]{2,1,0:T(8,128)(2,1)}, u32[]{:S(2)}, u32[]{:S(2)}) async-start(bf16[32,32,768]{2,1,0:T(8,128)(2,1)} %bitcast.18), calls=%async_computation.3 | async-start | bytes 3145728 | tf_op jit(solution)/shard_map/all_to_all | solution.py:185
  145.3 2.0 collective-permute-start.14
  147.3 1.0 convert_element_type.140
  148.3 1.0 fusion.16
  149.5 4.9 %collective-permute-done.10 = bf16[192,640]{1,0:T(8,128)(2,1)S(1)} collective-permute-done((bf16[192,640]{1,0:T(8,128)(2,1)}, bf16[192,640]{1,0:T(8,128)(2,1)S(1)}, u32[]{:S(2)}, u32[]{:S(2)}) %collective-permute-start.10) | collective-permute-done | bytes 245792 | tf_op jit(solution)/shard_map/ppermute | solution.py:31
  154.5 5.1 %collective-permute-done.14 = bf16[96,1280]{1,0:T(8,128)(2,1)S(1)} collective-permute-done((bf16[96,1280]{1,0:T(8,128)(2,1)}, bf16[96,1280]{1,0:T(8,128)(2,1)S(1)}, u32[]{:S(2)}, u32[]{:S(2)}) %collective-permute-start.14) | collective-permute-done | bytes 245792 | tf_op jit(solution)/shard_map/ppermute | solution.py:31
  159.6 0.8 pad_maximum_fusion.7.refs_2_
  160.4 0.9 collective-permute-done.13
  161.5 0.8 pad_maximum_fusion.6
  162.3 6.0 %all-to-all-done.3 = bf16[32,32,768]{2,1,0:T(8,128)(2,1)} async-done(((bf16[32,32,768]{2,1,0:T(8,128)(2,1)}), bf16[32,32,768]{2,1,0:T(8,128)(2,1)}, u32[]{:S(2)}, u32[]{:S(2)}) %all-to-all-start.3) | async-done | bytes 1572896 | tf_op jit(solution)/shard_map/all_to_all | solution.py:185
  168.3 2.6 %shard_map.105 = (f32[192,384]{1,0:T(8,128)S(1)}, bf16[192,384]{1,0:T(8,128)(2,1)S(1)}, f32[192,384]{1,0:T(8,128)S(1)}, bf16[192,384]{1,0:T(8,128)(2,1)S(1)}) custom-call(s32[1]{0:T(128)} %bitcast.here_ref, s32[1,1024]{1,0:T(1,128)S(1)} %sub.19.target_ref, bf16[1,384,4608]{2,1,0:T(8,128)(2,1)S(1)} %copy-done, bf16[1024,768]{1,0:T(8,128)(2,1)} %bitcast.11.part_ref), custom_call_target="tpu_custom_call" | custom-call | flops 603979776 | bytes 3047424 | tf_op jit(solution)/shard_map/pallas_call | solution.py:79
  171.0 1.7 fusion.35
  172.8 3.3 %collective-permute-start.20 = (bf16[96,1280]{1,0:T(8,128)(2,1)S(1)}, bf16[96,1280]{1,0:T(8,128)(2,1)S(1)}, u32[]{:S(2)}, u32[]{:S(2)}) collective-permute-start(bf16[96,1280]{1,0:T(8,128)(2,1)S(1)} %get-tuple-element.72), channel_id=1, source_target_pairs={{0,96},{32,64},{64,32},{96,0},{1,97},{33,65},{65,33},{97,1},{2,98}... | collective-permute-start | bytes 737288 | tf_op jit(solution)/shard_map/ppermute | solution.py:31
  176.0 2.9 %collective-permute-done.17 = bf16[192,384]{1,0:T(8,128)(2,1)S(1)} collective-permute-done((bf16[192,384]{1,0:T(8,128)(2,1)S(1)}, bf16[192,384]{1,0:T(8,128)(2,1)S(1)}, u32[]{:S(2)}, u32[]{:S(2)}) %collective-permute-start.17) | collective-permute-done | bytes 147488 | tf_op jit(solution)/shard_map/ppermute | solution.py:31
  179.1 2.8 %collective-permute-done.15 = bf16[192,384]{1,0:T(8,128)(2,1)S(1)} collective-permute-done((bf16[192,384]{1,0:T(8,128)(2,1)S(1)}, bf16[192,384]{1,0:T(8,128)(2,1)S(1)}, u32[]{:S(2)}, u32[]{:S(2)}) %collective-permute-start.15) | collective-permute-done | bytes 147488 | tf_op jit(solution)/shard_map/ppermute | solution.py:31
  181.9 0.5 collective-permute-start.16
  182.4 0.7 collective-permute-done.20
  183.2 0.2 collective-permute-done.18
  183.5 4.1 %collective-permute-done.16 = bf16[96,384]{1,0:T(8,128)(2,1)S(1)} collective-permute-done((bf16[96,384]{1,0:T(8,128)(2,1)S(1)}, bf16[96,384]{1,0:T(8,128)(2,1)S(1)}, u32[]{:S(2)}, u32[]{:S(2)}) %collective-permute-start.16) | collective-permute-done | bytes 73760 | tf_op jit(solution)/shard_map/ppermute | solution.py:31
  187.6 1.4 fusion.33
  189.1 1.8 collective-permute-start.23
  190.9 2.9 %collective-permute-start.24 = (bf16[96,768]{1,0:T(8,128)(2,1)S(1)}, bf16[96,768]{1,0:T(8,128)(2,1)S(1)}, u32[]{:S(2)}, u32[]{:S(2)}) collective-permute-start(bf16[96,768]{1,0:T(8,128)(2,1)S(1)} %get-tuple-element.68.refs_1_), channel_id=1, source_target_pairs={{0,96},{32,64},{64,32},{96,0},{1,97},{33,65},{65,33},{97,1},{2,98}... | collective-permute-start | bytes 442376 | tf_op jit(solution)/shard_map/ppermute | solution.py:31
  193.8 2.2 %pad_maximum_fusion = (f32[96,4608]{1,0:T(8,128)}, f32[96,4608]{1,0:T(8,128)}) fusion(f32[96,768]{1,0:T(8,128)S(1)} %get-tuple-element.69, f32[96,1280]{1,0:T(8,128)S(1)} %get-tuple-element.73, f32[96,1280]{1,0:T(8,128)S(1)} %copy-done.16, f32[96,1280]{1,0:T(8,128)S(1)} %copy-done.14, f32[96,768]{1,0:T(8,128)S(1)} %get-tuple-element.70, ...), kind=kLoop, calls=%fused_computation.8 | loop fusion | flops 2654208 | bytes 7077888 | tf_op jit(solution)/shard_map/concatenate | solution.py:221
  196.0 1.4 pad_maximum_fusion.2
  197.4 2.9 %shard_map.106.refs_0_ = bf16[384,4608]{1,0:T(8,128)(2,1)} custom-call(s32[1]{0:T(128)} %bitcast.here_ref, bf16[192,1280]{1,0:T(8,128)(2,1)S(1)} %copy-done.4, bf16[192,1280]{1,0:T(8,128)(2,1)S(1)} %copy-done.6, bf16[192,1280]{1,0:T(8,128)(2,1)} %pad_maximum_fusion.7.refs_2_, bf16[192,1280]{1,0:T(8,128)(2,1)} %collective-permute-done.19.refs_3_, ...), custom_call_target="tpu_custom_call" | custom-call | bytes 5898240 | tf_op jit(solution)/shard_map/pallas_call | solution.py:117
  200.3 2.0 collective-permute-done.23.refs_3_
  202.3 0.8 shard_map.107
  (97 shorter events, 2.8 us)
Async XLA Ops:
  7.5 7.5 %copy-start.21 = (s32[16384,1]{0,1:T(1,128)S(1)}, s32[16384,1]{0,1:T(1,128)}, u32[]{:S(2)}) copy-start(s32[16384,1]{0,1:T(1,128)} %param.9) | copy-start | bytes 196612
  7.5 42.2 %all-to-all-start = ((bf16[32,32,1280]{2,1,0:T(8,128)(2,1)}), bf16[32,32,1280]{2,1,0:T(8,128)(2,1)S(1)}, u32[]{:S(2)}, u32[]{:S(2)}) async-start(bf16[32,32,1280]{2,1,0:T(8,128)(2,1)} %bitcast.17), calls=%async_computation | async-start | bytes 5242880 | tf_op jit(solution)/shard_map/all_to_all | solution.py:185
  49.7 1.5 copy-start.1
  51.2 5.1 %copy-start = (bf16[1,384,4608]{2,1,0:T(8,128)(2,1)S(1)}, bf16[1,384,4608]{2,1,0:T(8,128)(2,1)}, u32[]{:S(2)}) copy-start(bf16[1,384,4608]{2,1,0:T(8,128)(2,1)} %head_ref.7) | copy-start | bytes 10616836
  51.2 39.7 %all-to-all-start.1 = ((bf16[32,32,1280]{2,1,0:T(8,128)(2,1)}), bf16[32,32,1280]{2,1,0:T(8,128)(2,1)}, u32[]{:S(2)}, u32[]{:S(2)}) async-start(bf16[32,32,1280]{2,1,0:T(8,128)(2,1)} %bitcast.16), calls=%async_computation.1 | async-start | bytes 5242880 | tf_op jit(solution)/shard_map/all_to_all | solution.py:185
  56.3 1.7 copy-start.2
  60.2 10.3 %collective-permute-start.2 = (bf16[192,640]{1,0:T(8,128)(2,1)S(1)}, bf16[192,640]{1,0:T(8,128)(2,1)S(1)}, u32[]{:S(2)}, u32[]{:S(2)}) collective-permute-start(bf16[192,640]{1,0:T(8,128)(2,1)S(1)} %get-tuple-element.39), channel_id=1, source_target_pairs={{0,96},{32,64},{64,32},{96,0},{1,97},{33,65},{65,33},{97,1},{2,98}... | collective-permute-start | bytes 737288 | tf_op jit(solution)/shard_map/ppermute | solution.py:31
  64.4 7.7 %collective-permute-start = (bf16[192,640]{1,0:T(8,128)(2,1)S(1)}, bf16[192,640]{1,0:T(8,128)(2,1)S(1)}, u32[]{:S(2)}, u32[]{:S(2)}) collective-permute-start(bf16[192,640]{1,0:T(8,128)(2,1)S(1)} %get-tuple-element.37), channel_id=1, source_target_pairs={{0,32},{32,0},{64,96},{96,64},{1,33},{33,1},{65,97},{97,65},{2,34}... | collective-permute-start | bytes 737288 | tf_op jit(solution)/shard_map/ppermute | solution.py:31
  70.7 5.0 %collective-permute-start.3 = (bf16[96,640]{1,0:T(8,128)(2,1)S(1)}, bf16[96,640]{1,0:T(8,128)(2,1)S(1)}, u32[]{:S(2)}, u32[]{:S(2)}) collective-permute-start(bf16[96,640]{1,0:T(8,128)(2,1)S(1)} %fusion.24), channel_id=1, source_target_pairs={{0,32},{32,0},{64,96},{96,64},{1,33},{33,1},{65,97},{97,65},{2,34}... | collective-permute-start | bytes 368648 | tf_op jit(solution)/shard_map/ppermute | solution.py:31
  72.1 6.2 %collective-permute-start.1 = (bf16[96,640]{1,0:T(8,128)(2,1)S(1)}, bf16[96,640]{1,0:T(8,128)(2,1)S(1)}, u32[]{:S(2)}, u32[]{:S(2)}) collective-permute-start(bf16[96,640]{1,0:T(8,128)(2,1)S(1)} %fusion.26), channel_id=1, source_target_pairs={{0,96},{32,64},{64,32},{96,0},{1,97},{33,65},{65,33},{97,1},{2,98}... | collective-permute-start | bytes 368648 | tf_op jit(solution)/shard_map/ppermute | solution.py:31
  90.9 39.4 %all-to-all-start.2 = ((bf16[32,32,1280]{2,1,0:T(8,128)(2,1)}), bf16[32,32,1280]{2,1,0:T(8,128)(2,1)}, u32[]{:S(2)}, u32[]{:S(2)}) async-start(bf16[32,32,1280]{2,1,0:T(8,128)(2,1)} %bitcast.15), calls=%async_computation.2 | async-start | bytes 5242880 | tf_op jit(solution)/shard_map/all_to_all | solution.py:185
  95.7 11.0 %copy-start.20 = (bf16[96,1280]{1,0:T(8,128)(2,1)S(1)}, bf16[96,1280]{1,0:T(8,128)(2,1)}, u32[]{:S(2)}) copy-start(bf16[96,1280]{1,0:T(8,128)(2,1)} %get-tuple-element.80) | copy-start | bytes 737284
  95.7 10.9 %collective-permute-start.8 = (bf16[96,1280]{1,0:T(8,128)(2,1)}, bf16[96,1280]{1,0:T(8,128)(2,1)S(1)}, u32[]{:S(2)}, u32[]{:S(2)}) collective-permute-start(bf16[96,1280]{1,0:T(8,128)(2,1)} %get-tuple-element.80), channel_id=1, source_target_pairs={{0,96},{32,64},{64,32},{96,0},{1,97},{33,65},{65,33},{97,1},{2,98}... | collective-permute-start | bytes 737288 | tf_op jit(solution)/shard_map/ppermute | solution.py:31
  103.2 9.0 %collective-permute-start.6 = (bf16[192,640]{1,0:T(8,128)(2,1)S(1)}, bf16[192,640]{1,0:T(8,128)(2,1)S(1)}, u32[]{:S(2)}, u32[]{:S(2)}) collective-permute-start(bf16[192,640]{1,0:T(8,128)(2,1)S(1)} %get-tuple-element.45), channel_id=1, source_target_pairs={{0,96},{32,64},{64,32},{96,0},{1,97},{33,65},{65,33},{97,1},{2,98}... | collective-permute-start | bytes 737288 | tf_op jit(solution)/shard_map/ppermute | solution.py:31
  103.4 9.0 %collective-permute-start.4 = (bf16[192,640]{1,0:T(8,128)(2,1)S(1)}, bf16[192,640]{1,0:T(8,128)(2,1)S(1)}, u32[]{:S(2)}, u32[]{:S(2)}) collective-permute-start(bf16[192,640]{1,0:T(8,128)(2,1)S(1)} %get-tuple-element.43), channel_id=1, source_target_pairs={{0,32},{32,0},{64,96},{96,64},{1,33},{33,1},{65,97},{97,65},{2,34}... | collective-permute-start | bytes 737288 | tf_op jit(solution)/shard_map/ppermute | solution.py:31
  106.7 17.6 %copy-start.3 = (bf16[192,1280]{1,0:T(8,128)(2,1)}, bf16[192,1280]{1,0:T(8,128)(2,1)S(1)}, u32[]{:S(2)}) copy-start(bf16[192,1280]{1,0:T(8,128)(2,1)S(1)} %pad_maximum_fusion.5.refs_0_) | copy-start | bytes 1474564
  106.7 17.7 %collective-permute-start.9 = (bf16[192,1280]{1,0:T(8,128)(2,1)S(1)}, bf16[192,1280]{1,0:T(8,128)(2,1)S(1)}, u32[]{:S(2)}, u32[]{:S(2)}) collective-permute-start(bf16[192,1280]{1,0:T(8,128)(2,1)S(1)} %pad_maximum_fusion.5.refs_0_), channel_id=1, source_target_pairs={{0,32},{32,0},{64,96},{96,64},{1,33},{33,1},{65,97},{97,65},{2,34}... | collective-permute-start | bytes 1474568 | tf_op jit(solution)/shard_map/ppermute | solution.py:31
  112.3 12.0 %collective-permute-start.7 = (bf16[96,640]{1,0:T(8,128)(2,1)S(1)}, bf16[96,640]{1,0:T(8,128)(2,1)S(1)}, u32[]{:S(2)}, u32[]{:S(2)}) collective-permute-start(bf16[96,640]{1,0:T(8,128)(2,1)S(1)} %fusion.20), channel_id=1, source_target_pairs={{0,32},{32,0},{64,96},{96,64},{1,33},{33,1},{65,97},{97,65},{2,34}... | collective-permute-start | bytes 368648 | tf_op jit(solution)/shard_map/ppermute | solution.py:31
  112.5 11.9 %collective-permute-start.5 = (bf16[96,640]{1,0:T(8,128)(2,1)S(1)}, bf16[96,640]{1,0:T(8,128)(2,1)S(1)}, u32[]{:S(2)}, u32[]{:S(2)}) collective-permute-start(bf16[96,640]{1,0:T(8,128)(2,1)S(1)} %fusion.22), channel_id=1, source_target_pairs={{0,96},{32,64},{64,32},{96,0},{1,97},{33,65},{65,33},{97,1},{2,98}... | collective-permute-start | bytes 368648 | tf_op jit(solution)/shard_map/ppermute | solution.py:31
  124.4 0.8 copy-start.5
  134.2 0.8 copy-start.7
  135.0 0.8 copy-start.9
  135.8 0.7 copy-start.11
  136.5 10.9 %collective-permute-start.12 = (bf16[192,640]{1,0:T(8,128)(2,1)}, bf16[192,640]{1,0:T(8,128)(2,1)}, u32[]{:S(2)}, u32[]{:S(2)}) collective-permute-start(bf16[192,640]{1,0:T(8,128)(2,1)} %get-tuple-element.52), channel_id=1, source_target_pairs={{0,96},{32,64},{64,32},{96,0},{1,97},{33,65},{65,33},{97,1},{2,98}... | collective-permute-start | bytes 737288 | tf_op jit(solution)/shard_map/ppermute | solution.py:31
  140.5 27.8 %all-to-all-start.3 = ((bf16[32,32,768]{2,1,0:T(8,128)(2,1)}), bf16[32,32,768]{2,1,0:T(8,128)(2,1)}, u32[]{:S(2)}, u32[]{:S(2)}) async-start(bf16[32,32,768]{2,1,0:T(8,128)(2,1)} %bitcast.18), calls=%async_computation.3 | async-start | bytes 3145728 | tf_op jit(solution)/shard_map/all_to_all | solution.py:185
  145.2 9.2 %copy-start.8 = (f32[192,640]{1,0:T(8,128)S(1)}, f32[192,640]{1,0:T(8,128)}, u32[]{:S(2)}) copy-start(f32[192,640]{1,0:T(8,128)} %copy-done.7) | copy-start | bytes 1474564
  145.2 14.4 %copy-start.19 = (bf16[96,1280]{1,0:T(8,128)(2,1)S(1)}, bf16[96,1280]{1,0:T(8,128)(2,1)}, u32[]{:S(2)}) copy-start(bf16[96,1280]{1,0:T(8,128)(2,1)} %get-tuple-element.76) | copy-start | bytes 737284
  145.2 16.2 %copy-start.10 = (f32[192,640]{1,0:T(8,128)S(1)}, f32[192,640]{1,0:T(8,128)}, u32[]{:S(2)}) copy-start(f32[192,640]{1,0:T(8,128)} %copy-done.9) | copy-start | bytes 1474564
  145.2 9.1 %collective-permute-start.10 = (bf16[192,640]{1,0:T(8,128)(2,1)}, bf16[192,640]{1,0:T(8,128)(2,1)S(1)}, u32[]{:S(2)}, u32[]{:S(2)}) collective-permute-start(bf16[192,640]{1,0:T(8,128)(2,1)} %copy-done.11), channel_id=1, source_target_pairs={{0,32},{32,0},{64,96},{96,64},{1,33},{33,1},{65,97},{97,65},{2,34}... | collective-permute-start | bytes 737288 | tf_op jit(solution)/shard_map/ppermute | solution.py:31
  145.3 14.3 %collective-permute-start.14 = (bf16[96,1280]{1,0:T(8,128)(2,1)}, bf16[96,1280]{1,0:T(8,128)(2,1)S(1)}, u32[]{:S(2)}, u32[]{:S(2)}) collective-permute-start(bf16[96,1280]{1,0:T(8,128)(2,1)} %get-tuple-element.76), channel_id=1, source_target_pairs={{0,32},{32,0},{64,96},{96,64},{1,33},{33,1},{65,97},{97,65},{2,34}... | collective-permute-start | bytes 737288 | tf_op jit(solution)/shard_map/ppermute | solution.py:31
  149.3 12.1 %collective-permute-start.13 = (bf16[96,640]{1,0:T(8,128)(2,1)S(1)}, bf16[96,640]{1,0:T(8,128)(2,1)S(1)}, u32[]{:S(2)}, u32[]{:S(2)}) collective-permute-start(bf16[96,640]{1,0:T(8,128)(2,1)S(1)} %fusion.16), channel_id=1, source_target_pairs={{0,32},{32,0},{64,96},{96,64},{1,33},{33,1},{65,97},{97,65},{2,34}... | collective-permute-start | bytes 368648 | tf_op jit(solution)/shard_map/ppermute | solution.py:31
  154.4 7.0 %collective-permute-start.11 = (bf16[96,640]{1,0:T(8,128)(2,1)S(1)}, bf16[96,640]{1,0:T(8,128)(2,1)S(1)}, u32[]{:S(2)}, u32[]{:S(2)}) collective-permute-start(bf16[96,640]{1,0:T(8,128)(2,1)S(1)} %fusion.18), channel_id=1, source_target_pairs={{0,96},{32,64},{64,32},{96,0},{1,97},{33,65},{65,33},{97,1},{2,98}... | collective-permute-start | bytes 368648 | tf_op jit(solution)/shard_map/ppermute | solution.py:31
  160.4 36.9 %collective-permute-start.19 = (bf16[192,1280]{1,0:T(8,128)(2,1)}, bf16[192,1280]{1,0:T(8,128)(2,1)}, u32[]{:S(2)}, u32[]{:S(2)}) collective-permute-start(bf16[192,1280]{1,0:T(8,128)(2,1)} %pad_maximum_fusion.7.refs_2_), channel_id=1, source_target_pairs={{0,96},{32,64},{64,32},{96,0},{1,97},{33,65},{65,33},{97,1},{2,98}... | collective-permute-start | bytes 1474568 | tf_op jit(solution)/shard_map/ppermute | solution.py:31
  168.3 2.7 %copy-start.18 = (f32[96,1280]{1,0:T(8,128)S(1)}, f32[96,1280]{1,0:T(8,128)}, u32[]{:S(2)}) copy-start(f32[96,1280]{1,0:T(8,128)} %pad_maximum_fusion.6) | copy-start | bytes 1474564
  170.9 8.0 %collective-permute-start.17 = (bf16[192,384]{1,0:T(8,128)(2,1)S(1)}, bf16[192,384]{1,0:T(8,128)(2,1)S(1)}, u32[]{:S(2)}, u32[]{:S(2)}) collective-permute-start(bf16[192,384]{1,0:T(8,128)(2,1)S(1)} %get-tuple-element.60), channel_id=1, source_target_pairs={{0,96},{32,64},{64,32},{96,0},{1,97},{33,65},{65,33},{97,1},{2,98}... | collective-permute-start | bytes 442376 | tf_op jit(solution)/shard_map/ppermute | solution.py:31
  172.8 10.3 %collective-permute-start.20 = (bf16[96,1280]{1,0:T(8,128)(2,1)S(1)}, bf16[96,1280]{1,0:T(8,128)(2,1)S(1)}, u32[]{:S(2)}, u32[]{:S(2)}) collective-permute-start(bf16[96,1280]{1,0:T(8,128)(2,1)S(1)} %get-tuple-element.72), channel_id=1, source_target_pairs={{0,96},{32,64},{64,32},{96,0},{1,97},{33,65},{65,33},{97,1},{2,98}... | collective-permute-start | bytes 737288 | tf_op jit(solution)/shard_map/ppermute | solution.py:31
  176.0 5.8 %collective-permute-start.15 = (bf16[192,384]{1,0:T(8,128)(2,1)S(1)}, bf16[192,384]{1,0:T(8,128)(2,1)S(1)}, u32[]{:S(2)}, u32[]{:S(2)}) collective-permute-start(bf16[192,384]{1,0:T(8,128)(2,1)S(1)} %get-tuple-element.58), channel_id=1, source_target_pairs={{0,32},{32,0},{64,96},{96,64},{1,33},{33,1},{65,97},{97,65},{2,34}... | collective-permute-start | bytes 442376 | tf_op jit(solution)/shard_map/ppermute | solution.py:31
  179.0 4.4 %collective-permute-start.18 = (bf16[96,384]{1,0:T(8,128)(2,1)S(1)}, bf16[96,384]{1,0:T(8,128)(2,1)S(1)}, u32[]{:S(2)}, u32[]{:S(2)}) collective-permute-start(bf16[96,384]{1,0:T(8,128)(2,1)S(1)} %fusion.28), channel_id=1, source_target_pairs={{0,32},{32,0},{64,96},{96,64},{1,33},{33,1},{65,97},{97,65},{2,34}... | collective-permute-start | bytes 221192 | tf_op jit(solution)/shard_map/ppermute | solution.py:31
  181.9 5.6 %collective-permute-start.16 = (bf16[96,384]{1,0:T(8,128)(2,1)S(1)}, bf16[96,384]{1,0:T(8,128)(2,1)S(1)}, u32[]{:S(2)}, u32[]{:S(2)}) collective-permute-start(bf16[96,384]{1,0:T(8,128)(2,1)S(1)} %fusion.30), channel_id=1, source_target_pairs={{0,96},{32,64},{64,32},{96,0},{1,97},{33,65},{65,33},{97,1},{2,98}... | collective-permute-start | bytes 221192 | tf_op jit(solution)/shard_map/ppermute | solution.py:31
  183.1 10.7 %copy-start.14 = (f32[96,1280]{1,0:T(8,128)S(1)}, f32[96,1280]{1,0:T(8,128)}, u32[]{:S(2)}) copy-start(f32[96,1280]{1,0:T(8,128)} %get-tuple-element.81) | copy-start | bytes 1474564
  183.1 10.7 %copy-start.15 = (f32[96,1280]{1,0:T(8,128)S(1)}, f32[96,1280]{1,0:T(8,128)}, u32[]{:S(2)}) copy-start(f32[96,1280]{1,0:T(8,128)} %get-tuple-element.82) | copy-start | bytes 1474564
  183.1 10.6 %copy-start.16 = (f32[96,1280]{1,0:T(8,128)S(1)}, f32[96,1280]{1,0:T(8,128)}, u32[]{:S(2)}) copy-start(f32[96,1280]{1,0:T(8,128)} %get-tuple-element.77) | copy-start | bytes 1474564
  183.1 10.6 %copy-start.17 = (f32[96,1280]{1,0:T(8,128)S(1)}, f32[96,1280]{1,0:T(8,128)}, u32[]{:S(2)}) copy-start(f32[96,1280]{1,0:T(8,128)} %get-tuple-element.78) | copy-start | bytes 1474564
  183.1 14.2 %collective-permute-start.21 = (bf16[192,1280]{1,0:T(8,128)(2,1)S(1)}, bf16[192,1280]{1,0:T(8,128)(2,1)S(1)}, u32[]{:S(2)}, u32[]{:S(2)}) collective-permute-start(bf16[192,1280]{1,0:T(8,128)(2,1)S(1)} %pad_maximum_fusion.8.refs_4_), channel_id=1, source_target_pairs={{0,32},{32,0},{64,96},{96,64},{1,33},{33,1},{65,97},{97,65},{2,34}... | collective-permute-start | bytes 1474568 | tf_op jit(solution)/shard_map/ppermute | solution.py:31
  189.0 11.3 %collective-permute-start.22 = (bf16[96,768]{1,0:T(8,128)(2,1)S(1)}, bf16[96,768]{1,0:T(8,128)(2,1)S(1)}, u32[]{:S(2)}, u32[]{:S(2)}) collective-permute-start(bf16[96,768]{1,0:T(8,128)(2,1)S(1)} %get-tuple-element.68.refs_1_), channel_id=1, source_target_pairs={{0,32},{32,0},{64,96},{96,64},{1,33},{33,1},{65,97},{97,65},{2,34}... | collective-permute-start | bytes 442376 | tf_op jit(solution)/shard_map/ppermute | solution.py:31
  189.1 13.3 %collective-permute-start.23 = (bf16[96,768]{1,0:T(8,128)(2,1)S(1)}, bf16[96,768]{1,0:T(8,128)(2,1)S(1)}, u32[]{:S(2)}, u32[]{:S(2)}) collective-permute-start(bf16[96,768]{1,0:T(8,128)(2,1)S(1)} %get-tuple-element.68.refs_1_), channel_id=1, source_target_pairs={{0,64},{32,96},{64,0},{96,32},{1,65},{33,97},{65,1},{97,33},{2,66}... | collective-permute-start | bytes 442376 | tf_op jit(solution)/shard_map/ppermute | solution.py:31
  190.9 11.4 %collective-permute-start.24 = (bf16[96,768]{1,0:T(8,128)(2,1)S(1)}, bf16[96,768]{1,0:T(8,128)(2,1)S(1)}, u32[]{:S(2)}, u32[]{:S(2)}) collective-permute-start(bf16[96,768]{1,0:T(8,128)(2,1)S(1)} %get-tuple-element.68.refs_1_), channel_id=1, source_target_pairs={{0,96},{32,64},{64,32},{96,0},{1,97},{33,65},{65,33},{97,1},{2,98}... | collective-permute-start | bytes 442376 | tf_op jit(solution)/shard_map/ppermute | solution.py:31
  193.8 2.2 %copy-start.12 = (f32[96,1280]{1,0:T(8,128)S(1)}, f32[96,1280]{1,0:T(8,128)}, u32[]{:S(2)}) copy-start(f32[96,1280]{1,0:T(8,128)} %get-tuple-element.83) | copy-start | bytes 1474564
  193.8 2.2 %copy-start.13 = (f32[96,1280]{1,0:T(8,128)S(1)}, f32[96,1280]{1,0:T(8,128)}, u32[]{:S(2)}) copy-start(f32[96,1280]{1,0:T(8,128)} %get-tuple-element.79) | copy-start | bytes 1474564
  196.0 1.4 copy-start.4
  196.0 1.5 copy-start.6

commit v8 on v4

--- a/solution.py
+++ b/solution.py
@@ -18,7 +18,7 @@
 GROUPS = 4
 OWNERS = 32
 CAPACITY = 32
-UNITS = (10, 10, 8, 8)
+UNITS = (8, 10, 10, 8)
 TILE = 2
 MIB = 1024 * 1024
 
@@ -163,19 +163,22 @@
     spans = [slice(low, high) for low, high in zip(edges, edges[1:])]
     states, rows, joined, fars, blocks, spots = [], [], [], [], [], []
     arrived, last = (), len(spans) - 1
+    picked = [
+        jnp.dot(dispatch, input_grad[:, span], preferred_element_type=jnp.float32).astype(jnp.bfloat16)
+        for span in spans
+    ]
     for number, span in enumerate(spans):
-        outgoing = jnp.dot(
-            dispatch, input_grad[:, span], preferred_element_type=jnp.float32
-        ).astype(jnp.bfloat16)
-        earlier_work = target if number == 1 else rows[: max(0, number - 1)]
+        outgoing = picked[number]
+        earlier_work = (target, picked) if number == 1 else rows[: max(0, number - 1)]
         outgoing = after(outgoing, arrived, earlier_work, joined[: max(0, number - 1)])
+        outgoing = after(outgoing, fars[: max(0, number - 2)])
         arrived = lax.all_to_all(outgoing, "vocab", split_axis=0, concat_axis=0, tiled=True)
         ready = after(arrived, rows)
         grad, *pieces = combine(here, target, head_grad, ready, span.start, TILE * unit)
+        if number == last:
+            pieces = after(pieces, fars[: number - 1])
         for flip, piece in enumerate(pieces, 1):
             grad = grad + swap_z(piece, flip).astype(jnp.float32)
-        if 1 <= number < last:
-            grad = after(grad, fars)
         states.append(update(grad, master[:, span], moment_one[:, span], moment_two[:, span]))
         block = states[-1][0].astype(jnp.bfloat16)
         rows.append(block)

time: 210 us -> 200 us (0.952)
  waiting for transfers between devices: 94 us -> 84.6 us
  local copies, waits for them, and re-layouts: 6.26 us -> 3.64 us
    ppermute x21, waiting for transfers between devices: 64.2 us -> 57.1 us  [swap_z(): return lax.ppermute(block, 'dp', [(i, i ^ flip) for i in range(GROUPS)])]
    unnamed x41 -> x27, local copies, waits for them, and re-layouts: 6.14 us -> 3.53 us
    all_to_all x4, starting transfers between devices: 27.5 us -> 24.9 us  [local(): lax.all_to_all(outgoing, 'vocab', split_axis=0, concat_axis=0, tiled=True)]
    ppermute x21, starting transfers between devices: 27.7 us -> 30.3 us  [swap_z(): return lax.ppermute(block, 'dp', [(i, i ^ flip) for i in range(GROUPS)])]
    all_to_all x4, waiting for transfers between devices: 29.8 us -> 27.5 us  [local(): lax.all_to_all(outgoing, 'vocab', split_axis=0, concat_axis=0, tiled=True)]
  transfers between devices with their start and end apart: 25 -> 25, of which waited for: 19 -> 18; matrix products, arithmetic and copies ran while one was open for 14% -> 15% of each run, Pallas kernels for 8% -> 9%
where the time goes in v8:
time: 200 us; the launch traced here: 199 us
  waiting for transfers between devices  84.6 us (42%)
  starting transfers between devices  55.2 us (28%)
  Pallas kernels  18.7 us (9%)
  other arithmetic  18.6 us (9%)
  matrix products  16.8 us (8%)
  local copies, waits for them, and re-layouts  3.64 us (2%)
    ppermute x21, waiting for transfers between devices, swap_z(): return lax.ppermute(block, 'dp', [(i, i ^ flip) for i in range(GROUPS)])  57.1 us
    ppermute x21, starting transfers between devices, swap_z(): return lax.ppermute(block, 'dp', [(i, i ^ flip) for i in range(GROUPS)])  30.3 us
    all_to_all x4, waiting for transfers between devices, local(): lax.all_to_all(outgoing, 'vocab', split_axis=0, concat_axis=0, tiled=True)  27.5 us
    all_to_all x4, starting transfers between devices, local(): lax.all_to_all(outgoing, 'vocab', split_axis=0, concat_axis=0, tiled=True)  24.9 us
    dot_general x4, matrix products, local(): jnp.dot(dispatch, input_grad[:, span], preferred_element_type=jnp.float32)  16.4 us
    pallas_call x4, Pallas kernels, combine(): pl.pallas_call(combine_body, grid=(width // tile,), out_shape=[jax.ShapeD...  14.7 us
    convert_element_type x4, other arithmetic, local(): block = states[-1][0].astype(jnp.bfloat16)  9.95 us
  transfers between devices with their start and end apart: 25, of which 18 were waited for; matrix products, arithmetic and copies ran while one was open for 15% of the time, Pallas kernels for 9%

profile of v8, /device:TPU:0, one launch (start us, length us, event | category | flops | bytes accessed | tf_op | source)
XLA Modules:
  0.0 198.6 jit_solution(2213843983640124539)
XLA Ops:
  0.6 0.5 broadcast.141
  1.1 1.6 reduce.7
  3.1 3.8 %fusion.3 = bf16[1024,1024]{1,0:T(8,128)(2,1)} fusion(bf16[512,4608]{1,0:T(8,128)(2,1)} %param.7, s32[512]{0:T(512)S(1)} %bitcast.20), kind=kOutput, calls=%fused_computation.8 | convolution fusion | flops 1075314688 | bytes 3147776 | tf_op jit(solution)/shard_map/dot_general | solution.py:167
  6.9 7.5 %all-to-all-start = ((bf16[32,32,1024]{2,1,0:T(8,128)(2,1)}), bf16[32,32,1024]{2,1,0:T(8,128)(2,1)S(1)}, u32[]{:S(2)}, u32[]{:S(2)}) async-start(bf16[32,32,1024]{2,1,0:T(8,128)(2,1)} %bitcast.18), calls=%async_computation | async-start | bytes 4194304 | tf_op jit(solution)/shard_map/all_to_all | solution.py:175
  14.9 0.6 select_reduce_fusion
  15.6 3.8 %fusion.4 = bf16[1024,1024]{1,0:T(8,128)(2,1)} fusion(bf16[512,4608]{1,0:T(8,128)(2,1)} %param.7, s32[512]{0:T(512)S(1)} %bitcast.21), kind=kOutput, calls=%fused_computation.9 | convolution fusion | flops 1075314688 | bytes 3147776 | tf_op jit(solution)/shard_map/dot_general | solution.py:167
  19.4 4.4 %convolution_convert_fusion = bf16[1024,1280]{1,0:T(8,128)(2,1)} fusion(bf16[512,4608]{1,0:T(8,128)(2,1)} %param.7, s32[512]{0:T(512)S(1)} %bitcast.22), kind=kOutput, calls=%fused_computation | convolution fusion | flops 1344012288 | bytes 3934208 | tf_op jit(solution)/shard_map/dot_general | solution.py:167
  23.8 4.4 %convolution_convert_fusion.1 = bf16[1024,1280]{1,0:T(8,128)(2,1)} fusion(bf16[512,4608]{1,0:T(8,128)(2,1)} %param.7, s32[512]{0:T(512)S(1)} %bitcast.23), kind=kOutput, calls=%fused_computation.1 | convolution fusion | flops 1344012288 | bytes 3934208 | tf_op jit(solution)/shard_map/dot_general | solution.py:167
  28.2 15.2 %all-to-all-done = bf16[32,32,1024]{2,1,0:T(8,128)(2,1)S(1)} async-done(((bf16[32,32,1024]{2,1,0:T(8,128)(2,1)}), bf16[32,32,1024]{2,1,0:T(8,128)(2,1)S(1)}, u32[]{:S(2)}, u32[]{:S(2)}) %all-to-all-start) | async-done | bytes 2097184 | tf_op jit(solution)/shard_map/all_to_all | solution.py:175
  43.4 1.4 copy-done.1
  44.8 5.1 %all-to-all-start.1 = ((bf16[32,32,1280]{2,1,0:T(8,128)(2,1)}), bf16[32,32,1280]{2,1,0:T(8,128)(2,1)}, u32[]{:S(2)}, u32[]{:S(2)}) async-start(bf16[32,32,1280]{2,1,0:T(8,128)(2,1)} %bitcast.16), calls=%async_computation.1 | async-start | bytes 5242880 | tf_op jit(solution)/shard_map/all_to_all | solution.py:175
  49.9 1.6 copy-done.2
  51.5 2.1 %shard_map.102 = (f32[96,1024]{1,0:T(8,128)S(1)}, bf16[96,1024]{1,0:T(8,128)(2,1)S(1)}, bf16[96,1024]{1,0:T(8,128)(2,1)S(1)}, bf16[96,1024]{1,0:T(8,128)(2,1)S(1)}) custom-call(s32[1]{0:T(128)} %bitcast.here_ref, s32[1,1024]{1,0:T(1,128)S(1)} %sub.19.target_ref, bf16[1,384,4608]{2,1,0:T(8,128)(2,1)S(1)} %copy-done, bf16[1024,1024]{1,0:T(8,128)(2,1)S(1)} %bitcast.14), custom_call_target="tpu_custom_call" | custom-call | flops 805306368 | bytes 4063232 | tf_op jit(solution)/shard_map/pallas_call | solution.py:67
  53.6 4.1 %collective-permute-start.2 = (bf16[96,1024]{1,0:T(8,128)(2,1)S(1)}, bf16[96,1024]{1,0:T(8,128)(2,1)S(1)}, u32[]{:S(2)}, u32[]{:S(2)}) collective-permute-start(bf16[96,1024]{1,0:T(8,128)(2,1)S(1)} %get-tuple-element.39), channel_id=1, source_target_pairs={{0,96},{32,64},{64,32},{96,0},{1,97},{33,65},{65,33},{97,1},{2,98}... | collective-permute-start | bytes 589832 | tf_op jit(solution)/shard_map/ppermute | solution.py:31
  57.7 0.9 collective-permute-start
  58.6 8.4 %collective-permute-done.2 = bf16[96,1024]{1,0:T(8,128)(2,1)S(1)} collective-permute-done((bf16[96,1024]{1,0:T(8,128)(2,1)S(1)}, bf16[96,1024]{1,0:T(8,128)(2,1)S(1)}, u32[]{:S(2)}, u32[]{:S(2)}) %collective-permute-start.2) | collective-permute-done | bytes 196640 | tf_op jit(solution)/shard_map/ppermute | solution.py:31
  67.1 0.7 collective-permute-done
  67.8 2.5 %fusion.25 = (bf16[96,1024]{1,0:T(8,128)(2,1)S(1)}, f32[96,1024]{1,0:T(8,128)}, f32[96,1024]{1,0:T(8,128)}, f32[96,1024]{1,0:T(8,128)}) fusion(f32[96,4608]{1,0:T(8,128)} %param.11, bf16[96,1024]{1,0:T(8,128)(2,1)S(1)} %collective-permute-done.2, bf16[96,1024]{1,0:T(8,128)(2,1)S(1)} %collective-permute-done.1, f32[96,1024]{1,0:T(8,128)S(1)} %get-tuple-element.36, ...), kind=kLoop, calls=%fused_computation.58 | loop fusion | flops 2162688 | bytes 3538944 | tf_op jit(solution)/shard_map/convert_element_type | solution.py:183
  70.3 2.9 %collective-permute-start.6 = (bf16[96,1024]{1,0:T(8,128)(2,1)S(1)}, bf16[96,1024]{1,0:T(8,128)(2,1)S(1)}, u32[]{:S(2)}, u32[]{:S(2)}) collective-permute-start(bf16[96,1024]{1,0:T(8,128)(2,1)S(1)} %get-tuple-element.80), channel_id=1, source_target_pairs={{0,96},{32,64},{64,32},{96,0},{1,97},{33,65},{65,33},{97,1},{2,98}... | collective-permute-start | bytes 589832 | tf_op jit(solution)/shard_map/ppermute | solution.py:31
  73.2 4.5 %collective-permute-done.6 = bf16[96,1024]{1,0:T(8,128)(2,1)S(1)} collective-permute-done((bf16[96,1024]{1,0:T(8,128)(2,1)S(1)}, bf16[96,1024]{1,0:T(8,128)(2,1)S(1)}, u32[]{:S(2)}, u32[]{:S(2)}) %collective-permute-start.6) | collective-permute-done | bytes 196640 | tf_op jit(solution)/shard_map/ppermute | solution.py:31
  77.7 0.8 pad_maximum_fusion.5.refs_0_
  78.5 6.0 %all-to-all-done.1 = bf16[32,32,1280]{2,1,0:T(8,128)(2,1)} async-done(((bf16[32,32,1280]{2,1,0:T(8,128)(2,1)}), bf16[32,32,1280]{2,1,0:T(8,128)(2,1)}, u32[]{:S(2)}, u32[]{:S(2)}) %all-to-all-start.1) | async-done | bytes 2621472 | tf_op jit(solution)/shard_map/all_to_all | solution.py:175
  84.5 4.8 %all-to-all-start.2 = ((bf16[32,32,1280]{2,1,0:T(8,128)(2,1)}), bf16[32,32,1280]{2,1,0:T(8,128)(2,1)}, u32[]{:S(2)}, u32[]{:S(2)}) async-start(bf16[32,32,1280]{2,1,0:T(8,128)(2,1)} %bitcast.15), calls=%async_computation.2 | async-start | bytes 5242880 | tf_op jit(solution)/shard_map/all_to_all | solution.py:175
  89.3 4.6 %shard_map.103 = (f32[96,1280]{1,0:T(8,128)S(1)}, bf16[96,1280]{1,0:T(8,128)(2,1)S(1)}, bf16[96,1280]{1,0:T(8,128)(2,1)S(1)}, bf16[96,1280]{1,0:T(8,128)(2,1)S(1)}) custom-call(s32[1]{0:T(128)} %bitcast.here_ref, s32[1,1024]{1,0:T(1,128)S(1)} %sub.19.target_ref, bf16[1,384,4608]{2,1,0:T(8,128)(2,1)S(1)} %copy-done, bf16[1024,1280]{1,0:T(8,128)(2,1)} %bitcast.7.part_ref), custom_call_target="tpu_custom_call" | custom-call | flops 1006632960 | bytes 5079040 | tf_op jit(solution)/shard_map/pallas_call | solution.py:67
  93.8 4.1 %collective-permute-start.5 = (bf16[96,1280]{1,0:T(8,128)(2,1)S(1)}, bf16[96,1280]{1,0:T(8,128)(2,1)S(1)}, u32[]{:S(2)}, u32[]{:S(2)}) collective-permute-start(bf16[96,1280]{1,0:T(8,128)(2,1)S(1)} %get-tuple-element.45), channel_id=1, source_target_pairs={{0,96},{32,64},{64,32},{96,0},{1,97},{33,65},{65,33},{97,1},{2,98}... | collective-permute-start | bytes 737288 | tf_op jit(solution)/shard_map/ppermute | solution.py:31
  98.0 0.9 collective-permute-start.3
  98.9 10.5 %collective-permute-done.5 = bf16[96,1280]{1,0:T(8,128)(2,1)S(1)} collective-permute-done((bf16[96,1280]{1,0:T(8,128)(2,1)S(1)}, bf16[96,1280]{1,0:T(8,128)(2,1)S(1)}, u32[]{:S(2)}, u32[]{:S(2)}) %collective-permute-start.5) | collective-permute-done | bytes 245792 | tf_op jit(solution)/shard_map/ppermute | solution.py:31
  109.4 0.7 collective-permute-done.3
  110.2 2.8 %fusion.23 = (bf16[96,1280]{1,0:T(8,128)(2,1)S(1)}, f32[96,1280]{1,0:T(8,128)}, f32[96,1280]{1,0:T(8,128)}, f32[96,1280]{1,0:T(8,128)}) fusion(f32[96,4608]{1,0:T(8,128)} %param.11, bf16[96,1280]{1,0:T(8,128)(2,1)S(1)} %collective-permute-done.5, bf16[96,1280]{1,0:T(8,128)(2,1)S(1)} %collective-permute-done.4, f32[96,1280]{1,0:T(8,128)S(1)} %get-tuple-element.42, ...), kind=kLoop, calls=%fused_computation.57 | loop fusion | flops 2703360 | bytes 4423680 | tf_op jit(solution)/shard_map/convert_element_type | solution.py:183
  112.9 2.9 %collective-permute-start.10 = (bf16[96,1280]{1,0:T(8,128)(2,1)S(1)}, bf16[96,1280]{1,0:T(8,128)(2,1)S(1)}, u32[]{:S(2)}, u32[]{:S(2)}) collective-permute-start(bf16[96,1280]{1,0:T(8,128)(2,1)S(1)} %get-tuple-element.76), channel_id=1, source_target_pairs={{0,96},{32,64},{64,32},{96,0},{1,97},{33,65},{65,33},{97,1},{2,98}... | collective-permute-start | bytes 737288 | tf_op jit(solution)/shard_map/ppermute | solution.py:31
  115.8 5.6 %collective-permute-done.10 = bf16[96,1280]{1,0:T(8,128)(2,1)S(1)} collective-permute-done((bf16[96,1280]{1,0:T(8,128)(2,1)S(1)}, bf16[96,1280]{1,0:T(8,128)(2,1)S(1)}, u32[]{:S(2)}, u32[]{:S(2)}) %collective-permute-start.10) | collective-permute-done | bytes 245792 | tf_op jit(solution)/shard_map/ppermute | solution.py:31
  121.4 0.8 pad_maximum_fusion.3.refs_2_
  122.2 1.7 all-to-all-done.2
  123.9 2.1 %collective-permute-done.11.refs_1_ = bf16[192,1024]{1,0:T(8,128)(2,1)} collective-permute-done((bf16[192,1024]{1,0:T(8,128)(2,1)}, bf16[192,1024]{1,0:T(8,128)(2,1)}, u32[]{:S(2)}, u32[]{:S(2)}) %collective-permute-start.11) | collective-permute-done | bytes 393248 | tf_op jit(solution)/shard_map/ppermute | solution.py:31
  126.0 7.5 %all-to-all-start.3 = ((bf16[32,32,1024]{2,1,0:T(8,128)(2,1)}), bf16[32,32,1024]{2,1,0:T(8,128)(2,1)}, u32[]{:S(2)}, u32[]{:S(2)}) async-start(bf16[32,32,1024]{2,1,0:T(8,128)(2,1)} %bitcast.17), calls=%async_computation.3 | async-start | bytes 4194304 | tf_op jit(solution)/shard_map/all_to_all | solution.py:175
  133.5 4.6 %shard_map.104 = (f32[96,1280]{1,0:T(8,128)S(1)}, bf16[96,1280]{1,0:T(8,128)(2,1)S(1)}, bf16[96,1280]{1,0:T(8,128)(2,1)S(1)}, bf16[96,1280]{1,0:T(8,128)(2,1)S(1)}) custom-call(s32[1]{0:T(128)} %bitcast.here_ref, s32[1,1024]{1,0:T(1,128)S(1)} %sub.19.target_ref, bf16[1,384,4608]{2,1,0:T(8,128)(2,1)S(1)} %copy-done, bf16[1024,1280]{1,0:T(8,128)(2,1)} %bitcast.9.part_ref), custom_call_target="tpu_custom_call" | custom-call | flops 1006632960 | bytes 5079040 | tf_op jit(solution)/shard_map/pallas_call | solution.py:67
  138.1 0.7 collective-permute-start.9
  138.8 1.7 collective-permute-start.8
  140.5 1.7 collective-permute-start.7
  142.2 0.3 collective-permute-start.12
  142.5 10.2 %collective-permute-done.9 = bf16[96,1280]{1,0:T(8,128)(2,1)S(1)} collective-permute-done((bf16[96,1280]{1,0:T(8,128)(2,1)S(1)}, bf16[96,1280]{1,0:T(8,128)(2,1)S(1)}, u32[]{:S(2)}, u32[]{:S(2)}) %collective-permute-start.9) | collective-permute-done | bytes 245792 | tf_op jit(solution)/shard_map/ppermute | solution.py:31
  152.7 1.6 collective-permute-done.7
  154.3 2.8 %fusion.21 = (bf16[96,1280]{1,0:T(8,128)(2,1)}, f32[96,1280]{1,0:T(8,128)}, f32[96,1280]{1,0:T(8,128)}, f32[96,1280]{1,0:T(8,128)}) fusion(f32[96,4608]{1,0:T(8,128)} %param.11, bf16[96,1280]{1,0:T(8,128)(2,1)S(1)} %collective-permute-done.9, bf16[96,1280]{1,0:T(8,128)(2,1)S(1)} %collective-permute-done.8, f32[96,1280]{1,0:T(8,128)S(1)} %get-tuple-element.48, ...), kind=kLoop, calls=%fused_computation.56 | loop fusion | flops 2703360 | bytes 4423680 | tf_op jit(solution)/shard_map/convert_element_type | solution.py:183
  157.2 0.6 collective-permute-start.16
  157.8 4.6 %all-to-all-done.3 = bf16[32,32,1024]{2,1,0:T(8,128)(2,1)} async-done(((bf16[32,32,1024]{2,1,0:T(8,128)(2,1)}), bf16[32,32,1024]{2,1,0:T(8,128)(2,1)}, u32[]{:S(2)}, u32[]{:S(2)}) %all-to-all-start.3) | async-done | bytes 2097184 | tf_op jit(solution)/shard_map/all_to_all | solution.py:175
  162.4 3.5 %shard_map.105 = (f32[96,1024]{1,0:T(8,128)S(1)}, bf16[96,1024]{1,0:T(8,128)(2,1)S(1)}, bf16[96,1024]{1,0:T(8,128)(2,1)S(1)}, bf16[96,1024]{1,0:T(8,128)(2,1)S(1)}) custom-call(s32[1]{0:T(128)} %bitcast.here_ref, s32[1,1024]{1,0:T(1,128)S(1)} %sub.19.target_ref, bf16[1,384,4608]{2,1,0:T(8,128)(2,1)S(1)} %copy-done, bf16[1024,1024]{1,0:T(8,128)(2,1)} %bitcast.11.part_ref), custom_call_target="tpu_custom_call" | custom-call | flops 805306368 | bytes 4063232 | tf_op jit(solution)/shard_map/pallas_call | solution.py:67
  166.0 0.7 collective-permute-start.15
  166.7 1.7 collective-permute-start.14
  168.4 1.7 collective-permute-start.13
  170.1 1.1 pad_maximum_fusion.4.refs_4_
  171.2 0.4 collective-permute-start.17
  171.6 6.3 %collective-permute-done.15 = bf16[96,1024]{1,0:T(8,128)(2,1)S(1)} collective-permute-done((bf16[96,1024]{1,0:T(8,128)(2,1)S(1)}, bf16[96,1024]{1,0:T(8,128)(2,1)S(1)}, u32[]{:S(2)}, u32[]{:S(2)}) %collective-permute-start.15) | collective-permute-done | bytes 196640 | tf_op jit(solution)/shard_map/ppermute | solution.py:31
  177.9 2.2 %collective-permute-done.13 = bf16[96,1024]{1,0:T(8,128)(2,1)S(1)} collective-permute-done((bf16[96,1024]{1,0:T(8,128)(2,1)S(1)}, bf16[96,1024]{1,0:T(8,128)(2,1)S(1)}, u32[]{:S(2)}, u32[]{:S(2)}) %collective-permute-start.13) | collective-permute-done | bytes 196640 | tf_op jit(solution)/shard_map/ppermute | solution.py:31
  180.2 1.8 fusion.19
  182.0 0.4 collective-permute-start.18
  182.4 1.8 collective-permute-start.19
  184.2 2.6 %collective-permute-start.20 = (bf16[96,1024]{1,0:T(8,128)(2,1)S(1)}, bf16[96,1024]{1,0:T(8,128)(2,1)S(1)}, u32[]{:S(2)}, u32[]{:S(2)}) collective-permute-start(bf16[96,1024]{1,0:T(8,128)(2,1)S(1)} %get-tuple-element.68.refs_1_), channel_id=1, source_target_pairs={{0,96},{32,64},{64,32},{96,0},{1,97},{33,65},{65,33},{97,1},{2,98}... | collective-permute-start | bytes 589832 | tf_op jit(solution)/shard_map/ppermute | solution.py:31
  186.8 2.1 %pad_maximum_fusion = (f32[96,4608]{1,0:T(8,128)}, f32[96,4608]{1,0:T(8,128)}) fusion(f32[96,1024]{1,0:T(8,128)S(1)} %get-tuple-element.69, f32[96,1280]{1,0:T(8,128)S(1)} %copy-done.7, f32[96,1280]{1,0:T(8,128)S(1)} %copy-done.5, f32[96,1024]{1,0:T(8,128)S(1)} %copy-done.10, f32[96,1024]{1,0:T(8,128)S(1)} %get-tuple-element.70, ...), kind=kLoop, calls=%fused_computation.10 | loop fusion | flops 2654208 | bytes 7077888 | tf_op jit(solution)/shard_map/concatenate | solution.py:202
  189.0 1.3 pad_maximum_fusion.2
  190.3 0.4 collective-permute-done.17.refs_5_
  190.7 3.0 %shard_map.106.refs_0_ = bf16[384,4608]{1,0:T(8,128)(2,1)} custom-call(s32[1]{0:T(128)} %bitcast.here_ref, bf16[192,1024]{1,0:T(8,128)(2,1)} %pad_maximum_fusion.5.refs_0_, bf16[192,1024]{1,0:T(8,128)(2,1)} %collective-permute-done.11.refs_1_, bf16[192,1280]{1,0:T(8,128)(2,1)} %pad_maximum_fusion.3.refs_2_, ...), custom_call_target="tpu_custom_call" | custom-call | bytes 5505024 | tf_op jit(solution)/shard_map/pallas_call | solution.py:106
  193.7 1.2 collective-permute-done.18.refs_2_
  194.9 2.7 %collective-permute-done.19.refs_3_ = bf16[96,1024]{1,0:T(8,128)(2,1)S(1)} collective-permute-done((bf16[96,1024]{1,0:T(8,128)(2,1)S(1)}, bf16[96,1024]{1,0:T(8,128)(2,1)S(1)}, u32[]{:S(2)}, u32[]{:S(2)}) %collective-permute-start.19) | collective-permute-done | bytes 196640 | tf_op jit(solution)/shard_map/ppermute | solution.py:31
  197.6 0.9 shard_map.107
  (45 shorter events, 0.8 us)
Async XLA Ops:
  6.9 7.5 %copy-start.12 = (s32[16384,1]{0,1:T(1,128)S(1)}, s32[16384,1]{0,1:T(1,128)}, u32[]{:S(2)}) copy-start(s32[16384,1]{0,1:T(1,128)} %param.9) | copy-start | bytes 196612
  6.9 36.5 %all-to-all-start = ((bf16[32,32,1024]{2,1,0:T(8,128)(2,1)}), bf16[32,32,1024]{2,1,0:T(8,128)(2,1)S(1)}, u32[]{:S(2)}, u32[]{:S(2)}) async-start(bf16[32,32,1024]{2,1,0:T(8,128)(2,1)} %bitcast.18), calls=%async_computation | async-start | bytes 4194304 | tf_op jit(solution)/shard_map/all_to_all | solution.py:175
  43.4 1.4 copy-start.1
  44.8 5.1 %copy-start = (bf16[1,384,4608]{2,1,0:T(8,128)(2,1)S(1)}, bf16[1,384,4608]{2,1,0:T(8,128)(2,1)}, u32[]{:S(2)}) copy-start(bf16[1,384,4608]{2,1,0:T(8,128)(2,1)} %head_ref.7) | copy-start | bytes 10616836
  44.8 39.7 %all-to-all-start.1 = ((bf16[32,32,1280]{2,1,0:T(8,128)(2,1)}), bf16[32,32,1280]{2,1,0:T(8,128)(2,1)}, u32[]{:S(2)}, u32[]{:S(2)}) async-start(bf16[32,32,1280]{2,1,0:T(8,128)(2,1)} %bitcast.16), calls=%async_computation.1 | async-start | bytes 5242880 | tf_op jit(solution)/shard_map/all_to_all | solution.py:175
  49.9 1.6 copy-start.2
  53.6 13.5 %collective-permute-start.2 = (bf16[96,1024]{1,0:T(8,128)(2,1)S(1)}, bf16[96,1024]{1,0:T(8,128)(2,1)S(1)}, u32[]{:S(2)}, u32[]{:S(2)}) collective-permute-start(bf16[96,1024]{1,0:T(8,128)(2,1)S(1)} %get-tuple-element.39), channel_id=1, source_target_pairs={{0,96},{32,64},{64,32},{96,0},{1,97},{33,65},{65,33},{97,1},{2,98}... | collective-permute-start | bytes 589832 | tf_op jit(solution)/shard_map/ppermute | solution.py:31
  57.7 9.4 %collective-permute-start.1 = (bf16[96,1024]{1,0:T(8,128)(2,1)S(1)}, bf16[96,1024]{1,0:T(8,128)(2,1)S(1)}, u32[]{:S(2)}, u32[]{:S(2)}) collective-permute-start(bf16[96,1024]{1,0:T(8,128)(2,1)S(1)} %get-tuple-element.38), channel_id=1, source_target_pairs={{0,64},{32,96},{64,0},{96,32},{1,65},{33,97},{65,1},{97,33},{2,66}... | collective-permute-start | bytes 589832 | tf_op jit(solution)/shard_map/ppermute | solution.py:31
  57.7 10.1 %collective-permute-start = (bf16[96,1024]{1,0:T(8,128)(2,1)S(1)}, bf16[96,1024]{1,0:T(8,128)(2,1)S(1)}, u32[]{:S(2)}, u32[]{:S(2)}) collective-permute-start(bf16[96,1024]{1,0:T(8,128)(2,1)S(1)} %get-tuple-element.37), channel_id=1, source_target_pairs={{0,32},{32,0},{64,96},{96,64},{1,33},{33,1},{65,97},{97,65},{2,34}... | collective-permute-start | bytes 589832 | tf_op jit(solution)/shard_map/ppermute | solution.py:31
  70.3 7.4 %collective-permute-start.6 = (bf16[96,1024]{1,0:T(8,128)(2,1)S(1)}, bf16[96,1024]{1,0:T(8,128)(2,1)S(1)}, u32[]{:S(2)}, u32[]{:S(2)}) collective-permute-start(bf16[96,1024]{1,0:T(8,128)(2,1)S(1)} %get-tuple-element.80), channel_id=1, source_target_pairs={{0,96},{32,64},{64,32},{96,0},{1,97},{33,65},{65,33},{97,1},{2,98}... | collective-permute-start | bytes 589832 | tf_op jit(solution)/shard_map/ppermute | solution.py:31
  84.5 39.4 %all-to-all-start.2 = ((bf16[32,32,1280]{2,1,0:T(8,128)(2,1)}), bf16[32,32,1280]{2,1,0:T(8,128)(2,1)}, u32[]{:S(2)}, u32[]{:S(2)}) async-start(bf16[32,32,1280]{2,1,0:T(8,128)(2,1)} %bitcast.15), calls=%async_computation.2 | async-start | bytes 5242880 | tf_op jit(solution)/shard_map/all_to_all | solution.py:175
  93.8 15.6 %collective-permute-start.5 = (bf16[96,1280]{1,0:T(8,128)(2,1)S(1)}, bf16[96,1280]{1,0:T(8,128)(2,1)S(1)}, u32[]{:S(2)}, u32[]{:S(2)}) collective-permute-start(bf16[96,1280]{1,0:T(8,128)(2,1)S(1)} %get-tuple-element.45), channel_id=1, source_target_pairs={{0,96},{32,64},{64,32},{96,0},{1,97},{33,65},{65,33},{97,1},{2,98}... | collective-permute-start | bytes 737288 | tf_op jit(solution)/shard_map/ppermute | solution.py:31
  98.0 11.5 %collective-permute-start.4 = (bf16[96,1280]{1,0:T(8,128)(2,1)S(1)}, bf16[96,1280]{1,0:T(8,128)(2,1)S(1)}, u32[]{:S(2)}, u32[]{:S(2)}) collective-permute-start(bf16[96,1280]{1,0:T(8,128)(2,1)S(1)} %get-tuple-element.44), channel_id=1, source_target_pairs={{0,64},{32,96},{64,0},{96,32},{1,65},{33,97},{65,1},{97,33},{2,66}... | collective-permute-start | bytes 737288 | tf_op jit(solution)/shard_map/ppermute | solution.py:31
  98.0 12.2 %collective-permute-start.3 = (bf16[96,1280]{1,0:T(8,128)(2,1)S(1)}, bf16[96,1280]{1,0:T(8,128)(2,1)S(1)}, u32[]{:S(2)}, u32[]{:S(2)}) collective-permute-start(bf16[96,1280]{1,0:T(8,128)(2,1)S(1)} %get-tuple-element.43), channel_id=1, source_target_pairs={{0,32},{32,0},{64,96},{96,64},{1,33},{33,1},{65,97},{97,65},{2,34}... | collective-permute-start | bytes 737288 | tf_op jit(solution)/shard_map/ppermute | solution.py:31
  112.9 8.4 %collective-permute-start.10 = (bf16[96,1280]{1,0:T(8,128)(2,1)S(1)}, bf16[96,1280]{1,0:T(8,128)(2,1)S(1)}, u32[]{:S(2)}, u32[]{:S(2)}) collective-permute-start(bf16[96,1280]{1,0:T(8,128)(2,1)S(1)} %get-tuple-element.76), channel_id=1, source_target_pairs={{0,96},{32,64},{64,32},{96,0},{1,97},{33,65},{65,33},{97,1},{2,98}... | collective-permute-start | bytes 737288 | tf_op jit(solution)/shard_map/ppermute | solution.py:31
  115.8 10.2 %collective-permute-start.11 = (bf16[192,1024]{1,0:T(8,128)(2,1)}, bf16[192,1024]{1,0:T(8,128)(2,1)}, u32[]{:S(2)}, u32[]{:S(2)}) collective-permute-start(bf16[192,1024]{1,0:T(8,128)(2,1)} %pad_maximum_fusion.5.refs_0_), channel_id=1, source_target_pairs={{0,32},{32,0},{64,96},{96,64},{1,33},{33,1},{65,97},{97,65},{2,34}... | collective-permute-start | bytes 1179656 | tf_op jit(solution)/shard_map/ppermute | solution.py:31
  126.0 36.4 %all-to-all-start.3 = ((bf16[32,32,1024]{2,1,0:T(8,128)(2,1)}), bf16[32,32,1024]{2,1,0:T(8,128)(2,1)}, u32[]{:S(2)}, u32[]{:S(2)}) async-start(bf16[32,32,1024]{2,1,0:T(8,128)(2,1)} %bitcast.17), calls=%async_computation.3 | async-start | bytes 4194304 | tf_op jit(solution)/shard_map/all_to_all | solution.py:175
  138.1 14.6 %collective-permute-start.9 = (bf16[96,1280]{1,0:T(8,128)(2,1)S(1)}, bf16[96,1280]{1,0:T(8,128)(2,1)S(1)}, u32[]{:S(2)}, u32[]{:S(2)}) collective-permute-start(bf16[96,1280]{1,0:T(8,128)(2,1)S(1)} %get-tuple-element.51), channel_id=1, source_target_pairs={{0,96},{32,64},{64,32},{96,0},{1,97},{33,65},{65,33},{97,1},{2,98}... | collective-permute-start | bytes 737288 | tf_op jit(solution)/shard_map/ppermute | solution.py:31
  138.8 13.9 %collective-permute-start.8 = (bf16[96,1280]{1,0:T(8,128)(2,1)S(1)}, bf16[96,1280]{1,0:T(8,128)(2,1)S(1)}, u32[]{:S(2)}, u32[]{:S(2)}) collective-permute-start(bf16[96,1280]{1,0:T(8,128)(2,1)S(1)} %get-tuple-element.50), channel_id=1, source_target_pairs={{0,64},{32,96},{64,0},{96,32},{1,65},{33,97},{65,1},{97,33},{2,66}... | collective-permute-start | bytes 737288 | tf_op jit(solution)/shard_map/ppermute | solution.py:31
  140.5 13.8 %collective-permute-start.7 = (bf16[96,1280]{1,0:T(8,128)(2,1)S(1)}, bf16[96,1280]{1,0:T(8,128)(2,1)S(1)}, u32[]{:S(2)}, u32[]{:S(2)}) collective-permute-start(bf16[96,1280]{1,0:T(8,128)(2,1)S(1)} %get-tuple-element.49), channel_id=1, source_target_pairs={{0,32},{32,0},{64,96},{96,64},{1,33},{33,1},{65,97},{97,65},{2,34}... | collective-permute-start | bytes 737288 | tf_op jit(solution)/shard_map/ppermute | solution.py:31
  142.2 23.7 %collective-permute-start.12 = (bf16[192,1280]{1,0:T(8,128)(2,1)}, bf16[192,1280]{1,0:T(8,128)(2,1)}, u32[]{:S(2)}, u32[]{:S(2)}) collective-permute-start(bf16[192,1280]{1,0:T(8,128)(2,1)} %pad_maximum_fusion.3.refs_2_), channel_id=1, source_target_pairs={{0,32},{32,0},{64,96},{96,64},{1,33},{33,1},{65,97},{97,65},{2,34}... | collective-permute-start | bytes 1474568 | tf_op jit(solution)/shard_map/ppermute | solution.py:31
  157.2 13.0 %collective-permute-start.16 = (bf16[96,1280]{1,0:T(8,128)(2,1)}, bf16[96,1280]{1,0:T(8,128)(2,1)}, u32[]{:S(2)}, u32[]{:S(2)}) collective-permute-start(bf16[96,1280]{1,0:T(8,128)(2,1)} %get-tuple-element.72), channel_id=1, source_target_pairs={{0,96},{32,64},{64,32},{96,0},{1,97},{33,65},{65,33},{97,1},{2,98}... | collective-permute-start | bytes 737288 | tf_op jit(solution)/shard_map/ppermute | solution.py:31
  166.0 12.0 %collective-permute-start.15 = (bf16[96,1024]{1,0:T(8,128)(2,1)S(1)}, bf16[96,1024]{1,0:T(8,128)(2,1)S(1)}, u32[]{:S(2)}, u32[]{:S(2)}) collective-permute-start(bf16[96,1024]{1,0:T(8,128)(2,1)S(1)} %get-tuple-element.61), channel_id=1, source_target_pairs={{0,96},{32,64},{64,32},{96,0},{1,97},{33,65},{65,33},{97,1},{2,98}... | collective-permute-start | bytes 589832 | tf_op jit(solution)/shard_map/ppermute | solution.py:31
  166.7 11.2 %collective-permute-start.14 = (bf16[96,1024]{1,0:T(8,128)(2,1)S(1)}, bf16[96,1024]{1,0:T(8,128)(2,1)S(1)}, u32[]{:S(2)}, u32[]{:S(2)}) collective-permute-start(bf16[96,1024]{1,0:T(8,128)(2,1)S(1)} %get-tuple-element.60), channel_id=1, source_target_pairs={{0,64},{32,96},{64,0},{96,32},{1,65},{33,97},{65,1},{97,33},{2,66}... | collective-permute-start | bytes 589832 | tf_op jit(solution)/shard_map/ppermute | solution.py:31
  168.4 11.8 %collective-permute-start.13 = (bf16[96,1024]{1,0:T(8,128)(2,1)S(1)}, bf16[96,1024]{1,0:T(8,128)(2,1)S(1)}, u32[]{:S(2)}, u32[]{:S(2)}) collective-permute-start(bf16[96,1024]{1,0:T(8,128)(2,1)S(1)} %get-tuple-element.59), channel_id=1, source_target_pairs={{0,32},{32,0},{64,96},{96,64},{1,33},{33,1},{65,97},{97,65},{2,34}... | collective-permute-start | bytes 589832 | tf_op jit(solution)/shard_map/ppermute | solution.py:31
  171.2 19.5 %collective-permute-start.17 = (bf16[192,1280]{1,0:T(8,128)(2,1)S(1)}, bf16[192,1280]{1,0:T(8,128)(2,1)S(1)}, u32[]{:S(2)}, u32[]{:S(2)}) collective-permute-start(bf16[192,1280]{1,0:T(8,128)(2,1)S(1)} %pad_maximum_fusion.4.refs_4_), channel_id=1, source_target_pairs={{0,32},{32,0},{64,96},{96,64},{1,33},{33,1},{65,97},{97,65},{2,34}... | collective-permute-start | bytes 1474568 | tf_op jit(solution)/shard_map/ppermute | solution.py:31
  180.2 6.6 %copy-start.5 = (f32[96,1280]{1,0:T(8,128)S(1)}, f32[96,1280]{1,0:T(8,128)}, u32[]{:S(2)}) copy-start(f32[96,1280]{1,0:T(8,128)} %get-tuple-element.77) | copy-start | bytes 1474564
  180.2 6.6 %copy-start.6 = (f32[96,1280]{1,0:T(8,128)S(1)}, f32[96,1280]{1,0:T(8,128)}, u32[]{:S(2)}) copy-start(f32[96,1280]{1,0:T(8,128)} %get-tuple-element.78) | copy-start | bytes 1474564
  180.2 6.6 %copy-start.7 = (f32[96,1280]{1,0:T(8,128)S(1)}, f32[96,1280]{1,0:T(8,128)}, u32[]{:S(2)}) copy-start(f32[96,1280]{1,0:T(8,128)} %get-tuple-element.73) | copy-start | bytes 1474564
  180.2 6.6 %copy-start.8 = (f32[96,1280]{1,0:T(8,128)S(1)}, f32[96,1280]{1,0:T(8,128)}, u32[]{:S(2)}) copy-start(f32[96,1280]{1,0:T(8,128)} %get-tuple-element.74) | copy-start | bytes 1474564
  180.2 6.6 %copy-start.10 = (f32[96,1024]{1,0:T(8,128)S(1)}, f32[96,1024]{1,0:T(8,128)}, u32[]{:S(2)}) copy-start(f32[96,1024]{1,0:T(8,128)} %get-tuple-element.81) | copy-start | bytes 1179652
  180.2 6.6 %copy-start.11 = (f32[96,1024]{1,0:T(8,128)S(1)}, f32[96,1024]{1,0:T(8,128)}, u32[]{:S(2)}) copy-start(f32[96,1024]{1,0:T(8,128)} %get-tuple-element.82) | copy-start | bytes 1179652
  182.0 12.9 %collective-permute-start.18 = (bf16[96,1024]{1,0:T(8,128)(2,1)S(1)}, bf16[96,1024]{1,0:T(8,128)(2,1)S(1)}, u32[]{:S(2)}, u32[]{:S(2)}) collective-permute-start(bf16[96,1024]{1,0:T(8,128)(2,1)S(1)} %get-tuple-element.68.refs_1_), channel_id=1, source_target_pairs={{0,32},{32,0},{64,96},{96,64},{1,33},{33,1},{65,97},{97,65},{2,34}... | collective-permute-start | bytes 589832 | tf_op jit(solution)/shard_map/ppermute | solution.py:31
  182.4 15.2 %collective-permute-start.19 = (bf16[96,1024]{1,0:T(8,128)(2,1)S(1)}, bf16[96,1024]{1,0:T(8,128)(2,1)S(1)}, u32[]{:S(2)}, u32[]{:S(2)}) collective-permute-start(bf16[96,1024]{1,0:T(8,128)(2,1)S(1)} %get-tuple-element.68.refs_1_), channel_id=1, source_target_pairs={{0,64},{32,96},{64,0},{96,32},{1,65},{33,97},{65,1},{97,33},{2,66}... | collective-permute-start | bytes 589832 | tf_op jit(solution)/shard_map/ppermute | solution.py:31
  184.2 13.4 %collective-permute-start.20 = (bf16[96,1024]{1,0:T(8,128)(2,1)S(1)}, bf16[96,1024]{1,0:T(8,128)(2,1)S(1)}, u32[]{:S(2)}, u32[]{:S(2)}) collective-permute-start(bf16[96,1024]{1,0:T(8,128)(2,1)S(1)} %get-tuple-element.68.refs_1_), channel_id=1, source_target_pairs={{0,96},{32,64},{64,32},{96,0},{1,97},{33,65},{65,33},{97,1},{2,98}... | collective-permute-start | bytes 589832 | tf_op jit(solution)/shard_map/ppermute | solution.py:31
  186.8 2.2 %copy-start.3 = (f32[96,1280]{1,0:T(8,128)S(1)}, f32[96,1280]{1,0:T(8,128)}, u32[]{:S(2)}) copy-start(f32[96,1280]{1,0:T(8,128)} %get-tuple-element.79) | copy-start | bytes 1474564
  186.8 2.2 %copy-start.4 = (f32[96,1280]{1,0:T(8,128)S(1)}, f32[96,1280]{1,0:T(8,128)}, u32[]{:S(2)}) copy-start(f32[96,1280]{1,0:T(8,128)} %get-tuple-element.75) | copy-start | bytes 1474564
  186.8 2.2 %copy-start.9 = (f32[96,1024]{1,0:T(8,128)S(1)}, f32[96,1024]{1,0:T(8,128)}, u32[]{:S(2)}) copy-start(f32[96,1024]{1,0:T(8,128)} %get-tuple-element.83) | copy-start | bytes 1179652

commit v9 on v8

--- a/solution.py
+++ b/solution.py
@@ -139,7 +139,7 @@
     order = jnp.arange(tok_rows, dtype=jnp.int32)
     earlier = (order[:, None] < order[None, :]).astype(jnp.bfloat16)
 
-    own = lax.dynamic_index_in_dim(owners, myself, 0, keepdims=False)
+    own = lax.dynamic_slice_in_dim(token_slab, myself * tok_rows, tok_rows, 0)[:, 0]
     named = own[None, :] == jnp.arange(OWNERS, dtype=jnp.int32)[:, None]
     before = jnp.dot(named.astype(jnp.bfloat16), earlier, preferred_element_type=jnp.float32)
     own_rank = jnp.sum(jnp.where(named, before, 0.0), axis=0).astype(jnp.int32)
@@ -196,8 +196,18 @@
     shape = (slab_rows, width)
     blocks = after(blocks, rows)
     table = place(None, here, blocks, tuple(spots), share, shape)
-    blocks = [block] + [swap_z(block, flip) for flip in range(1, GROUPS)]
-    spots = [(flip, 0, flip, span.start) for flip in range(GROUPS)]
+    half = (span.stop - span.start) // 2
+    blocks, spots = [], []
+    for start, (one, two) in ((0, (1, 3)), (half, (3, 1))):
+        part = block[:, start : start + half]
+        both = jnp.concatenate([part, swap_z(part, one)], axis=0)
+        spots += [
+            (len(blocks), 0, 0, span.start + start),
+            (len(blocks), share, one, span.start + start),
+            (len(blocks) + 1, 0, two, span.start + start),
+            (len(blocks) + 1, share, one ^ two, span.start + start),
+        ]
+        blocks += [both, swap_z(both, two)]
     table = place(table, here, blocks, tuple(spots), share, shape)
     return tuple(jnp.concatenate(parts, axis=1) for parts in zip(*states)) + (table,)
 

time: 200 us -> 199 us (level)
  waiting for transfers between devices: 84.6 us -> 87.4 us
  starting transfers between devices: 55.2 us -> 52.6 us
    ppermute x21 -> x22, waiting for transfers between devices: 57.1 us -> 60.2 us  [swap_z(): return lax.ppermute(block, 'dp', [(i, i ^ flip) for i in range(GROUPS)])]
    ppermute x21 -> x22, starting transfers between devices: 30.3 us -> 27.7 us  [swap_z(): return lax.ppermute(block, 'dp', [(i, i ^ flip) for i in range(GROUPS)])]
  transfers between devices with their start and end apart: 25 -> 26, of which waited for: 18 -> 17; matrix products, arithmetic and copies ran while one was open for 15% -> 15% of each run, Pallas kernels for 9% -> 9%
where the time goes in v9:
time: 199 us; the launch traced here: 198 us
  waiting for transfers between devices  87.4 us (44%)
  starting transfers between devices  52.6 us (26%)
  Pallas kernels  18.7 us (9%)
  other arithmetic  17.2 us (9%)
  matrix products  16.8 us (8%)
  local copies, waits for them, and re-layouts  3.83 us (2%)
    ppermute x22, waiting for transfers between devices, swap_z(): return lax.ppermute(block, 'dp', [(i, i ^ flip) for i in range(GROUPS)])  60.2 us
    ppermute x22, starting transfers between devices, swap_z(): return lax.ppermute(block, 'dp', [(i, i ^ flip) for i in range(GROUPS)])  27.7 us
    all_to_all x4, waiting for transfers between devices, local(): lax.all_to_all(outgoing, 'vocab', split_axis=0, concat_axis=0, tiled=True)  27.2 us
    all_to_all x4, starting transfers between devices, local(): lax.all_to_all(outgoing, 'vocab', split_axis=0, concat_axis=0, tiled=True)  24.9 us
    dot_general x4, matrix products, local(): jnp.dot(dispatch, input_grad[:, span], preferred_element_type=jnp.float32)  16.4 us
    pallas_call x4, Pallas kernels, combine(): pl.pallas_call(combine_body, grid=(width // tile,), out_shape=[jax.ShapeD...  14.7 us
    convert_element_type x4, other arithmetic, local(): block = states[-1][0].astype(jnp.bfloat16)  9.98 us
  transfers between devices with their start and end apart: 26, of which 17 were waited for; matrix products, arithmetic and copies ran while one was open for 15% of the time, Pallas kernels for 9%

profile of v9, /device:TPU:0, one launch (start us, length us, event | category | flops | bytes accessed | tf_op | source)
XLA Modules:
  0.0 197.7 jit_solution(16081938360177754985)
XLA Ops:
  0.6 0.7 constant_dynamic-slice_fusion
  1.3 0.2 fusion.7
  1.5 3.8 %fusion.3 = bf16[1024,1024]{1,0:T(8,128)(2,1)} fusion(bf16[512,4608]{1,0:T(8,128)(2,1)} %param.7, s32[512]{0:T(512)S(1)} %convert_add_fusion.4), kind=kOutput, calls=%fused_computation.8 | convolution fusion | flops 1075314688 | bytes 3147776 | tf_op jit(solution)/shard_map/dot_general | solution.py:167
  5.4 7.5 %all-to-all-start = ((bf16[32,32,1024]{2,1,0:T(8,128)(2,1)}), bf16[32,32,1024]{2,1,0:T(8,128)(2,1)S(1)}, u32[]{:S(2)}, u32[]{:S(2)}) async-start(bf16[32,32,1024]{2,1,0:T(8,128)(2,1)} %bitcast.15), calls=%async_computation | async-start | bytes 4194304 | tf_op jit(solution)/shard_map/all_to_all | solution.py:175
  13.6 0.6 select_reduce_fusion
  14.3 3.8 %fusion.4 = bf16[1024,1024]{1,0:T(8,128)(2,1)} fusion(bf16[512,4608]{1,0:T(8,128)(2,1)} %param.7, s32[512]{0:T(512)S(1)} %convert_add_fusion.4), kind=kOutput, calls=%fused_computation.9 | convolution fusion | flops 1075314688 | bytes 3147776 | tf_op jit(solution)/shard_map/dot_general | solution.py:167
  18.1 4.4 %convolution_convert_fusion = bf16[1024,1280]{1,0:T(8,128)(2,1)} fusion(bf16[512,4608]{1,0:T(8,128)(2,1)} %param.7, s32[512]{0:T(512)S(1)} %convert_add_fusion.4), kind=kOutput, calls=%fused_computation | convolution fusion | flops 1344012288 | bytes 3934208 | tf_op jit(solution)/shard_map/dot_general | solution.py:167
  22.5 4.4 %convolution_convert_fusion.1 = bf16[1024,1280]{1,0:T(8,128)(2,1)} fusion(bf16[512,4608]{1,0:T(8,128)(2,1)} %param.7, s32[512]{0:T(512)S(1)} %convert_add_fusion.4), kind=kOutput, calls=%fused_computation.1 | convolution fusion | flops 1344012288 | bytes 3934208 | tf_op jit(solution)/shard_map/dot_general | solution.py:167
  26.9 15.0 %all-to-all-done = bf16[32,32,1024]{2,1,0:T(8,128)(2,1)S(1)} async-done(((bf16[32,32,1024]{2,1,0:T(8,128)(2,1)}), bf16[32,32,1024]{2,1,0:T(8,128)(2,1)S(1)}, u32[]{:S(2)}, u32[]{:S(2)}) %all-to-all-start) | async-done | bytes 2097184 | tf_op jit(solution)/shard_map/all_to_all | solution.py:175
  41.8 1.4 copy-done.1
  43.2 5.1 %all-to-all-start.1 = ((bf16[32,32,1280]{2,1,0:T(8,128)(2,1)}), bf16[32,32,1280]{2,1,0:T(8,128)(2,1)}, u32[]{:S(2)}, u32[]{:S(2)}) async-start(bf16[32,32,1280]{2,1,0:T(8,128)(2,1)} %bitcast.13), calls=%async_computation.1 | async-start | bytes 5242880 | tf_op jit(solution)/shard_map/all_to_all | solution.py:175
  48.3 1.6 copy-done.2
  49.9 2.1 %shard_map.102 = (f32[96,1024]{1,0:T(8,128)S(1)}, bf16[96,1024]{1,0:T(8,128)(2,1)S(1)}, bf16[96,1024]{1,0:T(8,128)(2,1)S(1)}, bf16[96,1024]{1,0:T(8,128)(2,1)S(1)}) custom-call(s32[1]{0:T(128)} %bitcast.here_ref, s32[1,1024]{1,0:T(1,128)S(1)} %sub.19.target_ref, bf16[1,384,4608]{2,1,0:T(8,128)(2,1)S(1)} %copy-done, bf16[1024,1024]{1,0:T(8,128)(2,1)S(1)} %bitcast.11), custom_call_target="tpu_custom_call" | custom-call | flops 805306368 | bytes 4063232 | tf_op jit(solution)/shard_map/pallas_call | solution.py:67
  52.0 4.1 %collective-permute-start.2 = (bf16[96,1024]{1,0:T(8,128)(2,1)S(1)}, bf16[96,1024]{1,0:T(8,128)(2,1)S(1)}, u32[]{:S(2)}, u32[]{:S(2)}) collective-permute-start(bf16[96,1024]{1,0:T(8,128)(2,1)S(1)} %get-tuple-element.39), channel_id=1, source_target_pairs={{0,96},{32,64},{64,32},{96,0},{1,97},{33,65},{65,33},{97,1},{2,98}... | collective-permute-start | bytes 589832 | tf_op jit(solution)/shard_map/ppermute | solution.py:31
  56.1 0.9 collective-permute-start
  57.1 8.4 %collective-permute-done.2 = bf16[96,1024]{1,0:T(8,128)(2,1)S(1)} collective-permute-done((bf16[96,1024]{1,0:T(8,128)(2,1)S(1)}, bf16[96,1024]{1,0:T(8,128)(2,1)S(1)}, u32[]{:S(2)}, u32[]{:S(2)}) %collective-permute-start.2) | collective-permute-done | bytes 196640 | tf_op jit(solution)/shard_map/ppermute | solution.py:31
  65.5 0.7 collective-permute-done
  66.2 2.5 %fusion.25 = (bf16[96,1024]{1,0:T(8,128)(2,1)S(1)}, f32[96,1024]{1,0:T(8,128)}, f32[96,1024]{1,0:T(8,128)}, f32[96,1024]{1,0:T(8,128)}) fusion(f32[96,4608]{1,0:T(8,128)} %param.11, bf16[96,1024]{1,0:T(8,128)(2,1)S(1)} %collective-permute-done.2, bf16[96,1024]{1,0:T(8,128)(2,1)S(1)} %collective-permute-done.1, f32[96,1024]{1,0:T(8,128)S(1)} %get-tuple-element.36, ...), kind=kLoop, calls=%fused_computation.60 | loop fusion | flops 2162688 | bytes 3538944 | tf_op jit(solution)/shard_map/convert_element_type | solution.py:183
  68.8 2.9 %collective-permute-start.6 = (bf16[96,1024]{1,0:T(8,128)(2,1)S(1)}, bf16[96,1024]{1,0:T(8,128)(2,1)S(1)}, u32[]{:S(2)}, u32[]{:S(2)}) collective-permute-start(bf16[96,1024]{1,0:T(8,128)(2,1)S(1)} %get-tuple-element.80), channel_id=1, source_target_pairs={{0,96},{32,64},{64,32},{96,0},{1,97},{33,65},{65,33},{97,1},{2,98}... | collective-permute-start | bytes 589832 | tf_op jit(solution)/shard_map/ppermute | solution.py:31
  71.6 4.5 %collective-permute-done.6 = bf16[96,1024]{1,0:T(8,128)(2,1)S(1)} collective-permute-done((bf16[96,1024]{1,0:T(8,128)(2,1)S(1)}, bf16[96,1024]{1,0:T(8,128)(2,1)S(1)}, u32[]{:S(2)}, u32[]{:S(2)}) %collective-permute-start.6) | collective-permute-done | bytes 196640 | tf_op jit(solution)/shard_map/ppermute | solution.py:31
  76.1 0.8 pad_maximum_fusion.5.refs_0_
  76.9 6.0 %all-to-all-done.1 = bf16[32,32,1280]{2,1,0:T(8,128)(2,1)} async-done(((bf16[32,32,1280]{2,1,0:T(8,128)(2,1)}), bf16[32,32,1280]{2,1,0:T(8,128)(2,1)}, u32[]{:S(2)}, u32[]{:S(2)}) %all-to-all-start.1) | async-done | bytes 2621472 | tf_op jit(solution)/shard_map/all_to_all | solution.py:175
  82.9 4.8 %all-to-all-start.2 = ((bf16[32,32,1280]{2,1,0:T(8,128)(2,1)}), bf16[32,32,1280]{2,1,0:T(8,128)(2,1)}, u32[]{:S(2)}, u32[]{:S(2)}) async-start(bf16[32,32,1280]{2,1,0:T(8,128)(2,1)} %bitcast.12), calls=%async_computation.2 | async-start | bytes 5242880 | tf_op jit(solution)/shard_map/all_to_all | solution.py:175
  87.7 4.6 %shard_map.103 = (f32[96,1280]{1,0:T(8,128)S(1)}, bf16[96,1280]{1,0:T(8,128)(2,1)S(1)}, bf16[96,1280]{1,0:T(8,128)(2,1)S(1)}, bf16[96,1280]{1,0:T(8,128)(2,1)S(1)}) custom-call(s32[1]{0:T(128)} %bitcast.here_ref, s32[1,1024]{1,0:T(1,128)S(1)} %sub.19.target_ref, bf16[1,384,4608]{2,1,0:T(8,128)(2,1)S(1)} %copy-done, bf16[1024,1280]{1,0:T(8,128)(2,1)} %bitcast.5.part_ref), custom_call_target="tpu_custom_call" | custom-call | flops 1006632960 | bytes 5079040 | tf_op jit(solution)/shard_map/pallas_call | solution.py:67
  92.3 4.1 %collective-permute-start.5 = (bf16[96,1280]{1,0:T(8,128)(2,1)S(1)}, bf16[96,1280]{1,0:T(8,128)(2,1)S(1)}, u32[]{:S(2)}, u32[]{:S(2)}) collective-permute-start(bf16[96,1280]{1,0:T(8,128)(2,1)S(1)} %get-tuple-element.45), channel_id=1, source_target_pairs={{0,96},{32,64},{64,32},{96,0},{1,97},{33,65},{65,33},{97,1},{2,98}... | collective-permute-start | bytes 737288 | tf_op jit(solution)/shard_map/ppermute | solution.py:31
  96.4 0.9 collective-permute-start.3
  97.3 10.5 %collective-permute-done.5 = bf16[96,1280]{1,0:T(8,128)(2,1)S(1)} collective-permute-done((bf16[96,1280]{1,0:T(8,128)(2,1)S(1)}, bf16[96,1280]{1,0:T(8,128)(2,1)S(1)}, u32[]{:S(2)}, u32[]{:S(2)}) %collective-permute-start.5) | collective-permute-done | bytes 245792 | tf_op jit(solution)/shard_map/ppermute | solution.py:31
  107.9 0.7 collective-permute-done.3
  108.6 2.8 %fusion.23 = (bf16[96,1280]{1,0:T(8,128)(2,1)S(1)}, f32[96,1280]{1,0:T(8,128)}, f32[96,1280]{1,0:T(8,128)}, f32[96,1280]{1,0:T(8,128)}) fusion(f32[96,4608]{1,0:T(8,128)} %param.11, bf16[96,1280]{1,0:T(8,128)(2,1)S(1)} %collective-permute-done.5, bf16[96,1280]{1,0:T(8,128)(2,1)S(1)} %collective-permute-done.4, f32[96,1280]{1,0:T(8,128)S(1)} %get-tuple-element.42, ...), kind=kLoop, calls=%fused_computation.59 | loop fusion | flops 2703360 | bytes 4423680 | tf_op jit(solution)/shard_map/convert_element_type | solution.py:183
  111.4 2.9 %collective-permute-start.10 = (bf16[96,1280]{1,0:T(8,128)(2,1)S(1)}, bf16[96,1280]{1,0:T(8,128)(2,1)S(1)}, u32[]{:S(2)}, u32[]{:S(2)}) collective-permute-start(bf16[96,1280]{1,0:T(8,128)(2,1)S(1)} %get-tuple-element.76), channel_id=1, source_target_pairs={{0,96},{32,64},{64,32},{96,0},{1,97},{33,65},{65,33},{97,1},{2,98}... | collective-permute-start | bytes 737288 | tf_op jit(solution)/shard_map/ppermute | solution.py:31
  114.2 5.6 %collective-permute-done.10 = bf16[96,1280]{1,0:T(8,128)(2,1)S(1)} collective-permute-done((bf16[96,1280]{1,0:T(8,128)(2,1)S(1)}, bf16[96,1280]{1,0:T(8,128)(2,1)S(1)}, u32[]{:S(2)}, u32[]{:S(2)}) %collective-permute-start.10) | collective-permute-done | bytes 245792 | tf_op jit(solution)/shard_map/ppermute | solution.py:31
  119.8 0.8 pad_maximum_fusion.3.refs_2_
  120.7 1.7 all-to-all-done.2
  122.3 2.1 %collective-permute-done.11.refs_1_ = bf16[192,1024]{1,0:T(8,128)(2,1)} collective-permute-done((bf16[192,1024]{1,0:T(8,128)(2,1)}, bf16[192,1024]{1,0:T(8,128)(2,1)}, u32[]{:S(2)}, u32[]{:S(2)}) %collective-permute-start.11) | collective-permute-done | bytes 393248 | tf_op jit(solution)/shard_map/ppermute | solution.py:31
  124.4 7.5 %all-to-all-start.3 = ((bf16[32,32,1024]{2,1,0:T(8,128)(2,1)}), bf16[32,32,1024]{2,1,0:T(8,128)(2,1)}, u32[]{:S(2)}, u32[]{:S(2)}) async-start(bf16[32,32,1024]{2,1,0:T(8,128)(2,1)} %bitcast.14), calls=%async_computation.3 | async-start | bytes 4194304 | tf_op jit(solution)/shard_map/all_to_all | solution.py:175
  132.0 4.6 %shard_map.104 = (f32[96,1280]{1,0:T(8,128)S(1)}, bf16[96,1280]{1,0:T(8,128)(2,1)S(1)}, bf16[96,1280]{1,0:T(8,128)(2,1)S(1)}, bf16[96,1280]{1,0:T(8,128)(2,1)S(1)}) custom-call(s32[1]{0:T(128)} %bitcast.here_ref, s32[1,1024]{1,0:T(1,128)S(1)} %sub.19.target_ref, bf16[1,384,4608]{2,1,0:T(8,128)(2,1)S(1)} %copy-done, bf16[1024,1280]{1,0:T(8,128)(2,1)} %bitcast.7.part_ref), custom_call_target="tpu_custom_call" | custom-call | flops 1006632960 | bytes 5079040 | tf_op jit(solution)/shard_map/pallas_call | solution.py:67
  136.5 0.7 collective-permute-start.9
  137.2 1.7 collective-permute-start.8
  138.9 1.7 collective-permute-start.7
  140.7 0.3 collective-permute-start.12
  141.0 10.2 %collective-permute-done.9 = bf16[96,1280]{1,0:T(8,128)(2,1)S(1)} collective-permute-done((bf16[96,1280]{1,0:T(8,128)(2,1)S(1)}, bf16[96,1280]{1,0:T(8,128)(2,1)S(1)}, u32[]{:S(2)}, u32[]{:S(2)}) %collective-permute-start.9) | collective-permute-done | bytes 245792 | tf_op jit(solution)/shard_map/ppermute | solution.py:31
  151.1 1.6 collective-permute-done.7
  152.8 2.9 %fusion.21 = (bf16[96,1280]{1,0:T(8,128)(2,1)}, f32[96,1280]{1,0:T(8,128)}, f32[96,1280]{1,0:T(8,128)}, f32[96,1280]{1,0:T(8,128)}) fusion(f32[96,4608]{1,0:T(8,128)} %param.11, bf16[96,1280]{1,0:T(8,128)(2,1)S(1)} %collective-permute-done.9, bf16[96,1280]{1,0:T(8,128)(2,1)S(1)} %collective-permute-done.8, f32[96,1280]{1,0:T(8,128)S(1)} %get-tuple-element.48, ...), kind=kLoop, calls=%fused_computation.58 | loop fusion | flops 2703360 | bytes 4423680 | tf_op jit(solution)/shard_map/convert_element_type | solution.py:183
  155.6 0.6 collective-permute-start.16
  156.3 4.6 %all-to-all-done.3 = bf16[32,32,1024]{2,1,0:T(8,128)(2,1)} async-done(((bf16[32,32,1024]{2,1,0:T(8,128)(2,1)}), bf16[32,32,1024]{2,1,0:T(8,128)(2,1)}, u32[]{:S(2)}, u32[]{:S(2)}) %all-to-all-start.3) | async-done | bytes 2097184 | tf_op jit(solution)/shard_map/all_to_all | solution.py:175
  160.9 3.5 %shard_map.105 = (f32[96,1024]{1,0:T(8,128)S(1)}, bf16[96,1024]{1,0:T(8,128)(2,1)S(1)}, bf16[96,1024]{1,0:T(8,128)(2,1)S(1)}, bf16[96,1024]{1,0:T(8,128)(2,1)S(1)}) custom-call(s32[1]{0:T(128)} %bitcast.here_ref, s32[1,1024]{1,0:T(1,128)S(1)} %sub.19.target_ref, bf16[1,384,4608]{2,1,0:T(8,128)(2,1)S(1)} %copy-done, bf16[1024,1024]{1,0:T(8,128)(2,1)} %bitcast.9.part_ref), custom_call_target="tpu_custom_call" | custom-call | flops 805306368 | bytes 4063232 | tf_op jit(solution)/shard_map/pallas_call | solution.py:67
  164.4 0.7 collective-permute-start.15
  165.1 1.7 collective-permute-start.14
  166.8 1.7 collective-permute-start.13
  168.6 1.1 pad_maximum_fusion.4.refs_4_
  169.7 0.4 collective-permute-start.17
  170.0 6.3 %collective-permute-done.15 = bf16[96,1024]{1,0:T(8,128)(2,1)S(1)} collective-permute-done((bf16[96,1024]{1,0:T(8,128)(2,1)S(1)}, bf16[96,1024]{1,0:T(8,128)(2,1)S(1)}, u32[]{:S(2)}, u32[]{:S(2)}) %collective-permute-start.15) | collective-permute-done | bytes 196640 | tf_op jit(solution)/shard_map/ppermute | solution.py:31
  176.4 2.2 %collective-permute-done.13 = bf16[96,1024]{1,0:T(8,128)(2,1)S(1)} collective-permute-done((bf16[96,1024]{1,0:T(8,128)(2,1)S(1)}, bf16[96,1024]{1,0:T(8,128)(2,1)S(1)}, u32[]{:S(2)}, u32[]{:S(2)}) %collective-permute-start.13) | collective-permute-done | bytes 196640 | tf_op jit(solution)/shard_map/ppermute | solution.py:31
  178.6 1.8 fusion.19
  180.5 0.4 collective-permute-start.18
  180.8 0.9 collective-permute-start.20
  181.8 2.1 %pad_maximum_fusion = (f32[96,4608]{1,0:T(8,128)}, f32[96,4608]{1,0:T(8,128)}) fusion(f32[96,1024]{1,0:T(8,128)S(1)} %get-tuple-element.69, f32[96,1280]{1,0:T(8,128)S(1)} %copy-done.7, f32[96,1280]{1,0:T(8,128)S(1)} %copy-done.5, f32[96,1024]{1,0:T(8,128)S(1)} %copy-done.10, f32[96,1024]{1,0:T(8,128)S(1)} %get-tuple-element.70, ...), kind=kLoop, calls=%fused_computation.10 | loop fusion | flops 2654208 | bytes 7077888 | tf_op jit(solution)/shard_map/concatenate | solution.py:212
  183.9 5.7 %collective-permute-done.18 = bf16[96,512]{1,0:T(8,128)(2,1)S(1)} collective-permute-done((bf16[96,512]{1,0:T(8,128)(2,1)S(1)}, bf16[96,512]{1,0:T(8,128)(2,1)S(1)}, u32[]{:S(2)}, u32[]{:S(2)}) %collective-permute-start.18) | collective-permute-done | bytes 98336 | tf_op jit(solution)/shard_map/ppermute | solution.py:31
  189.6 0.7 collective-permute-start.19
  190.4 0.3 collective-permute-start.21
  190.7 1.3 pad_maximum_fusion.2
  192.0 3.0 %shard_map.106.refs_0_ = bf16[384,4608]{1,0:T(8,128)(2,1)} custom-call(s32[1]{0:T(128)} %bitcast.here_ref, bf16[192,1024]{1,0:T(8,128)(2,1)} %pad_maximum_fusion.5.refs_0_, bf16[192,1024]{1,0:T(8,128)(2,1)} %collective-permute-done.11.refs_1_, bf16[192,1280]{1,0:T(8,128)(2,1)} %pad_maximum_fusion.3.refs_2_, ...), custom_call_target="tpu_custom_call" | custom-call | bytes 5505024 | tf_op jit(solution)/shard_map/pallas_call | solution.py:106
  195.1 1.5 collective-permute-done.19.refs_2_
  196.6 0.9 shard_map.107
  (49 shorter events, 0.8 us)
Async XLA Ops:
  5.4 7.5 %copy-start.13 = (s32[16384,1]{0,1:T(1,128)S(1)}, s32[16384,1]{0,1:T(1,128)}, u32[]{:S(2)}) copy-start(s32[16384,1]{0,1:T(1,128)} %param.9) | copy-start | bytes 196612
  5.4 7.8 %copy-start.12 = (s32[16384,1]{0,1:T(1,128)S(1)}, s32[16384,1]{0,1:T(1,128)}, u32[]{:S(2)}) copy-start(s32[16384,1]{0,1:T(1,128)} %param.8) | copy-start | bytes 196612
  5.4 36.5 %all-to-all-start = ((bf16[32,32,1024]{2,1,0:T(8,128)(2,1)}), bf16[32,32,1024]{2,1,0:T(8,128)(2,1)S(1)}, u32[]{:S(2)}, u32[]{:S(2)}) async-start(bf16[32,32,1024]{2,1,0:T(8,128)(2,1)} %bitcast.15), calls=%async_computation | async-start | bytes 4194304 | tf_op jit(solution)/shard_map/all_to_all | solution.py:175
  41.8 1.4 copy-start.1
  43.2 5.1 %copy-start = (bf16[1,384,4608]{2,1,0:T(8,128)(2,1)S(1)}, bf16[1,384,4608]{2,1,0:T(8,128)(2,1)}, u32[]{:S(2)}) copy-start(bf16[1,384,4608]{2,1,0:T(8,128)(2,1)} %head_ref.7) | copy-start | bytes 10616836
  43.2 39.7 %all-to-all-start.1 = ((bf16[32,32,1280]{2,1,0:T(8,128)(2,1)}), bf16[32,32,1280]{2,1,0:T(8,128)(2,1)}, u32[]{:S(2)}, u32[]{:S(2)}) async-start(bf16[32,32,1280]{2,1,0:T(8,128)(2,1)} %bitcast.13), calls=%async_computation.1 | async-start | bytes 5242880 | tf_op jit(solution)/shard_map/all_to_all | solution.py:175
  48.3 1.6 copy-start.2
  52.0 13.5 %collective-permute-start.2 = (bf16[96,1024]{1,0:T(8,128)(2,1)S(1)}, bf16[96,1024]{1,0:T(8,128)(2,1)S(1)}, u32[]{:S(2)}, u32[]{:S(2)}) collective-permute-start(bf16[96,1024]{1,0:T(8,128)(2,1)S(1)} %get-tuple-element.39), channel_id=1, source_target_pairs={{0,96},{32,64},{64,32},{96,0},{1,97},{33,65},{65,33},{97,1},{2,98}... | collective-permute-start | bytes 589832 | tf_op jit(solution)/shard_map/ppermute | solution.py:31
  56.1 9.4 %collective-permute-start.1 = (bf16[96,1024]{1,0:T(8,128)(2,1)S(1)}, bf16[96,1024]{1,0:T(8,128)(2,1)S(1)}, u32[]{:S(2)}, u32[]{:S(2)}) collective-permute-start(bf16[96,1024]{1,0:T(8,128)(2,1)S(1)} %get-tuple-element.38), channel_id=1, source_target_pairs={{0,64},{32,96},{64,0},{96,32},{1,65},{33,97},{65,1},{97,33},{2,66}... | collective-permute-start | bytes 589832 | tf_op jit(solution)/shard_map/ppermute | solution.py:31
  56.1 10.1 %collective-permute-start = (bf16[96,1024]{1,0:T(8,128)(2,1)S(1)}, bf16[96,1024]{1,0:T(8,128)(2,1)S(1)}, u32[]{:S(2)}, u32[]{:S(2)}) collective-permute-start(bf16[96,1024]{1,0:T(8,128)(2,1)S(1)} %get-tuple-element.37), channel_id=1, source_target_pairs={{0,32},{32,0},{64,96},{96,64},{1,33},{33,1},{65,97},{97,65},{2,34}... | collective-permute-start | bytes 589832 | tf_op jit(solution)/shard_map/ppermute | solution.py:31
  68.8 7.4 %collective-permute-start.6 = (bf16[96,1024]{1,0:T(8,128)(2,1)S(1)}, bf16[96,1024]{1,0:T(8,128)(2,1)S(1)}, u32[]{:S(2)}, u32[]{:S(2)}) collective-permute-start(bf16[96,1024]{1,0:T(8,128)(2,1)S(1)} %get-tuple-element.80), channel_id=1, source_target_pairs={{0,96},{32,64},{64,32},{96,0},{1,97},{33,65},{65,33},{97,1},{2,98}... | collective-permute-start | bytes 589832 | tf_op jit(solution)/shard_map/ppermute | solution.py:31
  82.9 39.4 %all-to-all-start.2 = ((bf16[32,32,1280]{2,1,0:T(8,128)(2,1)}), bf16[32,32,1280]{2,1,0:T(8,128)(2,1)}, u32[]{:S(2)}, u32[]{:S(2)}) async-start(bf16[32,32,1280]{2,1,0:T(8,128)(2,1)} %bitcast.12), calls=%async_computation.2 | async-start | bytes 5242880 | tf_op jit(solution)/shard_map/all_to_all | solution.py:175
  92.3 15.6 %collective-permute-start.5 = (bf16[96,1280]{1,0:T(8,128)(2,1)S(1)}, bf16[96,1280]{1,0:T(8,128)(2,1)S(1)}, u32[]{:S(2)}, u32[]{:S(2)}) collective-permute-start(bf16[96,1280]{1,0:T(8,128)(2,1)S(1)} %get-tuple-element.45), channel_id=1, source_target_pairs={{0,96},{32,64},{64,32},{96,0},{1,97},{33,65},{65,33},{97,1},{2,98}... | collective-permute-start | bytes 737288 | tf_op jit(solution)/shard_map/ppermute | solution.py:31
  96.4 11.5 %collective-permute-start.4 = (bf16[96,1280]{1,0:T(8,128)(2,1)S(1)}, bf16[96,1280]{1,0:T(8,128)(2,1)S(1)}, u32[]{:S(2)}, u32[]{:S(2)}) collective-permute-start(bf16[96,1280]{1,0:T(8,128)(2,1)S(1)} %get-tuple-element.44), channel_id=1, source_target_pairs={{0,64},{32,96},{64,0},{96,32},{1,65},{33,97},{65,1},{97,33},{2,66}... | collective-permute-start | bytes 737288 | tf_op jit(solution)/shard_map/ppermute | solution.py:31
  96.4 12.2 %collective-permute-start.3 = (bf16[96,1280]{1,0:T(8,128)(2,1)S(1)}, bf16[96,1280]{1,0:T(8,128)(2,1)S(1)}, u32[]{:S(2)}, u32[]{:S(2)}) collective-permute-start(bf16[96,1280]{1,0:T(8,128)(2,1)S(1)} %get-tuple-element.43), channel_id=1, source_target_pairs={{0,32},{32,0},{64,96},{96,64},{1,33},{33,1},{65,97},{97,65},{2,34}... | collective-permute-start | bytes 737288 | tf_op jit(solution)/shard_map/ppermute | solution.py:31
  111.4 8.4 %collective-permute-start.10 = (bf16[96,1280]{1,0:T(8,128)(2,1)S(1)}, bf16[96,1280]{1,0:T(8,128)(2,1)S(1)}, u32[]{:S(2)}, u32[]{:S(2)}) collective-permute-start(bf16[96,1280]{1,0:T(8,128)(2,1)S(1)} %get-tuple-element.76), channel_id=1, source_target_pairs={{0,96},{32,64},{64,32},{96,0},{1,97},{33,65},{65,33},{97,1},{2,98}... | collective-permute-start | bytes 737288 | tf_op jit(solution)/shard_map/ppermute | solution.py:31
  114.2 10.2 %collective-permute-start.11 = (bf16[192,1024]{1,0:T(8,128)(2,1)}, bf16[192,1024]{1,0:T(8,128)(2,1)}, u32[]{:S(2)}, u32[]{:S(2)}) collective-permute-start(bf16[192,1024]{1,0:T(8,128)(2,1)} %pad_maximum_fusion.5.refs_0_), channel_id=1, source_target_pairs={{0,32},{32,0},{64,96},{96,64},{1,33},{33,1},{65,97},{97,65},{2,34}... | collective-permute-start | bytes 1179656 | tf_op jit(solution)/shard_map/ppermute | solution.py:31
  124.4 36.4 %all-to-all-start.3 = ((bf16[32,32,1024]{2,1,0:T(8,128)(2,1)}), bf16[32,32,1024]{2,1,0:T(8,128)(2,1)}, u32[]{:S(2)}, u32[]{:S(2)}) async-start(bf16[32,32,1024]{2,1,0:T(8,128)(2,1)} %bitcast.14), calls=%async_computation.3 | async-start | bytes 4194304 | tf_op jit(solution)/shard_map/all_to_all | solution.py:175
  136.5 14.6 %collective-permute-start.9 = (bf16[96,1280]{1,0:T(8,128)(2,1)S(1)}, bf16[96,1280]{1,0:T(8,128)(2,1)S(1)}, u32[]{:S(2)}, u32[]{:S(2)}) collective-permute-start(bf16[96,1280]{1,0:T(8,128)(2,1)S(1)} %get-tuple-element.51), channel_id=1, source_target_pairs={{0,96},{32,64},{64,32},{96,0},{1,97},{33,65},{65,33},{97,1},{2,98}... | collective-permute-start | bytes 737288 | tf_op jit(solution)/shard_map/ppermute | solution.py:31
  137.2 13.9 %collective-permute-start.8 = (bf16[96,1280]{1,0:T(8,128)(2,1)S(1)}, bf16[96,1280]{1,0:T(8,128)(2,1)S(1)}, u32[]{:S(2)}, u32[]{:S(2)}) collective-permute-start(bf16[96,1280]{1,0:T(8,128)(2,1)S(1)} %get-tuple-element.50), channel_id=1, source_target_pairs={{0,64},{32,96},{64,0},{96,32},{1,65},{33,97},{65,1},{97,33},{2,66}... | collective-permute-start | bytes 737288 | tf_op jit(solution)/shard_map/ppermute | solution.py:31
  138.9 13.8 %collective-permute-start.7 = (bf16[96,1280]{1,0:T(8,128)(2,1)S(1)}, bf16[96,1280]{1,0:T(8,128)(2,1)S(1)}, u32[]{:S(2)}, u32[]{:S(2)}) collective-permute-start(bf16[96,1280]{1,0:T(8,128)(2,1)S(1)} %get-tuple-element.49), channel_id=1, source_target_pairs={{0,32},{32,0},{64,96},{96,64},{1,33},{33,1},{65,97},{97,65},{2,34}... | collective-permute-start | bytes 737288 | tf_op jit(solution)/shard_map/ppermute | solution.py:31
  140.7 23.7 %collective-permute-start.12 = (bf16[192,1280]{1,0:T(8,128)(2,1)}, bf16[192,1280]{1,0:T(8,128)(2,1)}, u32[]{:S(2)}, u32[]{:S(2)}) collective-permute-start(bf16[192,1280]{1,0:T(8,128)(2,1)} %pad_maximum_fusion.3.refs_2_), channel_id=1, source_target_pairs={{0,32},{32,0},{64,96},{96,64},{1,33},{33,1},{65,97},{97,65},{2,34}... | collective-permute-start | bytes 1474568 | tf_op jit(solution)/shard_map/ppermute | solution.py:31
  155.6 13.0 %collective-permute-start.16 = (bf16[96,1280]{1,0:T(8,128)(2,1)}, bf16[96,1280]{1,0:T(8,128)(2,1)}, u32[]{:S(2)}, u32[]{:S(2)}) collective-permute-start(bf16[96,1280]{1,0:T(8,128)(2,1)} %get-tuple-element.72), channel_id=1, source_target_pairs={{0,96},{32,64},{64,32},{96,0},{1,97},{33,65},{65,33},{97,1},{2,98}... | collective-permute-start | bytes 737288 | tf_op jit(solution)/shard_map/ppermute | solution.py:31
  164.4 12.0 %collective-permute-start.15 = (bf16[96,1024]{1,0:T(8,128)(2,1)S(1)}, bf16[96,1024]{1,0:T(8,128)(2,1)S(1)}, u32[]{:S(2)}, u32[]{:S(2)}) collective-permute-start(bf16[96,1024]{1,0:T(8,128)(2,1)S(1)} %get-tuple-element.61), channel_id=1, source_target_pairs={{0,96},{32,64},{64,32},{96,0},{1,97},{33,65},{65,33},{97,1},{2,98}... | collective-permute-start | bytes 589832 | tf_op jit(solution)/shard_map/ppermute | solution.py:31
  165.1 11.2 %collective-permute-start.14 = (bf16[96,1024]{1,0:T(8,128)(2,1)S(1)}, bf16[96,1024]{1,0:T(8,128)(2,1)S(1)}, u32[]{:S(2)}, u32[]{:S(2)}) collective-permute-start(bf16[96,1024]{1,0:T(8,128)(2,1)S(1)} %get-tuple-element.60), channel_id=1, source_target_pairs={{0,64},{32,96},{64,0},{96,32},{1,65},{33,97},{65,1},{97,33},{2,66}... | collective-permute-start | bytes 589832 | tf_op jit(solution)/shard_map/ppermute | solution.py:31
  166.8 11.8 %collective-permute-start.13 = (bf16[96,1024]{1,0:T(8,128)(2,1)S(1)}, bf16[96,1024]{1,0:T(8,128)(2,1)S(1)}, u32[]{:S(2)}, u32[]{:S(2)}) collective-permute-start(bf16[96,1024]{1,0:T(8,128)(2,1)S(1)} %get-tuple-element.59), channel_id=1, source_target_pairs={{0,32},{32,0},{64,96},{96,64},{1,33},{33,1},{65,97},{97,65},{2,34}... | collective-permute-start | bytes 589832 | tf_op jit(solution)/shard_map/ppermute | solution.py:31
  169.7 22.4 %collective-permute-start.17 = (bf16[192,1280]{1,0:T(8,128)(2,1)S(1)}, bf16[192,1280]{1,0:T(8,128)(2,1)S(1)}, u32[]{:S(2)}, u32[]{:S(2)}) collective-permute-start(bf16[192,1280]{1,0:T(8,128)(2,1)S(1)} %pad_maximum_fusion.4.refs_4_), channel_id=1, source_target_pairs={{0,32},{32,0},{64,96},{96,64},{1,33},{33,1},{65,97},{97,65},{2,34}... | collective-permute-start | bytes 1474568 | tf_op jit(solution)/shard_map/ppermute | solution.py:31
  178.6 3.1 %copy-start.5 = (f32[96,1280]{1,0:T(8,128)S(1)}, f32[96,1280]{1,0:T(8,128)}, u32[]{:S(2)}) copy-start(f32[96,1280]{1,0:T(8,128)} %get-tuple-element.77) | copy-start | bytes 1474564
  178.6 3.1 %copy-start.6 = (f32[96,1280]{1,0:T(8,128)S(1)}, f32[96,1280]{1,0:T(8,128)}, u32[]{:S(2)}) copy-start(f32[96,1280]{1,0:T(8,128)} %get-tuple-element.78) | copy-start | bytes 1474564
  178.6 3.1 %copy-start.7 = (f32[96,1280]{1,0:T(8,128)S(1)}, f32[96,1280]{1,0:T(8,128)}, u32[]{:S(2)}) copy-start(f32[96,1280]{1,0:T(8,128)} %get-tuple-element.73) | copy-start | bytes 1474564
  178.6 3.1 %copy-start.8 = (f32[96,1280]{1,0:T(8,128)S(1)}, f32[96,1280]{1,0:T(8,128)}, u32[]{:S(2)}) copy-start(f32[96,1280]{1,0:T(8,128)} %get-tuple-element.74) | copy-start | bytes 1474564
  178.6 3.1 %copy-start.10 = (f32[96,1024]{1,0:T(8,128)S(1)}, f32[96,1024]{1,0:T(8,128)}, u32[]{:S(2)}) copy-start(f32[96,1024]{1,0:T(8,128)} %get-tuple-element.81) | copy-start | bytes 1179652
  178.6 3.1 %copy-start.11 = (f32[96,1024]{1,0:T(8,128)S(1)}, f32[96,1024]{1,0:T(8,128)}, u32[]{:S(2)}) copy-start(f32[96,1024]{1,0:T(8,128)} %get-tuple-element.82) | copy-start | bytes 1179652
  180.5 9.2 %collective-permute-start.18 = (bf16[96,512]{1,0:T(8,128)(2,1)S(1)}, bf16[96,512]{1,0:T(8,128)(2,1)S(1)}, u32[]{:S(2)}, u32[]{:S(2)}) collective-permute-start(bf16[96,512]{1,0:T(8,128)(2,1)S(1)} %get-tuple-element.85), channel_id=1, source_target_pairs={{0,32},{32,0},{64,96},{96,64},{1,33},{33,1},{65,97},{97,65},{2,34}... | collective-permute-start | bytes 294920 | tf_op jit(solution)/shard_map/ppermute | solution.py:31
  180.8 9.5 %collective-permute-start.20 = (bf16[96,512]{1,0:T(8,128)(2,1)S(1)}, bf16[96,512]{1,0:T(8,128)(2,1)S(1)}, u32[]{:S(2)}, u32[]{:S(2)}) collective-permute-start(bf16[96,512]{1,0:T(8,128)(2,1)S(1)} %get-tuple-element.84), channel_id=1, source_target_pairs={{0,96},{32,64},{64,32},{96,0},{1,97},{33,65},{65,33},{97,1},{2,98}... | collective-permute-start | bytes 294920 | tf_op jit(solution)/shard_map/ppermute | solution.py:31
  181.7 8.9 %copy-start.3 = (f32[96,1280]{1,0:T(8,128)S(1)}, f32[96,1280]{1,0:T(8,128)}, u32[]{:S(2)}) copy-start(f32[96,1280]{1,0:T(8,128)} %get-tuple-element.79) | copy-start | bytes 1474564
  181.7 8.9 %copy-start.4 = (f32[96,1280]{1,0:T(8,128)S(1)}, f32[96,1280]{1,0:T(8,128)}, u32[]{:S(2)}) copy-start(f32[96,1280]{1,0:T(8,128)} %get-tuple-element.75) | copy-start | bytes 1474564
  181.7 8.9 %copy-start.9 = (f32[96,1024]{1,0:T(8,128)S(1)}, f32[96,1024]{1,0:T(8,128)}, u32[]{:S(2)}) copy-start(f32[96,1024]{1,0:T(8,128)} %get-tuple-element.83) | copy-start | bytes 1179652
  189.6 7.0 %collective-permute-start.19 = (bf16[192,512]{1,0:T(8,128)(2,1)S(1)}, bf16[192,512]{1,0:T(8,128)(2,1)S(1)}, u32[]{:S(2)}, u32[]{:S(2)}) collective-permute-start(bf16[192,512]{1,0:T(8,128)(2,1)S(1)} %pad_maximum_fusion.6.refs_1_), channel_id=1, source_target_pairs={{0,96},{32,64},{64,32},{96,0},{1,97},{33,65},{65,33},{97,1},{2,98}... | collective-permute-start | bytes 589832 | tf_op jit(solution)/shard_map/ppermute | solution.py:31
  190.4 6.2 %collective-permute-start.21 = (bf16[192,512]{1,0:T(8,128)(2,1)S(1)}, bf16[192,512]{1,0:T(8,128)(2,1)S(1)}, u32[]{:S(2)}, u32[]{:S(2)}) collective-permute-start(bf16[192,512]{1,0:T(8,128)(2,1)S(1)} %pad_maximum_fusion.7.refs_3_), channel_id=1, source_target_pairs={{0,32},{32,0},{64,96},{96,64},{1,33},{33,1},{65,97},{97,65},{2,34}... | collective-permute-start | bytes 589832 | tf_op jit(solution)/shard_map/ppermute | solution.py:31

commit v10 on v9

--- a/solution.py
+++ b/solution.py
@@ -19,7 +19,7 @@
 OWNERS = 32
 CAPACITY = 32
 UNITS = (8, 10, 10, 8)
-TILE = 2
+PLACES = (20, 0, 10, 28)
 MIB = 1024 * 1024
 
 
@@ -59,14 +59,15 @@
         out_ref[...] = block.astype(out_ref.dtype)
 
 
-def combine(here, target, head_grad, part, start, tile):
+def combine(here, target, head_grad, part, start):
     slots = target.shape[1]
     width = part.shape[1]
     slab_rows = head_grad.shape[1]
     share = slab_rows // GROUPS
+    tile = width // 2
     return pl.pallas_call(
         combine_body,
-        grid=(width // tile,),
+        grid=(2,),
         out_shape=[jax.ShapeDtypeStruct((share, width), jnp.float32)]
         + [jax.ShapeDtypeStruct((share, width), jnp.bfloat16)] * (GROUPS - 1),
         in_specs=[
@@ -159,8 +160,7 @@
     target = target.reshape(1, slots)
 
     unit = width // sum(UNITS)
-    edges = [unit * sum(UNITS[:i]) for i in range(len(UNITS) + 1)]
-    spans = [slice(low, high) for low, high in zip(edges, edges[1:])]
+    spans = [slice(unit * at, unit * (at + size)) for at, size in zip(PLACES, UNITS)]
     states, rows, joined, fars, blocks, spots = [], [], [], [], [], []
     arrived, last = (), len(spans) - 1
     picked = [
@@ -174,7 +174,7 @@
         outgoing = after(outgoing, fars[: max(0, number - 2)])
         arrived = lax.all_to_all(outgoing, "vocab", split_axis=0, concat_axis=0, tiled=True)
         ready = after(arrived, rows)
-        grad, *pieces = combine(here, target, head_grad, ready, span.start, TILE * unit)
+        grad, *pieces = combine(here, target, head_grad, ready, span.start)
         if number == last:
             pieces = after(pieces, fars[: number - 1])
         for flip, piece in enumerate(pieces, 1):
@@ -209,7 +209,8 @@
         ]
         blocks += [both, swap_z(both, two)]
     table = place(table, here, blocks, tuple(spots), share, shape)
-    return tuple(jnp.concatenate(parts, axis=1) for parts in zip(*states)) + (table,)
+    in_place = [states[number] for number in sorted(range(len(PLACES)), key=PLACES.__getitem__)]
+    return tuple(jnp.concatenate(parts, axis=1) for parts in zip(*in_place)) + (table,)
 
 
 def solution(mesh):

time: 199 us -> 197 us (0.990)
  Pallas kernels: 18.7 us -> 14.7 us
    pallas_call x4, Pallas kernels: 14.7 us -> 10.7 us  [combine(): pl.pallas_call(combine_body, grid=(2,), out_shape=[jax.ShapeDtypeStruct((...]
    all_to_all x4, waiting for transfers between devices: 27.2 us -> 30.1 us  [local(): lax.all_to_all(outgoing, 'vocab', split_axis=0, concat_axis=0, tiled=True)]
  transfers between devices with their start and end apart: 26 -> 26, of which waited for: 17 -> 17; matrix products, arithmetic and copies ran while one was open for 15% -> 15% of each run, Pallas kernels for 9% -> 7%
where the time goes in v10:
time: 197 us; the launch traced here: 196 us
  waiting for transfers between devices  89.2 us (45%)
  starting transfers between devices  52.8 us (27%)
  other arithmetic  17.2 us (9%)
  matrix products  16.8 us (9%)
  Pallas kernels  14.7 us (7%)
  local copies, waits for them, and re-layouts  3.83 us (2%)
    ppermute x22, waiting for transfers between devices, swap_z(): return lax.ppermute(block, 'dp', [(i, i ^ flip) for i in range(GROUPS)])  59.1 us
    all_to_all x4, waiting for transfers between devices, local(): lax.all_to_all(outgoing, 'vocab', split_axis=0, concat_axis=0, tiled=True)  30.1 us
    ppermute x22, starting transfers between devices, swap_z(): return lax.ppermute(block, 'dp', [(i, i ^ flip) for i in range(GROUPS)])  27.9 us
    all_to_all x4, starting transfers between devices, local(): lax.all_to_all(outgoing, 'vocab', split_axis=0, concat_axis=0, tiled=True)  24.9 us
    dot_general x4, matrix products, local(): jnp.dot(dispatch, input_grad[:, span], preferred_element_type=jnp.float32)  16.4 us
    pallas_call x4, Pallas kernels, combine(): pl.pallas_call(combine_body, grid=(2,), out_shape=[jax.ShapeDtypeStruct((...  10.7 us
    convert_element_type x4, other arithmetic, local(): block = states[-1][0].astype(jnp.bfloat16)  9.98 us
    pallas_call x2, Pallas kernels, place(): pl.pallas_call(functools.partial(place_body, len(before), spots, share),...  3.97 us
  transfers between devices with their start and end apart: 26, of which 17 were waited for; matrix products, arithmetic and copies ran while one was open for 15% of the time, Pallas kernels for 7%

profile of v10, /device:TPU:0, one launch (start us, length us, event | category | flops | bytes accessed | tf_op | source)
XLA Modules:
  0.0 195.7 jit_solution(13634388358593959055)
XLA Ops:
  0.6 0.7 constant_dynamic-slice_fusion
  1.3 0.2 fusion.7
  1.5 3.8 %fusion.3 = bf16[1024,1024]{1,0:T(8,128)(2,1)} fusion(bf16[512,4608]{1,0:T(8,128)(2,1)} %param.7, s32[512]{0:T(512)S(1)} %convert_add_fusion.4), kind=kOutput, calls=%fused_computation.8 | convolution fusion | flops 1075314688 | bytes 3147776 | tf_op jit(solution)/shard_map/dot_general | solution.py:167
  5.4 7.5 %all-to-all-start = ((bf16[32,32,1024]{2,1,0:T(8,128)(2,1)}), bf16[32,32,1024]{2,1,0:T(8,128)(2,1)S(1)}, u32[]{:S(2)}, u32[]{:S(2)}) async-start(bf16[32,32,1024]{2,1,0:T(8,128)(2,1)} %bitcast.15), calls=%async_computation | async-start | bytes 4194304 | tf_op jit(solution)/shard_map/all_to_all | solution.py:175
  13.6 0.6 select_reduce_fusion
  14.3 3.8 %fusion.4 = bf16[1024,1024]{1,0:T(8,128)(2,1)} fusion(bf16[512,4608]{1,0:T(8,128)(2,1)} %param.7, s32[512]{0:T(512)S(1)} %convert_add_fusion.4), kind=kOutput, calls=%fused_computation.9 | convolution fusion | flops 1075314688 | bytes 3147776 | tf_op jit(solution)/shard_map/dot_general | solution.py:167
  18.1 4.4 %convolution_convert_fusion = bf16[1024,1280]{1,0:T(8,128)(2,1)} fusion(bf16[512,4608]{1,0:T(8,128)(2,1)} %param.7, s32[512]{0:T(512)S(1)} %convert_add_fusion.4), kind=kOutput, calls=%fused_computation | convolution fusion | flops 1344012288 | bytes 3934208 | tf_op jit(solution)/shard_map/dot_general | solution.py:167
  22.5 4.4 %convolution_convert_fusion.1 = bf16[1024,1280]{1,0:T(8,128)(2,1)} fusion(bf16[512,4608]{1,0:T(8,128)(2,1)} %param.7, s32[512]{0:T(512)S(1)} %convert_add_fusion.4), kind=kOutput, calls=%fused_computation.1 | convolution fusion | flops 1344012288 | bytes 3934208 | tf_op jit(solution)/shard_map/dot_general | solution.py:167
  26.9 15.0 %all-to-all-done = bf16[32,32,1024]{2,1,0:T(8,128)(2,1)S(1)} async-done(((bf16[32,32,1024]{2,1,0:T(8,128)(2,1)}), bf16[32,32,1024]{2,1,0:T(8,128)(2,1)S(1)}, u32[]{:S(2)}, u32[]{:S(2)}) %all-to-all-start) | async-done | bytes 2097184 | tf_op jit(solution)/shard_map/all_to_all | solution.py:175
  41.8 1.4 copy-done.1
  43.2 5.1 %all-to-all-start.1 = ((bf16[32,32,1280]{2,1,0:T(8,128)(2,1)}), bf16[32,32,1280]{2,1,0:T(8,128)(2,1)}, u32[]{:S(2)}, u32[]{:S(2)}) async-start(bf16[32,32,1280]{2,1,0:T(8,128)(2,1)} %bitcast.13), calls=%async_computation.1 | async-start | bytes 5242880 | tf_op jit(solution)/shard_map/all_to_all | solution.py:175
  48.3 1.6 copy-done.2
  49.9 1.6 shard_map.102
  51.5 4.1 %collective-permute-start.2 = (bf16[96,1024]{1,0:T(8,128)(2,1)S(1)}, bf16[96,1024]{1,0:T(8,128)(2,1)S(1)}, u32[]{:S(2)}, u32[]{:S(2)}) collective-permute-start(bf16[96,1024]{1,0:T(8,128)(2,1)S(1)} %get-tuple-element.40), channel_id=1, source_target_pairs={{0,96},{32,64},{64,32},{96,0},{1,97},{33,65},{65,33},{97,1},{2,98}... | collective-permute-start | bytes 589832 | tf_op jit(solution)/shard_map/ppermute | solution.py:31
  55.6 0.9 collective-permute-start
  56.6 8.4 %collective-permute-done.2 = bf16[96,1024]{1,0:T(8,128)(2,1)S(1)} collective-permute-done((bf16[96,1024]{1,0:T(8,128)(2,1)S(1)}, bf16[96,1024]{1,0:T(8,128)(2,1)S(1)}, u32[]{:S(2)}, u32[]{:S(2)}) %collective-permute-start.2) | collective-permute-done | bytes 196640 | tf_op jit(solution)/shard_map/ppermute | solution.py:31
  65.0 0.7 collective-permute-done
  65.7 2.5 %fusion.25 = (bf16[96,1024]{1,0:T(8,128)(2,1)S(1)}, f32[96,1024]{1,0:T(8,128)}, f32[96,1024]{1,0:T(8,128)}, f32[96,1024]{1,0:T(8,128)}) fusion(f32[96,4608]{1,0:T(8,128)} %param.11, bf16[96,1024]{1,0:T(8,128)(2,1)S(1)} %collective-permute-done.2, bf16[96,1024]{1,0:T(8,128)(2,1)S(1)} %collective-permute-done.1, f32[96,1024]{1,0:T(8,128)S(1)} %get-tuple-element.37, ...), kind=kLoop, calls=%fused_computation.60 | loop fusion | flops 2162688 | bytes 3538944 | tf_op jit(solution)/shard_map/convert_element_type | solution.py:183
  68.3 2.9 %collective-permute-start.6 = (bf16[96,1024]{1,0:T(8,128)(2,1)S(1)}, bf16[96,1024]{1,0:T(8,128)(2,1)S(1)}, u32[]{:S(2)}, u32[]{:S(2)}) collective-permute-start(bf16[96,1024]{1,0:T(8,128)(2,1)S(1)} %get-tuple-element.80), channel_id=1, source_target_pairs={{0,96},{32,64},{64,32},{96,0},{1,97},{33,65},{65,33},{97,1},{2,98}... | collective-permute-start | bytes 589832 | tf_op jit(solution)/shard_map/ppermute | solution.py:31
  71.1 4.5 %collective-permute-done.6 = bf16[96,1024]{1,0:T(8,128)(2,1)S(1)} collective-permute-done((bf16[96,1024]{1,0:T(8,128)(2,1)S(1)}, bf16[96,1024]{1,0:T(8,128)(2,1)S(1)}, u32[]{:S(2)}, u32[]{:S(2)}) %collective-permute-start.6) | collective-permute-done | bytes 196640 | tf_op jit(solution)/shard_map/ppermute | solution.py:31
  75.6 0.8 pad_maximum_fusion.5.refs_0_
  76.4 6.5 %all-to-all-done.1 = bf16[32,32,1280]{2,1,0:T(8,128)(2,1)} async-done(((bf16[32,32,1280]{2,1,0:T(8,128)(2,1)}), bf16[32,32,1280]{2,1,0:T(8,128)(2,1)}, u32[]{:S(2)}, u32[]{:S(2)}) %all-to-all-start.1) | async-done | bytes 2621472 | tf_op jit(solution)/shard_map/all_to_all | solution.py:175
  82.9 4.8 %all-to-all-start.2 = ((bf16[32,32,1280]{2,1,0:T(8,128)(2,1)}), bf16[32,32,1280]{2,1,0:T(8,128)(2,1)}, u32[]{:S(2)}, u32[]{:S(2)}) async-start(bf16[32,32,1280]{2,1,0:T(8,128)(2,1)} %bitcast.12), calls=%async_computation.2 | async-start | bytes 5242880 | tf_op jit(solution)/shard_map/all_to_all | solution.py:175
  87.7 3.2 %shard_map.103 = (f32[96,1280]{1,0:T(8,128)S(1)}, bf16[96,1280]{1,0:T(8,128)(2,1)S(1)}, bf16[96,1280]{1,0:T(8,128)(2,1)S(1)}, bf16[96,1280]{1,0:T(8,128)(2,1)S(1)}) custom-call(s32[1]{0:T(128)} %bitcast.here_ref, s32[1,1024]{1,0:T(1,128)S(1)} %sub.19.target_ref, bf16[1,384,4608]{2,1,0:T(8,128)(2,1)S(1)} %copy-done, bf16[1024,1280]{1,0:T(8,128)(2,1)} %bitcast.5.part_ref), custom_call_target="tpu_custom_call" | custom-call | flops 1006632960 | bytes 5079040 | tf_op jit(solution)/shard_map/pallas_call | solution.py:68
  91.0 4.3 %collective-permute-start.5 = (bf16[96,1280]{1,0:T(8,128)(2,1)S(1)}, bf16[96,1280]{1,0:T(8,128)(2,1)S(1)}, u32[]{:S(2)}, u32[]{:S(2)}) collective-permute-start(bf16[96,1280]{1,0:T(8,128)(2,1)S(1)} %get-tuple-element.45), channel_id=1, source_target_pairs={{0,96},{32,64},{64,32},{96,0},{1,97},{33,65},{65,33},{97,1},{2,98}... | collective-permute-start | bytes 737288 | tf_op jit(solution)/shard_map/ppermute | solution.py:31
  95.3 0.9 collective-permute-start.3
  96.2 10.5 %collective-permute-done.5 = bf16[96,1280]{1,0:T(8,128)(2,1)S(1)} collective-permute-done((bf16[96,1280]{1,0:T(8,128)(2,1)S(1)}, bf16[96,1280]{1,0:T(8,128)(2,1)S(1)}, u32[]{:S(2)}, u32[]{:S(2)}) %collective-permute-start.5) | collective-permute-done | bytes 245792 | tf_op jit(solution)/shard_map/ppermute | solution.py:31
  106.8 0.7 collective-permute-done.3
  107.5 2.8 %fusion.23 = (bf16[96,1280]{1,0:T(8,128)(2,1)S(1)}, f32[96,1280]{1,0:T(8,128)}, f32[96,1280]{1,0:T(8,128)}, f32[96,1280]{1,0:T(8,128)}) fusion(f32[96,4608]{1,0:T(8,128)} %param.11, bf16[96,1280]{1,0:T(8,128)(2,1)S(1)} %collective-permute-done.5, bf16[96,1280]{1,0:T(8,128)(2,1)S(1)} %collective-permute-done.4, f32[96,1280]{1,0:T(8,128)S(1)} %get-tuple-element.42, ...), kind=kLoop, calls=%fused_computation.59 | loop fusion | flops 2703360 | bytes 4423680 | tf_op jit(solution)/shard_map/convert_element_type | solution.py:183
  110.2 2.9 %collective-permute-start.10 = (bf16[96,1280]{1,0:T(8,128)(2,1)S(1)}, bf16[96,1280]{1,0:T(8,128)(2,1)S(1)}, u32[]{:S(2)}, u32[]{:S(2)}) collective-permute-start(bf16[96,1280]{1,0:T(8,128)(2,1)S(1)} %get-tuple-element.76), channel_id=1, source_target_pairs={{0,96},{32,64},{64,32},{96,0},{1,97},{33,65},{65,33},{97,1},{2,98}... | collective-permute-start | bytes 737288 | tf_op jit(solution)/shard_map/ppermute | solution.py:31
  113.1 5.6 %collective-permute-done.10 = bf16[96,1280]{1,0:T(8,128)(2,1)S(1)} collective-permute-done((bf16[96,1280]{1,0:T(8,128)(2,1)S(1)}, bf16[96,1280]{1,0:T(8,128)(2,1)S(1)}, u32[]{:S(2)}, u32[]{:S(2)}) %collective-permute-start.10) | collective-permute-done | bytes 245792 | tf_op jit(solution)/shard_map/ppermute | solution.py:31
  118.7 0.8 pad_maximum_fusion.3.refs_2_
  119.5 2.8 %all-to-all-done.2 = bf16[32,32,1280]{2,1,0:T(8,128)(2,1)} async-done(((bf16[32,32,1280]{2,1,0:T(8,128)(2,1)}), bf16[32,32,1280]{2,1,0:T(8,128)(2,1)}, u32[]{:S(2)}, u32[]{:S(2)}) %all-to-all-start.2) | async-done | bytes 2621472 | tf_op jit(solution)/shard_map/all_to_all | solution.py:175
  122.3 1.0 collective-permute-done.11.refs_1_
  123.3 7.5 %all-to-all-start.3 = ((bf16[32,32,1024]{2,1,0:T(8,128)(2,1)}), bf16[32,32,1024]{2,1,0:T(8,128)(2,1)}, u32[]{:S(2)}, u32[]{:S(2)}) async-start(bf16[32,32,1024]{2,1,0:T(8,128)(2,1)} %bitcast.14), calls=%async_computation.3 | async-start | bytes 4194304 | tf_op jit(solution)/shard_map/all_to_all | solution.py:175
  130.8 3.3 %shard_map.104 = (f32[96,1280]{1,0:T(8,128)S(1)}, bf16[96,1280]{1,0:T(8,128)(2,1)S(1)}, bf16[96,1280]{1,0:T(8,128)(2,1)S(1)}, bf16[96,1280]{1,0:T(8,128)(2,1)S(1)}) custom-call(s32[1]{0:T(128)} %bitcast.here_ref, s32[1,1024]{1,0:T(1,128)S(1)} %sub.19.target_ref, bf16[1,384,4608]{2,1,0:T(8,128)(2,1)S(1)} %copy-done, bf16[1024,1280]{1,0:T(8,128)(2,1)} %bitcast.7.part_ref), custom_call_target="tpu_custom_call" | custom-call | flops 1006632960 | bytes 5079040 | tf_op jit(solution)/shard_map/pallas_call | solution.py:68
  134.1 0.7 collective-permute-start.9
  134.8 1.7 collective-permute-start.8
  136.5 1.7 collective-permute-start.7
  138.2 0.3 collective-permute-start.12
  138.5 10.2 %collective-permute-done.9 = bf16[96,1280]{1,0:T(8,128)(2,1)S(1)} collective-permute-done((bf16[96,1280]{1,0:T(8,128)(2,1)S(1)}, bf16[96,1280]{1,0:T(8,128)(2,1)S(1)}, u32[]{:S(2)}, u32[]{:S(2)}) %collective-permute-start.9) | collective-permute-done | bytes 245792 | tf_op jit(solution)/shard_map/ppermute | solution.py:31
  148.7 1.6 collective-permute-done.7
  150.3 2.9 %fusion.21 = (bf16[96,1280]{1,0:T(8,128)(2,1)}, f32[96,1280]{1,0:T(8,128)}, f32[96,1280]{1,0:T(8,128)}, f32[96,1280]{1,0:T(8,128)}) fusion(f32[96,4608]{1,0:T(8,128)} %param.11, bf16[96,1280]{1,0:T(8,128)(2,1)S(1)} %collective-permute-done.9, bf16[96,1280]{1,0:T(8,128)(2,1)S(1)} %collective-permute-done.8, f32[96,1280]{1,0:T(8,128)S(1)} %get-tuple-element.48, ...), kind=kLoop, calls=%fused_computation.58 | loop fusion | flops 2703360 | bytes 4423680 | tf_op jit(solution)/shard_map/convert_element_type | solution.py:183
  153.2 0.7 collective-permute-start.16
  153.8 5.9 %all-to-all-done.3 = bf16[32,32,1024]{2,1,0:T(8,128)(2,1)} async-done(((bf16[32,32,1024]{2,1,0:T(8,128)(2,1)}), bf16[32,32,1024]{2,1,0:T(8,128)(2,1)}, u32[]{:S(2)}, u32[]{:S(2)}) %all-to-all-start.3) | async-done | bytes 2097184 | tf_op jit(solution)/shard_map/all_to_all | solution.py:175
  159.7 2.6 %shard_map.105 = (f32[96,1024]{1,0:T(8,128)S(1)}, bf16[96,1024]{1,0:T(8,128)(2,1)S(1)}, bf16[96,1024]{1,0:T(8,128)(2,1)S(1)}, bf16[96,1024]{1,0:T(8,128)(2,1)S(1)}) custom-call(s32[1]{0:T(128)} %bitcast.here_ref, s32[1,1024]{1,0:T(1,128)S(1)} %sub.19.target_ref, bf16[1,384,4608]{2,1,0:T(8,128)(2,1)S(1)} %copy-done, bf16[1024,1024]{1,0:T(8,128)(2,1)} %bitcast.9.part_ref), custom_call_target="tpu_custom_call" | custom-call | flops 805306368 | bytes 4063232 | tf_op jit(solution)/shard_map/pallas_call | solution.py:68
  162.4 0.7 collective-permute-start.15
  163.1 1.7 collective-permute-start.14
  164.8 1.7 collective-permute-start.13
  166.5 1.1 pad_maximum_fusion.4.refs_4_
  167.6 0.4 collective-permute-start.17
  168.0 6.3 %collective-permute-done.15 = bf16[96,1024]{1,0:T(8,128)(2,1)S(1)} collective-permute-done((bf16[96,1024]{1,0:T(8,128)(2,1)S(1)}, bf16[96,1024]{1,0:T(8,128)(2,1)S(1)}, u32[]{:S(2)}, u32[]{:S(2)}) %collective-permute-start.15) | collective-permute-done | bytes 196640 | tf_op jit(solution)/shard_map/ppermute | solution.py:31
  174.3 2.2 %collective-permute-done.13 = bf16[96,1024]{1,0:T(8,128)(2,1)S(1)} collective-permute-done((bf16[96,1024]{1,0:T(8,128)(2,1)S(1)}, bf16[96,1024]{1,0:T(8,128)(2,1)S(1)}, u32[]{:S(2)}, u32[]{:S(2)}) %collective-permute-start.13) | collective-permute-done | bytes 196640 | tf_op jit(solution)/shard_map/ppermute | solution.py:31
  176.6 1.8 fusion.19
  178.4 0.4 collective-permute-start.18
  178.8 0.9 collective-permute-start.20
  179.7 2.1 %pad_maximum_fusion = (f32[96,4608]{1,0:T(8,128)}, f32[96,4608]{1,0:T(8,128)}) fusion(f32[96,1024]{1,0:T(8,128)S(1)} %get-tuple-element.69, f32[96,1024]{1,0:T(8,128)S(1)} %copy-done.10, f32[96,1280]{1,0:T(8,128)S(1)} %copy-done.7, f32[96,1280]{1,0:T(8,128)S(1)} %copy-done.5, f32[96,1024]{1,0:T(8,128)S(1)} %get-tuple-element.70, ...), kind=kLoop, calls=%fused_computation.10 | loop fusion | flops 2654208 | bytes 7077888 | tf_op jit(solution)/shard_map/concatenate | solution.py:213
  181.8 5.7 %collective-permute-done.18 = bf16[96,512]{1,0:T(8,128)(2,1)S(1)} collective-permute-done((bf16[96,512]{1,0:T(8,128)(2,1)S(1)}, bf16[96,512]{1,0:T(8,128)(2,1)S(1)}, u32[]{:S(2)}, u32[]{:S(2)}) %collective-permute-start.18) | collective-permute-done | bytes 98336 | tf_op jit(solution)/shard_map/ppermute | solution.py:31
  187.6 0.8 collective-permute-start.19
  188.4 0.3 collective-permute-start.21
  188.6 1.3 pad_maximum_fusion.2
  190.0 3.0 %shard_map.106.refs_0_ = bf16[384,4608]{1,0:T(8,128)(2,1)} custom-call(s32[1]{0:T(128)} %bitcast.here_ref, bf16[192,1024]{1,0:T(8,128)(2,1)} %pad_maximum_fusion.5.refs_0_, bf16[192,1024]{1,0:T(8,128)(2,1)} %collective-permute-done.11.refs_1_, bf16[192,1280]{1,0:T(8,128)(2,1)} %pad_maximum_fusion.3.refs_2_, ...), custom_call_target="tpu_custom_call" | custom-call | bytes 5505024 | tf_op jit(solution)/shard_map/pallas_call | solution.py:107
  193.0 1.5 collective-permute-done.19.refs_2_
  194.6 0.9 shard_map.107
  (49 shorter events, 0.8 us)
Async XLA Ops:
  5.4 7.5 %copy-start.13 = (s32[16384,1]{0,1:T(1,128)S(1)}, s32[16384,1]{0,1:T(1,128)}, u32[]{:S(2)}) copy-start(s32[16384,1]{0,1:T(1,128)} %param.9) | copy-start | bytes 196612
  5.4 7.8 %copy-start.12 = (s32[16384,1]{0,1:T(1,128)S(1)}, s32[16384,1]{0,1:T(1,128)}, u32[]{:S(2)}) copy-start(s32[16384,1]{0,1:T(1,128)} %param.8) | copy-start | bytes 196612
  5.4 36.5 %all-to-all-start = ((bf16[32,32,1024]{2,1,0:T(8,128)(2,1)}), bf16[32,32,1024]{2,1,0:T(8,128)(2,1)S(1)}, u32[]{:S(2)}, u32[]{:S(2)}) async-start(bf16[32,32,1024]{2,1,0:T(8,128)(2,1)} %bitcast.15), calls=%async_computation | async-start | bytes 4194304 | tf_op jit(solution)/shard_map/all_to_all | solution.py:175
  41.8 1.4 copy-start.1
  43.2 5.1 %copy-start = (bf16[1,384,4608]{2,1,0:T(8,128)(2,1)S(1)}, bf16[1,384,4608]{2,1,0:T(8,128)(2,1)}, u32[]{:S(2)}) copy-start(bf16[1,384,4608]{2,1,0:T(8,128)(2,1)} %head_ref.7) | copy-start | bytes 10616836
  43.2 39.7 %all-to-all-start.1 = ((bf16[32,32,1280]{2,1,0:T(8,128)(2,1)}), bf16[32,32,1280]{2,1,0:T(8,128)(2,1)}, u32[]{:S(2)}, u32[]{:S(2)}) async-start(bf16[32,32,1280]{2,1,0:T(8,128)(2,1)} %bitcast.13), calls=%async_computation.1 | async-start | bytes 5242880 | tf_op jit(solution)/shard_map/all_to_all | solution.py:175
  48.3 1.6 copy-start.2
  51.5 13.5 %collective-permute-start.2 = (bf16[96,1024]{1,0:T(8,128)(2,1)S(1)}, bf16[96,1024]{1,0:T(8,128)(2,1)S(1)}, u32[]{:S(2)}, u32[]{:S(2)}) collective-permute-start(bf16[96,1024]{1,0:T(8,128)(2,1)S(1)} %get-tuple-element.40), channel_id=1, source_target_pairs={{0,96},{32,64},{64,32},{96,0},{1,97},{33,65},{65,33},{97,1},{2,98}... | collective-permute-start | bytes 589832 | tf_op jit(solution)/shard_map/ppermute | solution.py:31
  55.6 9.4 %collective-permute-start.1 = (bf16[96,1024]{1,0:T(8,128)(2,1)S(1)}, bf16[96,1024]{1,0:T(8,128)(2,1)S(1)}, u32[]{:S(2)}, u32[]{:S(2)}) collective-permute-start(bf16[96,1024]{1,0:T(8,128)(2,1)S(1)} %get-tuple-element.39), channel_id=1, source_target_pairs={{0,64},{32,96},{64,0},{96,32},{1,65},{33,97},{65,1},{97,33},{2,66}... | collective-permute-start | bytes 589832 | tf_op jit(solution)/shard_map/ppermute | solution.py:31
  55.6 10.1 %collective-permute-start = (bf16[96,1024]{1,0:T(8,128)(2,1)S(1)}, bf16[96,1024]{1,0:T(8,128)(2,1)S(1)}, u32[]{:S(2)}, u32[]{:S(2)}) collective-permute-start(bf16[96,1024]{1,0:T(8,128)(2,1)S(1)} %get-tuple-element.38), channel_id=1, source_target_pairs={{0,32},{32,0},{64,96},{96,64},{1,33},{33,1},{65,97},{97,65},{2,34}... | collective-permute-start | bytes 589832 | tf_op jit(solution)/shard_map/ppermute | solution.py:31
  68.3 7.4 %collective-permute-start.6 = (bf16[96,1024]{1,0:T(8,128)(2,1)S(1)}, bf16[96,1024]{1,0:T(8,128)(2,1)S(1)}, u32[]{:S(2)}, u32[]{:S(2)}) collective-permute-start(bf16[96,1024]{1,0:T(8,128)(2,1)S(1)} %get-tuple-element.80), channel_id=1, source_target_pairs={{0,96},{32,64},{64,32},{96,0},{1,97},{33,65},{65,33},{97,1},{2,98}... | collective-permute-start | bytes 589832 | tf_op jit(solution)/shard_map/ppermute | solution.py:31
  82.9 39.4 %all-to-all-start.2 = ((bf16[32,32,1280]{2,1,0:T(8,128)(2,1)}), bf16[32,32,1280]{2,1,0:T(8,128)(2,1)}, u32[]{:S(2)}, u32[]{:S(2)}) async-start(bf16[32,32,1280]{2,1,0:T(8,128)(2,1)} %bitcast.12), calls=%async_computation.2 | async-start | bytes 5242880 | tf_op jit(solution)/shard_map/all_to_all | solution.py:175
  91.0 15.8 %collective-permute-start.5 = (bf16[96,1280]{1,0:T(8,128)(2,1)S(1)}, bf16[96,1280]{1,0:T(8,128)(2,1)S(1)}, u32[]{:S(2)}, u32[]{:S(2)}) collective-permute-start(bf16[96,1280]{1,0:T(8,128)(2,1)S(1)} %get-tuple-element.45), channel_id=1, source_target_pairs={{0,96},{32,64},{64,32},{96,0},{1,97},{33,65},{65,33},{97,1},{2,98}... | collective-permute-start | bytes 737288 | tf_op jit(solution)/shard_map/ppermute | solution.py:31
  95.3 11.5 %collective-permute-start.4 = (bf16[96,1280]{1,0:T(8,128)(2,1)S(1)}, bf16[96,1280]{1,0:T(8,128)(2,1)S(1)}, u32[]{:S(2)}, u32[]{:S(2)}) collective-permute-start(bf16[96,1280]{1,0:T(8,128)(2,1)S(1)} %get-tuple-element.44), channel_id=1, source_target_pairs={{0,64},{32,96},{64,0},{96,32},{1,65},{33,97},{65,1},{97,33},{2,66}... | collective-permute-start | bytes 737288 | tf_op jit(solution)/shard_map/ppermute | solution.py:31
  95.3 12.2 %collective-permute-start.3 = (bf16[96,1280]{1,0:T(8,128)(2,1)S(1)}, bf16[96,1280]{1,0:T(8,128)(2,1)S(1)}, u32[]{:S(2)}, u32[]{:S(2)}) collective-permute-start(bf16[96,1280]{1,0:T(8,128)(2,1)S(1)} %get-tuple-element.43), channel_id=1, source_target_pairs={{0,32},{32,0},{64,96},{96,64},{1,33},{33,1},{65,97},{97,65},{2,34}... | collective-permute-start | bytes 737288 | tf_op jit(solution)/shard_map/ppermute | solution.py:31
  110.2 8.4 %collective-permute-start.10 = (bf16[96,1280]{1,0:T(8,128)(2,1)S(1)}, bf16[96,1280]{1,0:T(8,128)(2,1)S(1)}, u32[]{:S(2)}, u32[]{:S(2)}) collective-permute-start(bf16[96,1280]{1,0:T(8,128)(2,1)S(1)} %get-tuple-element.76), channel_id=1, source_target_pairs={{0,96},{32,64},{64,32},{96,0},{1,97},{33,65},{65,33},{97,1},{2,98}... | collective-permute-start | bytes 737288 | tf_op jit(solution)/shard_map/ppermute | solution.py:31
  113.1 10.2 %collective-permute-start.11 = (bf16[192,1024]{1,0:T(8,128)(2,1)}, bf16[192,1024]{1,0:T(8,128)(2,1)}, u32[]{:S(2)}, u32[]{:S(2)}) collective-permute-start(bf16[192,1024]{1,0:T(8,128)(2,1)} %pad_maximum_fusion.5.refs_0_), channel_id=1, source_target_pairs={{0,32},{32,0},{64,96},{96,64},{1,33},{33,1},{65,97},{97,65},{2,34}... | collective-permute-start | bytes 1179656 | tf_op jit(solution)/shard_map/ppermute | solution.py:31
  123.3 36.4 %all-to-all-start.3 = ((bf16[32,32,1024]{2,1,0:T(8,128)(2,1)}), bf16[32,32,1024]{2,1,0:T(8,128)(2,1)}, u32[]{:S(2)}, u32[]{:S(2)}) async-start(bf16[32,32,1024]{2,1,0:T(8,128)(2,1)} %bitcast.14), calls=%async_computation.3 | async-start | bytes 4194304 | tf_op jit(solution)/shard_map/all_to_all | solution.py:175
  134.1 14.6 %collective-permute-start.9 = (bf16[96,1280]{1,0:T(8,128)(2,1)S(1)}, bf16[96,1280]{1,0:T(8,128)(2,1)S(1)}, u32[]{:S(2)}, u32[]{:S(2)}) collective-permute-start(bf16[96,1280]{1,0:T(8,128)(2,1)S(1)} %get-tuple-element.51), channel_id=1, source_target_pairs={{0,96},{32,64},{64,32},{96,0},{1,97},{33,65},{65,33},{97,1},{2,98}... | collective-permute-start | bytes 737288 | tf_op jit(solution)/shard_map/ppermute | solution.py:31
  134.8 13.9 %collective-permute-start.8 = (bf16[96,1280]{1,0:T(8,128)(2,1)S(1)}, bf16[96,1280]{1,0:T(8,128)(2,1)S(1)}, u32[]{:S(2)}, u32[]{:S(2)}) collective-permute-start(bf16[96,1280]{1,0:T(8,128)(2,1)S(1)} %get-tuple-element.50), channel_id=1, source_target_pairs={{0,64},{32,96},{64,0},{96,32},{1,65},{33,97},{65,1},{97,33},{2,66}... | collective-permute-start | bytes 737288 | tf_op jit(solution)/shard_map/ppermute | solution.py:31
  136.5 13.8 %collective-permute-start.7 = (bf16[96,1280]{1,0:T(8,128)(2,1)S(1)}, bf16[96,1280]{1,0:T(8,128)(2,1)S(1)}, u32[]{:S(2)}, u32[]{:S(2)}) collective-permute-start(bf16[96,1280]{1,0:T(8,128)(2,1)S(1)} %get-tuple-element.49), channel_id=1, source_target_pairs={{0,32},{32,0},{64,96},{96,64},{1,33},{33,1},{65,97},{97,65},{2,34}... | collective-permute-start | bytes 737288 | tf_op jit(solution)/shard_map/ppermute | solution.py:31
  138.2 24.1 %collective-permute-start.12 = (bf16[192,1280]{1,0:T(8,128)(2,1)}, bf16[192,1280]{1,0:T(8,128)(2,1)}, u32[]{:S(2)}, u32[]{:S(2)}) collective-permute-start(bf16[192,1280]{1,0:T(8,128)(2,1)} %pad_maximum_fusion.3.refs_2_), channel_id=1, source_target_pairs={{0,32},{32,0},{64,96},{96,64},{1,33},{33,1},{65,97},{97,65},{2,34}... | collective-permute-start | bytes 1474568 | tf_op jit(solution)/shard_map/ppermute | solution.py:31
  153.2 13.4 %collective-permute-start.16 = (bf16[96,1280]{1,0:T(8,128)(2,1)}, bf16[96,1280]{1,0:T(8,128)(2,1)}, u32[]{:S(2)}, u32[]{:S(2)}) collective-permute-start(bf16[96,1280]{1,0:T(8,128)(2,1)} %get-tuple-element.72), channel_id=1, source_target_pairs={{0,96},{32,64},{64,32},{96,0},{1,97},{33,65},{65,33},{97,1},{2,98}... | collective-permute-start | bytes 737288 | tf_op jit(solution)/shard_map/ppermute | solution.py:31
  162.4 12.0 %collective-permute-start.15 = (bf16[96,1024]{1,0:T(8,128)(2,1)S(1)}, bf16[96,1024]{1,0:T(8,128)(2,1)S(1)}, u32[]{:S(2)}, u32[]{:S(2)}) collective-permute-start(bf16[96,1024]{1,0:T(8,128)(2,1)S(1)} %get-tuple-element.61), channel_id=1, source_target_pairs={{0,96},{32,64},{64,32},{96,0},{1,97},{33,65},{65,33},{97,1},{2,98}... | collective-permute-start | bytes 589832 | tf_op jit(solution)/shard_map/ppermute | solution.py:31
  163.1 11.2 %collective-permute-start.14 = (bf16[96,1024]{1,0:T(8,128)(2,1)S(1)}, bf16[96,1024]{1,0:T(8,128)(2,1)S(1)}, u32[]{:S(2)}, u32[]{:S(2)}) collective-permute-start(bf16[96,1024]{1,0:T(8,128)(2,1)S(1)} %get-tuple-element.60), channel_id=1, source_target_pairs={{0,64},{32,96},{64,0},{96,32},{1,65},{33,97},{65,1},{97,33},{2,66}... | collective-permute-start | bytes 589832 | tf_op jit(solution)/shard_map/ppermute | solution.py:31
  164.8 11.8 %collective-permute-start.13 = (bf16[96,1024]{1,0:T(8,128)(2,1)S(1)}, bf16[96,1024]{1,0:T(8,128)(2,1)S(1)}, u32[]{:S(2)}, u32[]{:S(2)}) collective-permute-start(bf16[96,1024]{1,0:T(8,128)(2,1)S(1)} %get-tuple-element.59), channel_id=1, source_target_pairs={{0,32},{32,0},{64,96},{96,64},{1,33},{33,1},{65,97},{97,65},{2,34}... | collective-permute-start | bytes 589832 | tf_op jit(solution)/shard_map/ppermute | solution.py:31
  167.6 22.3 %collective-permute-start.17 = (bf16[192,1280]{1,0:T(8,128)(2,1)S(1)}, bf16[192,1280]{1,0:T(8,128)(2,1)S(1)}, u32[]{:S(2)}, u32[]{:S(2)}) collective-permute-start(bf16[192,1280]{1,0:T(8,128)(2,1)S(1)} %pad_maximum_fusion.4.refs_4_), channel_id=1, source_target_pairs={{0,32},{32,0},{64,96},{96,64},{1,33},{33,1},{65,97},{97,65},{2,34}... | collective-permute-start | bytes 1474568 | tf_op jit(solution)/shard_map/ppermute | solution.py:31
  176.6 3.1 %copy-start.5 = (f32[96,1280]{1,0:T(8,128)S(1)}, f32[96,1280]{1,0:T(8,128)}, u32[]{:S(2)}) copy-start(f32[96,1280]{1,0:T(8,128)} %get-tuple-element.77) | copy-start | bytes 1474564
  176.6 3.1 %copy-start.6 = (f32[96,1280]{1,0:T(8,128)S(1)}, f32[96,1280]{1,0:T(8,128)}, u32[]{:S(2)}) copy-start(f32[96,1280]{1,0:T(8,128)} %get-tuple-element.78) | copy-start | bytes 1474564
  176.6 3.1 %copy-start.7 = (f32[96,1280]{1,0:T(8,128)S(1)}, f32[96,1280]{1,0:T(8,128)}, u32[]{:S(2)}) copy-start(f32[96,1280]{1,0:T(8,128)} %get-tuple-element.73) | copy-start | bytes 1474564
  176.6 3.1 %copy-start.8 = (f32[96,1280]{1,0:T(8,128)S(1)}, f32[96,1280]{1,0:T(8,128)}, u32[]{:S(2)}) copy-start(f32[96,1280]{1,0:T(8,128)} %get-tuple-element.74) | copy-start | bytes 1474564
  176.6 3.1 %copy-start.10 = (f32[96,1024]{1,0:T(8,128)S(1)}, f32[96,1024]{1,0:T(8,128)}, u32[]{:S(2)}) copy-start(f32[96,1024]{1,0:T(8,128)} %get-tuple-element.81) | copy-start | bytes 1179652
  176.6 3.1 %copy-start.11 = (f32[96,1024]{1,0:T(8,128)S(1)}, f32[96,1024]{1,0:T(8,128)}, u32[]{:S(2)}) copy-start(f32[96,1024]{1,0:T(8,128)} %get-tuple-element.82) | copy-start | bytes 1179652
  178.4 9.2 %collective-permute-start.18 = (bf16[96,512]{1,0:T(8,128)(2,1)S(1)}, bf16[96,512]{1,0:T(8,128)(2,1)S(1)}, u32[]{:S(2)}, u32[]{:S(2)}) collective-permute-start(bf16[96,512]{1,0:T(8,128)(2,1)S(1)} %get-tuple-element.85), channel_id=1, source_target_pairs={{0,32},{32,0},{64,96},{96,64},{1,33},{33,1},{65,97},{97,65},{2,34}... | collective-permute-start | bytes 294920 | tf_op jit(solution)/shard_map/ppermute | solution.py:31
  178.8 9.6 %collective-permute-start.20 = (bf16[96,512]{1,0:T(8,128)(2,1)S(1)}, bf16[96,512]{1,0:T(8,128)(2,1)S(1)}, u32[]{:S(2)}, u32[]{:S(2)}) collective-permute-start(bf16[96,512]{1,0:T(8,128)(2,1)S(1)} %get-tuple-element.84), channel_id=1, source_target_pairs={{0,96},{32,64},{64,32},{96,0},{1,97},{33,65},{65,33},{97,1},{2,98}... | collective-permute-start | bytes 294920 | tf_op jit(solution)/shard_map/ppermute | solution.py:31
  179.7 8.9 %copy-start.3 = (f32[96,1280]{1,0:T(8,128)S(1)}, f32[96,1280]{1,0:T(8,128)}, u32[]{:S(2)}) copy-start(f32[96,1280]{1,0:T(8,128)} %get-tuple-element.79) | copy-start | bytes 1474564
  179.7 8.9 %copy-start.4 = (f32[96,1280]{1,0:T(8,128)S(1)}, f32[96,1280]{1,0:T(8,128)}, u32[]{:S(2)}) copy-start(f32[96,1280]{1,0:T(8,128)} %get-tuple-element.75) | copy-start | bytes 1474564
  179.7 8.9 %copy-start.9 = (f32[96,1024]{1,0:T(8,128)S(1)}, f32[96,1024]{1,0:T(8,128)}, u32[]{:S(2)}) copy-start(f32[96,1024]{1,0:T(8,128)} %get-tuple-element.83) | copy-start | bytes 1179652
  187.6 7.0 %collective-permute-start.19 = (bf16[192,512]{1,0:T(8,128)(2,1)S(1)}, bf16[192,512]{1,0:T(8,128)(2,1)S(1)}, u32[]{:S(2)}, u32[]{:S(2)}) collective-permute-start(bf16[192,512]{1,0:T(8,128)(2,1)S(1)} %pad_maximum_fusion.6.refs_1_), channel_id=1, source_target_pairs={{0,96},{32,64},{64,32},{96,0},{1,97},{33,65},{65,33},{97,1},{2,98}... | collective-permute-start | bytes 589832 | tf_op jit(solution)/shard_map/ppermute | solution.py:31
  188.4 6.2 %collective-permute-start.21 = (bf16[192,512]{1,0:T(8,128)(2,1)S(1)}, bf16[192,512]{1,0:T(8,128)(2,1)S(1)}, u32[]{:S(2)}, u32[]{:S(2)}) collective-permute-start(bf16[192,512]{1,0:T(8,128)(2,1)S(1)} %pad_maximum_fusion.7.refs_3_), channel_id=1, source_target_pairs={{0,32},{32,0},{64,96},{96,64},{1,33},{33,1},{65,97},{97,65},{2,34}... | collective-permute-start | bytes 589832 | tf_op jit(solution)/shard_map/ppermute | solution.py:31

commit v11 on v10

--- a/solution.py
+++ b/solution.py
@@ -183,16 +183,20 @@
         block = states[-1][0].astype(jnp.bfloat16)
         rows.append(block)
         if number < last:
-            both = jnp.concatenate([block, swap_z(block, 3)], axis=0)
-            joined.append(both)
-            spots += [
-                (len(blocks), 0, 0, span.start),
-                (len(blocks), share, 3, span.start),
-                (len(blocks) + 1, 0, 1, span.start),
-                (len(blocks) + 1, share, 2, span.start),
-            ]
-            fars.append(swap_z(both, 1))
-            blocks += [both, fars[-1]]
+            cuts = [(0, (3, 1))] if number < last - 1 else [(0, (1, 3)), (block.shape[1] // 2, (3, 1))]
+            size = block.shape[1] // len(cuts)
+            for start, (one, two) in cuts:
+                part = block[:, start : start + size]
+                both = jnp.concatenate([part, swap_z(part, one)], axis=0)
+                joined.append(both)
+                fars.append(swap_z(both, two))
+                spots += [
+                    (len(blocks), 0, 0, span.start + start),
+                    (len(blocks), share, one, span.start + start),
+                    (len(blocks) + 1, 0, two, span.start + start),
+                    (len(blocks) + 1, share, one ^ two, span.start + start),
+                ]
+                blocks += [both, fars[-1]]
     shape = (slab_rows, width)
     blocks = after(blocks, rows)
     table = place(None, here, blocks, tuple(spots), share, shape)

time: 197 us -> 193 us (0.980)
  waiting for transfers between devices: 89.2 us -> 81 us
  starting transfers between devices: 52.8 us -> 55.7 us
    ppermute x22 -> x24, waiting for transfers between devices: 59.1 us -> 52 us  [swap_z(): return lax.ppermute(block, 'dp', [(i, i ^ flip) for i in range(GROUPS)])]
    concatenate x2 -> x6, other arithmetic: 0.03 us -> 3.62 us  [local(): both = jnp.concatenate([part, swap_z(part, one)], axis=0)]
    ppermute x22 -> x24, starting transfers between devices: 27.9 us -> 30.8 us  [swap_z(): return lax.ppermute(block, 'dp', [(i, i ^ flip) for i in range(GROUPS)])]
    concatenate x3 -> x0, other arithmetic: 2.72 us -> none  [local(): both = jnp.concatenate([block, swap_z(block, 3)], axis=0)]
  transfers between devices with their start and end apart: 26 -> 28, of which waited for: 17 -> 17; matrix products, arithmetic and copies ran while one was open for 15% -> 16% of each run, Pallas kernels for 7% -> 7%
where the time goes in v11:
time: 193 us; the launch traced here: 192 us
  waiting for transfers between devices  81 us (42%)
  starting transfers between devices  55.7 us (29%)
  other arithmetic  18 us (9%)
  matrix products  16.8 us (9%)
  Pallas kernels  14.8 us (8%)
  local copies, waits for them, and re-layouts  4.56 us (2%)
    ppermute x24, waiting for transfers between devices, swap_z(): return lax.ppermute(block, 'dp', [(i, i ^ flip) for i in range(GROUPS)])  52 us
    ppermute x24, starting transfers between devices, swap_z(): return lax.ppermute(block, 'dp', [(i, i ^ flip) for i in range(GROUPS)])  30.8 us
    all_to_all x4, waiting for transfers between devices, local(): lax.all_to_all(outgoing, 'vocab', split_axis=0, concat_axis=0, tiled=True)  29 us
    all_to_all x4, starting transfers between devices, local(): lax.all_to_all(outgoing, 'vocab', split_axis=0, concat_axis=0, tiled=True)  24.9 us
    dot_general x4, matrix products, local(): jnp.dot(dispatch, input_grad[:, span], preferred_element_type=jnp.float32)  16.4 us
    pallas_call x4, Pallas kernels, combine(): pl.pallas_call(combine_body, grid=(2,), out_shape=[jax.ShapeDtypeStruct((...  10.7 us
    convert_element_type x4, other arithmetic, local(): block = states[-1][0].astype(jnp.bfloat16)  9.91 us
    pallas_call x2, Pallas kernels, place(): pl.pallas_call(functools.partial(place_body, len(before), spots, share),...  4.01 us
  transfers between devices with their start and end apart: 28, of which 17 were waited for; matrix products, arithmetic and copies ran while one was open for 16% of the time, Pallas kernels for 7%

profile of v11, /device:TPU:0, one launch (start us, length us, event | category | flops | bytes accessed | tf_op | source)
XLA Modules:
  0.0 191.9 jit_solution(11804832523481814564)
XLA Ops:
  0.6 0.7 constant_dynamic-slice_fusion
  1.5 3.8 %fusion.3 = bf16[1024,1024]{1,0:T(8,128)(2,1)} fusion(bf16[512,4608]{1,0:T(8,128)(2,1)} %param.7, s32[512]{0:T(512)S(1)} %convert_add_fusion.4), kind=kOutput, calls=%fused_computation.8 | convolution fusion | flops 1075314688 | bytes 3147776 | tf_op jit(solution)/shard_map/dot_general | solution.py:167
  5.4 7.5 %all-to-all-start = ((bf16[32,32,1024]{2,1,0:T(8,128)(2,1)}), bf16[32,32,1024]{2,1,0:T(8,128)(2,1)S(1)}, u32[]{:S(2)}, u32[]{:S(2)}) async-start(bf16[32,32,1024]{2,1,0:T(8,128)(2,1)} %bitcast.15), calls=%async_computation | async-start | bytes 4194304 | tf_op jit(solution)/shard_map/all_to_all | solution.py:175
  13.6 0.6 select_reduce_fusion
  14.3 3.8 %fusion.4 = bf16[1024,1024]{1,0:T(8,128)(2,1)} fusion(bf16[512,4608]{1,0:T(8,128)(2,1)} %param.7, s32[512]{0:T(512)S(1)} %convert_add_fusion.4), kind=kOutput, calls=%fused_computation.9 | convolution fusion | flops 1075314688 | bytes 3147776 | tf_op jit(solution)/shard_map/dot_general | solution.py:167
  18.1 4.4 %convolution_convert_fusion = bf16[1024,1280]{1,0:T(8,128)(2,1)} fusion(bf16[512,4608]{1,0:T(8,128)(2,1)} %param.7, s32[512]{0:T(512)S(1)} %convert_add_fusion.4), kind=kOutput, calls=%fused_computation | convolution fusion | flops 1344012288 | bytes 3934208 | tf_op jit(solution)/shard_map/dot_general | solution.py:167
  22.5 4.4 %convolution_convert_fusion.1 = bf16[1024,1280]{1,0:T(8,128)(2,1)} fusion(bf16[512,4608]{1,0:T(8,128)(2,1)} %param.7, s32[512]{0:T(512)S(1)} %convert_add_fusion.4), kind=kOutput, calls=%fused_computation.1 | convolution fusion | flops 1344012288 | bytes 3934208 | tf_op jit(solution)/shard_map/dot_general | solution.py:167
  26.9 15.0 %all-to-all-done = bf16[32,32,1024]{2,1,0:T(8,128)(2,1)S(1)} async-done(((bf16[32,32,1024]{2,1,0:T(8,128)(2,1)}), bf16[32,32,1024]{2,1,0:T(8,128)(2,1)S(1)}, u32[]{:S(2)}, u32[]{:S(2)}) %all-to-all-start) | async-done | bytes 2097184 | tf_op jit(solution)/shard_map/all_to_all | solution.py:175
  41.9 1.4 copy-done.1
  43.2 5.1 %all-to-all-start.1 = ((bf16[32,32,1280]{2,1,0:T(8,128)(2,1)}), bf16[32,32,1280]{2,1,0:T(8,128)(2,1)}, u32[]{:S(2)}, u32[]{:S(2)}) async-start(bf16[32,32,1280]{2,1,0:T(8,128)(2,1)} %bitcast.13), calls=%async_computation.1 | async-start | bytes 5242880 | tf_op jit(solution)/shard_map/all_to_all | solution.py:175
  48.3 1.6 copy-done.2
  49.9 1.6 shard_map.102
  51.5 4.1 %collective-permute-start.2 = (bf16[96,1024]{1,0:T(8,128)(2,1)S(1)}, bf16[96,1024]{1,0:T(8,128)(2,1)S(1)}, u32[]{:S(2)}, u32[]{:S(2)}) collective-permute-start(bf16[96,1024]{1,0:T(8,128)(2,1)S(1)} %get-tuple-element.42), channel_id=1, source_target_pairs={{0,96},{32,64},{64,32},{96,0},{1,97},{33,65},{65,33},{97,1},{2,98}... | collective-permute-start | bytes 589832 | tf_op jit(solution)/shard_map/ppermute | solution.py:31
  55.7 0.9 collective-permute-start
  56.6 8.4 %collective-permute-done.2 = bf16[96,1024]{1,0:T(8,128)(2,1)S(1)} collective-permute-done((bf16[96,1024]{1,0:T(8,128)(2,1)S(1)}, bf16[96,1024]{1,0:T(8,128)(2,1)S(1)}, u32[]{:S(2)}, u32[]{:S(2)}) %collective-permute-start.2) | collective-permute-done | bytes 196640 | tf_op jit(solution)/shard_map/ppermute | solution.py:31
  65.0 0.7 collective-permute-done
  65.7 2.6 %fusion.25 = (bf16[96,1024]{1,0:T(8,128)(2,1)S(1)}, f32[96,1024]{1,0:T(8,128)}, f32[96,1024]{1,0:T(8,128)}, f32[96,1024]{1,0:T(8,128)}) fusion(f32[96,4608]{1,0:T(8,128)} %param.11, bf16[96,1024]{1,0:T(8,128)(2,1)S(1)} %collective-permute-done.2, bf16[96,1024]{1,0:T(8,128)(2,1)S(1)} %collective-permute-done.1, f32[96,1024]{1,0:T(8,128)S(1)} %get-tuple-element.39, ...), kind=kLoop, calls=%fused_computation.61 | loop fusion | flops 2162688 | bytes 3538944 | tf_op jit(solution)/shard_map/convert_element_type | solution.py:183
  68.3 2.9 %collective-permute-start.6 = (bf16[96,1024]{1,0:T(8,128)(2,1)S(1)}, bf16[96,1024]{1,0:T(8,128)(2,1)S(1)}, u32[]{:S(2)}, u32[]{:S(2)}) collective-permute-start(bf16[96,1024]{1,0:T(8,128)(2,1)S(1)} %get-tuple-element.84), channel_id=1, source_target_pairs={{0,96},{32,64},{64,32},{96,0},{1,97},{33,65},{65,33},{97,1},{2,98}... | collective-permute-start | bytes 589832 | tf_op jit(solution)/shard_map/ppermute | solution.py:31
  71.2 4.5 %collective-permute-done.6 = bf16[96,1024]{1,0:T(8,128)(2,1)S(1)} collective-permute-done((bf16[96,1024]{1,0:T(8,128)(2,1)S(1)}, bf16[96,1024]{1,0:T(8,128)(2,1)S(1)}, u32[]{:S(2)}, u32[]{:S(2)}) %collective-permute-start.6) | collective-permute-done | bytes 196640 | tf_op jit(solution)/shard_map/ppermute | solution.py:31
  75.7 0.8 pad_maximum_fusion.4.refs_0_
  76.5 6.5 %all-to-all-done.1 = bf16[32,32,1280]{2,1,0:T(8,128)(2,1)} async-done(((bf16[32,32,1280]{2,1,0:T(8,128)(2,1)}), bf16[32,32,1280]{2,1,0:T(8,128)(2,1)}, u32[]{:S(2)}, u32[]{:S(2)}) %all-to-all-start.1) | async-done | bytes 2621472 | tf_op jit(solution)/shard_map/all_to_all | solution.py:175
  82.9 4.8 %all-to-all-start.2 = ((bf16[32,32,1280]{2,1,0:T(8,128)(2,1)}), bf16[32,32,1280]{2,1,0:T(8,128)(2,1)}, u32[]{:S(2)}, u32[]{:S(2)}) async-start(bf16[32,32,1280]{2,1,0:T(8,128)(2,1)} %bitcast.12), calls=%async_computation.2 | async-start | bytes 5242880 | tf_op jit(solution)/shard_map/all_to_all | solution.py:175
  87.7 3.2 %shard_map.103 = (f32[96,1280]{1,0:T(8,128)S(1)}, bf16[96,1280]{1,0:T(8,128)(2,1)S(1)}, bf16[96,1280]{1,0:T(8,128)(2,1)S(1)}, bf16[96,1280]{1,0:T(8,128)(2,1)S(1)}) custom-call(s32[1]{0:T(128)} %bitcast.here_ref, s32[1,1024]{1,0:T(1,128)S(1)} %sub.19.target_ref, bf16[1,384,4608]{2,1,0:T(8,128)(2,1)S(1)} %copy-done, bf16[1024,1280]{1,0:T(8,128)(2,1)} %bitcast.5.part_ref), custom_call_target="tpu_custom_call" | custom-call | flops 1006632960 | bytes 5079040 | tf_op jit(solution)/shard_map/pallas_call | solution.py:68
  91.0 4.3 %collective-permute-start.5 = (bf16[96,1280]{1,0:T(8,128)(2,1)S(1)}, bf16[96,1280]{1,0:T(8,128)(2,1)S(1)}, u32[]{:S(2)}, u32[]{:S(2)}) collective-permute-start(bf16[96,1280]{1,0:T(8,128)(2,1)S(1)} %get-tuple-element.47), channel_id=1, source_target_pairs={{0,96},{32,64},{64,32},{96,0},{1,97},{33,65},{65,33},{97,1},{2,98}... | collective-permute-start | bytes 737288 | tf_op jit(solution)/shard_map/ppermute | solution.py:31
  95.3 0.9 collective-permute-start.3
  96.3 10.5 %collective-permute-done.5 = bf16[96,1280]{1,0:T(8,128)(2,1)S(1)} collective-permute-done((bf16[96,1280]{1,0:T(8,128)(2,1)S(1)}, bf16[96,1280]{1,0:T(8,128)(2,1)S(1)}, u32[]{:S(2)}, u32[]{:S(2)}) %collective-permute-start.5) | collective-permute-done | bytes 245792 | tf_op jit(solution)/shard_map/ppermute | solution.py:31
  106.8 0.7 collective-permute-done.3
  107.5 2.8 %fusion.23 = (bf16[96,1280]{1,0:T(8,128)(2,1)S(1)}, f32[96,1280]{1,0:T(8,128)}, f32[96,1280]{1,0:T(8,128)}, f32[96,1280]{1,0:T(8,128)}) fusion(f32[96,4608]{1,0:T(8,128)} %param.11, bf16[96,1280]{1,0:T(8,128)(2,1)S(1)} %collective-permute-done.5, bf16[96,1280]{1,0:T(8,128)(2,1)S(1)} %collective-permute-done.4, f32[96,1280]{1,0:T(8,128)S(1)} %get-tuple-element.44, ...), kind=kLoop, calls=%fused_computation.60 | loop fusion | flops 2703360 | bytes 4423680 | tf_op jit(solution)/shard_map/convert_element_type | solution.py:183
  110.3 2.9 %collective-permute-start.10 = (bf16[96,1280]{1,0:T(8,128)(2,1)S(1)}, bf16[96,1280]{1,0:T(8,128)(2,1)S(1)}, u32[]{:S(2)}, u32[]{:S(2)}) collective-permute-start(bf16[96,1280]{1,0:T(8,128)(2,1)S(1)} %get-tuple-element.80), channel_id=1, source_target_pairs={{0,96},{32,64},{64,32},{96,0},{1,97},{33,65},{65,33},{97,1},{2,98}... | collective-permute-start | bytes 737288 | tf_op jit(solution)/shard_map/ppermute | solution.py:31
  113.1 5.6 %collective-permute-done.10 = bf16[96,1280]{1,0:T(8,128)(2,1)S(1)} collective-permute-done((bf16[96,1280]{1,0:T(8,128)(2,1)S(1)}, bf16[96,1280]{1,0:T(8,128)(2,1)S(1)}, u32[]{:S(2)}, u32[]{:S(2)}) %collective-permute-start.10) | collective-permute-done | bytes 245792 | tf_op jit(solution)/shard_map/ppermute | solution.py:31
  118.7 0.9 pad_maximum_fusion.3.refs_2_
  119.6 2.8 %all-to-all-done.2 = bf16[32,32,1280]{2,1,0:T(8,128)(2,1)} async-done(((bf16[32,32,1280]{2,1,0:T(8,128)(2,1)}), bf16[32,32,1280]{2,1,0:T(8,128)(2,1)}, u32[]{:S(2)}, u32[]{:S(2)}) %all-to-all-start.2) | async-done | bytes 2621472 | tf_op jit(solution)/shard_map/all_to_all | solution.py:175
  122.4 1.0 collective-permute-done.11.refs_1_
  123.3 7.5 %all-to-all-start.3 = ((bf16[32,32,1024]{2,1,0:T(8,128)(2,1)}), bf16[32,32,1024]{2,1,0:T(8,128)(2,1)}, u32[]{:S(2)}, u32[]{:S(2)}) async-start(bf16[32,32,1024]{2,1,0:T(8,128)(2,1)} %bitcast.14), calls=%async_computation.3 | async-start | bytes 4194304 | tf_op jit(solution)/shard_map/all_to_all | solution.py:175
  130.8 3.3 %shard_map.104 = (f32[96,1280]{1,0:T(8,128)S(1)}, bf16[96,1280]{1,0:T(8,128)(2,1)S(1)}, bf16[96,1280]{1,0:T(8,128)(2,1)S(1)}, bf16[96,1280]{1,0:T(8,128)(2,1)S(1)}) custom-call(s32[1]{0:T(128)} %bitcast.here_ref, s32[1,1024]{1,0:T(1,128)S(1)} %sub.19.target_ref, bf16[1,384,4608]{2,1,0:T(8,128)(2,1)S(1)} %copy-done, bf16[1024,1280]{1,0:T(8,128)(2,1)} %bitcast.7.part_ref), custom_call_target="tpu_custom_call" | custom-call | flops 1006632960 | bytes 5079040 | tf_op jit(solution)/shard_map/pallas_call | solution.py:68
  134.1 0.7 collective-permute-start.9
  134.8 1.7 collective-permute-start.8
  136.5 1.7 collective-permute-start.7
  138.6 10.2 %collective-permute-done.9 = bf16[96,1280]{1,0:T(8,128)(2,1)S(1)} collective-permute-done((bf16[96,1280]{1,0:T(8,128)(2,1)S(1)}, bf16[96,1280]{1,0:T(8,128)(2,1)S(1)}, u32[]{:S(2)}, u32[]{:S(2)}) %collective-permute-start.9) | collective-permute-done | bytes 245792 | tf_op jit(solution)/shard_map/ppermute | solution.py:31
  148.7 1.6 collective-permute-done.7
  150.3 2.8 %fusion.21 = (bf16[96,1280]{1,0:T(8,128)(2,1)S(1)}, f32[96,1280]{1,0:T(8,128)}, f32[96,1280]{1,0:T(8,128)}, f32[96,1280]{1,0:T(8,128)}) fusion(f32[96,4608]{1,0:T(8,128)} %param.11, bf16[96,1280]{1,0:T(8,128)(2,1)S(1)} %collective-permute-done.9, bf16[96,1280]{1,0:T(8,128)(2,1)S(1)} %collective-permute-done.8, f32[96,1280]{1,0:T(8,128)S(1)} %get-tuple-element.50, ...), kind=kLoop, calls=%fused_computation.59 | loop fusion | flops 2703360 | bytes 4423680 | tf_op jit(solution)/shard_map/convert_element_type | solution.py:183
  153.1 0.7 fusion.27
  154.1 0.9 collective-permute-start.18
  155.0 4.7 %all-to-all-done.3 = bf16[32,32,1024]{2,1,0:T(8,128)(2,1)} async-done(((bf16[32,32,1024]{2,1,0:T(8,128)(2,1)}), bf16[32,32,1024]{2,1,0:T(8,128)(2,1)}, u32[]{:S(2)}, u32[]{:S(2)}) %all-to-all-start.3) | async-done | bytes 2097184 | tf_op jit(solution)/shard_map/all_to_all | solution.py:175
  159.7 2.6 %shard_map.105 = (f32[96,1024]{1,0:T(8,128)S(1)}, bf16[96,1024]{1,0:T(8,128)(2,1)S(1)}, bf16[96,1024]{1,0:T(8,128)(2,1)S(1)}, bf16[96,1024]{1,0:T(8,128)(2,1)S(1)}) custom-call(s32[1]{0:T(128)} %bitcast.here_ref, s32[1,1024]{1,0:T(1,128)S(1)} %sub.19.target_ref, bf16[1,384,4608]{2,1,0:T(8,128)(2,1)S(1)} %copy-done, bf16[1024,1024]{1,0:T(8,128)(2,1)} %bitcast.9.part_ref), custom_call_target="tpu_custom_call" | custom-call | flops 805306368 | bytes 4063232 | tf_op jit(solution)/shard_map/pallas_call | solution.py:68
  162.4 0.7 collective-permute-start.15
  163.1 1.7 collective-permute-start.14
  164.8 1.7 collective-permute-start.13
  166.6 1.0 pad_maximum_fusion.5.refs_4_
  167.6 0.7 collective-permute-start.17
  168.3 1.0 pad_maximum_fusion.6.refs_6_
  169.4 5.8 %collective-permute-done.15 = bf16[96,1024]{1,0:T(8,128)(2,1)S(1)} collective-permute-done((bf16[96,1024]{1,0:T(8,128)(2,1)S(1)}, bf16[96,1024]{1,0:T(8,128)(2,1)S(1)}, u32[]{:S(2)}, u32[]{:S(2)}) %collective-permute-start.15) | collective-permute-done | bytes 196640 | tf_op jit(solution)/shard_map/ppermute | solution.py:31
  175.2 1.4 collective-permute-done.13
  176.6 1.8 fusion.19
  178.4 0.4 collective-permute-start.20
  178.8 0.9 collective-permute-start.22
  179.7 2.1 %pad_maximum_fusion = (f32[96,4608]{1,0:T(8,128)}, f32[96,4608]{1,0:T(8,128)}) fusion(f32[96,1024]{1,0:T(8,128)S(1)} %get-tuple-element.73, f32[96,1024]{1,0:T(8,128)S(1)} %copy-done.10, f32[96,1280]{1,0:T(8,128)S(1)} %copy-done.7, f32[96,1280]{1,0:T(8,128)S(1)} %copy-done.5, f32[96,1024]{1,0:T(8,128)S(1)} %get-tuple-element.74, ...), kind=kLoop, calls=%fused_computation.10 | loop fusion | flops 2654208 | bytes 7077888 | tf_op jit(solution)/shard_map/concatenate | solution.py:217
  181.9 1.3 collective-permute-done.20
  183.2 1.2 collective-permute-start.21
  184.3 0.3 collective-permute-done.22
  184.7 1.7 collective-permute-start.23
  186.3 1.3 pad_maximum_fusion.2
  187.7 3.1 %shard_map.106.refs_0_ = bf16[384,4608]{1,0:T(8,128)(2,1)} custom-call(s32[1]{0:T(128)} %bitcast.here_ref, bf16[192,1024]{1,0:T(8,128)(2,1)} %pad_maximum_fusion.4.refs_0_, bf16[192,1024]{1,0:T(8,128)(2,1)} %collective-permute-done.11.refs_1_, bf16[192,1280]{1,0:T(8,128)(2,1)} %pad_maximum_fusion.3.refs_2_, ...), custom_call_target="tpu_custom_call" | custom-call | bytes 5505024 | tf_op jit(solution)/shard_map/pallas_call | solution.py:107
  190.8 0.9 shard_map.107
  (55 shorter events, 1.7 us)
Async XLA Ops:
  5.4 7.5 %copy-start.13 = (s32[16384,1]{0,1:T(1,128)S(1)}, s32[16384,1]{0,1:T(1,128)}, u32[]{:S(2)}) copy-start(s32[16384,1]{0,1:T(1,128)} %param.9) | copy-start | bytes 196612
  5.4 7.8 %copy-start.12 = (s32[16384,1]{0,1:T(1,128)S(1)}, s32[16384,1]{0,1:T(1,128)}, u32[]{:S(2)}) copy-start(s32[16384,1]{0,1:T(1,128)} %param.8) | copy-start | bytes 196612
  5.4 36.5 %all-to-all-start = ((bf16[32,32,1024]{2,1,0:T(8,128)(2,1)}), bf16[32,32,1024]{2,1,0:T(8,128)(2,1)S(1)}, u32[]{:S(2)}, u32[]{:S(2)}) async-start(bf16[32,32,1024]{2,1,0:T(8,128)(2,1)} %bitcast.15), calls=%async_computation | async-start | bytes 4194304 | tf_op jit(solution)/shard_map/all_to_all | solution.py:175
  41.9 1.4 copy-start.1
  43.2 5.1 %copy-start = (bf16[1,384,4608]{2,1,0:T(8,128)(2,1)S(1)}, bf16[1,384,4608]{2,1,0:T(8,128)(2,1)}, u32[]{:S(2)}) copy-start(bf16[1,384,4608]{2,1,0:T(8,128)(2,1)} %head_ref.7) | copy-start | bytes 10616836
  43.2 39.7 %all-to-all-start.1 = ((bf16[32,32,1280]{2,1,0:T(8,128)(2,1)}), bf16[32,32,1280]{2,1,0:T(8,128)(2,1)}, u32[]{:S(2)}, u32[]{:S(2)}) async-start(bf16[32,32,1280]{2,1,0:T(8,128)(2,1)} %bitcast.13), calls=%async_computation.1 | async-start | bytes 5242880 | tf_op jit(solution)/shard_map/all_to_all | solution.py:175
  48.3 1.6 copy-start.2
  51.5 13.5 %collective-permute-start.2 = (bf16[96,1024]{1,0:T(8,128)(2,1)S(1)}, bf16[96,1024]{1,0:T(8,128)(2,1)S(1)}, u32[]{:S(2)}, u32[]{:S(2)}) collective-permute-start(bf16[96,1024]{1,0:T(8,128)(2,1)S(1)} %get-tuple-element.42), channel_id=1, source_target_pairs={{0,96},{32,64},{64,32},{96,0},{1,97},{33,65},{65,33},{97,1},{2,98}... | collective-permute-start | bytes 589832 | tf_op jit(solution)/shard_map/ppermute | solution.py:31
  55.7 9.4 %collective-permute-start.1 = (bf16[96,1024]{1,0:T(8,128)(2,1)S(1)}, bf16[96,1024]{1,0:T(8,128)(2,1)S(1)}, u32[]{:S(2)}, u32[]{:S(2)}) collective-permute-start(bf16[96,1024]{1,0:T(8,128)(2,1)S(1)} %get-tuple-element.41), channel_id=1, source_target_pairs={{0,64},{32,96},{64,0},{96,32},{1,65},{33,97},{65,1},{97,33},{2,66}... | collective-permute-start | bytes 589832 | tf_op jit(solution)/shard_map/ppermute | solution.py:31
  55.7 10.1 %collective-permute-start = (bf16[96,1024]{1,0:T(8,128)(2,1)S(1)}, bf16[96,1024]{1,0:T(8,128)(2,1)S(1)}, u32[]{:S(2)}, u32[]{:S(2)}) collective-permute-start(bf16[96,1024]{1,0:T(8,128)(2,1)S(1)} %get-tuple-element.40), channel_id=1, source_target_pairs={{0,32},{32,0},{64,96},{96,64},{1,33},{33,1},{65,97},{97,65},{2,34}... | collective-permute-start | bytes 589832 | tf_op jit(solution)/shard_map/ppermute | solution.py:31
  68.3 7.4 %collective-permute-start.6 = (bf16[96,1024]{1,0:T(8,128)(2,1)S(1)}, bf16[96,1024]{1,0:T(8,128)(2,1)S(1)}, u32[]{:S(2)}, u32[]{:S(2)}) collective-permute-start(bf16[96,1024]{1,0:T(8,128)(2,1)S(1)} %get-tuple-element.84), channel_id=1, source_target_pairs={{0,96},{32,64},{64,32},{96,0},{1,97},{33,65},{65,33},{97,1},{2,98}... | collective-permute-start | bytes 589832 | tf_op jit(solution)/shard_map/ppermute | solution.py:31
  82.9 39.4 %all-to-all-start.2 = ((bf16[32,32,1280]{2,1,0:T(8,128)(2,1)}), bf16[32,32,1280]{2,1,0:T(8,128)(2,1)}, u32[]{:S(2)}, u32[]{:S(2)}) async-start(bf16[32,32,1280]{2,1,0:T(8,128)(2,1)} %bitcast.12), calls=%async_computation.2 | async-start | bytes 5242880 | tf_op jit(solution)/shard_map/all_to_all | solution.py:175
  91.0 15.8 %collective-permute-start.5 = (bf16[96,1280]{1,0:T(8,128)(2,1)S(1)}, bf16[96,1280]{1,0:T(8,128)(2,1)S(1)}, u32[]{:S(2)}, u32[]{:S(2)}) collective-permute-start(bf16[96,1280]{1,0:T(8,128)(2,1)S(1)} %get-tuple-element.47), channel_id=1, source_target_pairs={{0,96},{32,64},{64,32},{96,0},{1,97},{33,65},{65,33},{97,1},{2,98}... | collective-permute-start | bytes 737288 | tf_op jit(solution)/shard_map/ppermute | solution.py:31
  95.3 11.5 %collective-permute-start.4 = (bf16[96,1280]{1,0:T(8,128)(2,1)S(1)}, bf16[96,1280]{1,0:T(8,128)(2,1)S(1)}, u32[]{:S(2)}, u32[]{:S(2)}) collective-permute-start(bf16[96,1280]{1,0:T(8,128)(2,1)S(1)} %get-tuple-element.46), channel_id=1, source_target_pairs={{0,64},{32,96},{64,0},{96,32},{1,65},{33,97},{65,1},{97,33},{2,66}... | collective-permute-start | bytes 737288 | tf_op jit(solution)/shard_map/ppermute | solution.py:31
  95.3 12.2 %collective-permute-start.3 = (bf16[96,1280]{1,0:T(8,128)(2,1)S(1)}, bf16[96,1280]{1,0:T(8,128)(2,1)S(1)}, u32[]{:S(2)}, u32[]{:S(2)}) collective-permute-start(bf16[96,1280]{1,0:T(8,128)(2,1)S(1)} %get-tuple-element.45), channel_id=1, source_target_pairs={{0,32},{32,0},{64,96},{96,64},{1,33},{33,1},{65,97},{97,65},{2,34}... | collective-permute-start | bytes 737288 | tf_op jit(solution)/shard_map/ppermute | solution.py:31
  110.3 8.4 %collective-permute-start.10 = (bf16[96,1280]{1,0:T(8,128)(2,1)S(1)}, bf16[96,1280]{1,0:T(8,128)(2,1)S(1)}, u32[]{:S(2)}, u32[]{:S(2)}) collective-permute-start(bf16[96,1280]{1,0:T(8,128)(2,1)S(1)} %get-tuple-element.80), channel_id=1, source_target_pairs={{0,96},{32,64},{64,32},{96,0},{1,97},{33,65},{65,33},{97,1},{2,98}... | collective-permute-start | bytes 737288 | tf_op jit(solution)/shard_map/ppermute | solution.py:31
  113.1 10.2 %collective-permute-start.11 = (bf16[192,1024]{1,0:T(8,128)(2,1)}, bf16[192,1024]{1,0:T(8,128)(2,1)}, u32[]{:S(2)}, u32[]{:S(2)}) collective-permute-start(bf16[192,1024]{1,0:T(8,128)(2,1)} %pad_maximum_fusion.4.refs_0_), channel_id=1, source_target_pairs={{0,32},{32,0},{64,96},{96,64},{1,33},{33,1},{65,97},{97,65},{2,34}... | collective-permute-start | bytes 1179656 | tf_op jit(solution)/shard_map/ppermute | solution.py:31
  123.3 36.4 %all-to-all-start.3 = ((bf16[32,32,1024]{2,1,0:T(8,128)(2,1)}), bf16[32,32,1024]{2,1,0:T(8,128)(2,1)}, u32[]{:S(2)}, u32[]{:S(2)}) async-start(bf16[32,32,1024]{2,1,0:T(8,128)(2,1)} %bitcast.14), calls=%async_computation.3 | async-start | bytes 4194304 | tf_op jit(solution)/shard_map/all_to_all | solution.py:175
  134.1 14.6 %collective-permute-start.9 = (bf16[96,1280]{1,0:T(8,128)(2,1)S(1)}, bf16[96,1280]{1,0:T(8,128)(2,1)S(1)}, u32[]{:S(2)}, u32[]{:S(2)}) collective-permute-start(bf16[96,1280]{1,0:T(8,128)(2,1)S(1)} %get-tuple-element.53), channel_id=1, source_target_pairs={{0,96},{32,64},{64,32},{96,0},{1,97},{33,65},{65,33},{97,1},{2,98}... | collective-permute-start | bytes 737288 | tf_op jit(solution)/shard_map/ppermute | solution.py:31
  134.8 13.9 %collective-permute-start.8 = (bf16[96,1280]{1,0:T(8,128)(2,1)S(1)}, bf16[96,1280]{1,0:T(8,128)(2,1)S(1)}, u32[]{:S(2)}, u32[]{:S(2)}) collective-permute-start(bf16[96,1280]{1,0:T(8,128)(2,1)S(1)} %get-tuple-element.52), channel_id=1, source_target_pairs={{0,64},{32,96},{64,0},{96,32},{1,65},{33,97},{65,1},{97,33},{2,66}... | collective-permute-start | bytes 737288 | tf_op jit(solution)/shard_map/ppermute | solution.py:31
  136.5 13.8 %collective-permute-start.7 = (bf16[96,1280]{1,0:T(8,128)(2,1)S(1)}, bf16[96,1280]{1,0:T(8,128)(2,1)S(1)}, u32[]{:S(2)}, u32[]{:S(2)}) collective-permute-start(bf16[96,1280]{1,0:T(8,128)(2,1)S(1)} %get-tuple-element.51), channel_id=1, source_target_pairs={{0,32},{32,0},{64,96},{96,64},{1,33},{33,1},{65,97},{97,65},{2,34}... | collective-permute-start | bytes 737288 | tf_op jit(solution)/shard_map/ppermute | solution.py:31
  138.3 24.1 %collective-permute-start.12 = (bf16[192,1280]{1,0:T(8,128)(2,1)}, bf16[192,1280]{1,0:T(8,128)(2,1)}, u32[]{:S(2)}, u32[]{:S(2)}) collective-permute-start(bf16[192,1280]{1,0:T(8,128)(2,1)} %pad_maximum_fusion.3.refs_2_), channel_id=1, source_target_pairs={{0,32},{32,0},{64,96},{96,64},{1,33},{33,1},{65,97},{97,65},{2,34}... | collective-permute-start | bytes 1474568 | tf_op jit(solution)/shard_map/ppermute | solution.py:31
  153.8 12.7 %collective-permute-start.16 = (bf16[96,640]{1,0:T(8,128)(2,1)}, bf16[96,640]{1,0:T(8,128)(2,1)}, u32[]{:S(2)}, u32[]{:S(2)}) collective-permute-start(bf16[96,640]{1,0:T(8,128)(2,1)} %get-tuple-element.89), channel_id=1, source_target_pairs={{0,32},{32,0},{64,96},{96,64},{1,33},{33,1},{65,97},{97,65},{2,34}... | collective-permute-start | bytes 368648 | tf_op jit(solution)/shard_map/ppermute | solution.py:31
  154.1 14.2 %collective-permute-start.18 = (bf16[96,640]{1,0:T(8,128)(2,1)}, bf16[96,640]{1,0:T(8,128)(2,1)}, u32[]{:S(2)}, u32[]{:S(2)}) collective-permute-start(bf16[96,640]{1,0:T(8,128)(2,1)} %get-tuple-element.88), channel_id=1, source_target_pairs={{0,96},{32,64},{64,32},{96,0},{1,97},{33,65},{65,33},{97,1},{2,98}... | collective-permute-start | bytes 368648 | tf_op jit(solution)/shard_map/ppermute | solution.py:31
  162.4 12.8 %collective-permute-start.15 = (bf16[96,1024]{1,0:T(8,128)(2,1)S(1)}, bf16[96,1024]{1,0:T(8,128)(2,1)S(1)}, u32[]{:S(2)}, u32[]{:S(2)}) collective-permute-start(bf16[96,1024]{1,0:T(8,128)(2,1)S(1)} %get-tuple-element.63), channel_id=1, source_target_pairs={{0,96},{32,64},{64,32},{96,0},{1,97},{33,65},{65,33},{97,1},{2,98}... | collective-permute-start | bytes 589832 | tf_op jit(solution)/shard_map/ppermute | solution.py:31
  163.1 12.0 %collective-permute-start.14 = (bf16[96,1024]{1,0:T(8,128)(2,1)S(1)}, bf16[96,1024]{1,0:T(8,128)(2,1)S(1)}, u32[]{:S(2)}, u32[]{:S(2)}) collective-permute-start(bf16[96,1024]{1,0:T(8,128)(2,1)S(1)} %get-tuple-element.62), channel_id=1, source_target_pairs={{0,64},{32,96},{64,0},{96,32},{1,65},{33,97},{65,1},{97,33},{2,66}... | collective-permute-start | bytes 589832 | tf_op jit(solution)/shard_map/ppermute | solution.py:31
  164.8 11.8 %collective-permute-start.13 = (bf16[96,1024]{1,0:T(8,128)(2,1)S(1)}, bf16[96,1024]{1,0:T(8,128)(2,1)S(1)}, u32[]{:S(2)}, u32[]{:S(2)}) collective-permute-start(bf16[96,1024]{1,0:T(8,128)(2,1)S(1)} %get-tuple-element.61), channel_id=1, source_target_pairs={{0,32},{32,0},{64,96},{96,64},{1,33},{33,1},{65,97},{97,65},{2,34}... | collective-permute-start | bytes 589832 | tf_op jit(solution)/shard_map/ppermute | solution.py:31
  167.6 20.1 %collective-permute-start.17 = (bf16[192,640]{1,0:T(8,128)(2,1)S(1)}, bf16[192,640]{1,0:T(8,128)(2,1)S(1)}, u32[]{:S(2)}, u32[]{:S(2)}) collective-permute-start(bf16[192,640]{1,0:T(8,128)(2,1)S(1)} %pad_maximum_fusion.5.refs_4_), channel_id=1, source_target_pairs={{0,96},{32,64},{64,32},{96,0},{1,97},{33,65},{65,33},{97,1},{2,98}... | collective-permute-start | bytes 737288 | tf_op jit(solution)/shard_map/ppermute | solution.py:31
  169.3 18.4 %collective-permute-start.19 = (bf16[192,640]{1,0:T(8,128)(2,1)S(1)}, bf16[192,640]{1,0:T(8,128)(2,1)S(1)}, u32[]{:S(2)}, u32[]{:S(2)}) collective-permute-start(bf16[192,640]{1,0:T(8,128)(2,1)S(1)} %pad_maximum_fusion.6.refs_6_), channel_id=1, source_target_pairs={{0,32},{32,0},{64,96},{96,64},{1,33},{33,1},{65,97},{97,65},{2,34}... | collective-permute-start | bytes 737288 | tf_op jit(solution)/shard_map/ppermute | solution.py:31
  176.6 3.1 %copy-start.5 = (f32[96,1280]{1,0:T(8,128)S(1)}, f32[96,1280]{1,0:T(8,128)}, u32[]{:S(2)}) copy-start(f32[96,1280]{1,0:T(8,128)} %get-tuple-element.81) | copy-start | bytes 1474564
  176.6 3.1 %copy-start.6 = (f32[96,1280]{1,0:T(8,128)S(1)}, f32[96,1280]{1,0:T(8,128)}, u32[]{:S(2)}) copy-start(f32[96,1280]{1,0:T(8,128)} %get-tuple-element.82) | copy-start | bytes 1474564
  176.6 3.1 %copy-start.7 = (f32[96,1280]{1,0:T(8,128)S(1)}, f32[96,1280]{1,0:T(8,128)}, u32[]{:S(2)}) copy-start(f32[96,1280]{1,0:T(8,128)} %get-tuple-element.77) | copy-start | bytes 1474564
  176.6 3.1 %copy-start.8 = (f32[96,1280]{1,0:T(8,128)S(1)}, f32[96,1280]{1,0:T(8,128)}, u32[]{:S(2)}) copy-start(f32[96,1280]{1,0:T(8,128)} %get-tuple-element.78) | copy-start | bytes 1474564
  176.6 3.1 %copy-start.10 = (f32[96,1024]{1,0:T(8,128)S(1)}, f32[96,1024]{1,0:T(8,128)}, u32[]{:S(2)}) copy-start(f32[96,1024]{1,0:T(8,128)} %get-tuple-element.85) | copy-start | bytes 1179652
  176.6 3.1 %copy-start.11 = (f32[96,1024]{1,0:T(8,128)S(1)}, f32[96,1024]{1,0:T(8,128)}, u32[]{:S(2)}) copy-start(f32[96,1024]{1,0:T(8,128)} %get-tuple-element.86) | copy-start | bytes 1179652
  178.4 4.7 %collective-permute-start.20 = (bf16[96,512]{1,0:T(8,128)(2,1)S(1)}, bf16[96,512]{1,0:T(8,128)(2,1)S(1)}, u32[]{:S(2)}, u32[]{:S(2)}) collective-permute-start(bf16[96,512]{1,0:T(8,128)(2,1)S(1)} %get-tuple-element.91), channel_id=1, source_target_pairs={{0,32},{32,0},{64,96},{96,64},{1,33},{33,1},{65,97},{97,65},{2,34}... | collective-permute-start | bytes 294920 | tf_op jit(solution)/shard_map/ppermute | solution.py:31
  178.8 5.8 %collective-permute-start.22 = (bf16[96,512]{1,0:T(8,128)(2,1)S(1)}, bf16[96,512]{1,0:T(8,128)(2,1)S(1)}, u32[]{:S(2)}, u32[]{:S(2)}) collective-permute-start(bf16[96,512]{1,0:T(8,128)(2,1)S(1)} %get-tuple-element.90), channel_id=1, source_target_pairs={{0,96},{32,64},{64,32},{96,0},{1,97},{33,65},{65,33},{97,1},{2,98}... | collective-permute-start | bytes 294920 | tf_op jit(solution)/shard_map/ppermute | solution.py:31
  179.7 6.6 %copy-start.3 = (f32[96,1280]{1,0:T(8,128)S(1)}, f32[96,1280]{1,0:T(8,128)}, u32[]{:S(2)}) copy-start(f32[96,1280]{1,0:T(8,128)} %get-tuple-element.83) | copy-start | bytes 1474564
  179.7 6.6 %copy-start.4 = (f32[96,1280]{1,0:T(8,128)S(1)}, f32[96,1280]{1,0:T(8,128)}, u32[]{:S(2)}) copy-start(f32[96,1280]{1,0:T(8,128)} %get-tuple-element.79) | copy-start | bytes 1474564
  179.7 6.6 %copy-start.9 = (f32[96,1024]{1,0:T(8,128)S(1)}, f32[96,1024]{1,0:T(8,128)}, u32[]{:S(2)}) copy-start(f32[96,1024]{1,0:T(8,128)} %get-tuple-element.87) | copy-start | bytes 1179652
  183.2 7.6 %collective-permute-start.21 = (bf16[192,512]{1,0:T(8,128)(2,1)S(1)}, bf16[192,512]{1,0:T(8,128)(2,1)S(1)}, u32[]{:S(2)}, u32[]{:S(2)}) collective-permute-start(bf16[192,512]{1,0:T(8,128)(2,1)S(1)} %pad_maximum_fusion.7.refs_1_), channel_id=1, source_target_pairs={{0,96},{32,64},{64,32},{96,0},{1,97},{33,65},{65,33},{97,1},{2,98}... | collective-permute-start | bytes 589832 | tf_op jit(solution)/shard_map/ppermute | solution.py:31
  184.7 6.1 %collective-permute-start.23 = (bf16[192,512]{1,0:T(8,128)(2,1)S(1)}, bf16[192,512]{1,0:T(8,128)(2,1)S(1)}, u32[]{:S(2)}, u32[]{:S(2)}) collective-permute-start(bf16[192,512]{1,0:T(8,128)(2,1)S(1)} %pad_maximum_fusion.8.refs_3_), channel_id=1, source_target_pairs={{0,32},{32,0},{64,96},{96,64},{1,33},{33,1},{65,97},{97,65},{2,34}... | collective-permute-start | bytes 589832 | tf_op jit(solution)/shard_map/ppermute | solution.py:31
